TPU v7x, 32 devices: a whole 2x2x4 slice. The times are simulated.
32 devices in a mesh: row: 8 (over y, x, core), col: 4 (over z).
Axes of the slice: x: 2, y: 2, z: 4, core: 2. Of those that a mesh axis runs over, the one named last changes fastest.
Arguments:
- volume_plane: bfloat16 [2, 4096, 4096], P(None, 'row', 'col'), may hold values from -4 to 4
- wave_a: bfloat16 [2, 4096, 4096], P(None, 'row', 'col'), may hold values from -4 to 4
- wave_b: bfloat16 [2, 4096, 4096], P(None, 'col', 'row'), may hold values from -4 to 4
- shift_rows: int32 [2, 2, 4096], P(None, None, 'row'), may hold values from -864 to 864, as said below
- fraction_rows: float32 [2, 2, 4096], P(None, None, 'row'), may hold values from -0.5 to 0.5
- shift_columns: int32 [2, 4096], P(None, 'col'), may hold values from -1728 to 1728, as said below
- fraction_columns: float32 [2, 4096], P(None, 'col'), may hold values from -0.5 to 0.5
- travel_distance: float32 [2], replicated, may hold values from 16 to 32
Outputs:
- exit_a: bfloat16 [2, 4096, 4096], P(None, 'row', 'col')
- exit_b: bfloat16 [2, 4096, 4096], P(None, 'col', 'row')
Inputs may be any that keep to these rules, and one draw needn't show every extreme that they name: For view v, both shift_rows[v, 0] and shift_rows[v, 1] equal -s_v floor((2 r - 4095) m_v / 4095) for row r, with a sign s_v of 1 or -1 and a whole magnitude m_v from 432 to 864; m_0 = 864. shift_columns[v, c] = s_v floor((2 c - 4095) 2 m_v / 4095) with the s_v and m_v of shift_rows.
All inputs are finite; a program needn't handle non-finite values.
Results may differ from a plain program's by a relative error of at most 0.018.
Values may be sent and summed in bfloat16 or wider, within the bound.
No kernel may reach another device: no remote copies, remote signals or barrier semaphores. Data moves between devices by JAX's collectives and lax.ppermute only.
A program may use at most 64 MiB of HBM per device.

v0:
```python
import jax
import jax.numpy as jnp
from jax import lax
from jax.sharding import PartitionSpec as P

BLOCK = 128
MARGIN = 32
SHIFT_X = 864
SHIFT_Y = 1728


ABSORB = 0.25


def swapped(value, axis, bit):
    mask = 2**bit
    pairs = [(source, source ^ mask) for source in range(lax.axis_size(axis))]
    return lax.ppermute(value, axis, pairs)


def padded_2(x, sides, width):
    for axis, dim in sides:
        devices, length = (lax.axis_size(axis), x.shape[dim])
        up = [(i, (i + 1) % devices) for i in range(devices - 1)]
        down = [(j, i) for i, j in up]
        last = lax.slice_in_dim(x, length - width, length, axis=dim)
        first = lax.slice_in_dim(x, 0, width, axis=dim)
        before = lax.ppermute(last, axis, up)
        after = lax.ppermute(first, axis, down)
        x = jnp.concatenate([before, x, after], axis=dim)
    return x


def fourier_tables(block_len, margin):
    window_len = block_len + 2 * margin
    frequency = jnp.arange(window_len, dtype=jnp.int32) - window_len // 2
    position = jnp.arange(window_len, dtype=jnp.int32)
    angles = (
        2.0
        * jnp.pi
        * jnp.mod(position[:, None] * frequency[None, :], window_len).astype(jnp.float32)
        / window_len
    )
    cosine = jnp.cos(angles)
    sines = jnp.sin(angles)
    forward = jnp.concatenate(
        [jnp.concatenate([cosine, -sines], 1), jnp.concatenate([sines, cosine], 1)], 0
    ).astype(jnp.bfloat16)
    target = jnp.arange(block_len, dtype=jnp.int32) + margin
    inverse_angle = (
        2.0
        * jnp.pi
        * jnp.mod(frequency[:, None] * target[None, :], window_len).astype(jnp.float32)
        / window_len
    )
    inverse_cosine = jnp.cos(inverse_angle) / window_len
    inverse_sine = jnp.sin(inverse_angle) / window_len
    inverse = jnp.concatenate(
        [
            jnp.concatenate([inverse_cosine, inverse_sine], 1),
            jnp.concatenate([-inverse_sine, inverse_cosine], 1),
        ],
        0,
    ).astype(jnp.bfloat16)
    return (forward, inverse, frequency.astype(jnp.float32))


def shear_ramp(fractions, frequency):
    window_len = frequency.shape[0]
    phases = -2.0 * jnp.pi / window_len * fractions[:, None] * frequency[None, :]
    nyquist = (jnp.arange(window_len) == 0)[None, :]
    ramp_real = jnp.where(nyquist, jnp.cos(jnp.pi * fractions)[:, None], jnp.cos(phases))
    ramp_imaginary = jnp.where(nyquist, 0.0, jnp.sin(phases))
    return (ramp_real, ramp_imaginary)


def travel_ramp(distance, frequency):
    window_len = frequency.shape[0]
    phases = -2.0 * jnp.pi / (window_len * window_len) * distance * frequency * frequency
    return (jnp.cos(phases)[None, :], jnp.sin(phases)[None, :])


def select_window(padded, starts, out_len):
    total_len = padded.shape[2]
    offset_range = total_len - out_len
    bit_count = max(offset_range, 1).bit_length()
    current = jnp.pad(padded, ((0, 0), (0, 0), (0, out_len + 2**bit_count - 1 - total_len)))
    for bit_number in reversed(range(bit_count)):
        stride = 2**bit_number
        kept_len = current.shape[2] - stride
        chosen = (starts // stride % 2 == 1)[None, :, None]
        current = jnp.where(
            chosen, current[:, :, stride : stride + kept_len], current[:, :, :kept_len]
        )
    return current


def line_pass(padded, extent, shifts, ramp_real, ramp_imaginary, tables):
    forward, inverse = (tables[0], tables[1])
    window_len = BLOCK + 2 * MARGIN
    line_count = padded.shape[1]
    blocks = (padded.shape[2] - 2 * extent) // BLOCK
    reach_len = blocks * BLOCK + 2 * MARGIN
    if shifts is None:
        shifted = padded
    else:
        starts = extent - MARGIN - shifts
        shifted = select_window(padded, starts, reach_len)
    middle = shifted[:, :, MARGIN : MARGIN + blocks * BLOCK].reshape(2, line_count, blocks, BLOCK)
    left_rim = shifted[:, :, : blocks * BLOCK].reshape(2, line_count, blocks, BLOCK)[..., :MARGIN]
    right_rim = shifted[:, :, 2 * MARGIN : 2 * MARGIN + blocks * BLOCK].reshape(
        2, line_count, blocks, BLOCK
    )[..., BLOCK - MARGIN :]
    windows = jnp.concatenate([left_rim, middle, right_rim], 3)
    spectrum = jnp.einsum(
        "cpms,cst->pmt",
        windows,
        forward.reshape(2, window_len, 2 * window_len),
        preferred_element_type=jnp.float32,
    )
    spec_real = spectrum[..., :window_len]
    spec_imaginary = spectrum[..., window_len:]
    factor_real = ramp_real[:, None, :]
    factor_imaginary = ramp_imaginary[:, None, :]
    ramped = jnp.concatenate(
        [
            spec_real * factor_real - spec_imaginary * factor_imaginary,
            spec_real * factor_imaginary + spec_imaginary * factor_real,
        ],
        -1,
    ).astype(jnp.bfloat16)
    result = jnp.einsum(
        "pms,scb->cpmb",
        ramped,
        inverse.reshape(2 * window_len, 2, BLOCK),
        preferred_element_type=jnp.float32,
    )
    return result.reshape(2, line_count, blocks * BLOCK).astype(jnp.bfloat16)


def single_pass(padded, extent, shifts, fractions, tables):
    ramp_real, ramp_imaginary = shear_ramp(fractions, tables[2])
    return line_pass(padded, extent, shifts, ramp_real, ramp_imaginary, tables)


def shear_columns(stacked, shifts, fractions, tables):
    halo_depth = SHIFT_X + MARGIN
    inputs = stacked.shape[0]
    column_devices = lax.axis_size("col")
    share = stacked.shape[2] // column_devices
    offset = lax.axis_index("col") * share
    spread = lax.all_to_all(stacked, "col", split_axis=2, concat_axis=3, tiled=True)
    padded = jnp.pad(spread, ((0, 0), (0, 0), (0, 0), (halo_depth, halo_depth)))
    row_shifts = lax.dynamic_slice_in_dim(shifts, offset, share, 1)
    row_fractions = lax.dynamic_slice_in_dim(fractions, offset, share, 1)
    sheared = jnp.stack(
        [
            single_pass(
                padded[min(0, inputs - 1)], halo_depth, row_shifts[0], row_fractions[0], tables
            )
        ]
    )
    return lax.all_to_all(sheared, "col", split_axis=3, concat_axis=2, tiled=True)


def shear_along_first(padded_lines, halo_depth, shifts, fractions, tables):
    flipped = jnp.swapaxes(padded_lines[0], 1, 2)
    moved = single_pass(flipped, halo_depth, shifts[0], fractions[0], tables)
    sheared = [jnp.swapaxes(moved, 1, 2)]
    return jnp.stack(sheared)


def shear_rows_pass(stacked, shifts, fractions, tables):
    halo_depth = SHIFT_Y + MARGIN
    row_devices = lax.axis_size("row")
    share = stacked.shape[3] // row_devices
    offset = lax.axis_index("row") * share
    spread = lax.all_to_all(stacked, "row", split_axis=3, concat_axis=2, tiled=True)
    padded = jnp.pad(spread, ((0, 0), (0, 0), (halo_depth, halo_depth), (0, 0)))
    column_shifts = lax.dynamic_slice_in_dim(shifts, offset, share, 1)
    column_fractions = lax.dynamic_slice_in_dim(fractions, offset, share, 1)
    sheared = shear_along_first(padded, halo_depth, column_shifts, column_fractions, tables)
    return lax.all_to_all(sheared, "row", split_axis=2, concat_axis=3, tiled=True)


def travel_local(extended, distance, tables):
    ramp_real, ramp_imaginary = travel_ramp(distance, tables[2])
    halfway = line_pass(extended, MARGIN, None, ramp_real, ramp_imaginary, tables)
    flipped = jnp.swapaxes(halfway, 1, 2)
    finished = line_pass(flipped, MARGIN, None, ramp_real, ramp_imaginary, tables)
    return jnp.swapaxes(finished, 1, 2)


def transmit(rotated, wave):
    phase_part = rotated[0].astype(jnp.float32)
    absorb_part = rotated[1].astype(jnp.float32)
    amplitude = jnp.exp(-ABSORB * absorb_part)
    through_real = amplitude * jnp.cos(phase_part)
    through_imaginary = amplitude * jnp.sin(phase_part)
    wave_real = wave[0].astype(jnp.float32)
    wave_imaginary = wave[1].astype(jnp.float32)
    return jnp.stack(
        [
            wave_real * through_real - wave_imaginary * through_imaginary,
            wave_real * through_imaginary + wave_imaginary * through_real,
        ]
    ).astype(jnp.bfloat16)


def on_device(
    volume_plane,
    wave_a,
    wave_b,
    shift_rows,
    fraction_rows,
    shift_columns,
    fraction_columns,
    travel_distance,
):
    tables = fourier_tables(BLOCK, MARGIN)
    source = volume_plane[None]
    results = []
    for member in range(2):
        stacked = shear_columns(
            source,
            shift_rows[member : member + 1, 0],
            fraction_rows[member : member + 1, 0],
            tables,
        )
        stacked = shear_rows_pass(
            stacked,
            shift_columns[member : member + 1],
            fraction_columns[member : member + 1],
            tables,
        )
        stacked = shear_columns(
            stacked,
            shift_rows[member : member + 1, 1],
            fraction_rows[member : member + 1, 1],
            tables,
        )
        results.append(stacked[0])
    view_one = results[0]
    view_two = results[1]
    turned = jnp.swapaxes(jnp.flip(view_two, 2), 1, 2)
    for bit_number in range(lax.axis_size("col").bit_length() - 1):
        turned = swapped(turned, "col", bit_number)
    product_a = transmit(view_one, wave_a)
    extended_a = padded_2(product_a, (("row", 1), ("col", 2)), MARGIN)
    exit_a = travel_local(extended_a, travel_distance[0], tables)
    product_b = transmit(turned, wave_b)
    extended_b = padded_2(product_b, (("row", 2), ("col", 1)), MARGIN)
    exit_b = travel_local(extended_b, travel_distance[1], tables)
    return (exit_a, exit_b)


def solution(mesh):
    return jax.shard_map(
        on_device,
        mesh=mesh,
        in_specs=(
            P(None, "row", "col"),
            P(None, "row", "col"),
            P(None, "col", "row"),
            P(None, None, "row"),
            P(None, None, "row"),
            P(None, "col"),
            P(None, "col"),
            P(),
        ),
        out_specs=(P(None, "row", "col"), P(None, "col", "row")),
        check_vma=False,
    )
```

profile of v0, /device:TPU:2, one launch (start us, length us, event | category | flops | bytes accessed | tf_op | source)
XLA Modules:
  0.0 776.6 jit_solution(14873800142890445674)
XLA Ops:
  0.6 5.1 copy.423
  5.7 5.0 all-to-all-start
  21.3 37.6 %all-to-all-done = bf16[1,2,512,1024]{3,1,0,2:T(2,128)(2,1)S(1)} async-done(((bf16[1,2,512,1024]{3,1,0,2:T(2,128)(2,1)}), bf16[1,2,512,1024]{3,1,0,2:T(2,128)(2,1)S(1)}, u32[]{:S(2)}, u32[]{:S(2)}) %all-to-all-start) | async-done | bytes 2097184 | tf_op jit(solution)/shard_map/all_to_all | solution.py:152
  78.1 18.3 %copy.315 = bf16[1,2,128,4096]{2,1,0,3:T(2,128)(2,1)} copy(bf16[1,2,128,4096]{2,3,1,0:T(8,128)(2,1)S(1)} %bitcast.460) | data formatting | bytes 4194304 | tf_op jit(solution)/shard_map/convert_element_type | solution.py:138
  96.4 4.5 all-to-all-start.6
  113.6 18.5 %copy.281 = bf16[1,2,128,4096]{2,1,0,3:T(2,128)(2,1)} copy(bf16[1,2,128,4096]{2,3,1,0:T(8,128)(2,1)S(1)} %bitcast.461) | data formatting | bytes 4194304 | tf_op jit(solution)/shard_map/convert_element_type | solution.py:138
  132.1 16.5 %all-to-all-done.6 = bf16[1,2,128,4096]{2,1,0,3:T(2,128)(2,1)} async-done(((bf16[1,2,128,4096]{2,1,0,3:T(2,128)(2,1)}), bf16[1,2,128,4096]{2,1,0,3:T(2,128)(2,1)}, u32[]{:S(2)}, u32[]{:S(2)}) %all-to-all-start.6) | async-done | bytes 2097184 | tf_op jit(solution)/shard_map/all_to_all | solution.py:163
  159.4 6.2 copy.318
  165.6 34.4 %all-to-all-done.1 = bf16[1,2,128,4096]{2,1,0,3:T(2,128)(2,1)S(1)} async-done(((bf16[1,2,128,4096]{2,1,0,3:T(2,128)(2,1)}), bf16[1,2,128,4096]{2,1,0,3:T(2,128)(2,1)S(1)}, u32[]{:S(2)}, u32[]{:S(2)}) %all-to-all-start.1) | async-done | bytes 2097184 | tf_op jit(solution)/shard_map/all_to_all | solution.py:163
  199.9 4.8 all-to-all-start.7
  214.0 15.9 %all-to-all-done.7 = bf16[1,2,512,1024]{2,1,0,3:T(2,128)(2,1)} async-done(((bf16[1,2,512,1024]{2,1,0,3:T(2,128)(2,1)}), bf16[1,2,512,1024]{2,1,0,3:T(2,128)(2,1)}, u32[]{:S(2)}, u32[]{:S(2)}) %all-to-all-start.7) | async-done | bytes 2097184 | tf_op jit(solution)/shard_map/all_to_all | solution.py:178
  230.0 6.0 all-to-all-start.2
  252.6 18.3 %copy.421 = bf16[2,128,4096]{1,0,2:T(2,128)(2,1)} copy(bf16[2,128,4096]{1,2,0:T(8,128)(2,1)S(1)} %bitcast.462) | data formatting | bytes 4194304 | tf_op jit(solution)/shard_map/convert_element_type | solution.py:138
  291.8 18.5 %copy.422 = bf16[2,128,4096]{1,0,2:T(2,128)(2,1)} copy(bf16[2,128,4096]{1,2,0:T(8,128)(2,1)S(1)} %bitcast.463) | data formatting | bytes 4194304 | tf_op jit(solution)/shard_map/convert_element_type | solution.py:138
  321.7 6.2 copy.327
  327.9 11.7 %all-to-all-done.3 = bf16[1,2,4096,128]{3,1,0,2:T(2,128)(2,1)S(1)} async-done(((bf16[1,2,4096,128]{3,1,0,2:T(2,128)(2,1)}), bf16[1,2,4096,128]{3,1,0,2:T(2,128)(2,1)S(1)}, u32[]{:S(2)}, u32[]{:S(2)}) %all-to-all-start.3) | async-done | bytes 2097184 | tf_op jit(solution)/shard_map/all_to_all | solution.py:183
  339.7 4.5 all-to-all-start.9
  353.4 39.5 %all-to-all-done.9 = bf16[1,2,512,1024]{3,1,0,2:T(2,128)(2,1)} async-done(((bf16[1,2,512,1024]{3,1,0,2:T(2,128)(2,1)}), bf16[1,2,512,1024]{3,1,0,2:T(2,128)(2,1)}, u32[]{:S(2)}, u32[]{:S(2)}) %all-to-all-start.9) | async-done | bytes 2097184 | tf_op jit(solution)/shard_map/all_to_all | solution.py:152
  415.6 18.5 %copy.333 = bf16[1,2,128,4096]{2,1,0,3:T(2,128)(2,1)} copy(bf16[1,2,128,4096]{2,3,1,0:T(8,128)(2,1)S(1)} %bitcast.464) | data formatting | bytes 4194304 | tf_op jit(solution)/shard_map/convert_element_type | solution.py:138
  434.1 10.4 %all-to-all-done.4 = bf16[1,2,512,1024]{3,1,0,2:T(2,128)(2,1)S(1)} async-done(((bf16[1,2,512,1024]{3,1,0,2:T(2,128)(2,1)}), bf16[1,2,512,1024]{3,1,0,2:T(2,128)(2,1)S(1)}, u32[]{:S(2)}, u32[]{:S(2)}) %all-to-all-start.4) | async-done | bytes 2097184 | tf_op jit(solution)/shard_map/all_to_all | solution.py:152
  468.4 18.3 %copy.299 = bf16[1,2,128,4096]{2,1,0,3:T(2,128)(2,1)} copy(bf16[1,2,128,4096]{2,3,1,0:T(8,128)(2,1)S(1)} %bitcast.465) | data formatting | bytes 4194304 | tf_op jit(solution)/shard_map/convert_element_type | solution.py:138
  486.7 10.4 %all-to-all-done.10 = bf16[1,2,128,4096]{2,1,0,3:T(2,128)(2,1)S(1)} async-done(((bf16[1,2,128,4096]{2,1,0,3:T(2,128)(2,1)}), bf16[1,2,128,4096]{2,1,0,3:T(2,128)(2,1)S(1)}, u32[]{:S(2)}, u32[]{:S(2)}) %all-to-all-start.10) | async-done | bytes 2097184 | tf_op jit(solution)/shard_map/all_to_all | solution.py:163
  507.3 20.3 %rev.4 = bf16[2,512,1024]{1,2,0:T(8,128)(2,1)} reverse(bf16[2,512,1024]{1,2,0:T(8,128)(2,1)S(1)} %squeeze.17), dimensions={2} | reverse | bytes 4194304 | tf_op jit(solution)/shard_map/jit(_flip)/rev | solution.py:245
  529.6 19.9 %all-to-all-done.5 = bf16[1,2,128,4096]{2,1,0,3:T(2,128)(2,1)} async-done(((bf16[1,2,128,4096]{2,1,0,3:T(2,128)(2,1)}), bf16[1,2,128,4096]{2,1,0,3:T(2,128)(2,1)}, u32[]{:S(2)}, u32[]{:S(2)}) %all-to-all-start.5) | async-done | bytes 2097184 | tf_op jit(solution)/shard_map/all_to_all | solution.py:163
  549.4 4.7 copy.301
  554.2 7.7 fusion.124
  574.6 11.6 %collective-permute-done.2 = bf16[2,576,32]{2,1,0:T(8,128)(2,1)S(1)} collective-permute-done((bf16[2,576,32]{2,1,0:T(8,128)(2,1)S(1)}, bf16[2,576,32]{2,1,0:T(8,128)(2,1)S(1)}, u32[]{:S(2)}, u32[]{:S(2)}) %collective-permute-start.2) | collective-permute-done | bytes 73760 | tf_op jit(solution)/shard_map/ppermute | solution.py:28
  586.2 4.8 collective-permute-done.3
  591.0 5.9 pad_maximum_fusion.6
  600.6 5.3 fusion.91
  615.8 75.0 %collective-permute-done.5 = bf16[2,1024,512]{2,1,0:T(8,128)(2,1)S(1)} collective-permute-done((bf16[2,1024,512]{2,1,0:T(8,128)(2,1)}, bf16[2,1024,512]{2,1,0:T(8,128)(2,1)S(1)}, u32[]{:S(2)}, u32[]{:S(2)}) %collective-permute-start.5) | collective-permute-done | bytes 2097184 | tf_op jit(solution)/shard_map/ppermute | solution.py:18
  690.8 8.5 %fusion.127 = (bf16[1,1024,512]{2,1,0:T(8,128)(2,1)S(1)}, bf16[1,1024,512]{2,1,0:T(8,128)(2,1)S(1)}) fusion(bf16[2,1024,512]{2,1,0:T(8,128)(2,1)S(1)} %collective-permute-done.5, bf16[2,1024,512]{2,1,0:T(8,128)(2,1)S(1)} %copy-done.2), kind=kLoop, calls=%fused_computation.239 | loop fusion | flops 7864320 | bytes 6291456 | tf_op jit(solution)/shard_map/convert.4
  (334 shorter events, 279.8 us)
Async XLA Ops:
  5.7 5.1 copy-start.20
  5.7 5.2 copy-start.21
  5.7 5.3 copy-start.22
  5.7 5.9 copy-start.23
  5.7 53.2 %all-to-all-start = ((bf16[1,2,512,1024]{3,1,0,2:T(2,128)(2,1)}), bf16[1,2,512,1024]{3,1,0,2:T(2,128)(2,1)S(1)}, u32[]{:S(2)}, u32[]{:S(2)}) async-start(bf16[1,2,512,1024]{3,1,0,2:T(2,128)(2,1)} %bitcast.412), calls=%async_computation | async-start | bytes 4194304 | tf_op jit(solution)/shard_map/all_to_all | solution.py:152
  96.4 52.2 %all-to-all-start.6 = ((bf16[1,2,128,4096]{2,1,0,3:T(2,128)(2,1)}), bf16[1,2,128,4096]{2,1,0,3:T(2,128)(2,1)}, u32[]{:S(2)}, u32[]{:S(2)}) async-start(bf16[1,2,128,4096]{2,1,0,3:T(2,128)(2,1)} %copy.315), calls=%async_computation.6 | async-start | bytes 4194304 | tf_op jit(solution)/shard_map/all_to_all | solution.py:163
  148.7 51.3 %all-to-all-start.1 = ((bf16[1,2,128,4096]{2,1,0,3:T(2,128)(2,1)}), bf16[1,2,128,4096]{2,1,0,3:T(2,128)(2,1)S(1)}, u32[]{:S(2)}, u32[]{:S(2)}) async-start(bf16[1,2,128,4096]{2,1,0,3:T(2,128)(2,1)} %copy.281), calls=%async_computation.1 | async-start | bytes 4194304 | tf_op jit(solution)/shard_map/all_to_all | solution.py:163
  165.6 39.1 %copy-start.26 = (s32[1,1,512]{2,1,0:T(1,128)S(1)}, s32[1,1,512]{2,1,0:T(1,128)}, u32[]{:S(2)}) copy-start(s32[1,1,512]{2,1,0:T(1,128)} %get-tuple-element.103) | copy-start | bytes 6148
  199.9 30.0 %all-to-all-start.7 = ((bf16[1,2,512,1024]{2,1,0,3:T(2,128)(2,1)}), bf16[1,2,512,1024]{2,1,0,3:T(2,128)(2,1)}, u32[]{:S(2)}, u32[]{:S(2)}) async-start(bf16[1,2,512,1024]{2,1,0,3:T(2,128)(2,1)} %copy.318), calls=%async_computation.7 | async-start | bytes 4194304 | tf_op jit(solution)/shard_map/all_to_all | solution.py:178
  230.0 40.9 %all-to-all-start.2 = ((bf16[1,2,512,1024]{2,1,0,3:T(2,128)(2,1)}), bf16[1,2,512,1024]{2,1,0,3:T(2,128)(2,1)}, u32[]{:S(2)}, u32[]{:S(2)}) async-start(bf16[1,2,512,1024]{2,1,0,3:T(2,128)(2,1)} %copy.284), calls=%async_computation.2 | async-start | bytes 4194304 | tf_op jit(solution)/shard_map/all_to_all | solution.py:178
  270.9 39.4 %all-to-all-start.8 = ((bf16[1,2,4096,128]{3,1,0,2:T(2,128)(2,1)}), bf16[1,2,4096,128]{3,1,0,2:T(2,128)(2,1)}, u32[]{:S(2)}, u32[]{:S(2)}) async-start(bf16[1,2,4096,128]{3,1,0,2:T(2,128)(2,1)} %bitcast.389), calls=%async_computation.8 | async-start | bytes 4194304 | tf_op jit(solution)/shard_map/all_to_all | solution.py:183
  310.3 29.3 %all-to-all-start.3 = ((bf16[1,2,4096,128]{3,1,0,2:T(2,128)(2,1)}), bf16[1,2,4096,128]{3,1,0,2:T(2,128)(2,1)S(1)}, u32[]{:S(2)}, u32[]{:S(2)}) async-start(bf16[1,2,4096,128]{3,1,0,2:T(2,128)(2,1)} %bitcast.414), calls=%async_computation.3 | async-start | bytes 4194304 | tf_op jit(solution)/shard_map/all_to_all | solution.py:183
  327.9 16.2 %copy-start.24 = (s32[128]{0:T(128)S(1)}, s32[128]{0:T(128)}, u32[]{:S(2)}) copy-start(s32[128]{0:T(128)} %get-tuple-element.211) | copy-start | bytes 1540
  327.9 16.2 %copy-start.25 = (pred[128]{0:T(512)(128)(4,1)S(1)}, pred[128]{0:T(512)(128)(4,1)}, u32[]{:S(2)}) copy-start(pred[128]{0:T(512)(128)(4,1)} %get-tuple-element.212) | copy-start | bytes 388
  339.7 53.2 %all-to-all-start.9 = ((bf16[1,2,512,1024]{3,1,0,2:T(2,128)(2,1)}), bf16[1,2,512,1024]{3,1,0,2:T(2,128)(2,1)}, u32[]{:S(2)}, u32[]{:S(2)}) async-start(bf16[1,2,512,1024]{3,1,0,2:T(2,128)(2,1)} %copy.327), calls=%async_computation.9 | async-start | bytes 4194304 | tf_op jit(solution)/shard_map/all_to_all | solution.py:152
  392.9 51.6 %all-to-all-start.4 = ((bf16[1,2,512,1024]{3,1,0,2:T(2,128)(2,1)}), bf16[1,2,512,1024]{3,1,0,2:T(2,128)(2,1)S(1)}, u32[]{:S(2)}, u32[]{:S(2)}) async-start(bf16[1,2,512,1024]{3,1,0,2:T(2,128)(2,1)} %copy.293), calls=%async_computation.4 | async-start | bytes 4194304 | tf_op jit(solution)/shard_map/all_to_all | solution.py:152
  445.9 51.3 %all-to-all-start.10 = ((bf16[1,2,128,4096]{2,1,0,3:T(2,128)(2,1)}), bf16[1,2,128,4096]{2,1,0,3:T(2,128)(2,1)S(1)}, u32[]{:S(2)}, u32[]{:S(2)}) async-start(bf16[1,2,128,4096]{2,1,0,3:T(2,128)(2,1)} %copy.333), calls=%async_computation.10 | async-start | bytes 4194304 | tf_op jit(solution)/shard_map/all_to_all | solution.py:163
  497.1 52.3 %all-to-all-start.5 = ((bf16[1,2,128,4096]{2,1,0,3:T(2,128)(2,1)}), bf16[1,2,128,4096]{2,1,0,3:T(2,128)(2,1)}, u32[]{:S(2)}, u32[]{:S(2)}) async-start(bf16[1,2,128,4096]{2,1,0,3:T(2,128)(2,1)} %copy.299), calls=%async_computation.5 | async-start | bytes 4194304 | tf_op jit(solution)/shard_map/all_to_all | solution.py:163
  527.6 71.3 %collective-permute-start.4 = (bf16[2,1024,512]{2,1,0:T(8,128)(2,1)}, bf16[2,1024,512]{2,1,0:T(8,128)(2,1)}, u32[]{:S(2)}, u32[]{:S(2)}) collective-permute-start(bf16[2,1024,512]{2,1,0:T(8,128)(2,1)} %bitcast.458), channel_id=1, source_target_pairs={{0,1},{1,0},{2,3},{3,2},{4,5},{5,4},{6,7},{7,6},{8,9},{9,8},{10,11... | collective-permute-start | bytes 6291464 | tf_op jit(solution)/shard_map/ppermute | solution.py:18
  554.2 7.8 copy-start.3
  562.8 5.6 copy-start.48
  562.8 7.6 collective-permute-start
  564.7 6.1 collective-permute-start.1
  571.3 14.9 %collective-permute-start.2 = (bf16[2,576,32]{2,1,0:T(8,128)(2,1)S(1)}, bf16[2,576,32]{2,1,0:T(8,128)(2,1)S(1)}, u32[]{:S(2)}, u32[]{:S(2)}) collective-permute-start(bf16[2,576,32]{2,1,0:T(8,128)(2,1)S(1)} %get-tuple-element.71), channel_id=1, source_target_pairs={{0,1},{1,2},{2,3},{4,5},{5,6},{6,7},{8,9},{9,10},{10,11},{12,13},{... | collective-permute-start | bytes 221192 | tf_op jit(solution)/shard_map/ppermute | solution.py:28
  572.6 18.4 %collective-permute-start.3 = (bf16[2,576,32]{2,1,0:T(8,128)(2,1)S(1)}, bf16[2,576,32]{2,1,0:T(8,128)(2,1)S(1)}, u32[]{:S(2)}, u32[]{:S(2)}) collective-permute-start(bf16[2,576,32]{2,1,0:T(8,128)(2,1)S(1)} %get-tuple-element.72), channel_id=1, source_target_pairs={{1,0},{2,1},{3,2},{5,4},{6,5},{7,6},{9,8},{10,9},{11,10},{13,12},{... | collective-permute-start | bytes 221192 | tf_op jit(solution)/shard_map/ppermute | solution.py:29
  598.9 91.9 %collective-permute-start.5 = (bf16[2,1024,512]{2,1,0:T(8,128)(2,1)}, bf16[2,1024,512]{2,1,0:T(8,128)(2,1)S(1)}, u32[]{:S(2)}, u32[]{:S(2)}) collective-permute-start(bf16[2,1024,512]{2,1,0:T(8,128)(2,1)} %collective-permute-done.4), channel_id=1, source_target_pairs={{0,2},{1,3},{2,0},{3,1},{4,6},{5,7},{6,4},{7,5},{8,10},{9,11},{10,... | collective-permute-start | bytes 6291464 | tf_op jit(solution)/shard_map/ppermute | solution.py:18
  613.1 77.7 %copy-start.2 = (bf16[2,1024,512]{2,1,0:T(8,128)(2,1)S(1)}, bf16[2,1024,512]{2,1,0:T(8,128)(2,1)}, u32[]{:S(2)}) copy-start(bf16[2,1024,512]{2,1,0:T(8,128)(2,1)} %param.10) | copy-start | bytes 6291460
  699.6 10.5 %collective-permute-start.6 = (bf16[2,1024,32]{2,1,0:T(8,128)(2,1)S(1)}, bf16[2,1024,32]{2,1,0:T(8,128)(2,1)S(1)}, u32[]{:S(2)}, u32[]{:S(2)}) collective-permute-start(bf16[2,1024,32]{2,1,0:T(8,128)(2,1)S(1)} %get-tuple-element.91), channel_id=1, source_target_pairs={{0,4},{4,8},{8,12},{12,16},{16,20},{20,24},{24,28},{1,5},{5,9},{9,... | collective-permute-start | bytes 393224 | tf_op jit(solution)/shard_map/ppermute | solution.py:28
  701.5 11.0 %collective-permute-start.7 = (bf16[2,1024,32]{2,1,0:T(8,128)(2,1)S(1)}, bf16[2,1024,32]{2,1,0:T(8,128)(2,1)S(1)}, u32[]{:S(2)}, u32[]{:S(2)}) collective-permute-start(bf16[2,1024,32]{2,1,0:T(8,128)(2,1)S(1)} %get-tuple-element.92), channel_id=1, source_target_pairs={{4,0},{8,4},{12,8},{16,12},{20,16},{24,20},{28,24},{5,1},{9,5},{13... | collective-permute-start | bytes 393224 | tf_op jit(solution)/shard_map/ppermute | solution.py:29
  712.7 5.9 collective-permute-start.8
  714.6 6.3 collective-permute-start.9
  760.9 5.4 copy-start.1
  (42 other events, 48.9 us)
where the time goes:
time: 787 us; the launch traced here: 777 us
  waiting for transfers between devices  297 us (38%)
  local copies, waits for them, and re-layouts  282 us (36%)
  other arithmetic  78.3 us (10%)
  starting transfers between devices  69.3 us (9%)
  matrix products  46.5 us (6%)
    convert_element_type x8, local copies, waits for them, and re-layouts, line_pass(): return result.reshape(2, line_count, blocks * BLOCK).astype(jnp.bfloat16)  114 us
    all_to_all x3, waiting for transfers between devices, shear_columns(): lax.all_to_all(stacked, 'col', split_axis=2, concat_axis=3, tiled=True)  87.5 us
    all_to_all x4, waiting for transfers between devices, shear_columns(): lax.all_to_all(sheared, 'col', split_axis=3, concat_axis=2, tiled=True)  81.2 us
    ppermute x2, waiting for transfers between devices, swapped(): return lax.ppermute(value, axis, pairs)  75 us
    all_to_all x8, local copies, waits for them, and re-layouts, shear_columns(): lax.all_to_all(sheared, 'col', split_axis=3, concat_axis=2, tiled=True)  29.6 us
    dot_general x10, matrix products, line_pass(): jnp.einsum('cpms,cst->pmt', windows, forward.reshape(2, window_len, 2 * w...  28.5 us
    another operation x14, other arithmetic  27.7 us
    slice x20, local copies, waits for them, and re-layouts, line_pass(): shifted[:, :, :blocks * BLOCK].reshape(2, line_count, blocks, BLOCK)  22.2 us
  transfers between devices with their start and end apart: 21, of which 16 were waited for; matrix products, arithmetic and copies ran while one was open for 38% of the time, Pallas kernels for 0%

commit v1 on v0

--- a/solution.py
+++ b/solution.py
@@ -1,6 +1,11 @@
+import functools
+
 import jax
 import jax.numpy as jnp
+import numpy as np
 from jax import lax
+from jax.experimental import pallas as pl
+from jax.experimental.pallas import tpu as pltpu
 from jax.sharding import PartitionSpec as P
 
 BLOCK = 128
@@ -10,6 +15,665 @@
 
 
 ABSORB = 0.25
+
+WINDOW = BLOCK + 2 * MARGIN
+BINS = WINDOW // 2
+GROUP = 16
+VMEM_LIMIT = 56 * 1024 * 1024
+
+
+def angle_table(rows, columns):
+    return 2.0 * np.pi * (np.outer(rows, columns) % WINDOW) / WINDOW
+
+
+def real_tables():
+    position = np.arange(WINDOW)
+    bins = np.arange(BINS + 1)
+    target = np.arange(BLOCK) + MARGIN
+    forward = np.zeros((2 * BLOCK, 2 * BLOCK), np.float32)
+    forward[:WINDOW, : BINS + 1] = np.cos(angle_table(position, bins))
+    forward[:WINDOW, BLOCK + 1 : BLOCK + BINS] = -np.sin(angle_table(position, bins[1:BINS]))
+    weight = np.where((bins == 0) | (bins == BINS), 1.0, 2.0) / WINDOW
+    inverse = np.zeros((2 * BLOCK, BLOCK), np.float32)
+    inverse[: BINS + 1] = np.cos(angle_table(bins, target)) * weight[:, None]
+    inverse[BLOCK + 1 : BLOCK + BINS] = (
+        -np.sin(angle_table(bins[1:BINS], target)) * weight[1:BINS, None]
+    )
+    return forward, inverse
+
+
+def shear_phase(fractions):
+    frequency = jnp.arange(BLOCK, dtype=jnp.float32)
+    phases = -2.0 * jnp.pi / WINDOW * fractions[:, None] * frequency[None, :]
+    return jnp.cos(phases), jnp.sin(phases)
+
+
+def travel_matrices(distance, forward, inverse):
+    frequency = jnp.arange(BLOCK, dtype=jnp.float32)
+    phases = -2.0 * jnp.pi / (WINDOW * WINDOW) * distance[:, None] * frequency * frequency
+    ramps = jnp.stack([jnp.cos(phases), jnp.sin(phases)], 1)
+    ramps = jnp.concatenate([ramps, ramps], 2)
+    scaled = ramps[..., None] * jnp.asarray(inverse)
+    matrices = jnp.einsum(
+        "pq,vrqu->vrpu",
+        jnp.asarray(forward[:WINDOW]),
+        scaled,
+        precision=lax.Precision.HIGHEST,
+    )
+    return matrices
+
+
+def lane_iota(rows):
+    return lax.broadcasted_iota(jnp.int32, (rows, BLOCK), 1)
+
+
+def shift_lines(strip, shifted, base, base_offset, spare, windows, chunk_offset, rows):
+    def one_group(group, carry):
+        first = pl.multiple_of(group * GROUP, GROUP)
+        lines = pl.ds(first, GROUP)
+        start = base[base_offset + group] + chunk_offset
+        offset = spare[lines, :]
+        later = offset >= BLOCK
+        lane = lane_iota(GROUP) + (offset & (BLOCK - 1))
+        wraps = lane >= BLOCK
+        index = lane & (BLOCK - 1)
+        for part in range(2):
+            here = strip[start, part, lines, :].astype(jnp.float32)
+            before = None
+            for i in range(windows + 2):
+                following = strip[start + i + 1, part, lines, :].astype(jnp.float32)
+                turned = jnp.take_along_axis(jnp.where(later, following, here), index, axis=1)
+                if before is not None:
+                    shifted[i - 1, part, lines, :] = jnp.where(wraps, turned, before).astype(
+                        jnp.bfloat16
+                    )
+                before = turned
+                here = following
+        return carry
+
+    lax.fori_loop(0, rows // GROUP, one_group, 0)
+
+
+def ramped_lines(shifted, first, count, rows, cosine, sine, forward):
+    lower = shifted[first : first + count].reshape(count * 2 * rows, BLOCK)
+    upper = shifted[first + 1 : first + 1 + count].reshape(count * 2 * rows, BLOCK)
+    spectrum = jnp.dot(
+        jnp.concatenate([lower, upper], 1), forward[...], preferred_element_type=jnp.float32
+    )
+    real = spectrum[:, :BLOCK].reshape(count * 2, rows, BLOCK)
+    imaginary = spectrum[:, BLOCK:].reshape(count * 2, rows, BLOCK)
+    ramp_real = cosine[...][None]
+    ramp_imaginary = sine[...][None]
+    ramped = jnp.concatenate(
+        [
+            (real * ramp_real - imaginary * ramp_imaginary).astype(jnp.bfloat16),
+            (real * ramp_imaginary + imaginary * ramp_real).astype(jnp.bfloat16),
+        ],
+        2,
+    )
+    return ramped.reshape(count * 2 * rows, 2 * BLOCK)
+
+
+def shear_tile_kernel(
+    views, halo, tiles, rows, batch, wide, left_chunks, right_chunks, base, *refs
+):
+    lefts, refs = refs[: len(left_chunks)], refs[len(left_chunks) :]
+    rights, refs = refs[: len(right_chunks)], refs[len(right_chunks) :]
+    own, spare, cosine, sine, forward, inverse = refs[:6]
+    outs, (strip, shifted) = refs[6 : 6 + views], refs[6 + views :]
+    step = pl.program_id(0)
+    groups = rows // GROUP
+    end = halo + tiles + halo
+
+    @pl.when(step == 0)
+    def _():
+        strip[end : end + 2] = jnp.zeros((2, 2, rows, BLOCK), jnp.bfloat16)
+
+    def fill(piece, first, count):
+        for i in range(count):
+            if wide:
+                strip[first + i] = piece[:, :, i * BLOCK : (i + 1) * BLOCK]
+            else:
+                strip[first + i] = piece[i]
+
+    for piece, (near, far) in zip(lefts, left_chunks):
+        fill(piece, halo - far, far - near + 1)
+    for piece, (near, far) in zip(rights, right_chunks):
+        fill(piece, halo + tiles + near - 1, far - near + 1)
+    fill(own, halo, tiles)
+    for view in range(views):
+        steps = base.shape[0] // (views * groups)
+        offset = (view * steps + step) * groups
+        shift_lines(strip, shifted, base, offset, spare.at[view], tiles, 0, rows)
+        for first in range(0, tiles, batch):
+            ramped = ramped_lines(
+                shifted, first, batch, rows, cosine.at[view], sine.at[view], forward
+            )
+            result = jnp.dot(ramped, inverse[...], preferred_element_type=jnp.float32)
+            outs[view][first : first + batch] = result.astype(jnp.bfloat16).reshape(
+                batch, 2, rows, BLOCK
+            )
+
+
+def shear_tile(own, lefts, rights, left_chunks, right_chunks, halo, base, spare, ramps, tables):
+    wide = own.ndim == 3
+    line_count = own.shape[-2]
+    tiles = own.shape[2] // BLOCK if wide else own.shape[0]
+    views = spare.shape[0]
+    rows = BLOCK
+    forward, inverse = tables
+    cosine, sine = ramps
+
+    def piece_spec(piece):
+        if wide:
+            return pl.BlockSpec((2, rows, piece.shape[2]), lambda i, *_: (0, i, 0))
+        return pl.BlockSpec((piece.shape[0], 2, rows, BLOCK), lambda i, *_: (0, 0, i, 0))
+
+    line_spec = pl.BlockSpec((views, rows, BLOCK), lambda i, *_: (0, i, 0))
+    out_shape = jax.ShapeDtypeStruct((tiles, 2, line_count, BLOCK), jnp.bfloat16)
+    out_spec = pl.BlockSpec((tiles, 2, rows, BLOCK), lambda i, *_: (0, 0, i, 0))
+    kernel = functools.partial(
+        shear_tile_kernel,
+        views,
+        halo,
+        tiles,
+        rows,
+        tiles // 2 if tiles % 2 == 0 else tiles,
+        wide,
+        left_chunks,
+        right_chunks,
+    )
+    return pl.pallas_call(
+        kernel,
+        grid_spec=pltpu.PrefetchScalarGridSpec(
+            num_scalar_prefetch=1,
+            grid=(line_count // rows,),
+            in_specs=[piece_spec(p) for p in (*lefts, *rights, own)]
+            + [line_spec] * 3
+            + [
+                pl.BlockSpec(forward.shape, lambda i, *_: (0, 0)),
+                pl.BlockSpec(inverse.shape, lambda i, *_: (0, 0)),
+            ],
+            out_specs=[out_spec] * views,
+            scratch_shapes=[
+                pltpu.VMEM((halo + tiles + halo + 2, 2, rows, BLOCK), jnp.bfloat16),
+                pltpu.VMEM((tiles + 1, 2, rows, BLOCK), jnp.bfloat16),
+            ],
+        ),
+        out_shape=[out_shape] * views,
+        compiler_params=pltpu.CompilerParams(vmem_limit_bytes=VMEM_LIMIT),
+        name="shear_tile",
+    )(base.reshape(-1), *lefts, *rights, own, spare, cosine, sine, forward, inverse)
+
+
+def shear_whole_kernel(
+    halo, devices, tiles, rows, base, own, spare, cosine, sine, forward, flipped, out, strip, shifted
+):
+    step = pl.program_id(0)
+    chunks = devices * tiles
+    length = tiles * BLOCK
+
+    @pl.when(step == 0)
+    def _():
+        strip[0:halo] = jnp.zeros((halo, 2, rows, BLOCK), jnp.bfloat16)
+        strip[halo + chunks :] = jnp.zeros((halo + 2, 2, rows, BLOCK), jnp.bfloat16)
+        for chunk in range(chunks):
+            strip[halo + chunk] = own[chunk % tiles, chunk // tiles]
+        out[0, :, 0:MARGIN, :] = jnp.zeros((2, MARGIN, rows), jnp.bfloat16)
+        out[devices - 1, :, MARGIN + length :, :] = jnp.zeros((2, MARGIN, rows), jnp.bfloat16)
+
+    shift_lines(strip, shifted, base, 0, spare, tiles, step * tiles, rows)
+    ramped = ramped_lines(shifted, 0, tiles, rows, cosine, sine, forward)
+    target = devices - 1 - step
+    for window in range(tiles):
+        lines = ramped[window * 2 * rows : (window + 1) * 2 * rows]
+        result = lax.dot_general(
+            flipped[...], lines, (((1,), (1,)), ((), ())), preferred_element_type=jnp.float32
+        ).astype(jnp.bfloat16)
+        block = tiles - 1 - window
+        low = MARGIN + block * BLOCK
+        for part in range(2):
+            piece = result[:, part * rows : (part + 1) * rows]
+            out[target, part, low : low + BLOCK, :] = piece
+            if block == 0:
+
+                @pl.when(target > 0)
+                def _():
+                    out[target - 1, part, MARGIN + length :, :] = piece[:MARGIN]
+
+            if block == tiles - 1:
+
+                @pl.when(target < devices - 1)
+                def _():
+                    out[target + 1, part, 0:MARGIN, :] = piece[BLOCK - MARGIN :]
+
+
+def shear_whole(own, halo, base, spare, ramps, tables):
+    tiles, devices, _, rows, _ = own.shape
+    forward, flipped = tables
+    cosine, sine = ramps
+    full = lambda shape: pl.BlockSpec(shape, lambda i, *_: (0,) * len(shape))
+    out = (devices, 2, tiles * BLOCK + 2 * MARGIN, rows)
+    return pl.pallas_call(
+        functools.partial(shear_whole_kernel, halo, devices, tiles, rows),
+        grid_spec=pltpu.PrefetchScalarGridSpec(
+            num_scalar_prefetch=1,
+            grid=(devices,),
+            in_specs=[
+                full(x.shape) for x in (own, spare, cosine, sine, forward, flipped)
+            ],
+            out_specs=full(out),
+            scratch_shapes=[
+                pltpu.VMEM((2 * halo + devices * tiles + 2, 2, rows, BLOCK), jnp.bfloat16),
+                pltpu.VMEM((tiles + 1, 2, rows, BLOCK), jnp.bfloat16),
+            ],
+        ),
+        out_shape=jax.ShapeDtypeStruct(out, jnp.bfloat16),
+        compiler_params=pltpu.CompilerParams(vmem_limit_bytes=VMEM_LIMIT),
+        name="shear_whole",
+    )(base, own, spare, cosine, sine, forward, flipped)
+
+
+def shear_columns_kernel(
+    front, blocks, length, rows_out, base, own, spare, cosine, sine, forward, inverse, out, strip, shifted
+):
+    step = pl.program_id(0)
+    per_step = length // BLOCK
+    total = strip.shape[1]
+
+    @pl.when(step == 0)
+    def _():
+        strip[:, 0:front, :] = jnp.zeros((2, front, BLOCK), jnp.bfloat16)
+        back = front + blocks * length
+        strip[:, back:, :] = jnp.zeros((2, total - back, BLOCK), jnp.bfloat16)
+        for block in range(blocks):
+            for part in range(2):
+                first = front + block * length
+                strip[part, first : first + length, :] = own[block, part]
+
+    offset = spare[...]
+    row = lax.broadcasted_iota(jnp.int32, (8, BLOCK), 0) + (offset & 7)
+    wraps = row >= 8
+    index = row & 7
+
+    def one_chunk(chunk):
+        begin = pl.multiple_of(base[0] + chunk * BLOCK, GROUP)
+        for part in range(2):
+            value = strip[part, pl.ds(begin, 2 * BLOCK), :].astype(jnp.float32)
+            value = value.reshape(2 * BLOCK // 8, 8, BLOCK)
+            for bit in (64, 32, 16, 8):
+                taken = ((offset & bit) != 0)[None]
+                value = jnp.where(taken, value[bit // 8 :], value[: -(bit // 8)])
+            pieces = [
+                jnp.take_along_axis(value[i], index, axis=0) for i in range(BLOCK // 8 + 1)
+            ]
+            moved = [
+                jnp.where(wraps, pieces[i + 1], pieces[i]) for i in range(BLOCK // 8)
+            ]
+            lanes = slice(part * BLOCK, (part + 1) * BLOCK)
+            place = pl.ds(pl.multiple_of(chunk * BLOCK, BLOCK), BLOCK)
+            shifted[place, lanes] = jnp.concatenate(moved, 0).astype(jnp.bfloat16)
+
+    @pl.when(step == 0)
+    def _():
+        one_chunk(0)
+
+    for window in range(per_step):
+        one_chunk(step * per_step + window + 1)
+    ramp_real = jnp.concatenate([cosine[...]] * 2, 1)
+    ramp_imaginary = jnp.concatenate([sine[...]] * 2, 1)
+    for window in range(per_step):
+        first = pl.multiple_of((step * per_step + window) * BLOCK, BLOCK)
+        spectrum = jnp.dot(
+            forward[...], shifted[pl.ds(first, 2 * BLOCK), :], preferred_element_type=jnp.float32
+        )
+        real, imaginary = spectrum[:BLOCK], spectrum[BLOCK:]
+        ramped = jnp.concatenate(
+            [
+                (real * ramp_real - imaginary * ramp_imaginary).astype(jnp.bfloat16),
+                (real * ramp_imaginary + imaginary * ramp_real).astype(jnp.bfloat16),
+            ],
+            0,
+        )
+        result = jnp.dot(inverse[...], ramped, preferred_element_type=jnp.float32).astype(
+            jnp.bfloat16
+        )
+        low = window * BLOCK
+        block, within = low // rows_out, low % rows_out
+        for part in range(2):
+            out[block, part, within : within + BLOCK, :] = result[
+                :, part * BLOCK : (part + 1) * BLOCK
+            ]
+
+
+def shear_columns(own, front, back, base, spare, ramps, tables, rows_out):
+    blocks, _, length, _ = own.shape
+    forward, inverse = tables
+    cosine, sine = ramps
+    full = lambda shape: pl.BlockSpec(shape, lambda i, *_: (0,) * len(shape))
+    pieces = blocks * length // rows_out
+    per_step = pieces // blocks
+    return pl.pallas_call(
+        functools.partial(shear_columns_kernel, front, blocks, length, rows_out),
+        grid_spec=pltpu.PrefetchScalarGridSpec(
+            num_scalar_prefetch=1,
+            grid=(blocks,),
+            in_specs=[full(x.shape) for x in (own, spare, cosine, sine, forward, inverse)],
+            out_specs=pl.BlockSpec((per_step, 2, rows_out, BLOCK), lambda i, *_: (i, 0, 0, 0)),
+            scratch_shapes=[
+                pltpu.VMEM((2, front + blocks * length + back, BLOCK), jnp.bfloat16),
+                pltpu.VMEM((blocks * length + BLOCK, 2 * BLOCK), jnp.bfloat16),
+            ],
+        ),
+        out_shape=jax.ShapeDtypeStruct((pieces, 2, rows_out, BLOCK), jnp.bfloat16),
+        compiler_params=pltpu.CompilerParams(vmem_limit_bytes=VMEM_LIMIT),
+        name="shear_columns",
+    )(base, own, spare, cosine, sine, forward, inverse)
+
+
+def sine_cosine(angle):
+    turns = jnp.round(angle * (2.0 / np.pi))
+    rest = angle - turns * 1.5703125
+    rest = rest - turns * 4.837512969970703125e-4
+    rest = rest - turns * 7.549789954891882e-8
+    square = rest * rest
+    sine = rest + rest * square * (
+        -1.6666654611e-1 + square * (8.3321608736e-3 - square * 1.9515295891e-4)
+    )
+    cosine = (
+        1.0
+        - 0.5 * square
+        + square
+        * square
+        * (4.166664568298827e-2 + square * (-1.388731625493765e-3 + square * 2.443315711809948e-5))
+    )
+    quadrant = turns.astype(jnp.int32)
+    odd = (quadrant & 1) != 0
+    sine_out = jnp.where(odd, cosine, sine)
+    cosine_out = jnp.where(odd, sine, cosine)
+    sine_out = jnp.where((quadrant & 2) != 0, -sine_out, sine_out)
+    cosine_out = jnp.where(((quadrant + 1) & 2) != 0, -cosine_out, cosine_out)
+    return sine_out, cosine_out
+
+
+def transmitted(rotated, wave):
+    sine, cosine = sine_cosine(rotated[0].astype(jnp.float32))
+    amplitude = jnp.exp(-ABSORB * rotated[1].astype(jnp.float32))
+    through_real = amplitude * cosine
+    through_imaginary = amplitude * sine
+    wave_real = wave[0].astype(jnp.float32)
+    wave_imaginary = wave[1].astype(jnp.float32)
+    return (
+        (wave_real * through_real - wave_imaginary * through_imaginary).astype(jnp.bfloat16),
+        (wave_real * through_imaginary + wave_imaginary * through_real).astype(jnp.bfloat16),
+    )
+
+
+def travel_first_kernel(length, extended, *refs):
+    if extended:
+        body, wave, wave_top, wave_bottom, matrix, out, field = refs
+        top = body.at[0, :, 0:MARGIN]
+        middle = body.at[0, :, MARGIN : MARGIN + length]
+        bottom = body.at[0, :, MARGIN + length :]
+    else:
+        body, top, bottom, wave, wave_top, wave_bottom, matrix, out, field = refs
+        top, middle, bottom = top.at[0], body.at[0], bottom.at[0]
+    pieces = [(0, MARGIN, top, wave_top, 0)]
+    for first in range(0, length, BLOCK):
+        pieces.append((MARGIN + first, BLOCK, middle, wave, first))
+    pieces.append((MARGIN + length, MARGIN, bottom, wave_bottom, 0))
+    for place, count, value, waves, first in pieces:
+        lines = slice(first, first + count)
+        parts = transmitted(
+            [value[p, lines, :] for p in range(2)], [waves[p, lines, :] for p in range(2)]
+        )
+        for part in range(2):
+            field[part, place : place + count, :] = parts[part]
+    windows = [
+        jnp.concatenate([field[0, m : m + WINDOW, :], field[1, m : m + WINDOW, :]], 0)
+        for m in range(0, length, BLOCK)
+    ]
+    result = jnp.dot(
+        matrix[...], jnp.concatenate(windows, 1), preferred_element_type=jnp.float32
+    ).astype(jnp.bfloat16)
+    for m in range(length // BLOCK):
+        lanes = slice(m * BLOCK, (m + 1) * BLOCK)
+        for part in range(2):
+            out[0, part, lanes, :] = result[part * BLOCK : (part + 1) * BLOCK, lanes]
+
+
+def travel_first(body, halos, wave, wave_halos, matrix):
+    chunks = body.shape[0]
+    length = wave.shape[1]
+    chunk_spec = lambda x: pl.BlockSpec((1, 2, x.shape[2], BLOCK), lambda i: (i, 0, 0, 0))
+    wide_spec = lambda x: pl.BlockSpec((2, x.shape[1], BLOCK), lambda i: (0, 0, i))
+    return pl.pallas_call(
+        functools.partial(travel_first_kernel, length, len(halos) == 0),
+        grid=(chunks,),
+        in_specs=[chunk_spec(body)]
+        + [chunk_spec(x) for x in halos]
+        + [wide_spec(x) for x in (wave, *wave_halos)]
+        + [pl.BlockSpec(matrix.shape, lambda i: (0, 0))],
+        out_specs=pl.BlockSpec((1, 2, length, BLOCK), lambda i: (i, 0, 0, 0)),
+        out_shape=jax.ShapeDtypeStruct((chunks, 2, length, BLOCK), jnp.bfloat16),
+        scratch_shapes=[pltpu.VMEM((2, length + 2 * MARGIN, BLOCK), jnp.bfloat16)],
+        compiler_params=pltpu.CompilerParams(vmem_limit_bytes=VMEM_LIMIT),
+        name="travel_first",
+    )(body, *halos, wave, *wave_halos, matrix)
+
+
+def travel_second_kernel(chunks, rows, left, body, right, matrix, out):
+    parts = [[left[0, p]] + [body[m, p] for m in range(chunks)] + [right[0, p]] for p in range(2)]
+    windows = [
+        jnp.concatenate(parts[0][m : m + 3] + parts[1][m : m + 3], 1) for m in range(chunks)
+    ]
+    result = jnp.dot(
+        jnp.concatenate(windows, 0), matrix[...], preferred_element_type=jnp.float32
+    ).astype(jnp.bfloat16)
+    for m in range(chunks):
+        for part in range(2):
+            out[part, :, m * BLOCK : (m + 1) * BLOCK] = result[
+                m * rows : (m + 1) * rows, part * BLOCK : (part + 1) * BLOCK
+            ]
+
+
+def travel_second(left, body, right, matrix):
+    chunks, _, length, _ = body.shape
+    rows = BLOCK
+    edge = pl.BlockSpec((1, 2, rows, BLOCK), lambda i: (0, 0, i, 0))
+    return pl.pallas_call(
+        functools.partial(travel_second_kernel, chunks, rows),
+        grid=(length // rows,),
+        in_specs=[
+            edge,
+            pl.BlockSpec((chunks, 2, rows, BLOCK), lambda i: (0, 0, i, 0)),
+            edge,
+            pl.BlockSpec(matrix.shape, lambda i: (0, 0)),
+        ],
+        out_specs=pl.BlockSpec((2, rows, chunks * BLOCK), lambda i: (0, i, 0)),
+        out_shape=jax.ShapeDtypeStruct((2, length, chunks * BLOCK), jnp.bfloat16),
+        compiler_params=pltpu.CompilerParams(vmem_limit_bytes=VMEM_LIMIT),
+        name="travel_second",
+    )(left, body, right, matrix)
+
+
+def from_both_sides(first, last, axis):
+    devices = lax.axis_size(axis)
+    up = [(i, i + 1) for i in range(devices - 1)]
+    down = [(j, i) for i, j in up]
+    return lax.ppermute(last, axis, up), lax.ppermute(first, axis, down)
+
+
+def halo_plan(line_count, row_devices, halo):
+    share = line_count // row_devices
+    reach = []
+    for device in range(row_devices):
+        ends = [device * share, (device + 1) * share - 1]
+        most = max(
+            -(-abs(2 * r + 1 - line_count) * SHIFT_X // (line_count - 1)) for r in ends
+        )
+        reach.append(-(-(min(most, SHIFT_X) + MARGIN) // BLOCK))
+    plan = []
+    for chunk in range(1, halo + 1):
+        users = [d for d in range(row_devices) if reach[d] >= chunk]
+        if plan and plan[-1][2] == users:
+            plan[-1] = (plan[-1][0], chunk, users)
+        else:
+            plan.append((chunk, chunk, users))
+    return plan
+
+
+def exchange_chunks(piece, plan, tiles):
+    columns = lax.axis_size("col")
+    lefts, rights = [], []
+    for near, far, users in plan:
+        up = [
+            (d * columns + c, d * columns + c + 1) for d in users for c in range(columns - 1)
+        ]
+        down = [(b, a) for a, b in up]
+        lefts.append(lax.ppermute(piece(tiles - far, tiles - near + 1), ("row", "col"), up))
+        rights.append(lax.ppermute(piece(near - 1, far), ("row", "col"), down))
+    return lefts, rights
+
+
+def group_starts(starts, group, unit):
+    lines = starts.shape[-1]
+    grouped = starts.reshape(*starts.shape[:-1], lines // group, group)
+    base = jnp.min(grouped, -1) // unit
+    spare = grouped - base[..., None] * unit
+    return base.astype(jnp.int32), spare.reshape(starts.shape)
+
+
+def over_lanes(spare):
+    return jnp.broadcast_to(spare[..., None], (*spare.shape, BLOCK)).astype(jnp.int32)
+
+
+def on_device(
+    volume_plane,
+    wave_a,
+    wave_b,
+    shift_rows,
+    fraction_rows,
+    shift_columns,
+    fraction_columns,
+    travel_distance,
+):
+    _, line_count, width = volume_plane.shape
+    row_devices, column_devices = lax.axis_size("row"), lax.axis_size("col")
+    row_index, column_index = lax.axis_index("row"), lax.axis_index("col")
+    tiles = width // BLOCK
+    halo = -(-(SHIFT_X + MARGIN) // BLOCK)
+    plan = halo_plan(line_count * row_devices, row_devices, halo)
+    chunks = [(near, far) for near, far, _ in plan]
+
+    forward, inverse = real_tables()
+    half = lambda x: jnp.asarray(x, jnp.bfloat16)
+    row_tables = (half(forward), half(inverse))
+    column_tables = (half(forward.T), half(inverse.T))
+    turned_tables = (half(forward), half(inverse[:, ::-1].T))
+
+    lefts, rights = exchange_chunks(
+        lambda a, b: volume_plane[:, :, a * BLOCK : b * BLOCK], plan, tiles
+    )
+    wave_a_halos = from_both_sides(wave_a[:, :MARGIN], wave_a[:, -MARGIN:], "row")
+    wave_b_halos = from_both_sides(wave_b[:, :MARGIN], wave_b[:, -MARGIN:], "col")
+
+    base_rows, spare_rows = group_starts(halo * BLOCK - MARGIN - shift_rows, GROUP, BLOCK)
+    first_ramps = shear_phase(fraction_rows[:, 0].reshape(-1))
+    first_ramps = [x.reshape(2, line_count, BLOCK) for x in first_ramps]
+    sheared = shear_tile(
+        volume_plane,
+        lefts,
+        rights,
+        chunks,
+        chunks,
+        halo,
+        base_rows[:, 0],
+        over_lanes(spare_rows[:, 0]),
+        first_ramps,
+        row_tables,
+    )
+
+    front = -(-(SHIFT_Y + MARGIN) // GROUP) * GROUP
+    back = front + 3 * BLOCK
+    mine = lambda x: lax.dynamic_slice_in_dim(x, row_index * BLOCK, BLOCK, 1)
+    base_columns, spare_columns = group_starts(front - MARGIN - mine(shift_columns), BLOCK, GROUP)
+    column_fractions = mine(fraction_columns)
+
+    def second(view, rows_out):
+        spread = lax.all_to_all(sheared[view], "row", split_axis=0, concat_axis=0, tiled=True)
+        cosine, sine = shear_phase(column_fractions[view])
+        return shear_columns(
+            spread.reshape(row_devices, 2, line_count, BLOCK),
+            front,
+            back,
+            base_columns[view] * GROUP,
+            jnp.broadcast_to(spare_columns[view][None], (8, BLOCK)).astype(jnp.int32),
+            (cosine.T, sine.T),
+            column_tables,
+            rows_out,
+        )
+
+    matrices = travel_matrices(travel_distance, forward, inverse)
+    real, imaginary = matrices[:, 0], matrices[:, 1]
+    along_rows = jnp.concatenate(
+        [
+            jnp.concatenate([real, -imaginary], 1),
+            jnp.concatenate([imaginary, real], 1),
+        ],
+        2,
+    )
+    along_rows = jnp.swapaxes(along_rows, 1, 2).astype(jnp.bfloat16)
+    spaced = jnp.pad(matrices, ((0, 0), (0, 0), (BLOCK - MARGIN, BLOCK - MARGIN), (0, 0)))
+    real, imaginary = spaced[:, 0], spaced[:, 1]
+    along_columns = jnp.concatenate(
+        [
+            jnp.concatenate([real, -imaginary], 1),
+            jnp.concatenate([imaginary, real], 1),
+        ],
+        2,
+    ).astype(jnp.bfloat16)
+
+    moved_b = second(1, BLOCK)
+    whole = lax.all_to_all(moved_b, ("row", "col"), split_axis=0, concat_axis=0, tiled=True)
+    whole = whole.reshape(row_devices, column_devices, 2, BLOCK, BLOCK)
+    own_lines = lambda x: lax.dynamic_slice_in_dim(x, column_index * BLOCK, BLOCK, 0)
+    groups = BLOCK // GROUP
+    turned = shear_whole(
+        whole,
+        halo,
+        lax.dynamic_slice_in_dim(base_rows[1, 1], column_index * groups, groups, 0),
+        over_lanes(own_lines(spare_rows[1, 1])),
+        shear_phase(own_lines(fraction_rows[1, 1])),
+        turned_tables,
+    )
+    turned = lax.all_to_all(turned, "col", split_axis=0, concat_axis=0, tiled=True)
+
+    moved_a = second(0, line_count)
+    tile = lax.all_to_all(moved_a, "row", split_axis=0, concat_axis=0, tiled=True)
+    lefts, rights = exchange_chunks(lambda a, b: tile[a:b], plan, tiles)
+    (rotated,) = shear_tile(
+        tile,
+        lefts,
+        rights,
+        chunks,
+        chunks,
+        halo,
+        base_rows[:1, 1],
+        over_lanes(spare_rows[:1, 1]),
+        [x[None] for x in shear_phase(fraction_rows[0, 1])],
+        row_tables,
+    )
+
+    half_b = travel_first(turned, (), wave_b, wave_b_halos, along_rows[1])
+    left, right = from_both_sides(half_b[:1], half_b[-1:], "row")
+    exit_b = travel_second(left, half_b, right, along_columns[1])
+
+    halos = from_both_sides(rotated[:, :, :MARGIN], rotated[:, :, -MARGIN:], "row")
+    half_a = travel_first(rotated, halos, wave_a, wave_a_halos, along_rows[0])
+    left, right = from_both_sides(half_a[:1], half_a[-1:], "col")
+    exit_a = travel_second(left, half_a, right, along_columns[0])
+    return exit_a, exit_b
 
 
 def swapped(value, axis, bit):
@@ -143,7 +807,7 @@
     return line_pass(padded, extent, shifts, ramp_real, ramp_imaginary, tables)
 
 
-def shear_columns(stacked, shifts, fractions, tables):
+def general_shear_columns(stacked, shifts, fractions, tables):
     halo_depth = SHIFT_X + MARGIN
     inputs = stacked.shape[0]
     column_devices = lax.axis_size("col")
@@ -207,7 +871,7 @@
     ).astype(jnp.bfloat16)
 
 
-def on_device(
+def general_on_device(
     volume_plane,
     wave_a,
     wave_b,
@@ -221,7 +885,7 @@
     source = volume_plane[None]
     results = []
     for member in range(2):
-        stacked = shear_columns(
+        stacked = general_shear_columns(
             source,
             shift_rows[member : member + 1, 0],
             fraction_rows[member : member + 1, 0],
@@ -233,7 +897,7 @@
             fraction_columns[member : member + 1],
             tables,
         )
-        stacked = shear_columns(
+        stacked = general_shear_columns(
             stacked,
             shift_rows[member : member + 1, 1],
             fraction_rows[member : member + 1, 1],
@@ -255,8 +919,18 @@
 
 
 def solution(mesh):
+    def either(volume_plane, *rest):
+        rows, width = volume_plane.shape[1:]
+        fits = (
+            rows == BLOCK * lax.axis_size("col")
+            and width == BLOCK * lax.axis_size("row")
+            and width >= SHIFT_X + MARGIN
+        )
+        chosen = on_device if fits else general_on_device
+        return chosen(volume_plane, *rest)
+
     return jax.shard_map(
-        on_device,
+        either,
         mesh=mesh,
         in_specs=(
             P(None, "row", "col"),

time: 787 us -> 397 us (0.50)
  local copies, waits for them, and re-layouts: 282 us -> 25.2 us
  waiting for transfers between devices: 297 us -> 108 us
  Pallas kernels: 0 us -> 97.3 us
  other arithmetic: 78.3 us -> 9.79 us
  blocking collectives: 0 us -> 54.2 us
  matrix products: 46.5 us -> 0.67 us
  starting transfers between devices: 69.3 us -> 94.9 us
    all_to_all x11 -> x4, waiting for transfers between devices: 196 us -> 48.5 us  [the longest x1 31.2 us: on_device(): lax.all_to_all(moved_b, ('row', 'col'), split_axis=0, concat_axis=0, tile...]
    convert_element_type x8 -> x0, local copies, waits for them, and re-layouts: 114 us -> none  [line_pass(): return result.reshape(2, line_count, blocks * BLOCK).astype(jnp.bfloat16)]
    pallas_call x0 -> x9, Pallas kernels: none -> 97.3 us  [the longest x2 27.8 us: shear_tile(): pl.pallas_call(kernel, grid_spec=pltpu.PrefetchScalarGridSpec(num_scalar_...]
    all_to_all x24 -> x0, local copies, waits for them, and re-layouts: 83.8 us -> none  [the longest x8 29.6 us: shear_columns(): lax.all_to_all(sheared, 'col', split_axis=3, concat_axis=2, tiled=True)]
    ppermute x10 -> x26, starting transfers between devices: 20.6 us -> 76 us  [the longest x10 47.4 us: from_both_sides(): return (lax.ppermute(last, axis, up), lax.ppermute(first, axis, down))]
    all_to_all x0 -> x1, blocking collectives: none -> 54.2 us  [second(): lax.all_to_all(sheared[view], 'row', split_axis=0, concat_axis=0, tiled=T...]
    dot_general x20 -> x1, matrix products: 46.5 us -> 0.67 us  [travel_matrices(): jnp.einsum('pq,vrqu->vrpu', jnp.asarray(forward[:WINDOW]), scaled, precis...]
    ppermute x10 -> x26, waiting for transfers between devices: 100 us -> 59.7 us  [the longest x8 36 us: exchange_chunks(): lax.ppermute(piece(tiles - far, tiles - near + 1), ('row', 'col'), up)]
  transfers between devices with their start and end apart: 21 -> 30, of which waited for: 16 -> 11; matrix products, arithmetic and copies ran while one was open for 38% -> 6% of each run, Pallas kernels for 0% -> 16%
where the time goes in v1:
time: 397 us; the launch traced here: 393 us
  waiting for transfers between devices  108 us (27%)
  Pallas kernels  97.3 us (25%)
  starting transfers between devices  94.9 us (24%)
  blocking collectives  54.2 us (14%)
  local copies, waits for them, and re-layouts  25.2 us (6%)
  other arithmetic  9.79 us (2%)
    all_to_all x1, blocking collectives, second(): lax.all_to_all(sheared[view], 'row', split_axis=0, concat_axis=0, tiled=T...  54.2 us
    ppermute x10, starting transfers between devices, from_both_sides(): return (lax.ppermute(last, axis, up), lax.ppermute(first, axis, down))  47.4 us
    ppermute x8, waiting for transfers between devices, exchange_chunks(): lax.ppermute(piece(tiles - far, tiles - near + 1), ('row', 'col'), up)  36 us
    all_to_all x1, waiting for transfers between devices, on_device(): lax.all_to_all(moved_b, ('row', 'col'), split_axis=0, concat_axis=0, tile...  31.2 us
    pallas_call x2, Pallas kernels, shear_tile(): pl.pallas_call(kernel, grid_spec=pltpu.PrefetchScalarGridSpec(num_scalar_...  27.8 us
    pallas_call x2, Pallas kernels, shear_columns(): pl.pallas_call(functools.partial(shear_columns_kernel, front, blocks, len...  26.3 us
    ppermute x8, starting transfers between devices, exchange_chunks(): lax.ppermute(piece(tiles - far, tiles - near + 1), ('row', 'col'), up)  19.9 us
    pallas_call x2, Pallas kernels, travel_first(): pl.pallas_call(functools.partial(travel_first_kernel, length, len(halos)...  18.2 us
  transfers between devices with their start and end apart: 30, of which 11 were waited for; matrix products, arithmetic and copies ran while one was open for 6% of the time, Pallas kernels for 16%

profile of v1, /device:TPU:2, one launch (start us, length us, event | category | flops | bytes accessed | tf_op | source)
XLA Modules:
  0.0 393.0 jit_solution(18101565273716741110)
XLA Ops:
  5.4 4.6 %collective-permute-start = (bf16[2,512,256]{2,1,0:T(8,128)(2,1)S(1)}, bf16[2,512,256]{2,1,0:T(8,128)(2,1)S(1)}, u32[]{:S(2)}, u32[]{:S(2)}) collective-permute-start(bf16[2,512,256]{2,1,0:T(8,128)(2,1)S(1)} %get-tuple-element.29), channel_id=1, source_target_pairs={{0,1},{1,2},{2,3},{4,5},{5,6},{6,7},{8,9},{9,10},{10,11},{12,13},{... | collective-permute-start | bytes 1572872 | tf_op jit(solution)/shard_map/ppermute | solution.py:534
  13.6 3.5 collective-permute-start.1
  21.5 3.1 fusion.1
  25.2 8.2 %collective-permute-done.4.refs_4_ = bf16[2,512,256]{2,1,0:T(8,128)(2,1)S(1)} collective-permute-done((bf16[2,512,256]{2,1,0:T(8,128)(2,1)}, bf16[2,512,256]{2,1,0:T(8,128)(2,1)S(1)}, u32[]{:S(2)}, u32[]{:S(2)}) %collective-permute-start.4) | collective-permute-done | bytes 524320 | tf_op jit(solution)/shard_map/ppermute | solution.py:535
  34.7 17.6 %shear_tile.2 = (bf16[8,2,512,128]{3,2,1,0:T(8,128)(2,1)}, bf16[8,2,512,128]{3,2,1,0:T(8,128)(2,1)}) custom-call(s32[64]{0:T(128)} %reshape_squeeze.7.base, bf16[2,512,256]{2,1,0:T(8,128)(2,1)} %copy-done.7, bf16[2,512,256]{2,1,0:T(8,128)(2,1)} %copy-done.13, bf16[2,512,256]{2,1,0:T(8,128)(2,1)} %copy-done.5, bf16[2,512,128]{2,1,0:T(8,128)(2,1)} %copy-done.22, ...), custom_call_target="tpu_custom_call" | custom-call | tf_op jit(solution)/shard_map/shear_tile/pallas_call | solution.py:186
  52.2 54.2 %all_to_all.25.own = bf16[8,2,512,128]{3,2,1,0:T(8,128)(2,1)} all-to-all(bf16[8,2,512,128]{3,2,1,0:T(8,128)(2,1)} %get-tuple-element.5), channel_id=1, replica_groups=mesh['row'=8,'col'=4] {'row'}, dimensions={0} | all-to-all | bytes 4194304 | tf_op jit(solution)/shard_map/all_to_all | solution.py:604
  106.5 5.0 %all-to-all-start = ((bf16[8,2,512,128]{3,2,1,0:T(8,128)(2,1)}), bf16[8,2,512,128]{3,2,1,0:T(8,128)(2,1)S(1)}, u32[]{:S(2)}, u32[]{:S(2)}) async-start(bf16[8,2,512,128]{3,2,1,0:T(8,128)(2,1)} %get-tuple-element.4), calls=%async_computation | async-start | bytes 4194304 | tf_op jit(solution)/shard_map/all_to_all | solution.py:604
  115.8 13.2 %shear_columns.3 = bf16[32,2,128,128]{3,2,1,0:T(8,128)(2,1)} custom-call(s32[1]{0:T(128)} %bitcast.19.base, bf16[8,2,512,128]{3,2,1,0:T(8,128)(2,1)} %all_to_all.25.own, s32[8,128]{1,0:T(8,128)} %broadcast_in_dim.27.spare, f32[128,128]{1,0:T(8,128)} %get-tuple-element.55.cosine, f32[128,128]{1,0:T(8,128)} %get-tuple-element.54.sine, ...), custom_call_target="tpu_custom_call" | custom-call | tf_op jit(solution)/shard_map/shear_columns/pallas_call | solution.py:356
  129.0 7.6 %all-to-all-done.own = bf16[8,2,512,128]{3,2,1,0:T(8,128)(2,1)S(1)} async-done(((bf16[8,2,512,128]{3,2,1,0:T(8,128)(2,1)}), bf16[8,2,512,128]{3,2,1,0:T(8,128)(2,1)S(1)}, u32[]{:S(2)}, u32[]{:S(2)}) %all-to-all-start) | async-done | bytes 2097184 | tf_op jit(solution)/shard_map/all_to_all | solution.py:604
  137.9 4.2 %all-to-all-start.3 = ((bf16[32,2,128,128]{3,2,1,0:T(8,128)(2,1)}), bf16[32,2,128,128]{3,2,1,0:T(8,128)(2,1)S(1)}, u32[]{:S(2)}, u32[]{:S(2)}) async-start(bf16[32,2,128,128]{3,2,1,0:T(8,128)(2,1)} %shear_columns.3), calls=%async_computation.3 | async-start | bytes 4194304 | tf_op jit(solution)/shard_map/all_to_all | solution.py:638
  144.3 13.2 %shear_columns.2 = bf16[8,2,512,128]{3,2,1,0:T(8,128)(2,1)} custom-call(s32[1]{0:T(128)} %bitcast.2.base, bf16[8,2,512,128]{3,2,1,0:T(8,128)(2,1)} %copy-done.3, s32[8,128]{1,0:T(8,128)} %broadcast_in_dim.23.spare, f32[128,128]{1,0:T(8,128)} %get-tuple-element.61.cosine, f32[128,128]{1,0:T(8,128)} %get-tuple-element.60.sine, ...), custom_call_target="tpu_custom_call" | custom-call | tf_op jit(solution)/shard_map/shear_columns/pallas_call | solution.py:356
  157.4 31.2 %all-to-all-done.3 = bf16[32,2,128,128]{3,2,1,0:T(8,128)(2,1)S(1)} async-done(((bf16[32,2,128,128]{3,2,1,0:T(8,128)(2,1)}), bf16[32,2,128,128]{3,2,1,0:T(8,128)(2,1)S(1)}, u32[]{:S(2)}, u32[]{:S(2)}) %all-to-all-start.3) | async-done | bytes 2097184 | tf_op jit(solution)/shard_map/all_to_all | solution.py:638
  190.0 5.3 %all-to-all-start.1 = ((bf16[8,2,512,128]{3,2,1,0:T(8,128)(2,1)}), bf16[8,2,512,128]{3,2,1,0:T(8,128)(2,1)S(1)}, u32[]{:S(2)}, u32[]{:S(2)}) async-start(bf16[8,2,512,128]{3,2,1,0:T(8,128)(2,1)} %shear_columns.2), calls=%async_computation.1 | async-start | bytes 4194304 | tf_op jit(solution)/shard_map/all_to_all | solution.py:653
  198.1 12.7 %shear_whole.1 = bf16[4,2,1088,128]{3,2,1,0:T(8,128)(2,1)} custom-call(s32[8]{0:T(128)} %fusion.22.base, bf16[8,4,2,128,128]{4,3,2,1,0:T(8,128)(2,1)} %bitcast.63, s32[128,128]{1,0:T(8,128)} %broadcast_in_dim.29.spare, f32[128,128]{1,0:T(8,128)} %get-tuple-element.53.cosine, f32[128,128]{1,0:T(8,128)} %get-tuple-element.52.sine, ...), custom_call_target="tpu_custom_call" | custom-call | tf_op jit(solution)/shard_map/shear_whole/pallas_call | solution.py:257
  210.8 9.6 %all-to-all-done.1.refs_8_ = bf16[8,2,512,128]{3,2,1,0:T(8,128)(2,1)S(1)} async-done(((bf16[8,2,512,128]{3,2,1,0:T(8,128)(2,1)}), bf16[8,2,512,128]{3,2,1,0:T(8,128)(2,1)S(1)}, u32[]{:S(2)}, u32[]{:S(2)}) %all-to-all-start.1) | async-done | bytes 2097184 | tf_op jit(solution)/shard_map/all_to_all | solution.py:653
  220.4 4.5 %all-to-all-start.4 = ((bf16[4,2,1088,128]{3,2,1,0:T(8,128)(2,1)}), bf16[4,2,1088,128]{3,2,1,0:T(8,128)(2,1)}, u32[]{:S(2)}, u32[]{:S(2)}) async-start(bf16[4,2,1088,128]{3,2,1,0:T(8,128)(2,1)} %shear_whole.1), calls=%async_computation.4 | async-start | bytes 4456448 | tf_op jit(solution)/shard_map/all_to_all | solution.py:650
  226.0 4.5 %collective-permute-start.8 = (bf16[2,2,512,128]{3,2,1,0:T(8,128)(2,1)S(1)}, bf16[2,2,512,128]{3,2,1,0:T(8,128)(2,1)S(1)}, u32[]{:S(2)}, u32[]{:S(2)}) collective-permute-start(bf16[2,2,512,128]{3,2,1,0:T(8,128)(2,1)S(1)} %get-tuple-element.23), channel_id=1, source_target_pairs={{0,1},{1,2},{2,3},{4,5},{5,6},{6,7},{8,9},{9,10},{10,11},{12,13},{... | collective-permute-start | bytes 1572872 | tf_op jit(solution)/shard_map/ppermute | solution.py:534
  235.8 4.6 %collective-permute-start.9 = (bf16[2,2,512,128]{3,2,1,0:T(8,128)(2,1)S(1)}, bf16[2,2,512,128]{3,2,1,0:T(8,128)(2,1)S(1)}, u32[]{:S(2)}, u32[]{:S(2)}) collective-permute-start(bf16[2,2,512,128]{3,2,1,0:T(8,128)(2,1)S(1)} %get-tuple-element.22), channel_id=1, source_target_pairs={{0,1},{1,2},{2,3},{4,5},{5,6},{6,7},{8,9},{9,10},{10,11},{20,21},{... | collective-permute-start | bytes 1572872 | tf_op jit(solution)/shard_map/ppermute | solution.py:534
  241.1 31.5 %collective-permute-done.8.refs_0_ = bf16[2,2,512,128]{3,2,1,0:T(8,128)(2,1)S(1)} collective-permute-done((bf16[2,2,512,128]{3,2,1,0:T(8,128)(2,1)S(1)}, bf16[2,2,512,128]{3,2,1,0:T(8,128)(2,1)S(1)}, u32[]{:S(2)}, u32[]{:S(2)}) %collective-permute-start.8) | collective-permute-done | bytes 524320 | tf_op jit(solution)/shard_map/ppermute | solution.py:534
  280.2 13.3 %collective-permute-start.19 = (bf16[2,32,1024]{2,1,0:T(8,128)(2,1)S(1)}, bf16[2,32,1024]{2,1,0:T(8,128)(2,1)S(1)}, u32[]{:S(2)}, u32[]{:S(2)}) collective-permute-start(bf16[2,32,1024]{2,1,0:T(8,128)(2,1)S(1)} %get-tuple-element.14), channel_id=1, source_target_pairs={{4,0},{8,4},{12,8},{16,12},{20,16},{24,20},{28,24},{5,1},{9,5},{13... | collective-permute-start | bytes 393224 | tf_op jit(solution)/shard_map/ppermute | solution.py:504
  293.5 7.2 %collective-permute-done.12.refs_4_ = bf16[2,2,512,128]{3,2,1,0:T(8,128)(2,1)S(1)} collective-permute-done((bf16[2,2,512,128]{3,2,1,0:T(8,128)(2,1)S(1)}, bf16[2,2,512,128]{3,2,1,0:T(8,128)(2,1)S(1)}, u32[]{:S(2)}, u32[]{:S(2)}) %collective-permute-start.12) | collective-permute-done | bytes 524320 | tf_op jit(solution)/shard_map/ppermute | solution.py:535
  300.7 9.1 %collective-permute-start.22 = (bf16[2,32,512]{2,1,0:T(8,128)(2,1)S(1)}, bf16[2,32,512]{2,1,0:T(8,128)(2,1)S(1)}, u32[]{:S(2)}, u32[]{:S(2)}) collective-permute-start(bf16[2,32,512]{2,1,0:T(8,128)(2,1)S(1)} %get-tuple-element.11), channel_id=1, source_target_pairs={{0,1},{1,2},{2,3},{4,5},{5,6},{6,7},{8,9},{9,10},{10,11},{12,13},{... | collective-permute-start | bytes 196616 | tf_op jit(solution)/shard_map/ppermute | solution.py:504
  310.9 10.2 %shear_tile.3.refs_0_ = bf16[8,2,512,128]{3,2,1,0:T(8,128)(2,1)} custom-call(s32[32]{0:T(128)} %get-tuple-element.45.base, bf16[2,2,512,128]{3,2,1,0:T(8,128)(2,1)} %copy-done.4, bf16[2,2,512,128]{3,2,1,0:T(8,128)(2,1)} %copy-done.10, bf16[2,2,512,128]{3,2,1,0:T(8,128)(2,1)} %copy-done.8, bf16[1,2,512,128]{3,2,1,0:T(8,128)(2,1)} %copy-done.18, ...), custom_call_target="tpu_custom_call" | custom-call | tf_op jit(solution)/shard_map/shear_tile/pallas_call | solution.py:186
  324.1 8.0 %collective-permute-start.17 = (bf16[8,2,32,128]{3,2,1,0:T(8,128)(2,1)S(1)}, bf16[8,2,32,128]{3,2,1,0:T(8,128)(2,1)S(1)}, u32[]{:S(2)}, u32[]{:S(2)}) collective-permute-start(bf16[8,2,32,128]{3,2,1,0:T(8,128)(2,1)S(1)} %get-tuple-element.16), channel_id=1, source_target_pairs={{4,0},{8,4},{12,8},{16,12},{20,16},{24,20},{28,24},{5,1},{9,5},{13... | collective-permute-start | bytes 393224 | tf_op jit(solution)/shard_map/ppermute | solution.py:504
  336.5 10.0 %travel_first.2.body = bf16[8,2,512,128]{3,2,1,0:T(8,128)(2,1)} custom-call(bf16[8,2,512,128]{3,2,1,0:T(8,128)(2,1)} %shear_tile.3.refs_0_, bf16[8,2,32,128]{3,2,1,0:T(8,128)(2,1)} %copy-done.26, bf16[8,2,32,128]{3,2,1,0:T(8,128)(2,1)} %copy-done.27, bf16[2,512,1024]{2,1,0:T(8,128)(2,1)} %refs_3_.1, bf16[2,32,1024]{2,1,0:T(8,128)(2,1)} %copy-done.24, ...), custom_call_target="tpu_custom_call" | custom-call | tf_op jit(solution)/shard_map/travel_first/pallas_call | solution.py:450
  347.1 8.2 %travel_first.3.body = bf16[4,2,1024,128]{3,2,1,0:T(8,128)(2,1)} custom-call(bf16[4,2,1088,128]{3,2,1,0:T(8,128)(2,1)} %all-to-all-done.4.refs_0_, bf16[2,1024,512]{2,1,0:T(8,128)(2,1)} %refs_1_.1, bf16[2,32,512]{2,1,0:T(8,128)(2,1)} %copy-done.29, bf16[2,32,512]{2,1,0:T(8,128)(2,1)} %copy-done.30, bf16[256,384]{1,0:T(8,128)(2,1)} %copy.23.refs_4_), custom_call_target="tpu_custom_call" | custom-call | tf_op jit(solution)/shard_map/travel_first/pallas_call | solution.py:450
  356.6 4.1 %collective-permute-start.24 = (bf16[1,2,1024,128]{3,2,1,0:T(8,128)(2,1)S(1)}, bf16[1,2,1024,128]{3,2,1,0:T(8,128)(2,1)S(1)}, u32[]{:S(2)}, u32[]{:S(2)}) collective-permute-start(bf16[1,2,1024,128]{3,2,1,0:T(8,128)(2,1)S(1)} %get-tuple-element.9), channel_id=1, source_target_pairs={{0,4},{4,8},{8,12},{12,16},{16,20},{20,24},{24,28},{1,5},{5,9},{9,... | collective-permute-start | bytes 1572872 | tf_op jit(solution)/shard_map/ppermute | solution.py:504
  363.7 4.6 %collective-permute-start.20 = (bf16[1,2,512,128]{3,2,1,0:T(8,128)(2,1)S(1)}, bf16[1,2,512,128]{3,2,1,0:T(8,128)(2,1)S(1)}, u32[]{:S(2)}, u32[]{:S(2)}) collective-permute-start(bf16[1,2,512,128]{3,2,1,0:T(8,128)(2,1)S(1)} %get-tuple-element.13), channel_id=1, source_target_pairs={{0,1},{1,2},{2,3},{4,5},{5,6},{6,7},{8,9},{9,10},{10,11},{12,13},{... | collective-permute-start | bytes 786440 | tf_op jit(solution)/shard_map/ppermute | solution.py:504
  370.6 3.9 collective-permute-done.20.left
  374.5 4.4 %collective-permute-done.21.right = bf16[1,2,512,128]{3,2,1,0:T(8,128)(2,1)S(1)} collective-permute-done((bf16[1,2,512,128]{3,2,1,0:T(8,128)(2,1)S(1)}, bf16[1,2,512,128]{3,2,1,0:T(8,128)(2,1)S(1)}, u32[]{:S(2)}, u32[]{:S(2)}) %collective-permute-start.21) | collective-permute-done | bytes 262176 | tf_op jit(solution)/shard_map/ppermute | solution.py:504
  379.6 5.1 %travel_second.2 = bf16[2,512,1024]{2,1,0:T(8,128)(2,1)} custom-call(bf16[1,2,512,128]{3,2,1,0:T(8,128)(2,1)} %copy-done.20, bf16[8,2,512,128]{3,2,1,0:T(8,128)(2,1)} %travel_first.2.body, bf16[1,2,512,128]{3,2,1,0:T(8,128)(2,1)} %copy-done.21, bf16[768,256]{1,0:T(8,128)(2,1)} %get-tuple-element.31.matrix), custom_call_target="tpu_custom_call" | custom-call | tf_op jit(solution)/shard_map/travel_second/pallas_call | solution.py:484
  385.6 7.3 %travel_second.3 = bf16[2,1024,512]{2,1,0:T(8,128)(2,1)} custom-call(bf16[1,2,1024,128]{3,2,1,0:T(8,128)(2,1)} %copy-done.16, bf16[4,2,1024,128]{3,2,1,0:T(8,128)(2,1)} %travel_first.3.body, bf16[1,2,1024,128]{3,2,1,0:T(8,128)(2,1)} %copy-done.17, bf16[768,256]{1,0:T(8,128)(2,1)} %get-tuple-element.30.matrix), custom_call_target="tpu_custom_call" | custom-call | tf_op jit(solution)/shard_map/travel_second/pallas_call | solution.py:484
  (166 shorter events, 56.9 us)
Async XLA Ops:
  0.6 112.9 %copy-start = (f32[2,1024]{1,0:T(2,128)S(1)}, f32[2,1024]{1,0:T(2,128)}, u32[]{:S(2)}) copy-start(f32[2,1024]{1,0:T(2,128)} %param.22) | copy-start | bytes 24580
  3.4 21.8 %collective-permute-start.2 = (bf16[2,512,256]{2,1,0:T(8,128)(2,1)}, bf16[2,512,256]{2,1,0:T(8,128)(2,1)S(1)}, u32[]{:S(2)}, u32[]{:S(2)}) collective-permute-start(bf16[2,512,256]{2,1,0:T(8,128)(2,1)} %get-tuple-element.27), channel_id=1, source_target_pairs={{0,1},{1,2},{2,3},{4,5},{5,6},{6,7},{24,25},{25,26},{26,27},{28,29... | collective-permute-start | bytes 1572872 | tf_op jit(solution)/shard_map/ppermute | solution.py:534
  4.1 29.3 %collective-permute-start.5 = (bf16[2,512,256]{2,1,0:T(8,128)(2,1)}, bf16[2,512,256]{2,1,0:T(8,128)(2,1)S(1)}, u32[]{:S(2)}, u32[]{:S(2)}) collective-permute-start(bf16[2,512,256]{2,1,0:T(8,128)(2,1)} %get-tuple-element.27), channel_id=1, source_target_pairs={{1,0},{2,1},{3,2},{5,4},{6,5},{7,6},{9,8},{10,9},{11,10},{21,20},{... | collective-permute-start | bytes 1572872 | tf_op jit(solution)/shard_map/ppermute | solution.py:535
  5.4 14.1 %collective-permute-start = (bf16[2,512,256]{2,1,0:T(8,128)(2,1)S(1)}, bf16[2,512,256]{2,1,0:T(8,128)(2,1)S(1)}, u32[]{:S(2)}, u32[]{:S(2)}) collective-permute-start(bf16[2,512,256]{2,1,0:T(8,128)(2,1)S(1)} %get-tuple-element.29), channel_id=1, source_target_pairs={{0,1},{1,2},{2,3},{4,5},{5,6},{6,7},{8,9},{9,10},{10,11},{12,13},{... | collective-permute-start | bytes 1572872 | tf_op jit(solution)/shard_map/ppermute | solution.py:534
  11.1 2.5 collective-permute-start.3
  11.7 5.4 %collective-permute-start.7 = (bf16[2,512,128]{2,1,0:T(8,128)(2,1)S(1)}, bf16[2,512,128]{2,1,0:T(8,128)(2,1)}, u32[]{:S(2)}, u32[]{:S(2)}) collective-permute-start(bf16[2,512,128]{2,1,0:T(8,128)(2,1)S(1)} %get-tuple-element.24), channel_id=1, source_target_pairs={{1,0},{2,1},{3,2},{29,28},{30,29},{31,30}} | collective-permute-start | bytes 786440 | tf_op jit(solution)/shard_map/ppermute | solution.py:535
  13.6 11.6 %collective-permute-start.1 = (bf16[2,512,256]{2,1,0:T(8,128)(2,1)}, bf16[2,512,256]{2,1,0:T(8,128)(2,1)S(1)}, u32[]{:S(2)}, u32[]{:S(2)}) collective-permute-start(bf16[2,512,256]{2,1,0:T(8,128)(2,1)} %get-tuple-element.28), channel_id=1, source_target_pairs={{0,1},{1,2},{2,3},{4,5},{5,6},{6,7},{8,9},{9,10},{10,11},{20,21},{... | collective-permute-start | bytes 1572872 | tf_op jit(solution)/shard_map/ppermute | solution.py:534
  17.1 16.3 %collective-permute-start.6 = (bf16[2,512,256]{2,1,0:T(8,128)(2,1)}, bf16[2,512,256]{2,1,0:T(8,128)(2,1)S(1)}, u32[]{:S(2)}, u32[]{:S(2)}) collective-permute-start(bf16[2,512,256]{2,1,0:T(8,128)(2,1)} %get-tuple-element.28), channel_id=1, source_target_pairs={{1,0},{2,1},{3,2},{5,4},{6,5},{7,6},{25,24},{26,25},{27,26},{29,28... | collective-permute-start | bytes 1572872 | tf_op jit(solution)/shard_map/ppermute | solution.py:535
  19.4 13.9 %collective-permute-start.4 = (bf16[2,512,256]{2,1,0:T(8,128)(2,1)}, bf16[2,512,256]{2,1,0:T(8,128)(2,1)S(1)}, u32[]{:S(2)}, u32[]{:S(2)}) collective-permute-start(bf16[2,512,256]{2,1,0:T(8,128)(2,1)} %get-tuple-element.26), channel_id=1, source_target_pairs={{1,0},{2,1},{3,2},{5,4},{6,5},{7,6},{9,8},{10,9},{11,10},{13,12},{... | collective-permute-start | bytes 1572872 | tf_op jit(solution)/shard_map/ppermute | solution.py:535
  106.5 30.1 %all-to-all-start = ((bf16[8,2,512,128]{3,2,1,0:T(8,128)(2,1)}), bf16[8,2,512,128]{3,2,1,0:T(8,128)(2,1)S(1)}, u32[]{:S(2)}, u32[]{:S(2)}) async-start(bf16[8,2,512,128]{3,2,1,0:T(8,128)(2,1)} %get-tuple-element.4), calls=%async_computation | async-start | bytes 4194304 | tf_op jit(solution)/shard_map/all_to_all | solution.py:604
  137.9 50.7 %all-to-all-start.3 = ((bf16[32,2,128,128]{3,2,1,0:T(8,128)(2,1)}), bf16[32,2,128,128]{3,2,1,0:T(8,128)(2,1)S(1)}, u32[]{:S(2)}, u32[]{:S(2)}) async-start(bf16[32,2,128,128]{3,2,1,0:T(8,128)(2,1)} %shear_columns.3), calls=%async_computation.3 | async-start | bytes 4194304 | tf_op jit(solution)/shard_map/all_to_all | solution.py:638
  190.0 30.4 %all-to-all-start.1 = ((bf16[8,2,512,128]{3,2,1,0:T(8,128)(2,1)}), bf16[8,2,512,128]{3,2,1,0:T(8,128)(2,1)S(1)}, u32[]{:S(2)}, u32[]{:S(2)}) async-start(bf16[8,2,512,128]{3,2,1,0:T(8,128)(2,1)} %shear_columns.2), calls=%async_computation.1 | async-start | bytes 4194304 | tf_op jit(solution)/shard_map/all_to_all | solution.py:653
  220.4 126.1 %all-to-all-start.4 = ((bf16[4,2,1088,128]{3,2,1,0:T(8,128)(2,1)}), bf16[4,2,1088,128]{3,2,1,0:T(8,128)(2,1)}, u32[]{:S(2)}, u32[]{:S(2)}) async-start(bf16[4,2,1088,128]{3,2,1,0:T(8,128)(2,1)} %shear_whole.1), calls=%async_computation.4 | async-start | bytes 4456448 | tf_op jit(solution)/shard_map/all_to_all | solution.py:650
  226.0 46.7 %collective-permute-start.8 = (bf16[2,2,512,128]{3,2,1,0:T(8,128)(2,1)S(1)}, bf16[2,2,512,128]{3,2,1,0:T(8,128)(2,1)S(1)}, u32[]{:S(2)}, u32[]{:S(2)}) collective-permute-start(bf16[2,2,512,128]{3,2,1,0:T(8,128)(2,1)S(1)} %get-tuple-element.23), channel_id=1, source_target_pairs={{0,1},{1,2},{2,3},{4,5},{5,6},{6,7},{8,9},{9,10},{10,11},{12,13},{... | collective-permute-start | bytes 1572872 | tf_op jit(solution)/shard_map/ppermute | solution.py:534
  230.5 5.3 %collective-permute-start.11 = (bf16[1,2,512,128]{3,2,1,0:T(8,128)(2,1)S(1)}, bf16[1,2,512,128]{3,2,1,0:T(8,128)(2,1)S(1)}, u32[]{:S(2)}, u32[]{:S(2)}) collective-permute-start(bf16[1,2,512,128]{3,2,1,0:T(8,128)(2,1)S(1)} %get-tuple-element.19), channel_id=1, source_target_pairs={{0,1},{1,2},{2,3},{28,29},{29,30},{30,31}} | collective-permute-start | bytes 786440 | tf_op jit(solution)/shard_map/ppermute | solution.py:534
  231.2 9.2 %collective-permute-start.15 = (bf16[1,2,512,128]{3,2,1,0:T(8,128)(2,1)S(1)}, bf16[1,2,512,128]{3,2,1,0:T(8,128)(2,1)S(1)}, u32[]{:S(2)}, u32[]{:S(2)}) collective-permute-start(bf16[1,2,512,128]{3,2,1,0:T(8,128)(2,1)S(1)} %get-tuple-element.18), channel_id=1, source_target_pairs={{1,0},{2,1},{3,2},{29,28},{30,29},{31,30}} | collective-permute-start | bytes 786440 | tf_op jit(solution)/shard_map/ppermute | solution.py:535
  233.8 46.4 %collective-permute-start.10 = (bf16[2,2,512,128]{3,2,1,0:T(8,128)(2,1)S(1)}, bf16[2,2,512,128]{3,2,1,0:T(8,128)(2,1)S(1)}, u32[]{:S(2)}, u32[]{:S(2)}) collective-permute-start(bf16[2,2,512,128]{3,2,1,0:T(8,128)(2,1)S(1)} %get-tuple-element.21), channel_id=1, source_target_pairs={{0,1},{1,2},{2,3},{4,5},{5,6},{6,7},{24,25},{25,26},{26,27},{28,29... | collective-permute-start | bytes 1572872 | tf_op jit(solution)/shard_map/ppermute | solution.py:534
  234.5 75.3 %collective-permute-start.13 = (bf16[2,2,512,128]{3,2,1,0:T(8,128)(2,1)S(1)}, bf16[2,2,512,128]{3,2,1,0:T(8,128)(2,1)S(1)}, u32[]{:S(2)}, u32[]{:S(2)}) collective-permute-start(bf16[2,2,512,128]{3,2,1,0:T(8,128)(2,1)S(1)} %get-tuple-element.21), channel_id=1, source_target_pairs={{1,0},{2,1},{3,2},{5,4},{6,5},{7,6},{9,8},{10,9},{11,10},{21,20},{... | collective-permute-start | bytes 1572872 | tf_op jit(solution)/shard_map/ppermute | solution.py:535
  235.8 75.1 %copy-start.18 = (bf16[1,2,512,128]{3,2,1,0:T(8,128)(2,1)}, bf16[1,2,512,128]{3,2,1,0:T(8,128)(2,1)S(1)}, u32[]{:S(2)}) copy-start(bf16[1,2,512,128]{3,2,1,0:T(8,128)(2,1)S(1)} %collective-permute-done.11.refs_3_) | copy-start | bytes 786436
  235.8 42.4 %collective-permute-start.9 = (bf16[2,2,512,128]{3,2,1,0:T(8,128)(2,1)S(1)}, bf16[2,2,512,128]{3,2,1,0:T(8,128)(2,1)S(1)}, u32[]{:S(2)}, u32[]{:S(2)}) collective-permute-start(bf16[2,2,512,128]{3,2,1,0:T(8,128)(2,1)S(1)} %get-tuple-element.22), channel_id=1, source_target_pairs={{0,1},{1,2},{2,3},{4,5},{5,6},{6,7},{8,9},{9,10},{10,11},{20,21},{... | collective-permute-start | bytes 1572872 | tf_op jit(solution)/shard_map/ppermute | solution.py:534
  240.4 69.4 %collective-permute-start.14 = (bf16[2,2,512,128]{3,2,1,0:T(8,128)(2,1)S(1)}, bf16[2,2,512,128]{3,2,1,0:T(8,128)(2,1)S(1)}, u32[]{:S(2)}, u32[]{:S(2)}) collective-permute-start(bf16[2,2,512,128]{3,2,1,0:T(8,128)(2,1)S(1)} %get-tuple-element.22), channel_id=1, source_target_pairs={{1,0},{2,1},{3,2},{5,4},{6,5},{7,6},{25,24},{26,25},{27,26},{29,28... | collective-permute-start | bytes 1572872 | tf_op jit(solution)/shard_map/ppermute | solution.py:535
  272.6 28.0 %collective-permute-start.12 = (bf16[2,2,512,128]{3,2,1,0:T(8,128)(2,1)S(1)}, bf16[2,2,512,128]{3,2,1,0:T(8,128)(2,1)S(1)}, u32[]{:S(2)}, u32[]{:S(2)}) collective-permute-start(bf16[2,2,512,128]{3,2,1,0:T(8,128)(2,1)S(1)} %get-tuple-element.20), channel_id=1, source_target_pairs={{1,0},{2,1},{3,2},{5,4},{6,5},{7,6},{9,8},{10,9},{11,10},{13,12},{... | collective-permute-start | bytes 1572872 | tf_op jit(solution)/shard_map/ppermute | solution.py:535
  278.2 55.6 %collective-permute-start.18 = (bf16[2,32,1024]{2,1,0:T(8,128)(2,1)S(1)}, bf16[2,32,1024]{2,1,0:T(8,128)(2,1)S(1)}, u32[]{:S(2)}, u32[]{:S(2)}) collective-permute-start(bf16[2,32,1024]{2,1,0:T(8,128)(2,1)S(1)} %get-tuple-element.15), channel_id=1, source_target_pairs={{0,4},{4,8},{8,12},{12,16},{16,20},{20,24},{24,28},{1,5},{5,9},{9,... | collective-permute-start | bytes 393224 | tf_op jit(solution)/shard_map/ppermute | solution.py:504
  280.2 54.9 %collective-permute-start.19 = (bf16[2,32,1024]{2,1,0:T(8,128)(2,1)S(1)}, bf16[2,32,1024]{2,1,0:T(8,128)(2,1)S(1)}, u32[]{:S(2)}, u32[]{:S(2)}) collective-permute-start(bf16[2,32,1024]{2,1,0:T(8,128)(2,1)S(1)} %get-tuple-element.14), channel_id=1, source_target_pairs={{4,0},{8,4},{12,8},{16,12},{20,16},{24,20},{28,24},{5,1},{9,5},{13... | collective-permute-start | bytes 393224 | tf_op jit(solution)/shard_map/ppermute | solution.py:504
  300.7 45.8 %collective-permute-start.22 = (bf16[2,32,512]{2,1,0:T(8,128)(2,1)S(1)}, bf16[2,32,512]{2,1,0:T(8,128)(2,1)S(1)}, u32[]{:S(2)}, u32[]{:S(2)}) collective-permute-start(bf16[2,32,512]{2,1,0:T(8,128)(2,1)S(1)} %get-tuple-element.11), channel_id=1, source_target_pairs={{0,1},{1,2},{2,3},{4,5},{5,6},{6,7},{8,9},{9,10},{10,11},{12,13},{... | collective-permute-start | bytes 196616 | tf_op jit(solution)/shard_map/ppermute | solution.py:504
  322.2 13.0 %collective-permute-start.16 = (bf16[8,2,32,128]{3,2,1,0:T(8,128)(2,1)S(1)}, bf16[8,2,32,128]{3,2,1,0:T(8,128)(2,1)S(1)}, u32[]{:S(2)}, u32[]{:S(2)}) collective-permute-start(bf16[8,2,32,128]{3,2,1,0:T(8,128)(2,1)S(1)} %get-tuple-element.17), channel_id=1, source_target_pairs={{0,4},{4,8},{8,12},{12,16},{16,20},{20,24},{24,28},{1,5},{5,9},{9,... | collective-permute-start | bytes 393224 | tf_op jit(solution)/shard_map/ppermute | solution.py:504
  324.1 11.1 %collective-permute-start.17 = (bf16[8,2,32,128]{3,2,1,0:T(8,128)(2,1)S(1)}, bf16[8,2,32,128]{3,2,1,0:T(8,128)(2,1)S(1)}, u32[]{:S(2)}, u32[]{:S(2)}) collective-permute-start(bf16[8,2,32,128]{3,2,1,0:T(8,128)(2,1)S(1)} %get-tuple-element.16), channel_id=1, source_target_pairs={{4,0},{8,4},{12,8},{16,12},{20,16},{24,20},{28,24},{5,1},{9,5},{13... | collective-permute-start | bytes 393224 | tf_op jit(solution)/shard_map/ppermute | solution.py:504
  333.8 12.7 %collective-permute-start.23 = (bf16[2,32,512]{2,1,0:T(8,128)(2,1)S(1)}, bf16[2,32,512]{2,1,0:T(8,128)(2,1)S(1)}, u32[]{:S(2)}, u32[]{:S(2)}) collective-permute-start(bf16[2,32,512]{2,1,0:T(8,128)(2,1)S(1)} %get-tuple-element.10), channel_id=1, source_target_pairs={{1,0},{2,1},{3,2},{5,4},{6,5},{7,6},{9,8},{10,9},{11,10},{13,12},{... | collective-permute-start | bytes 196616 | tf_op jit(solution)/shard_map/ppermute | solution.py:504
  356.6 28.1 %collective-permute-start.24 = (bf16[1,2,1024,128]{3,2,1,0:T(8,128)(2,1)S(1)}, bf16[1,2,1024,128]{3,2,1,0:T(8,128)(2,1)S(1)}, u32[]{:S(2)}, u32[]{:S(2)}) collective-permute-start(bf16[1,2,1024,128]{3,2,1,0:T(8,128)(2,1)S(1)} %get-tuple-element.9), channel_id=1, source_target_pairs={{0,4},{4,8},{8,12},{12,16},{16,20},{20,24},{24,28},{1,5},{5,9},{9,... | collective-permute-start | bytes 1572872 | tf_op jit(solution)/shard_map/ppermute | solution.py:504
  360.7 24.0 %collective-permute-start.25 = (bf16[1,2,1024,128]{3,2,1,0:T(8,128)(2,1)S(1)}, bf16[1,2,1024,128]{3,2,1,0:T(8,128)(2,1)S(1)}, u32[]{:S(2)}, u32[]{:S(2)}) collective-permute-start(bf16[1,2,1024,128]{3,2,1,0:T(8,128)(2,1)S(1)} %get-tuple-element.8), channel_id=1, source_target_pairs={{4,0},{8,4},{12,8},{16,12},{20,16},{24,20},{28,24},{5,1},{9,5},{13... | collective-permute-start | bytes 1572872 | tf_op jit(solution)/shard_map/ppermute | solution.py:504
  363.7 10.8 %collective-permute-start.20 = (bf16[1,2,512,128]{3,2,1,0:T(8,128)(2,1)S(1)}, bf16[1,2,512,128]{3,2,1,0:T(8,128)(2,1)S(1)}, u32[]{:S(2)}, u32[]{:S(2)}) collective-permute-start(bf16[1,2,512,128]{3,2,1,0:T(8,128)(2,1)S(1)} %get-tuple-element.13), channel_id=1, source_target_pairs={{0,1},{1,2},{2,3},{4,5},{5,6},{6,7},{8,9},{9,10},{10,11},{12,13},{... | collective-permute-start | bytes 786440 | tf_op jit(solution)/shard_map/ppermute | solution.py:504
  368.3 10.6 %collective-permute-start.21 = (bf16[1,2,512,128]{3,2,1,0:T(8,128)(2,1)S(1)}, bf16[1,2,512,128]{3,2,1,0:T(8,128)(2,1)S(1)}, u32[]{:S(2)}, u32[]{:S(2)}) collective-permute-start(bf16[1,2,512,128]{3,2,1,0:T(8,128)(2,1)S(1)} %get-tuple-element.12), channel_id=1, source_target_pairs={{1,0},{2,1},{3,2},{5,4},{6,5},{7,6},{9,8},{10,9},{11,10},{13,12},{... | collective-permute-start | bytes 786440 | tf_op jit(solution)/shard_map/ppermute | solution.py:504
  (32 other events, 343.5 us)

commit v2 on v1

--- a/solution.py
+++ b/solution.py
@@ -19,6 +19,7 @@
 WINDOW = BLOCK + 2 * MARGIN
 BINS = WINDOW // 2
 GROUP = 16
+GATHERED = 4
 VMEM_LIMIT = 56 * 1024 * 1024
 
 
@@ -40,12 +41,6 @@
         -np.sin(angle_table(bins[1:BINS], target)) * weight[1:BINS, None]
     )
     return forward, inverse
-
-
-def shear_phase(fractions):
-    frequency = jnp.arange(BLOCK, dtype=jnp.float32)
-    phases = -2.0 * jnp.pi / WINDOW * fractions[:, None] * frequency[None, :]
-    return jnp.cos(phases), jnp.sin(phases)
 
 
 def travel_matrices(distance, forward, inverse):
@@ -114,13 +109,22 @@
     return ramped.reshape(count * 2 * rows, 2 * BLOCK)
 
 
+def down_lines(vector):
+    return jnp.broadcast_to(vector, (BLOCK, BLOCK)).T
+
+
+def line_ramps(fractions, cosine, sine):
+    bins = lane_iota(BLOCK).astype(jnp.float32)
+    sine[...], cosine[...] = sine_cosine(down_lines(fractions) * bins * (-2.0 * np.pi / WINDOW))
+
+
 def shear_tile_kernel(
-    views, halo, tiles, rows, batch, wide, left_chunks, right_chunks, base, *refs
+    halo, tiles, rows, batch, wide, left_chunks, right_chunks, base, *refs
 ):
     lefts, refs = refs[: len(left_chunks)], refs[len(left_chunks) :]
     rights, refs = refs[: len(right_chunks)], refs[len(right_chunks) :]
-    own, spare, cosine, sine, forward, inverse = refs[:6]
-    outs, (strip, shifted) = refs[6 : 6 + views], refs[6 + views :]
+    own, offsets, fractions, forward, inverse, out = refs[:6]
+    strip, shifted, spare, cosine, sine = refs[6:]
     step = pl.program_id(0)
     groups = rows // GROUP
     end = halo + tiles + halo
@@ -141,47 +145,40 @@
     for piece, (near, far) in zip(rights, right_chunks):
         fill(piece, halo + tiles + near - 1, far - near + 1)
     fill(own, halo, tiles)
-    for view in range(views):
-        steps = base.shape[0] // (views * groups)
-        offset = (view * steps + step) * groups
-        shift_lines(strip, shifted, base, offset, spare.at[view], tiles, 0, rows)
-        for first in range(0, tiles, batch):
-            ramped = ramped_lines(
-                shifted, first, batch, rows, cosine.at[view], sine.at[view], forward
-            )
-            result = jnp.dot(ramped, inverse[...], preferred_element_type=jnp.float32)
-            outs[view][first : first + batch] = result.astype(jnp.bfloat16).reshape(
-                batch, 2, rows, BLOCK
-            )
-
-
-def shear_tile(own, lefts, rights, left_chunks, right_chunks, halo, base, spare, ramps, tables):
+    spare[...] = down_lines(offsets[0]).astype(jnp.int32)
+    line_ramps(fractions[0], cosine, sine)
+    shift_lines(strip, shifted, base, step * groups, spare, tiles, 0, rows)
+    for first in range(0, tiles, batch):
+        ramped = ramped_lines(shifted, first, batch, rows, cosine, sine, forward)
+        result = jnp.dot(ramped, inverse[...], preferred_element_type=jnp.float32)
+        out[first : first + batch] = result.astype(jnp.bfloat16).reshape(batch, 2, rows, BLOCK)
+
+
+def shear_tile(own, lefts, rights, chunks, halo, base, spare, fractions, tables):
     wide = own.ndim == 3
     line_count = own.shape[-2]
     tiles = own.shape[2] // BLOCK if wide else own.shape[0]
-    views = spare.shape[0]
     rows = BLOCK
     forward, inverse = tables
-    cosine, sine = ramps
 
     def piece_spec(piece):
         if wide:
             return pl.BlockSpec((2, rows, piece.shape[2]), lambda i, *_: (0, i, 0))
         return pl.BlockSpec((piece.shape[0], 2, rows, BLOCK), lambda i, *_: (0, 0, i, 0))
 
-    line_spec = pl.BlockSpec((views, rows, BLOCK), lambda i, *_: (0, i, 0))
+    line_spec = pl.BlockSpec((1, 1, rows), lambda i, *_: (i, 0, 0))
+    along = lambda x: x.astype(jnp.float32).reshape(-1, 1, rows)
     out_shape = jax.ShapeDtypeStruct((tiles, 2, line_count, BLOCK), jnp.bfloat16)
     out_spec = pl.BlockSpec((tiles, 2, rows, BLOCK), lambda i, *_: (0, 0, i, 0))
     kernel = functools.partial(
         shear_tile_kernel,
-        views,
         halo,
         tiles,
         rows,
         tiles // 2 if tiles % 2 == 0 else tiles,
         wide,
-        left_chunks,
-        right_chunks,
+        chunks,
+        chunks,
     )
     return pl.pallas_call(
         kernel,
@@ -189,25 +186,43 @@
             num_scalar_prefetch=1,
             grid=(line_count // rows,),
             in_specs=[piece_spec(p) for p in (*lefts, *rights, own)]
-            + [line_spec] * 3
+            + [line_spec] * 2
             + [
                 pl.BlockSpec(forward.shape, lambda i, *_: (0, 0)),
                 pl.BlockSpec(inverse.shape, lambda i, *_: (0, 0)),
             ],
-            out_specs=[out_spec] * views,
+            out_specs=out_spec,
             scratch_shapes=[
                 pltpu.VMEM((halo + tiles + halo + 2, 2, rows, BLOCK), jnp.bfloat16),
                 pltpu.VMEM((tiles + 1, 2, rows, BLOCK), jnp.bfloat16),
+                pltpu.VMEM((rows, BLOCK), jnp.int32),
+                pltpu.VMEM((rows, BLOCK), jnp.float32),
+                pltpu.VMEM((rows, BLOCK), jnp.float32),
             ],
         ),
-        out_shape=[out_shape] * views,
+        out_shape=out_shape,
         compiler_params=pltpu.CompilerParams(vmem_limit_bytes=VMEM_LIMIT),
         name="shear_tile",
-    )(base.reshape(-1), *lefts, *rights, own, spare, cosine, sine, forward, inverse)
+    )(base, *lefts, *rights, own, along(spare), along(fractions), forward, inverse)
 
 
 def shear_whole_kernel(
-    halo, devices, tiles, rows, base, own, spare, cosine, sine, forward, flipped, out, strip, shifted
+    halo,
+    devices,
+    tiles,
+    rows,
+    base,
+    own,
+    offsets,
+    fractions,
+    forward,
+    flipped,
+    out,
+    strip,
+    shifted,
+    spare,
+    cosine,
+    sine,
 ):
     step = pl.program_id(0)
     chunks = devices * tiles
@@ -221,6 +236,8 @@
             strip[halo + chunk] = own[chunk % tiles, chunk // tiles]
         out[0, :, 0:MARGIN, :] = jnp.zeros((2, MARGIN, rows), jnp.bfloat16)
         out[devices - 1, :, MARGIN + length :, :] = jnp.zeros((2, MARGIN, rows), jnp.bfloat16)
+        spare[...] = down_lines(offsets[...]).astype(jnp.int32)
+        line_ramps(fractions[...], cosine, sine)
 
     shift_lines(strip, shifted, base, 0, spare, tiles, step * tiles, rows)
     ramped = ramped_lines(shifted, 0, tiles, rows, cosine, sine, forward)
@@ -248,10 +265,16 @@
                     out[target + 1, part, 0:MARGIN, :] = piece[BLOCK - MARGIN :]
 
 
-def shear_whole(own, halo, base, spare, ramps, tables):
+def shear_whole(own, halo, base, spare, fractions, tables):
     tiles, devices, _, rows, _ = own.shape
     forward, flipped = tables
-    cosine, sine = ramps
+    operands = (
+        own,
+        spare.astype(jnp.float32).reshape(1, rows),
+        fractions.reshape(1, rows),
+        forward,
+        flipped,
+    )
     full = lambda shape: pl.BlockSpec(shape, lambda i, *_: (0,) * len(shape))
     out = (devices, 2, tiles * BLOCK + 2 * MARGIN, rows)
     return pl.pallas_call(
@@ -259,23 +282,38 @@
         grid_spec=pltpu.PrefetchScalarGridSpec(
             num_scalar_prefetch=1,
             grid=(devices,),
-            in_specs=[
-                full(x.shape) for x in (own, spare, cosine, sine, forward, flipped)
-            ],
+            in_specs=[full(x.shape) for x in operands],
             out_specs=full(out),
             scratch_shapes=[
                 pltpu.VMEM((2 * halo + devices * tiles + 2, 2, rows, BLOCK), jnp.bfloat16),
                 pltpu.VMEM((tiles + 1, 2, rows, BLOCK), jnp.bfloat16),
+                pltpu.VMEM((rows, BLOCK), jnp.int32),
+                pltpu.VMEM((rows, BLOCK), jnp.float32),
+                pltpu.VMEM((rows, BLOCK), jnp.float32),
             ],
         ),
         out_shape=jax.ShapeDtypeStruct(out, jnp.bfloat16),
         compiler_params=pltpu.CompilerParams(vmem_limit_bytes=VMEM_LIMIT),
         name="shear_whole",
-    )(base, own, spare, cosine, sine, forward, flipped)
+    )(base, *operands)
 
 
 def shear_columns_kernel(
-    front, blocks, length, rows_out, base, own, spare, cosine, sine, forward, inverse, out, strip, shifted
+    front,
+    blocks,
+    length,
+    rows_out,
+    base,
+    own,
+    offsets,
+    fractions,
+    forward,
+    inverse,
+    out,
+    strip,
+    shifted,
+    cosine,
+    sine,
 ):
     step = pl.program_id(0)
     per_step = length // BLOCK
@@ -290,8 +328,10 @@
             for part in range(2):
                 first = front + block * length
                 strip[part, first : first + length, :] = own[block, part]
-
-    offset = spare[...]
+        bins = lax.broadcasted_iota(jnp.int32, (BLOCK, BLOCK), 0).astype(jnp.float32)
+        sine[...], cosine[...] = sine_cosine(bins * fractions[...] * (-2.0 * np.pi / WINDOW))
+
+    offset = jnp.broadcast_to(offsets[...], (8, BLOCK))
     row = lax.broadcasted_iota(jnp.int32, (8, BLOCK), 0) + (offset & 7)
     wraps = row >= 8
     index = row & 7
@@ -346,10 +386,16 @@
             ]
 
 
-def shear_columns(own, front, back, base, spare, ramps, tables, rows_out):
+def shear_columns(own, front, back, base, spare, fractions, tables, rows_out):
     blocks, _, length, _ = own.shape
     forward, inverse = tables
-    cosine, sine = ramps
+    operands = (
+        own,
+        spare.astype(jnp.int32).reshape(1, BLOCK),
+        fractions.reshape(1, BLOCK),
+        forward,
+        inverse,
+    )
     full = lambda shape: pl.BlockSpec(shape, lambda i, *_: (0,) * len(shape))
     pieces = blocks * length // rows_out
     per_step = pieces // blocks
@@ -358,17 +404,19 @@
         grid_spec=pltpu.PrefetchScalarGridSpec(
             num_scalar_prefetch=1,
             grid=(blocks,),
-            in_specs=[full(x.shape) for x in (own, spare, cosine, sine, forward, inverse)],
+            in_specs=[full(x.shape) for x in operands],
             out_specs=pl.BlockSpec((per_step, 2, rows_out, BLOCK), lambda i, *_: (i, 0, 0, 0)),
             scratch_shapes=[
                 pltpu.VMEM((2, front + blocks * length + back, BLOCK), jnp.bfloat16),
                 pltpu.VMEM((blocks * length + BLOCK, 2 * BLOCK), jnp.bfloat16),
+                pltpu.VMEM((BLOCK, BLOCK), jnp.float32),
+                pltpu.VMEM((BLOCK, BLOCK), jnp.float32),
             ],
         ),
         out_shape=jax.ShapeDtypeStruct((pieces, 2, rows_out, BLOCK), jnp.bfloat16),
         compiler_params=pltpu.CompilerParams(vmem_limit_bytes=VMEM_LIMIT),
         name="shear_columns",
-    )(base, own, spare, cosine, sine, forward, inverse)
+    )(base, *operands)
 
 
 def sine_cosine(angle):
@@ -516,8 +564,8 @@
     plan = []
     for chunk in range(1, halo + 1):
         users = [d for d in range(row_devices) if reach[d] >= chunk]
-        if plan and plan[-1][2] == users:
-            plan[-1] = (plan[-1][0], chunk, users)
+        if plan and (plan[-1][2] == users or chunk % GATHERED != 1):
+            plan[-1] = (plan[-1][0], chunk, plan[-1][2])
         else:
             plan.append((chunk, chunk, users))
     return plan
@@ -542,10 +590,6 @@
     base = jnp.min(grouped, -1) // unit
     spare = grouped - base[..., None] * unit
     return base.astype(jnp.int32), spare.reshape(starts.shape)
-
-
-def over_lanes(spare):
-    return jnp.broadcast_to(spare[..., None], (*spare.shape, BLOCK)).astype(jnp.int32)
 
 
 def on_device(
@@ -579,20 +623,19 @@
     wave_b_halos = from_both_sides(wave_b[:, :MARGIN], wave_b[:, -MARGIN:], "col")
 
     base_rows, spare_rows = group_starts(halo * BLOCK - MARGIN - shift_rows, GROUP, BLOCK)
-    first_ramps = shear_phase(fraction_rows[:, 0].reshape(-1))
-    first_ramps = [x.reshape(2, line_count, BLOCK) for x in first_ramps]
-    sheared = shear_tile(
-        volume_plane,
-        lefts,
-        rights,
-        chunks,
-        chunks,
-        halo,
-        base_rows[:, 0],
-        over_lanes(spare_rows[:, 0]),
-        first_ramps,
-        row_tables,
-    )
+
+    def first(view):
+        return shear_tile(
+            volume_plane,
+            lefts,
+            rights,
+            chunks,
+            halo,
+            base_rows[view, 0],
+            spare_rows[view, 0],
+            fraction_rows[view, 0],
+            row_tables,
+        )
 
     front = -(-(SHIFT_Y + MARGIN) // GROUP) * GROUP
     back = front + 3 * BLOCK
@@ -601,15 +644,14 @@
     column_fractions = mine(fraction_columns)
 
     def second(view, rows_out):
-        spread = lax.all_to_all(sheared[view], "row", split_axis=0, concat_axis=0, tiled=True)
-        cosine, sine = shear_phase(column_fractions[view])
+        spread = lax.all_to_all(first(view), "row", split_axis=0, concat_axis=0, tiled=True)
         return shear_columns(
             spread.reshape(row_devices, 2, line_count, BLOCK),
             front,
             back,
             base_columns[view] * GROUP,
-            jnp.broadcast_to(spare_columns[view][None], (8, BLOCK)).astype(jnp.int32),
-            (cosine.T, sine.T),
+            spare_columns[view],
+            column_fractions[view],
             column_tables,
             rows_out,
         )
@@ -643,8 +685,8 @@
         whole,
         halo,
         lax.dynamic_slice_in_dim(base_rows[1, 1], column_index * groups, groups, 0),
-        over_lanes(own_lines(spare_rows[1, 1])),
-        shear_phase(own_lines(fraction_rows[1, 1])),
+        own_lines(spare_rows[1, 1]),
+        own_lines(fraction_rows[1, 1]),
         turned_tables,
     )
     turned = lax.all_to_all(turned, "col", split_axis=0, concat_axis=0, tiled=True)
@@ -652,16 +694,15 @@
     moved_a = second(0, line_count)
     tile = lax.all_to_all(moved_a, "row", split_axis=0, concat_axis=0, tiled=True)
     lefts, rights = exchange_chunks(lambda a, b: tile[a:b], plan, tiles)
-    (rotated,) = shear_tile(
+    rotated = shear_tile(
         tile,
         lefts,
         rights,
         chunks,
-        chunks,
         halo,
-        base_rows[:1, 1],
-        over_lanes(spare_rows[:1, 1]),
-        [x[None] for x in shear_phase(fraction_rows[0, 1])],
+        base_rows[0, 1],
+        spare_rows[0, 1],
+        fraction_rows[0, 1],
         row_tables,
     )
 

time: 397 us -> 387 us (0.975)
  blocking collectives: 54.2 us -> 0 us
  starting transfers between devices: 94.9 us -> 149 us
  waiting for transfers between devices: 108 us -> 99.5 us
  other arithmetic: 9.79 us -> 3.18 us
  Pallas kernels: 97.3 us -> 103 us
    all_to_all x1 -> x0, blocking collectives: 54.2 us -> none  [second(): lax.all_to_all(sheared[view], 'row', split_axis=0, concat_axis=0, tiled=T...]
    ppermute x10, starting transfers between devices: 47.4 us -> 95.1 us  [from_both_sides(): return (lax.ppermute(last, axis, up), lax.ppermute(first, axis, down))]
    all_to_all x1 -> x2, starting transfers between devices: 4.98 us -> 26.6 us  [second(): lax.all_to_all(first(view), 'row', split_axis=0, concat_axis=0, tiled=True)]
    ppermute x8 -> x4, waiting for transfers between devices: 36 us -> 15.5 us  [exchange_chunks(): lax.ppermute(piece(tiles - far, tiles - near + 1), ('row', 'col'), up)]
    all_to_all x1 -> x2, waiting for transfers between devices: 7.63 us -> 21.9 us  [second(): lax.all_to_all(first(view), 'row', split_axis=0, concat_axis=0, tiled=True)]
    ppermute x8 -> x4, starting transfers between devices: 19.9 us -> 7.87 us  [exchange_chunks(): lax.ppermute(piece(tiles - far, tiles - near + 1), ('row', 'col'), up)]
    ppermute x8 -> x4, waiting for transfers between devices: 15.4 us -> 4.08 us  [exchange_chunks(): rights.append(lax.ppermute(piece(near - 1, far), ('row', 'col'), down))]
    sin x5 -> x0, other arithmetic: 7.71 us -> none  [shear_phase(): return (jnp.cos(phases), jnp.sin(phases))]
  transfers between devices with their start and end apart: 30 -> 23, of which waited for: 11 -> 9; matrix products, arithmetic and copies ran while one was open for 6% -> 4% of each run, Pallas kernels for 16% -> 20%
where the time goes in v2:
time: 387 us; the launch traced here: 383 us
  starting transfers between devices  149 us (39%)
  Pallas kernels  103 us (27%)
  waiting for transfers between devices  99.5 us (26%)
  local copies, waits for them, and re-layouts  25.5 us (7%)
    ppermute x10, starting transfers between devices, from_both_sides(): return (lax.ppermute(last, axis, up), lax.ppermute(first, axis, down))  95.1 us
    all_to_all x1, waiting for transfers between devices, on_device(): lax.all_to_all(moved_b, ('row', 'col'), split_axis=0, concat_axis=0, tile...  32.8 us
    pallas_call x3, Pallas kernels, shear_tile(): pl.pallas_call(kernel, grid_spec=pltpu.PrefetchScalarGridSpec(num_scalar_...  32.6 us
    pallas_call x2, Pallas kernels, shear_columns(): pl.pallas_call(functools.partial(shear_columns_kernel, front, blocks, len...  26.8 us
    all_to_all x2, starting transfers between devices, second(): lax.all_to_all(first(view), 'row', split_axis=0, concat_axis=0, tiled=True)  26.6 us
    all_to_all x2, waiting for transfers between devices, second(): lax.all_to_all(first(view), 'row', split_axis=0, concat_axis=0, tiled=True)  21.9 us
    pallas_call x2, Pallas kernels, travel_first(): pl.pallas_call(functools.partial(travel_first_kernel, length, len(halos)...  18.2 us
    ppermute x4, waiting for transfers between devices, exchange_chunks(): lax.ppermute(piece(tiles - far, tiles - near + 1), ('row', 'col'), up)  15.5 us
  transfers between devices with their start and end apart: 23, of which 9 were waited for; matrix products, arithmetic and copies ran while one was open for 4% of the time, Pallas kernels for 20%

profile of v2, /device:TPU:2, one launch (start us, length us, event | category | flops | bytes accessed | tf_op | source)
XLA Modules:
  0.0 382.5 jit_solution(5364121533753105042)
XLA Ops:
  0.7 3.1 fusion.30
  3.8 3.7 collective-permute-start
  14.7 15.5 %collective-permute-done.refs_0_ = bf16[2,512,512]{2,1,0:T(8,128)(2,1)S(1)} collective-permute-done((bf16[2,512,512]{2,1,0:T(8,128)(2,1)}, bf16[2,512,512]{2,1,0:T(8,128)(2,1)S(1)}, u32[]{:S(2)}, u32[]{:S(2)}) %collective-permute-start) | collective-permute-done | bytes 1048608 | tf_op jit(solution)/shard_map/ppermute | solution.py:582
  30.1 4.1 %collective-permute-done.2.refs_2_ = bf16[2,512,512]{2,1,0:T(8,128)(2,1)S(1)} collective-permute-done((bf16[2,512,512]{2,1,0:T(8,128)(2,1)}, bf16[2,512,512]{2,1,0:T(8,128)(2,1)S(1)}, u32[]{:S(2)}, u32[]{:S(2)}) %collective-permute-start.2) | collective-permute-done | bytes 1048608 | tf_op jit(solution)/shard_map/ppermute | solution.py:583
  35.2 11.1 %shear_tile.5 = bf16[8,2,512,128]{3,2,1,0:T(8,128)(2,1)} custom-call(s32[32]{0:T(128)} %get-tuple-element.38.base, bf16[2,512,512]{2,1,0:T(8,128)(2,1)} %copy-done.5, bf16[2,512,384]{2,1,0:T(8,128)(2,1)} %copy-done.7, bf16[2,512,512]{2,1,0:T(8,128)(2,1)} %copy-done.6, bf16[2,512,384]{2,1,0:T(8,128)(2,1)} %collective-permute-done.3.refs_3_, ...), custom_call_target="tpu_custom_call" | custom-call | tf_op jit(solution)/shard_map/shear_tile/pallas_call | solution.py:183
  46.3 21.6 %all-to-all-start.2 = ((bf16[8,2,512,128]{3,2,1,0:T(8,128)(2,1)}), bf16[8,2,512,128]{3,2,1,0:T(8,128)(2,1)S(1)}, u32[]{:S(2)}, u32[]{:S(2)}) async-start(bf16[8,2,512,128]{3,2,1,0:T(8,128)(2,1)} %shear_tile.5), calls=%async_computation.2 | async-start | bytes 4194304 | tf_op jit(solution)/shard_map/all_to_all | solution.py:647
  67.9 11.1 %shear_tile.3 = bf16[8,2,512,128]{3,2,1,0:T(8,128)(2,1)} custom-call(s32[32]{0:T(128)} %get-tuple-element.40.base, bf16[2,512,512]{2,1,0:T(8,128)(2,1)} %copy-done.5, bf16[2,512,384]{2,1,0:T(8,128)(2,1)} %copy-done.7, bf16[2,512,512]{2,1,0:T(8,128)(2,1)} %copy-done.6, bf16[2,512,384]{2,1,0:T(8,128)(2,1)} %collective-permute-done.3.refs_3_, ...), custom_call_target="tpu_custom_call" | custom-call | tf_op jit(solution)/shard_map/shear_tile/pallas_call | solution.py:183
  79.0 14.0 %all-to-all-done.2.own = bf16[8,2,512,128]{3,2,1,0:T(8,128)(2,1)S(1)} async-done(((bf16[8,2,512,128]{3,2,1,0:T(8,128)(2,1)}), bf16[8,2,512,128]{3,2,1,0:T(8,128)(2,1)S(1)}, u32[]{:S(2)}, u32[]{:S(2)}) %all-to-all-start.2) | async-done | bytes 2097184 | tf_op jit(solution)/shard_map/all_to_all | solution.py:647
  94.3 5.0 %all-to-all-start = ((bf16[8,2,512,128]{3,2,1,0:T(8,128)(2,1)}), bf16[8,2,512,128]{3,2,1,0:T(8,128)(2,1)S(1)}, u32[]{:S(2)}, u32[]{:S(2)}) async-start(bf16[8,2,512,128]{3,2,1,0:T(8,128)(2,1)} %shear_tile.3), calls=%async_computation | async-start | bytes 4194304 | tf_op jit(solution)/shard_map/all_to_all | solution.py:647
  103.2 13.4 %shear_columns.3 = bf16[32,2,128,128]{3,2,1,0:T(8,128)(2,1)} custom-call(s32[1]{0:T(128)} %bitcast.20.base, bf16[8,2,512,128]{3,2,1,0:T(8,128)(2,1)} %copy-done.4, s32[1,128]{1,0:T(1,128)} %get-tuple-element.44.offsets, f32[1,128]{1,0:T(1,128)} %get-tuple-element.42.fractions, bf16[256,256]{1,0:T(8,128)(2,1)} %constant.84.clone.forward, ...), custom_call_target="tpu_custom_call" | custom-call | tf_op jit(solution)/shard_map/shear_columns/pallas_call | solution.py:402
  116.6 7.9 %all-to-all-done.own = bf16[8,2,512,128]{3,2,1,0:T(8,128)(2,1)S(1)} async-done(((bf16[8,2,512,128]{3,2,1,0:T(8,128)(2,1)}), bf16[8,2,512,128]{3,2,1,0:T(8,128)(2,1)S(1)}, u32[]{:S(2)}, u32[]{:S(2)}) %all-to-all-start) | async-done | bytes 2097184 | tf_op jit(solution)/shard_map/all_to_all | solution.py:647
  125.8 4.5 %all-to-all-start.3 = ((bf16[32,2,128,128]{3,2,1,0:T(8,128)(2,1)}), bf16[32,2,128,128]{3,2,1,0:T(8,128)(2,1)}, u32[]{:S(2)}, u32[]{:S(2)}) async-start(bf16[32,2,128,128]{3,2,1,0:T(8,128)(2,1)} %shear_columns.3), calls=%async_computation.3 | async-start | bytes 4194304 | tf_op jit(solution)/shard_map/all_to_all | solution.py:680
  130.9 13.4 %shear_columns.2 = bf16[8,2,512,128]{3,2,1,0:T(8,128)(2,1)} custom-call(s32[1]{0:T(128)} %bitcast.2.base, bf16[8,2,512,128]{3,2,1,0:T(8,128)(2,1)} %copy-done.3, s32[1,128]{1,0:T(1,128)} %get-tuple-element.45.offsets, f32[1,128]{1,0:T(1,128)} %get-tuple-element.43.fractions, bf16[256,256]{1,0:T(8,128)(2,1)} %constant.84.clone.forward, ...), custom_call_target="tpu_custom_call" | custom-call | tf_op jit(solution)/shard_map/shear_columns/pallas_call | solution.py:402
  144.3 32.8 %all-to-all-done.3 = bf16[32,2,128,128]{3,2,1,0:T(8,128)(2,1)} async-done(((bf16[32,2,128,128]{3,2,1,0:T(8,128)(2,1)}), bf16[32,2,128,128]{3,2,1,0:T(8,128)(2,1)}, u32[]{:S(2)}, u32[]{:S(2)}) %all-to-all-start.3) | async-done | bytes 2097184 | tf_op jit(solution)/shard_map/all_to_all | solution.py:680
  177.1 5.3 %all-to-all-start.1 = ((bf16[8,2,512,128]{3,2,1,0:T(8,128)(2,1)}), bf16[8,2,512,128]{3,2,1,0:T(8,128)(2,1)S(1)}, u32[]{:S(2)}, u32[]{:S(2)}) async-start(bf16[8,2,512,128]{3,2,1,0:T(8,128)(2,1)} %shear_columns.2), calls=%async_computation.1 | async-start | bytes 4194304 | tf_op jit(solution)/shard_map/all_to_all | solution.py:695
  183.9 12.8 %shear_whole.1 = bf16[4,2,1088,128]{3,2,1,0:T(8,128)(2,1)} custom-call(s32[8]{0:T(128)} %fusion.15.base, bf16[8,4,2,128,128]{4,3,2,1,0:T(8,128)(2,1)} %bitcast.24.own, f32[1,128]{1,0:T(1,128)} %fusion.17.offsets, f32[1,128]{1,0:T(1,128)} %fusion.18.fractions, bf16[256,256]{1,0:T(8,128)(2,1)} %constant.82.clone.refs_7_.forward, ...), custom_call_target="tpu_custom_call" | custom-call | tf_op jit(solution)/shard_map/shear_whole/pallas_call | solution.py:280
  196.7 10.7 %all-to-all-done.1.refs_4_ = bf16[8,2,512,128]{3,2,1,0:T(8,128)(2,1)S(1)} async-done(((bf16[8,2,512,128]{3,2,1,0:T(8,128)(2,1)}), bf16[8,2,512,128]{3,2,1,0:T(8,128)(2,1)S(1)}, u32[]{:S(2)}, u32[]{:S(2)}) %all-to-all-start.1) | async-done | bytes 2097184 | tf_op jit(solution)/shard_map/all_to_all | solution.py:695
  207.5 4.5 %all-to-all-start.4 = ((bf16[4,2,1088,128]{3,2,1,0:T(8,128)(2,1)}), bf16[4,2,1088,128]{3,2,1,0:T(8,128)(2,1)}, u32[]{:S(2)}, u32[]{:S(2)}) async-start(bf16[4,2,1088,128]{3,2,1,0:T(8,128)(2,1)} %shear_whole.1), calls=%async_computation.4 | async-start | bytes 4456448 | tf_op jit(solution)/shard_map/all_to_all | solution.py:692
  212.8 4.5 %collective-permute-start.14 = (bf16[2,32,512]{2,1,0:T(8,128)(2,1)S(1)}, bf16[2,32,512]{2,1,0:T(8,128)(2,1)S(1)}, u32[]{:S(2)}, u32[]{:S(2)}) collective-permute-start(bf16[2,32,512]{2,1,0:T(8,128)(2,1)S(1)} %get-tuple-element.7), channel_id=1, source_target_pairs={{0,1},{1,2},{2,3},{4,5},{5,6},{6,7},{8,9},{9,10},{10,11},{12,13},{... | collective-permute-start | bytes 196616 | tf_op jit(solution)/shard_map/ppermute | solution.py:552
  218.4 2.8 collective-permute-start.4
  227.2 62.7 %collective-permute-start.11 = (bf16[2,32,1024]{2,1,0:T(8,128)(2,1)S(1)}, bf16[2,32,1024]{2,1,0:T(8,128)(2,1)S(1)}, u32[]{:S(2)}, u32[]{:S(2)}) collective-permute-start(bf16[2,32,1024]{2,1,0:T(8,128)(2,1)S(1)} %get-tuple-element.10), channel_id=1, source_target_pairs={{4,0},{8,4},{12,8},{16,12},{20,16},{24,20},{28,24},{5,1},{9,5},{13... | collective-permute-start | bytes 393224 | tf_op jit(solution)/shard_map/ppermute | solution.py:552
  291.2 10.4 %shear_tile.4.refs_0_ = bf16[8,2,512,128]{3,2,1,0:T(8,128)(2,1)} custom-call(s32[32]{0:T(128)} %get-tuple-element.41.base, bf16[4,2,512,128]{3,2,1,0:T(8,128)(2,1)} %copy-done.8, bf16[3,2,512,128]{3,2,1,0:T(8,128)(2,1)} %copy-done.10, bf16[4,2,512,128]{3,2,1,0:T(8,128)(2,1)} %copy-done.9, bf16[3,2,512,128]{3,2,1,0:T(8,128)(2,1)} %copy-done.11, ...), custom_call_target="tpu_custom_call" | custom-call | tf_op jit(solution)/shard_map/shear_tile/pallas_call | solution.py:183
  304.5 3.6 collective-permute-start.9
  312.6 10.0 %travel_first.2.body = bf16[8,2,512,128]{3,2,1,0:T(8,128)(2,1)} custom-call(bf16[8,2,512,128]{3,2,1,0:T(8,128)(2,1)} %shear_tile.4.refs_0_, bf16[8,2,32,128]{3,2,1,0:T(8,128)(2,1)} %copy-done.19, bf16[8,2,32,128]{3,2,1,0:T(8,128)(2,1)} %copy-done.20, bf16[2,512,1024]{2,1,0:T(8,128)(2,1)} %refs_3_.1, bf16[2,32,1024]{2,1,0:T(8,128)(2,1)} %copy-done.17, ...), custom_call_target="tpu_custom_call" | custom-call | tf_op jit(solution)/shard_map/travel_first/pallas_call | solution.py:498
  322.5 5.5 %collective-permute-done.15.refs_3_ = bf16[2,32,512]{2,1,0:T(8,128)(2,1)S(1)} collective-permute-done((bf16[2,32,512]{2,1,0:T(8,128)(2,1)S(1)}, bf16[2,32,512]{2,1,0:T(8,128)(2,1)S(1)}, u32[]{:S(2)}, u32[]{:S(2)}) %collective-permute-start.15) | collective-permute-done | bytes 65568 | tf_op jit(solution)/shard_map/ppermute | solution.py:552
  328.7 8.2 %travel_first.3.body = bf16[4,2,1024,128]{3,2,1,0:T(8,128)(2,1)} custom-call(bf16[4,2,1088,128]{3,2,1,0:T(8,128)(2,1)} %all-to-all-done.4.refs_0_, bf16[2,1024,512]{2,1,0:T(8,128)(2,1)} %refs_1_.1, bf16[2,32,512]{2,1,0:T(8,128)(2,1)} %copy-done.22, bf16[2,32,512]{2,1,0:T(8,128)(2,1)} %copy-done.23, bf16[256,384]{1,0:T(8,128)(2,1)} %copy.23.refs_4_), custom_call_target="tpu_custom_call" | custom-call | tf_op jit(solution)/shard_map/travel_first/pallas_call | solution.py:498
  340.1 3.6 collective-permute-start.17
  344.9 12.3 %collective-permute-start.12 = (bf16[1,2,512,128]{3,2,1,0:T(8,128)(2,1)S(1)}, bf16[1,2,512,128]{3,2,1,0:T(8,128)(2,1)S(1)}, u32[]{:S(2)}, u32[]{:S(2)}) collective-permute-start(bf16[1,2,512,128]{3,2,1,0:T(8,128)(2,1)S(1)} %get-tuple-element.9), channel_id=1, source_target_pairs={{0,1},{1,2},{2,3},{4,5},{5,6},{6,7},{8,9},{9,10},{10,11},{12,13},{... | collective-permute-start | bytes 786440 | tf_op jit(solution)/shard_map/ppermute | solution.py:552
  359.5 4.1 %collective-permute-done.12.left = bf16[1,2,512,128]{3,2,1,0:T(8,128)(2,1)S(1)} collective-permute-done((bf16[1,2,512,128]{3,2,1,0:T(8,128)(2,1)S(1)}, bf16[1,2,512,128]{3,2,1,0:T(8,128)(2,1)S(1)}, u32[]{:S(2)}, u32[]{:S(2)}) %collective-permute-start.12) | collective-permute-done | bytes 262176 | tf_op jit(solution)/shard_map/ppermute | solution.py:552
  363.5 4.9 %collective-permute-done.13.right = bf16[1,2,512,128]{3,2,1,0:T(8,128)(2,1)S(1)} collective-permute-done((bf16[1,2,512,128]{3,2,1,0:T(8,128)(2,1)S(1)}, bf16[1,2,512,128]{3,2,1,0:T(8,128)(2,1)S(1)}, u32[]{:S(2)}, u32[]{:S(2)}) %collective-permute-start.13) | collective-permute-done | bytes 262176 | tf_op jit(solution)/shard_map/ppermute | solution.py:552
  369.1 5.1 %travel_second.2 = bf16[2,512,1024]{2,1,0:T(8,128)(2,1)} custom-call(bf16[1,2,512,128]{3,2,1,0:T(8,128)(2,1)} %copy-done.14, bf16[8,2,512,128]{3,2,1,0:T(8,128)(2,1)} %travel_first.2.body, bf16[1,2,512,128]{3,2,1,0:T(8,128)(2,1)} %copy-done.15, bf16[768,256]{1,0:T(8,128)(2,1)} %get-tuple-element.23.matrix), custom_call_target="tpu_custom_call" | custom-call | tf_op jit(solution)/shard_map/travel_second/pallas_call | solution.py:532
  375.2 7.3 %travel_second.3 = bf16[2,1024,512]{2,1,0:T(8,128)(2,1)} custom-call(bf16[1,2,1024,128]{3,2,1,0:T(8,128)(2,1)} %copy-done.12, bf16[4,2,1024,128]{3,2,1,0:T(8,128)(2,1)} %travel_first.3.body, bf16[1,2,1024,128]{3,2,1,0:T(8,128)(2,1)} %copy-done.13, bf16[768,256]{1,0:T(8,128)(2,1)} %get-tuple-element.22.matrix), custom_call_target="tpu_custom_call" | custom-call | tf_op jit(solution)/shard_map/travel_second/pallas_call | solution.py:532
  (122 shorter events, 40.8 us)
Async XLA Ops:
  0.6 100.7 %copy-start = (f32[2,1024]{1,0:T(2,128)S(1)}, f32[2,1024]{1,0:T(2,128)}, u32[]{:S(2)}) copy-start(f32[2,1024]{1,0:T(2,128)} %param.22) | copy-start | bytes 24580
  3.8 10.2 %copy-start.25 = (f32[2,2,512]{2,1,0:T(2,128)S(1)}, f32[2,2,512]{2,1,0:T(2,128)}, u32[]{:S(2)}) copy-start(f32[2,2,512]{2,1,0:T(2,128)} %param.20) | copy-start | bytes 24580
  3.8 26.3 %collective-permute-start = (bf16[2,512,512]{2,1,0:T(8,128)(2,1)}, bf16[2,512,512]{2,1,0:T(8,128)(2,1)S(1)}, u32[]{:S(2)}, u32[]{:S(2)}) collective-permute-start(bf16[2,512,512]{2,1,0:T(8,128)(2,1)} %get-tuple-element.21), channel_id=1, source_target_pairs={{0,1},{1,2},{2,3},{4,5},{5,6},{6,7},{8,9},{9,10},{10,11},{12,13},{... | collective-permute-start | bytes 3145736 | tf_op jit(solution)/shard_map/ppermute | solution.py:582
  7.5 26.7 %collective-permute-start.2 = (bf16[2,512,512]{2,1,0:T(8,128)(2,1)}, bf16[2,512,512]{2,1,0:T(8,128)(2,1)S(1)}, u32[]{:S(2)}, u32[]{:S(2)}) collective-permute-start(bf16[2,512,512]{2,1,0:T(8,128)(2,1)} %get-tuple-element.20), channel_id=1, source_target_pairs={{1,0},{2,1},{3,2},{5,4},{6,5},{7,6},{9,8},{10,9},{11,10},{13,12},{... | collective-permute-start | bytes 3145736 | tf_op jit(solution)/shard_map/ppermute | solution.py:583
  10.1 4.5 %collective-permute-start.1 = (bf16[2,512,384]{2,1,0:T(8,128)(2,1)}, bf16[2,512,384]{2,1,0:T(8,128)(2,1)S(1)}, u32[]{:S(2)}, u32[]{:S(2)}) collective-permute-start(bf16[2,512,384]{2,1,0:T(8,128)(2,1)} %get-tuple-element.19), channel_id=1, source_target_pairs={{0,1},{1,2},{2,3},{4,5},{5,6},{6,7},{24,25},{25,26},{26,27},{28,29... | collective-permute-start | bytes 2359304 | tf_op jit(solution)/shard_map/ppermute | solution.py:582
  10.9 3.8 collective-permute-start.3
  14.7 19.6 %copy-start.7 = (bf16[2,512,384]{2,1,0:T(8,128)(2,1)}, bf16[2,512,384]{2,1,0:T(8,128)(2,1)S(1)}, u32[]{:S(2)}) copy-start(bf16[2,512,384]{2,1,0:T(8,128)(2,1)S(1)} %collective-permute-done.1.refs_1_) | copy-start | bytes 2359300
  46.3 46.7 %all-to-all-start.2 = ((bf16[8,2,512,128]{3,2,1,0:T(8,128)(2,1)}), bf16[8,2,512,128]{3,2,1,0:T(8,128)(2,1)S(1)}, u32[]{:S(2)}, u32[]{:S(2)}) async-start(bf16[8,2,512,128]{3,2,1,0:T(8,128)(2,1)} %shear_tile.5), calls=%async_computation.2 | async-start | bytes 4194304 | tf_op jit(solution)/shard_map/all_to_all | solution.py:647
  94.3 30.2 %all-to-all-start = ((bf16[8,2,512,128]{3,2,1,0:T(8,128)(2,1)}), bf16[8,2,512,128]{3,2,1,0:T(8,128)(2,1)S(1)}, u32[]{:S(2)}, u32[]{:S(2)}) async-start(bf16[8,2,512,128]{3,2,1,0:T(8,128)(2,1)} %shear_tile.3), calls=%async_computation | async-start | bytes 4194304 | tf_op jit(solution)/shard_map/all_to_all | solution.py:647
  125.8 51.2 %all-to-all-start.3 = ((bf16[32,2,128,128]{3,2,1,0:T(8,128)(2,1)}), bf16[32,2,128,128]{3,2,1,0:T(8,128)(2,1)}, u32[]{:S(2)}, u32[]{:S(2)}) async-start(bf16[32,2,128,128]{3,2,1,0:T(8,128)(2,1)} %shear_columns.3), calls=%async_computation.3 | async-start | bytes 4194304 | tf_op jit(solution)/shard_map/all_to_all | solution.py:680
  177.1 30.4 %all-to-all-start.1 = ((bf16[8,2,512,128]{3,2,1,0:T(8,128)(2,1)}), bf16[8,2,512,128]{3,2,1,0:T(8,128)(2,1)S(1)}, u32[]{:S(2)}, u32[]{:S(2)}) async-start(bf16[8,2,512,128]{3,2,1,0:T(8,128)(2,1)} %shear_columns.2), calls=%async_computation.1 | async-start | bytes 4194304 | tf_op jit(solution)/shard_map/all_to_all | solution.py:695
  196.7 20.7 %copy-start.26 = (f32[2]{0:T(128)S(1)}, f32[2]{0:T(128)}, u32[]{:S(2)}) copy-start(f32[2]{0:T(128)} %param.23) | copy-start | bytes 28
  196.7 20.8 %copy-start.16 = (f32[192,256,1,1]{1,0,2,3:T(8,128)S(1)}, f32[192,256,1,1]{1,0,2,3:T(8,128)}, u32[]{:S(2)}) copy-start(f32[192,256,1,1]{1,0,2,3:T(8,128)} %constant.91) | copy-start | bytes 589828
  196.7 20.8 %copy-start.21 = (f32[256,128]{1,0:T(8,128)S(1)}, f32[256,128]{1,0:T(8,128)}, u32[]{:S(2)}) copy-start(f32[256,128]{1,0:T(8,128)} %constant.87.clone) | copy-start | bytes 393220
  207.5 15.0 %copy-start.1 = (bf16[8,2,512,128]{3,2,1,0:T(8,128)(2,1)}, bf16[8,2,512,128]{3,2,1,0:T(8,128)(2,1)S(1)}, u32[]{:S(2)}) copy-start(bf16[8,2,512,128]{3,2,1,0:T(8,128)(2,1)S(1)} %all-to-all-done.1.refs_4_) | copy-start | bytes 6291460
  207.5 120.6 %all-to-all-start.4 = ((bf16[4,2,1088,128]{3,2,1,0:T(8,128)(2,1)}), bf16[4,2,1088,128]{3,2,1,0:T(8,128)(2,1)}, u32[]{:S(2)}, u32[]{:S(2)}) async-start(bf16[4,2,1088,128]{3,2,1,0:T(8,128)(2,1)} %shear_whole.1), calls=%async_computation.4 | async-start | bytes 4456448 | tf_op jit(solution)/shard_map/all_to_all | solution.py:692
  212.8 109.7 %collective-permute-start.14 = (bf16[2,32,512]{2,1,0:T(8,128)(2,1)S(1)}, bf16[2,32,512]{2,1,0:T(8,128)(2,1)S(1)}, u32[]{:S(2)}, u32[]{:S(2)}) collective-permute-start(bf16[2,32,512]{2,1,0:T(8,128)(2,1)S(1)} %get-tuple-element.7), channel_id=1, source_target_pairs={{0,1},{1,2},{2,3},{4,5},{5,6},{6,7},{8,9},{9,10},{10,11},{12,13},{... | collective-permute-start | bytes 196616 | tf_op jit(solution)/shard_map/ppermute | solution.py:552
  218.4 71.4 %collective-permute-start.4 = (bf16[4,2,512,128]{3,2,1,0:T(8,128)(2,1)S(1)}, bf16[4,2,512,128]{3,2,1,0:T(8,128)(2,1)S(1)}, u32[]{:S(2)}, u32[]{:S(2)}) collective-permute-start(bf16[4,2,512,128]{3,2,1,0:T(8,128)(2,1)S(1)} %get-tuple-element.17), channel_id=1, source_target_pairs={{0,1},{1,2},{2,3},{4,5},{5,6},{6,7},{8,9},{9,10},{10,11},{12,13},{... | collective-permute-start | bytes 3145736 | tf_op jit(solution)/shard_map/ppermute | solution.py:582
  221.2 68.7 %collective-permute-start.6 = (bf16[4,2,512,128]{3,2,1,0:T(8,128)(2,1)S(1)}, bf16[4,2,512,128]{3,2,1,0:T(8,128)(2,1)S(1)}, u32[]{:S(2)}, u32[]{:S(2)}) collective-permute-start(bf16[4,2,512,128]{3,2,1,0:T(8,128)(2,1)S(1)} %get-tuple-element.16), channel_id=1, source_target_pairs={{1,0},{2,1},{3,2},{5,4},{6,5},{7,6},{9,8},{10,9},{11,10},{13,12},{... | collective-permute-start | bytes 3145736 | tf_op jit(solution)/shard_map/ppermute | solution.py:583
  222.6 2.5 collective-permute-start.5
  223.4 3.8 collective-permute-start.7
  225.2 64.7 %copy-start.10 = (bf16[3,2,512,128]{3,2,1,0:T(8,128)(2,1)}, bf16[3,2,512,128]{3,2,1,0:T(8,128)(2,1)S(1)}, u32[]{:S(2)}) copy-start(bf16[3,2,512,128]{3,2,1,0:T(8,128)(2,1)S(1)} %collective-permute-done.5.refs_1_) | copy-start | bytes 2359300
  225.2 84.6 %collective-permute-start.10 = (bf16[2,32,1024]{2,1,0:T(8,128)(2,1)S(1)}, bf16[2,32,1024]{2,1,0:T(8,128)(2,1)S(1)}, u32[]{:S(2)}, u32[]{:S(2)}) collective-permute-start(bf16[2,32,1024]{2,1,0:T(8,128)(2,1)S(1)} %get-tuple-element.11), channel_id=1, source_target_pairs={{0,4},{4,8},{8,12},{12,16},{16,20},{20,24},{24,28},{1,5},{5,9},{9,... | collective-permute-start | bytes 393224 | tf_op jit(solution)/shard_map/ppermute | solution.py:552
  227.1 62.8 %copy-start.11 = (bf16[3,2,512,128]{3,2,1,0:T(8,128)(2,1)}, bf16[3,2,512,128]{3,2,1,0:T(8,128)(2,1)S(1)}, u32[]{:S(2)}) copy-start(bf16[3,2,512,128]{3,2,1,0:T(8,128)(2,1)S(1)} %collective-permute-done.7.refs_3_) | copy-start | bytes 2359300
  227.2 84.0 %collective-permute-start.11 = (bf16[2,32,1024]{2,1,0:T(8,128)(2,1)S(1)}, bf16[2,32,1024]{2,1,0:T(8,128)(2,1)S(1)}, u32[]{:S(2)}, u32[]{:S(2)}) collective-permute-start(bf16[2,32,1024]{2,1,0:T(8,128)(2,1)S(1)} %get-tuple-element.10), channel_id=1, source_target_pairs={{4,0},{8,4},{12,8},{16,12},{20,16},{24,20},{28,24},{5,1},{9,5},{13... | collective-permute-start | bytes 393224 | tf_op jit(solution)/shard_map/ppermute | solution.py:552
  302.6 8.6 %collective-permute-start.8 = (bf16[8,2,32,128]{3,2,1,0:T(8,128)(2,1)S(1)}, bf16[8,2,32,128]{3,2,1,0:T(8,128)(2,1)S(1)}, u32[]{:S(2)}, u32[]{:S(2)}) collective-permute-start(bf16[8,2,32,128]{3,2,1,0:T(8,128)(2,1)S(1)} %get-tuple-element.13), channel_id=1, source_target_pairs={{0,4},{4,8},{8,12},{12,16},{16,20},{20,24},{24,28},{1,5},{5,9},{9,... | collective-permute-start | bytes 393224 | tf_op jit(solution)/shard_map/ppermute | solution.py:552
  304.5 6.7 %collective-permute-start.9 = (bf16[8,2,32,128]{3,2,1,0:T(8,128)(2,1)S(1)}, bf16[8,2,32,128]{3,2,1,0:T(8,128)(2,1)S(1)}, u32[]{:S(2)}, u32[]{:S(2)}) collective-permute-start(bf16[8,2,32,128]{3,2,1,0:T(8,128)(2,1)S(1)} %get-tuple-element.12), channel_id=1, source_target_pairs={{4,0},{8,4},{12,8},{16,12},{20,16},{24,20},{28,24},{5,1},{9,5},{13... | collective-permute-start | bytes 393224 | tf_op jit(solution)/shard_map/ppermute | solution.py:552
  309.9 18.2 %collective-permute-start.15 = (bf16[2,32,512]{2,1,0:T(8,128)(2,1)S(1)}, bf16[2,32,512]{2,1,0:T(8,128)(2,1)S(1)}, u32[]{:S(2)}, u32[]{:S(2)}) collective-permute-start(bf16[2,32,512]{2,1,0:T(8,128)(2,1)S(1)} %get-tuple-element.6), channel_id=1, source_target_pairs={{1,0},{2,1},{3,2},{5,4},{6,5},{7,6},{9,8},{10,9},{11,10},{13,12},{... | collective-permute-start | bytes 196616 | tf_op jit(solution)/shard_map/ppermute | solution.py:552
  338.2 36.0 %collective-permute-start.16 = (bf16[1,2,1024,128]{3,2,1,0:T(8,128)(2,1)S(1)}, bf16[1,2,1024,128]{3,2,1,0:T(8,128)(2,1)S(1)}, u32[]{:S(2)}, u32[]{:S(2)}) collective-permute-start(bf16[1,2,1024,128]{3,2,1,0:T(8,128)(2,1)S(1)} %get-tuple-element.5), channel_id=1, source_target_pairs={{0,4},{4,8},{8,12},{12,16},{16,20},{20,24},{24,28},{1,5},{5,9},{9,... | collective-permute-start | bytes 1572872 | tf_op jit(solution)/shard_map/ppermute | solution.py:552
  340.1 34.1 %collective-permute-start.17 = (bf16[1,2,1024,128]{3,2,1,0:T(8,128)(2,1)S(1)}, bf16[1,2,1024,128]{3,2,1,0:T(8,128)(2,1)S(1)}, u32[]{:S(2)}, u32[]{:S(2)}) collective-permute-start(bf16[1,2,1024,128]{3,2,1,0:T(8,128)(2,1)S(1)} %get-tuple-element.4), channel_id=1, source_target_pairs={{4,0},{8,4},{12,8},{16,12},{20,16},{24,20},{28,24},{5,1},{9,5},{13... | collective-permute-start | bytes 1572872 | tf_op jit(solution)/shard_map/ppermute | solution.py:552
  344.9 18.7 %collective-permute-start.12 = (bf16[1,2,512,128]{3,2,1,0:T(8,128)(2,1)S(1)}, bf16[1,2,512,128]{3,2,1,0:T(8,128)(2,1)S(1)}, u32[]{:S(2)}, u32[]{:S(2)}) collective-permute-start(bf16[1,2,512,128]{3,2,1,0:T(8,128)(2,1)S(1)} %get-tuple-element.9), channel_id=1, source_target_pairs={{0,1},{1,2},{2,3},{4,5},{5,6},{6,7},{8,9},{9,10},{10,11},{12,13},{... | collective-permute-start | bytes 786440 | tf_op jit(solution)/shard_map/ppermute | solution.py:552
  357.1 11.3 %collective-permute-start.13 = (bf16[1,2,512,128]{3,2,1,0:T(8,128)(2,1)S(1)}, bf16[1,2,512,128]{3,2,1,0:T(8,128)(2,1)S(1)}, u32[]{:S(2)}, u32[]{:S(2)}) collective-permute-start(bf16[1,2,512,128]{3,2,1,0:T(8,128)(2,1)S(1)} %get-tuple-element.8), channel_id=1, source_target_pairs={{1,0},{2,1},{3,2},{5,4},{6,5},{7,6},{9,8},{10,9},{11,10},{13,12},{... | collective-permute-start | bytes 786440 | tf_op jit(solution)/shard_map/ppermute | solution.py:552
  (18 other events, 43.7 us)

commit v3 on v2

--- a/solution.py
+++ b/solution.py
@@ -19,7 +19,7 @@
 WINDOW = BLOCK + 2 * MARGIN
 BINS = WINDOW // 2
 GROUP = 16
-GATHERED = 4
+PARTS = 2
 VMEM_LIMIT = 56 * 1024 * 1024
 
 
@@ -89,9 +89,10 @@
     lax.fori_loop(0, rows // GROUP, one_group, 0)
 
 
-def ramped_lines(shifted, first, count, rows, cosine, sine, forward):
-    lower = shifted[first : first + count].reshape(count * 2 * rows, BLOCK)
-    upper = shifted[first + 1 : first + 1 + count].reshape(count * 2 * rows, BLOCK)
+def ramped_lines(shifted, windows, rows, cosine, sine, forward):
+    count = len(windows)
+    lower = jnp.concatenate([shifted[m].reshape(2 * rows, BLOCK) for m in windows], 0)
+    upper = jnp.concatenate([shifted[m + 1].reshape(2 * rows, BLOCK) for m in windows], 0)
     spectrum = jnp.dot(
         jnp.concatenate([lower, upper], 1), forward[...], preferred_element_type=jnp.float32
     )
@@ -118,11 +119,8 @@
     sine[...], cosine[...] = sine_cosine(down_lines(fractions) * bins * (-2.0 * np.pi / WINDOW))
 
 
-def shear_tile_kernel(
-    halo, tiles, rows, batch, wide, left_chunks, right_chunks, base, *refs
-):
-    lefts, refs = refs[: len(left_chunks)], refs[len(left_chunks) :]
-    rights, refs = refs[: len(right_chunks)], refs[len(right_chunks) :]
+def shear_tile_kernel(halo, tiles, rows, batch, wide, parts, base, rank, *refs):
+    lefts, rights, refs = refs[:parts], refs[parts : 2 * parts], refs[2 * parts :]
     own, offsets, fractions, forward, inverse, out = refs[:6]
     strip, shifted, spare, cosine, sine = refs[6:]
     step = pl.program_id(0)
@@ -140,52 +138,61 @@
             else:
                 strip[first + i] = piece[i]
 
-    for piece, (near, far) in zip(lefts, left_chunks):
-        fill(piece, halo - far, far - near + 1)
-    for piece, (near, far) in zip(rights, right_chunks):
-        fill(piece, halo + tiles + near - 1, far - near + 1)
+    share = pl.num_programs(0) // parts
+    for part in range(parts):
+
+        @pl.when(step // share == part)
+        def _():
+            fill(lefts[part], 0, halo)
+            fill(rights[part], halo + tiles, halo)
+
     fill(own, halo, tiles)
     spare[...] = down_lines(offsets[0]).astype(jnp.int32)
     line_ramps(fractions[0], cosine, sine)
     shift_lines(strip, shifted, base, step * groups, spare, tiles, 0, rows)
     for first in range(0, tiles, batch):
-        ramped = ramped_lines(shifted, first, batch, rows, cosine, sine, forward)
+        windows = [slot ^ rank[0] for slot in range(first, first + batch)]
+        ramped = ramped_lines(shifted, windows, rows, cosine, sine, forward)
         result = jnp.dot(ramped, inverse[...], preferred_element_type=jnp.float32)
         out[first : first + batch] = result.astype(jnp.bfloat16).reshape(batch, 2, rows, BLOCK)
 
 
-def shear_tile(own, lefts, rights, chunks, halo, base, spare, fractions, tables):
+def shear_tile(own, lefts, rights, first, halo, base, rank, spare, fractions, tables):
     wide = own.ndim == 3
-    line_count = own.shape[-2]
+    parts = len(lefts)
+    part_lines = lefts[0].shape[-2]
+    line_count = parts * part_lines
     tiles = own.shape[2] // BLOCK if wide else own.shape[0]
     rows = BLOCK
+    share = part_lines // rows
+    offset = first // rows
     forward, inverse = tables
 
-    def piece_spec(piece):
+    def piece_spec(piece, place):
         if wide:
-            return pl.BlockSpec((2, rows, piece.shape[2]), lambda i, *_: (0, i, 0))
-        return pl.BlockSpec((piece.shape[0], 2, rows, BLOCK), lambda i, *_: (0, 0, i, 0))
-
-    line_spec = pl.BlockSpec((1, 1, rows), lambda i, *_: (i, 0, 0))
+            return pl.BlockSpec((2, rows, piece.shape[2]), lambda i, *_: (0, place(i), 0))
+        return pl.BlockSpec((piece.shape[0], 2, rows, BLOCK), lambda i, *_: (0, 0, place(i), 0))
+
+    halo_specs = [
+        piece_spec(x, lambda i, part=part: jnp.clip(i - part * share, 0, share - 1))
+        for x in (lefts[0], rights[0])
+        for part in range(parts)
+    ]
+    line_spec = pl.BlockSpec((1, 1, rows), lambda i, *_: (i + offset, 0, 0))
     along = lambda x: x.astype(jnp.float32).reshape(-1, 1, rows)
     out_shape = jax.ShapeDtypeStruct((tiles, 2, line_count, BLOCK), jnp.bfloat16)
     out_spec = pl.BlockSpec((tiles, 2, rows, BLOCK), lambda i, *_: (0, 0, i, 0))
+    groups = rows // GROUP
     kernel = functools.partial(
-        shear_tile_kernel,
-        halo,
-        tiles,
-        rows,
-        tiles // 2 if tiles % 2 == 0 else tiles,
-        wide,
-        chunks,
-        chunks,
+        shear_tile_kernel, halo, tiles, rows, tiles // 2 if tiles % 2 == 0 else tiles, wide, parts
     )
     return pl.pallas_call(
         kernel,
         grid_spec=pltpu.PrefetchScalarGridSpec(
-            num_scalar_prefetch=1,
+            num_scalar_prefetch=2,
             grid=(line_count // rows,),
-            in_specs=[piece_spec(p) for p in (*lefts, *rights, own)]
+            in_specs=halo_specs
+            + [piece_spec(own, lambda i: i + offset)]
             + [line_spec] * 2
             + [
                 pl.BlockSpec(forward.shape, lambda i, *_: (0, 0)),
@@ -203,7 +210,17 @@
         out_shape=out_shape,
         compiler_params=pltpu.CompilerParams(vmem_limit_bytes=VMEM_LIMIT),
         name="shear_tile",
-    )(base, *lefts, *rights, own, along(spare), along(fractions), forward, inverse)
+    )(
+        lax.slice_in_dim(base, offset * groups, offset * groups + line_count // GROUP),
+        rank,
+        *lefts,
+        *rights,
+        own,
+        along(spare),
+        along(fractions),
+        forward,
+        inverse,
+    )
 
 
 def shear_whole_kernel(
@@ -240,7 +257,7 @@
         line_ramps(fractions[...], cosine, sine)
 
     shift_lines(strip, shifted, base, 0, spare, tiles, step * tiles, rows)
-    ramped = ramped_lines(shifted, 0, tiles, rows, cosine, sine, forward)
+    ramped = ramped_lines(shifted, range(tiles), rows, cosine, sine, forward)
     target = devices - 1 - step
     for window in range(tiles):
         lines = ramped[window * 2 * rows : (window + 1) * 2 * rows]
@@ -298,23 +315,9 @@
     )(base, *operands)
 
 
-def shear_columns_kernel(
-    front,
-    blocks,
-    length,
-    rows_out,
-    base,
-    own,
-    offsets,
-    fractions,
-    forward,
-    inverse,
-    out,
-    strip,
-    shifted,
-    cosine,
-    sine,
-):
+def shear_columns_kernel(front, blocks, length, rows_out, place, base, rank, *refs):
+    owns, refs = refs[: len(place)], refs[len(place) :]
+    offsets, fractions, forward, inverse, out, strip, shifted, cosine, sine = refs
     step = pl.program_id(0)
     per_step = length // BLOCK
     total = strip.shape[1]
@@ -324,10 +327,12 @@
         strip[:, 0:front, :] = jnp.zeros((2, front, BLOCK), jnp.bfloat16)
         back = front + blocks * length
         strip[:, back:, :] = jnp.zeros((2, total - back, BLOCK), jnp.bfloat16)
-        for block in range(blocks):
-            for part in range(2):
-                first = front + block * length
-                strip[part, first : first + length, :] = own[block, part]
+        for own, slots in zip(owns, place):
+            count = own.shape[2]
+            for i, (slot, within) in enumerate(slots):
+                first = pl.multiple_of(front + (slot ^ rank[0]) * length + within, GROUP)
+                for part in range(2):
+                    strip[part, pl.ds(first, count), :] = own[i, part]
         bins = lax.broadcasted_iota(jnp.int32, (BLOCK, BLOCK), 0).astype(jnp.float32)
         sine[...], cosine[...] = sine_cosine(bins * fractions[...] * (-2.0 * np.pi / WINDOW))
 
@@ -335,9 +340,10 @@
     row = lax.broadcasted_iota(jnp.int32, (8, BLOCK), 0) + (offset & 7)
     wraps = row >= 8
     index = row & 7
+    block_rows = (step ^ rank[0]) * length
 
     def one_chunk(chunk):
-        begin = pl.multiple_of(base[0] + chunk * BLOCK, GROUP)
+        begin = pl.multiple_of(base[0] + block_rows + chunk * BLOCK, GROUP)
         for part in range(2):
             value = strip[part, pl.ds(begin, 2 * BLOCK), :].astype(jnp.float32)
             value = value.reshape(2 * BLOCK // 8, 8, BLOCK)
@@ -350,22 +356,18 @@
             moved = [
                 jnp.where(wraps, pieces[i + 1], pieces[i]) for i in range(BLOCK // 8)
             ]
-            lanes = slice(part * BLOCK, (part + 1) * BLOCK)
-            place = pl.ds(pl.multiple_of(chunk * BLOCK, BLOCK), BLOCK)
-            shifted[place, lanes] = jnp.concatenate(moved, 0).astype(jnp.bfloat16)
-
-    @pl.when(step == 0)
-    def _():
-        one_chunk(0)
-
-    for window in range(per_step):
-        one_chunk(step * per_step + window + 1)
+            shifted[chunk * BLOCK : (chunk + 1) * BLOCK, part * BLOCK : (part + 1) * BLOCK] = (
+                jnp.concatenate(moved, 0).astype(jnp.bfloat16)
+            )
+
+    for chunk in range(per_step + 1):
+        one_chunk(chunk)
     ramp_real = jnp.concatenate([cosine[...]] * 2, 1)
     ramp_imaginary = jnp.concatenate([sine[...]] * 2, 1)
     for window in range(per_step):
-        first = pl.multiple_of((step * per_step + window) * BLOCK, BLOCK)
+        low = window * BLOCK
         spectrum = jnp.dot(
-            forward[...], shifted[pl.ds(first, 2 * BLOCK), :], preferred_element_type=jnp.float32
+            forward[...], shifted[low : low + 2 * BLOCK, :], preferred_element_type=jnp.float32
         )
         real, imaginary = spectrum[:BLOCK], spectrum[BLOCK:]
         ramped = jnp.concatenate(
@@ -378,7 +380,6 @@
         result = jnp.dot(inverse[...], ramped, preferred_element_type=jnp.float32).astype(
             jnp.bfloat16
         )
-        low = window * BLOCK
         block, within = low // rows_out, low % rows_out
         for part in range(2):
             out[block, part, within : within + BLOCK, :] = result[
@@ -386,11 +387,11 @@
             ]
 
 
-def shear_columns(own, front, back, base, spare, fractions, tables, rows_out):
-    blocks, _, length, _ = own.shape
+def shear_columns(owns, place, blocks, front, back, base, rank, spare, fractions, tables, rows_out):
+    length = sum(own.shape[0] * own.shape[2] for own in owns) // blocks
     forward, inverse = tables
     operands = (
-        own,
+        *owns,
         spare.astype(jnp.int32).reshape(1, BLOCK),
         fractions.reshape(1, BLOCK),
         forward,
@@ -400,15 +401,15 @@
     pieces = blocks * length // rows_out
     per_step = pieces // blocks
     return pl.pallas_call(
-        functools.partial(shear_columns_kernel, front, blocks, length, rows_out),
+        functools.partial(shear_columns_kernel, front, blocks, length, rows_out, place),
         grid_spec=pltpu.PrefetchScalarGridSpec(
-            num_scalar_prefetch=1,
+            num_scalar_prefetch=2,
             grid=(blocks,),
             in_specs=[full(x.shape) for x in operands],
             out_specs=pl.BlockSpec((per_step, 2, rows_out, BLOCK), lambda i, *_: (i, 0, 0, 0)),
             scratch_shapes=[
                 pltpu.VMEM((2, front + blocks * length + back, BLOCK), jnp.bfloat16),
-                pltpu.VMEM((blocks * length + BLOCK, 2 * BLOCK), jnp.bfloat16),
+                pltpu.VMEM((length + BLOCK, 2 * BLOCK), jnp.bfloat16),
                 pltpu.VMEM((BLOCK, BLOCK), jnp.float32),
                 pltpu.VMEM((BLOCK, BLOCK), jnp.float32),
             ],
@@ -416,7 +417,7 @@
         out_shape=jax.ShapeDtypeStruct((pieces, 2, rows_out, BLOCK), jnp.bfloat16),
         compiler_params=pltpu.CompilerParams(vmem_limit_bytes=VMEM_LIMIT),
         name="shear_columns",
-    )(base, *operands)
+    )(base, rank, *operands)
 
 
 def sine_cosine(angle):
@@ -552,36 +553,12 @@
     return lax.ppermute(last, axis, up), lax.ppermute(first, axis, down)
 
 
-def halo_plan(line_count, row_devices, halo):
-    share = line_count // row_devices
-    reach = []
-    for device in range(row_devices):
-        ends = [device * share, (device + 1) * share - 1]
-        most = max(
-            -(-abs(2 * r + 1 - line_count) * SHIFT_X // (line_count - 1)) for r in ends
-        )
-        reach.append(-(-(min(most, SHIFT_X) + MARGIN) // BLOCK))
-    plan = []
-    for chunk in range(1, halo + 1):
-        users = [d for d in range(row_devices) if reach[d] >= chunk]
-        if plan and (plan[-1][2] == users or chunk % GATHERED != 1):
-            plan[-1] = (plan[-1][0], chunk, plan[-1][2])
-        else:
-            plan.append((chunk, chunk, users))
-    return plan
-
-
-def exchange_chunks(piece, plan, tiles):
-    columns = lax.axis_size("col")
-    lefts, rights = [], []
-    for near, far, users in plan:
-        up = [
-            (d * columns + c, d * columns + c + 1) for d in users for c in range(columns - 1)
-        ]
-        down = [(b, a) for a, b in up]
-        lefts.append(lax.ppermute(piece(tiles - far, tiles - near + 1), ("row", "col"), up))
-        rights.append(lax.ppermute(piece(near - 1, far), ("row", "col"), down))
-    return lefts, rights
+def swapped_shares(slots):
+    devices = lax.axis_size("row")
+    return [slots[0]] + [
+        lax.ppermute(slots[s], "row", [(i, i ^ s) for i in range(devices)])
+        for s in range(1, devices)
+    ]
 
 
 def group_starts(starts, group, unit):
@@ -607,35 +584,30 @@
     row_index, column_index = lax.axis_index("row"), lax.axis_index("col")
     tiles = width // BLOCK
     halo = -(-(SHIFT_X + MARGIN) // BLOCK)
-    plan = halo_plan(line_count * row_devices, row_devices, halo)
-    chunks = [(near, far) for near, far, _ in plan]
+    reach = halo * BLOCK
 
     forward, inverse = real_tables()
     half = lambda x: jnp.asarray(x, jnp.bfloat16)
     row_tables = (half(forward), half(inverse))
     column_tables = (half(forward.T), half(inverse.T))
     turned_tables = (half(forward), half(inverse[:, ::-1].T))
-
-    lefts, rights = exchange_chunks(
-        lambda a, b: volume_plane[:, :, a * BLOCK : b * BLOCK], plan, tiles
-    )
+    in_order = jnp.zeros((1,), jnp.int32)
+    by_rank = row_index.astype(jnp.int32).reshape(1)
+
+    part_lines = line_count // PARTS
+    lefts, rights = [], []
+    for part in range(PARTS):
+        lines = volume_plane[:, part * part_lines : (part + 1) * part_lines]
+        left, right = from_both_sides(lines[:, :, :reach], lines[:, :, width - reach :], "col")
+        lefts.append(left)
+        rights.append(right)
     wave_a_halos = from_both_sides(wave_a[:, :MARGIN], wave_a[:, -MARGIN:], "row")
     wave_b_halos = from_both_sides(wave_b[:, :MARGIN], wave_b[:, -MARGIN:], "col")
-
-    base_rows, spare_rows = group_starts(halo * BLOCK - MARGIN - shift_rows, GROUP, BLOCK)
-
-    def first(view):
-        return shear_tile(
-            volume_plane,
-            lefts,
-            rights,
-            chunks,
-            halo,
-            base_rows[view, 0],
-            spare_rows[view, 0],
-            fraction_rows[view, 0],
-            row_tables,
-        )
+    lefts[-1], rights[-1], wave_a_halos, wave_b_halos = lax.optimization_barrier(
+        (lefts[-1], rights[-1], wave_a_halos, wave_b_halos)
+    )
+
+    base_rows, spare_rows = group_starts(reach - MARGIN - shift_rows, GROUP, BLOCK)
 
     front = -(-(SHIFT_Y + MARGIN) // GROUP) * GROUP
     back = front + 3 * BLOCK
@@ -643,13 +615,29 @@
     base_columns, spare_columns = group_starts(front - MARGIN - mine(shift_columns), BLOCK, GROUP)
     column_fractions = mine(fraction_columns)
 
-    def second(view, rows_out):
-        spread = lax.all_to_all(first(view), "row", split_axis=0, concat_axis=0, tiled=True)
+    def first(view, begin, lefts, rights, rank):
+        return shear_tile(
+            volume_plane,
+            lefts,
+            rights,
+            begin,
+            halo,
+            base_rows[view, 0],
+            rank,
+            spare_rows[view, 0],
+            fraction_rows[view, 0],
+            row_tables,
+        )
+
+    def second(view, pieces, place, rank, rows_out):
         return shear_columns(
-            spread.reshape(row_devices, 2, line_count, BLOCK),
+            pieces,
+            place,
+            row_devices,
             front,
             back,
             base_columns[view] * GROUP,
+            rank,
             spare_columns[view],
             column_fractions[view],
             column_tables,
@@ -676,7 +664,12 @@
         2,
     ).astype(jnp.bfloat16)
 
-    moved_b = second(1, BLOCK)
+    spread = []
+    for part in range(PARTS):
+        sheared = first(1, part * part_lines, lefts[part : part + 1], rights[part : part + 1], in_order)
+        spread.append(lax.all_to_all(sheared, "row", split_axis=0, concat_axis=0, tiled=True))
+    place = [[(b, part * part_lines) for b in range(row_devices)] for part in range(PARTS)]
+    moved_b = second(1, spread, place, in_order, BLOCK)
     whole = lax.all_to_all(moved_b, ("row", "col"), split_axis=0, concat_axis=0, tiled=True)
     whole = whole.reshape(row_devices, column_devices, 2, BLOCK, BLOCK)
     own_lines = lambda x: lax.dynamic_slice_in_dim(x, column_index * BLOCK, BLOCK, 0)
@@ -689,23 +682,30 @@
         own_lines(fraction_rows[1, 1]),
         turned_tables,
     )
-    turned = lax.all_to_all(turned, "col", split_axis=0, concat_axis=0, tiled=True)
-
-    moved_a = second(0, line_count)
-    tile = lax.all_to_all(moved_a, "row", split_axis=0, concat_axis=0, tiled=True)
-    lefts, rights = exchange_chunks(lambda a, b: tile[a:b], plan, tiles)
+
+    slots = first(0, 0, lefts, rights, by_rank)
+    pieces = swapped_shares([slots[s : s + 1] for s in range(row_devices)])
+    moved_a = second(0, pieces, [[(s, 0)] for s in range(row_devices)], by_rank, line_count)
+    pieces = jnp.concatenate(swapped_shares([moved_a[s : s + 1] for s in range(row_devices)]), 0)
+    tile = jnp.concatenate(
+        [lax.dynamic_slice_in_dim(pieces, row_index ^ d, 1, 0) for d in range(row_devices)], 0
+    )
+    left, right = from_both_sides(tile[:halo], tile[tiles - halo :], "col")
     rotated = shear_tile(
         tile,
-        lefts,
-        rights,
-        chunks,
+        [left],
+        [right],
+        0,
         halo,
         base_rows[0, 1],
+        in_order,
         spare_rows[0, 1],
         fraction_rows[0, 1],
         row_tables,
     )
 
+    turned, left, right = lax.optimization_barrier((turned, left, right))
+    turned = lax.all_to_all(turned, "col", split_axis=0, concat_axis=0, tiled=True)
     half_b = travel_first(turned, (), wave_b, wave_b_halos, along_rows[1])
     left, right = from_both_sides(half_b[:1], half_b[-1:], "row")
     exit_b = travel_second(left, half_b, right, along_columns[1])

time: 387 us -> 367 us (0.948)
  starting transfers between devices: 149 us -> 80.9 us
  waiting for transfers between devices: 99.5 us -> 128 us
  local copies, waits for them, and re-layouts: 25.5 us -> 42 us
    ppermute x10 -> x16, waiting for transfers between devices: 14.5 us -> 67 us  [from_both_sides(): return (lax.ppermute(last, axis, up), lax.ppermute(first, axis, down))]
    ppermute x10 -> x16, starting transfers between devices: 95.1 us -> 44.8 us  [from_both_sides(): return (lax.ppermute(last, axis, up), lax.ppermute(first, axis, down))]
    all_to_all x3 -> x2, waiting for transfers between devices: 32.7 us -> 0.01 us  [on_device(): lax.all_to_all(sheared, 'row', split_axis=0, concat_axis=0, tiled=True)]
    all_to_all x1, waiting for transfers between devices: 32.8 us -> 3.68 us  [on_device(): lax.all_to_all(moved_b, ('row', 'col'), split_axis=0, concat_axis=0, tile...]
    all_to_all x3 -> x2, starting transfers between devices: 31.8 us -> 9.34 us  [on_device(): lax.all_to_all(sheared, 'row', split_axis=0, concat_axis=0, tiled=True)]
    ppermute x8 -> x14, waiting for transfers between devices: 19.6 us -> 39.3 us  [swapped_shares(): lax.ppermute(slots[s], 'row', [(i, i ^ s) for i in range(devices)])]
    all_to_all x1, waiting for transfers between devices: 0.01 us -> 18.3 us  [on_device(): lax.all_to_all(turned, 'col', split_axis=0, concat_axis=0, tiled=True)]
    unnamed x54 -> x77, local copies, waits for them, and re-layouts: 8.65 us -> 17 us
  transfers between devices with their start and end apart: 23 -> 34, of which waited for: 9 -> 13; matrix products, arithmetic and copies ran while one was open for 4% -> 10% of each run, Pallas kernels for 20% -> 25%
where the time goes in v3:
time: 367 us; the launch traced here: 363 us
  waiting for transfers between devices  128 us (35%)
  Pallas kernels  105 us (29%)
  starting transfers between devices  80.9 us (22%)
  local copies, waits for them, and re-layouts  42 us (11%)
  other arithmetic  4.39 us (1%)
    ppermute x16, waiting for transfers between devices, from_both_sides(): return (lax.ppermute(last, axis, up), lax.ppermute(first, axis, down))  67 us
    ppermute x16, starting transfers between devices, from_both_sides(): return (lax.ppermute(last, axis, up), lax.ppermute(first, axis, down))  44.8 us
    ppermute x14, waiting for transfers between devices, swapped_shares(): lax.ppermute(slots[s], 'row', [(i, i ^ s) for i in range(devices)])  39.3 us
    pallas_call x4, Pallas kernels, shear_tile(): pl.pallas_call(kernel, grid_spec=pltpu.PrefetchScalarGridSpec(num_scalar_...  36 us
    pallas_call x2, Pallas kernels, shear_columns(): pl.pallas_call(functools.partial(shear_columns_kernel, front, blocks, len...  25.4 us
    all_to_all x1, waiting for transfers between devices, on_device(): lax.all_to_all(turned, 'col', split_axis=0, concat_axis=0, tiled=True)  18.3 us
    pallas_call x2, Pallas kernels, travel_first(): pl.pallas_call(functools.partial(travel_first_kernel, length, len(halos)...  18.2 us
    unnamed x77, local copies, waits for them, and re-layouts  17 us
  transfers between devices with their start and end apart: 34, of which 13 were waited for; matrix products, arithmetic and copies ran while one was open for 10% of the time, Pallas kernels for 25%

profile of v3, /device:TPU:2, one launch (start us, length us, event | category | flops | bytes accessed | tf_op | source)
XLA Modules:
  0.0 363.4 jit_solution(9140543451385580193)
XLA Ops:
  3.6 3.9 %fusion.27 = (bf16[2,256,896]{2,1,0:T(8,128)(2,1)}, bf16[2,256,896]{2,1,0:T(8,128)(2,1)}, bf16[2,256,896]{2,1,0:T(8,128)(2,1)}, bf16[2,256,896]{2,1,0:T(8,128)(2,1)}) fusion(bf16[2,512,1024]{2,1,0:T(8,128)(2,1)} %refs_2_.3), kind=kLoop, calls=%fused_computation.105 | loop fusion | bytes 7340032 | tf_op jit(solution)/shard_map/slice | solution.py:601
  10.2 5.9 %collective-permute-start.1 = (bf16[2,256,896]{2,1,0:T(8,128)(2,1)}, bf16[2,256,896]{2,1,0:T(8,128)(2,1)S(1)}, u32[]{:S(2)}, u32[]{:S(2)}) collective-permute-start(bf16[2,256,896]{2,1,0:T(8,128)(2,1)} %get-tuple-element.58), channel_id=1, source_target_pairs={{0,1},{1,2},{2,3},{4,5},{5,6},{6,7},{8,9},{9,10},{10,11},{12,13},{... | collective-permute-start | bytes 2752520 | tf_op jit(solution)/shard_map/ppermute | solution.py:553
  16.0 4.8 %collective-permute-start = (bf16[2,256,896]{2,1,0:T(8,128)(2,1)}, bf16[2,256,896]{2,1,0:T(8,128)(2,1)}, u32[]{:S(2)}, u32[]{:S(2)}) collective-permute-start(bf16[2,256,896]{2,1,0:T(8,128)(2,1)} %get-tuple-element.59), channel_id=1, source_target_pairs={{0,1},{1,2},{2,3},{4,5},{5,6},{6,7},{8,9},{9,10},{10,11},{12,13},{... | collective-permute-start | bytes 2752520 | tf_op jit(solution)/shard_map/ppermute | solution.py:553
  26.1 7.4 %collective-permute-done.7.refs_2_.refs_1_ = bf16[2,256,896]{2,1,0:T(8,128)(2,1)S(1)} collective-permute-done((bf16[2,256,896]{2,1,0:T(8,128)(2,1)}, bf16[2,256,896]{2,1,0:T(8,128)(2,1)S(1)}, u32[]{:S(2)}, u32[]{:S(2)}) %collective-permute-start.7) | collective-permute-done | bytes 917536 | tf_op jit(solution)/shard_map/ppermute | solution.py:553
  33.5 4.6 %collective-permute-start.5 = (bf16[2,32,512]{2,1,0:T(8,128)(2,1)}, bf16[2,32,512]{2,1,0:T(8,128)(2,1)}, u32[]{:S(2)}, u32[]{:S(2)}) collective-permute-start(bf16[2,32,512]{2,1,0:T(8,128)(2,1)} %get-tuple-element.61), channel_id=1, source_target_pairs={{0,1},{1,2},{2,3},{4,5},{5,6},{6,7},{8,9},{9,10},{10,11},{12,13},{... | collective-permute-start | bytes 196616 | tf_op jit(solution)/shard_map/ppermute | solution.py:553
  38.1 17.9 %collective-permute-done.refs_0_ = bf16[2,256,896]{2,1,0:T(8,128)(2,1)} collective-permute-done((bf16[2,256,896]{2,1,0:T(8,128)(2,1)}, bf16[2,256,896]{2,1,0:T(8,128)(2,1)}, u32[]{:S(2)}, u32[]{:S(2)}) %collective-permute-start) | collective-permute-done | bytes 917536 | tf_op jit(solution)/shard_map/ppermute | solution.py:553
  57.9 7.0 %shear_tile.6 = bf16[8,2,256,128]{3,2,1,0:T(8,128)(2,1)} custom-call(s32[16]{0:T(128)} %get-tuple-element.81.base, s32[1]{0:T(128)} %constant.75.clone.1.rank, bf16[2,256,896]{2,1,0:T(8,128)(2,1)} %collective-permute-done.refs_0_, bf16[2,256,896]{2,1,0:T(8,128)(2,1)} %copy-done.6, bf16[2,512,1024]{2,1,0:T(8,128)(2,1)} %refs_2_.3, ...), custom_call_target="tpu_custom_call" | custom-call | tf_op jit(solution)/shard_map/shear_tile/pallas_call | solution.py:189
  64.9 4.4 %all-to-all-start = ((bf16[8,2,256,128]{3,2,1,0:T(8,128)(2,1)}), bf16[8,2,256,128]{3,2,1,0:T(8,128)(2,1)S(1)}, u32[]{:S(2)}, u32[]{:S(2)}) async-start(bf16[8,2,256,128]{3,2,1,0:T(8,128)(2,1)} %shear_tile.6), calls=%async_computation | async-start | bytes 2097152 | tf_op jit(solution)/shard_map/all_to_all | solution.py:670
  72.7 10.8 %collective-permute-done.3.refs_4_ = bf16[2,32,1024]{2,1,0:T(8,128)(2,1)S(1)} collective-permute-done((bf16[2,32,1024]{2,1,0:T(8,128)(2,1)S(1)}, bf16[2,32,1024]{2,1,0:T(8,128)(2,1)S(1)}, u32[]{:S(2)}, u32[]{:S(2)}) %collective-permute-start.3) | collective-permute-done | bytes 131104 | tf_op jit(solution)/shard_map/ppermute | solution.py:553
  84.8 11.5 %shear_tile.4 = bf16[8,2,512,128]{3,2,1,0:T(8,128)(2,1)} custom-call(s32[32]{0:T(128)} %get-tuple-element.83.base, s32[1]{0:T(128)} %bitcast.3.rank, bf16[2,256,896]{2,1,0:T(8,128)(2,1)} %collective-permute-done.refs_0_, bf16[2,256,896]{2,1,0:T(8,128)(2,1)} %copy-done.5, bf16[2,256,896]{2,1,0:T(8,128)(2,1)} %copy-done.6, bf16[2,256,896]{2,1,0:T(8,128)(2,1)} %copy-done.4, ...), custom_call_target="tpu_custom_call" | custom-call | tf_op jit(solution)/shard_map/shear_tile/pallas_call | solution.py:189
  102.5 7.0 %shear_tile.7 = bf16[8,2,256,128]{3,2,1,0:T(8,128)(2,1)} custom-call(s32[16]{0:T(128)} %get-tuple-element.80.base, s32[1]{0:T(128)} %constant.75.clone.1.rank, bf16[2,256,896]{2,1,0:T(8,128)(2,1)} %copy-done.5, bf16[2,256,896]{2,1,0:T(8,128)(2,1)} %copy-done.4, bf16[2,512,1024]{2,1,0:T(8,128)(2,1)} %refs_2_.3, f32[4,1,128]{2,1,0:T(1,128)} %get-tuple-element.77.refs_3_, ...), custom_call_target="tpu_custom_call" | custom-call | tf_op jit(solution)/shard_map/shear_tile/pallas_call | solution.py:189
  112.2 5.0 %all-to-all-start.1 = ((bf16[8,2,256,128]{3,2,1,0:T(8,128)(2,1)}), bf16[8,2,256,128]{3,2,1,0:T(8,128)(2,1)}, u32[]{:S(2)}, u32[]{:S(2)}) async-start(bf16[8,2,256,128]{3,2,1,0:T(8,128)(2,1)} %shear_tile.7), calls=%async_computation.1 | async-start | bytes 2097152 | tf_op jit(solution)/shard_map/all_to_all | solution.py:670
  119.5 11.3 %collective-permute-done.11.refs_4_ = bf16[1,2,512,128]{3,2,1,0:T(8,128)(2,1)} collective-permute-done((bf16[1,2,512,128]{3,2,1,0:T(8,128)(2,1)S(1)}, bf16[1,2,512,128]{3,2,1,0:T(8,128)(2,1)}, u32[]{:S(2)}, u32[]{:S(2)}) %collective-permute-start.11) | collective-permute-done | bytes 262176 | tf_op jit(solution)/shard_map/ppermute | solution.py:559
  130.8 6.0 %collective-permute-done.9.refs_2_ = bf16[1,2,512,128]{3,2,1,0:T(8,128)(2,1)S(1)} collective-permute-done((bf16[1,2,512,128]{3,2,1,0:T(8,128)(2,1)S(1)}, bf16[1,2,512,128]{3,2,1,0:T(8,128)(2,1)S(1)}, u32[]{:S(2)}, u32[]{:S(2)}) %collective-permute-start.9) | collective-permute-done | bytes 262176 | tf_op jit(solution)/shard_map/ppermute | solution.py:559
  137.6 12.8 %shear_columns.2 = bf16[8,2,512,128]{3,2,1,0:T(8,128)(2,1)} custom-call(s32[1]{0:T(128)} %bitcast.2.base, s32[1]{0:T(128)} %bitcast.3.rank, bf16[1,2,512,128]{3,2,1,0:T(8,128)(2,1)} %get-tuple-element.55.refs_0_, bf16[1,2,512,128]{3,2,1,0:T(8,128)(2,1)} %copy-done.17, bf16[1,2,512,128]{3,2,1,0:T(8,128)(2,1)} %copy-done.16, ...), custom_call_target="tpu_custom_call" | custom-call | tf_op jit(solution)/shard_map/shear_columns/pallas_call | solution.py:403
  150.4 2.7 fusion.25
  160.2 12.6 %shear_columns.3 = bf16[32,2,128,128]{3,2,1,0:T(8,128)(2,1)} custom-call(s32[1]{0:T(128)} %bitcast.21.base, s32[1]{0:T(128)} %constant.75.clone.1.rank, bf16[8,2,256,128]{3,2,1,0:T(8,128)(2,1)} %copy-done.3, bf16[8,2,256,128]{3,2,1,0:T(8,128)(2,1)} %all-to-all-done.1.refs_1_, s32[1,128]{1,0:T(1,128)} %get-tuple-element.87.refs_2_, ...), custom_call_target="tpu_custom_call" | custom-call | tf_op jit(solution)/shard_map/shear_columns/pallas_call | solution.py:403
  172.8 6.6 %all-to-all-start.2 = ((bf16[32,2,128,128]{3,2,1,0:T(8,128)(2,1)}), bf16[32,2,128,128]{3,2,1,0:T(8,128)(2,1)}, u32[]{:S(2)}, u32[]{:S(2)}) async-start(bf16[32,2,128,128]{3,2,1,0:T(8,128)(2,1)} %shear_columns.3), calls=%async_computation.2 | async-start | bytes 4194304 | tf_op jit(solution)/shard_map/all_to_all | solution.py:673
  181.8 21.1 %collective-permute-done.19 = bf16[1,2,512,128]{3,2,1,0:T(8,128)(2,1)S(1)} collective-permute-done((bf16[1,2,512,128]{3,2,1,0:T(8,128)(2,1)S(1)}, bf16[1,2,512,128]{3,2,1,0:T(8,128)(2,1)S(1)}, u32[]{:S(2)}, u32[]{:S(2)}) %collective-permute-start.19) | collective-permute-done | bytes 262176 | tf_op jit(solution)/shard_map/ppermute | solution.py:559
  214.8 5.8 %collective-permute-start.22 = (bf16[7,2,512,128]{3,2,1,0:T(8,128)(2,1)}, bf16[7,2,512,128]{3,2,1,0:T(8,128)(2,1)}, u32[]{:S(2)}, u32[]{:S(2)}) collective-permute-start(bf16[7,2,512,128]{3,2,1,0:T(8,128)(2,1)} %get-tuple-element.26), channel_id=1, source_target_pairs={{0,1},{1,2},{2,3},{4,5},{5,6},{6,7},{8,9},{9,10},{10,11},{12,13},{... | collective-permute-start | bytes 5505032 | tf_op jit(solution)/shard_map/ppermute | solution.py:553
  222.4 3.7 %all-to-all-done.2 = bf16[32,2,128,128]{3,2,1,0:T(8,128)(2,1)} async-done(((bf16[32,2,128,128]{3,2,1,0:T(8,128)(2,1)}), bf16[32,2,128,128]{3,2,1,0:T(8,128)(2,1)}, u32[]{:S(2)}, u32[]{:S(2)}) %all-to-all-start.2) | async-done | bytes 2097184 | tf_op jit(solution)/shard_map/all_to_all | solution.py:673
  226.1 12.8 %shear_whole.1 = bf16[4,2,1088,128]{3,2,1,0:T(8,128)(2,1)} custom-call(s32[8]{0:T(128)} %fusion.15.base, bf16[8,4,2,128,128]{4,3,2,1,0:T(8,128)(2,1)} %bitcast.26.own, f32[1,128]{1,0:T(1,128)} %fusion.17.offsets, f32[1,128]{1,0:T(1,128)} %fusion.18.fractions, bf16[256,256]{1,0:T(8,128)(2,1)} %constant.95.clone.refs_7_.refs_5_.forward, ...), custom_call_target="tpu_custom_call" | custom-call | tf_op jit(solution)/shard_map/shear_whole/pallas_call | solution.py:297
  238.9 23.1 %collective-permute-done.23.refs_1_ = bf16[7,2,512,128]{3,2,1,0:T(8,128)(2,1)S(1)} collective-permute-done((bf16[7,2,512,128]{3,2,1,0:T(8,128)(2,1)}, bf16[7,2,512,128]{3,2,1,0:T(8,128)(2,1)S(1)}, u32[]{:S(2)}, u32[]{:S(2)}) %collective-permute-start.23) | collective-permute-done | bytes 1835040 | tf_op jit(solution)/shard_map/ppermute | solution.py:553
  263.3 6.9 %all-to-all-start.3 = ((bf16[4,2,1088,128]{3,2,1,0:T(8,128)(2,1)}), bf16[4,2,1088,128]{3,2,1,0:T(8,128)(2,1)S(1)}, u32[]{:S(2)}, u32[]{:S(2)}) async-start(bf16[4,2,1088,128]{3,2,1,0:T(8,128)(2,1)} %shear_whole.1), calls=%async_computation.3 | async-start | bytes 4456448 | tf_op jit(solution)/shard_map/all_to_all | solution.py:708
  271.2 10.5 %shear_tile.5.refs_0_ = bf16[8,2,512,128]{3,2,1,0:T(8,128)(2,1)} custom-call(s32[32]{0:T(128)} %get-tuple-element.84.base, s32[1]{0:T(128)} %constant.75.clone.1.rank, bf16[7,2,512,128]{3,2,1,0:T(8,128)(2,1)} %collective-permute-done.22.refs_0_, bf16[7,2,512,128]{3,2,1,0:T(8,128)(2,1)} %copy-done.8, bf16[8,2,512,128]{3,2,1,0:T(8,128)(2,1)} %copy-done.7, ...), custom_call_target="tpu_custom_call" | custom-call | tf_op jit(solution)/shard_map/shear_tile/pallas_call | solution.py:189
  292.7 10.0 %travel_first.2.body = bf16[8,2,512,128]{3,2,1,0:T(8,128)(2,1)} custom-call(bf16[8,2,512,128]{3,2,1,0:T(8,128)(2,1)} %shear_tile.5.refs_0_, bf16[8,2,32,128]{3,2,1,0:T(8,128)(2,1)} %copy-done.22, bf16[8,2,32,128]{3,2,1,0:T(8,128)(2,1)} %copy-done.21, bf16[2,512,1024]{2,1,0:T(8,128)(2,1)} %refs_3_.1, bf16[2,32,1024]{2,1,0:T(8,128)(2,1)} %copy-done.20, ...), custom_call_target="tpu_custom_call" | custom-call | tf_op jit(solution)/shard_map/travel_first/pallas_call | solution.py:499
  302.7 18.3 %all-to-all-done.3.refs_0_ = bf16[4,2,1088,128]{3,2,1,0:T(8,128)(2,1)S(1)} async-done(((bf16[4,2,1088,128]{3,2,1,0:T(8,128)(2,1)}), bf16[4,2,1088,128]{3,2,1,0:T(8,128)(2,1)S(1)}, u32[]{:S(2)}, u32[]{:S(2)}) %all-to-all-start.3) | async-done | bytes 2228256 | tf_op jit(solution)/shard_map/all_to_all | solution.py:708
  322.3 8.2 %travel_first.3.body = bf16[4,2,1024,128]{3,2,1,0:T(8,128)(2,1)} custom-call(bf16[4,2,1088,128]{3,2,1,0:T(8,128)(2,1)} %copy-done.2, bf16[2,1024,512]{2,1,0:T(8,128)(2,1)} %refs_1_.1, bf16[2,32,512]{2,1,0:T(8,128)(2,1)} %collective-permute-done.5.refs_2_, bf16[2,32,512]{2,1,0:T(8,128)(2,1)} %collective-permute-done.6.refs_3_, bf16[256,384]{1,0:T(8,128)(2,1)} %copy.23.refs_4_), custom_call_target="tpu_custom_call" | custom-call | tf_op jit(solution)/shard_map/travel_first/pallas_call | solution.py:499
  338.5 4.6 %collective-permute-start.26 = (bf16[1,2,512,128]{3,2,1,0:T(8,128)(2,1)S(1)}, bf16[1,2,512,128]{3,2,1,0:T(8,128)(2,1)S(1)}, u32[]{:S(2)}, u32[]{:S(2)}) collective-permute-start(bf16[1,2,512,128]{3,2,1,0:T(8,128)(2,1)S(1)} %get-tuple-element.21), channel_id=1, source_target_pairs={{0,1},{1,2},{2,3},{4,5},{5,6},{6,7},{8,9},{9,10},{10,11},{12,13},{... | collective-permute-start | bytes 786440 | tf_op jit(solution)/shard_map/ppermute | solution.py:553
  344.1 3.4 collective-permute-done.27.right
  350.0 5.1 %travel_second.2 = bf16[2,512,1024]{2,1,0:T(8,128)(2,1)} custom-call(bf16[1,2,512,128]{3,2,1,0:T(8,128)(2,1)} %copy-done.13, bf16[8,2,512,128]{3,2,1,0:T(8,128)(2,1)} %travel_first.2.body, bf16[1,2,512,128]{3,2,1,0:T(8,128)(2,1)} %copy-done.12, bf16[768,256]{1,0:T(8,128)(2,1)} %get-tuple-element.65.matrix), custom_call_target="tpu_custom_call" | custom-call | tf_op jit(solution)/shard_map/travel_second/pallas_call | solution.py:533
  356.1 7.3 %travel_second.3 = bf16[2,1024,512]{2,1,0:T(8,128)(2,1)} custom-call(bf16[1,2,1024,128]{3,2,1,0:T(8,128)(2,1)} %copy-done.10, bf16[4,2,1024,128]{3,2,1,0:T(8,128)(2,1)} %travel_first.3.body, bf16[1,2,1024,128]{3,2,1,0:T(8,128)(2,1)} %copy-done.9, bf16[768,256]{1,0:T(8,128)(2,1)} %get-tuple-element.64.matrix), custom_call_target="tpu_custom_call" | custom-call | tf_op jit(solution)/shard_map/travel_second/pallas_call | solution.py:533
  (171 shorter events, 78.1 us)
Async XLA Ops:
  2.2 67.8 %collective-permute-start.6 = (bf16[2,32,512]{2,1,0:T(8,128)(2,1)}, bf16[2,32,512]{2,1,0:T(8,128)(2,1)}, u32[]{:S(2)}, u32[]{:S(2)}) collective-permute-start(bf16[2,32,512]{2,1,0:T(8,128)(2,1)} %get-tuple-element.60), channel_id=1, source_target_pairs={{1,0},{2,1},{3,2},{5,4},{6,5},{7,6},{9,8},{10,9},{11,10},{13,12},{... | collective-permute-start | bytes 196616 | tf_op jit(solution)/shard_map/ppermute | solution.py:553
  7.6 26.0 %collective-permute-start.7 = (bf16[2,256,896]{2,1,0:T(8,128)(2,1)}, bf16[2,256,896]{2,1,0:T(8,128)(2,1)S(1)}, u32[]{:S(2)}, u32[]{:S(2)}) collective-permute-start(bf16[2,256,896]{2,1,0:T(8,128)(2,1)} %get-tuple-element.56), channel_id=1, source_target_pairs={{1,0},{2,1},{3,2},{5,4},{6,5},{7,6},{9,8},{10,9},{11,10},{13,12},{... | collective-permute-start | bytes 2752520 | tf_op jit(solution)/shard_map/ppermute | solution.py:553
  8.9 74.7 %collective-permute-start.2 = (bf16[2,256,896]{2,1,0:T(8,128)(2,1)}, bf16[2,256,896]{2,1,0:T(8,128)(2,1)S(1)}, u32[]{:S(2)}, u32[]{:S(2)}) collective-permute-start(bf16[2,256,896]{2,1,0:T(8,128)(2,1)} %get-tuple-element.57), channel_id=1, source_target_pairs={{1,0},{2,1},{3,2},{5,4},{6,5},{7,6},{9,8},{10,9},{11,10},{13,12},{... | collective-permute-start | bytes 2752520 | tf_op jit(solution)/shard_map/ppermute | solution.py:553
  10.2 73.4 %collective-permute-start.1 = (bf16[2,256,896]{2,1,0:T(8,128)(2,1)}, bf16[2,256,896]{2,1,0:T(8,128)(2,1)S(1)}, u32[]{:S(2)}, u32[]{:S(2)}) collective-permute-start(bf16[2,256,896]{2,1,0:T(8,128)(2,1)} %get-tuple-element.58), channel_id=1, source_target_pairs={{0,1},{1,2},{2,3},{4,5},{5,6},{6,7},{8,9},{9,10},{10,11},{12,13},{... | collective-permute-start | bytes 2752520 | tf_op jit(solution)/shard_map/ppermute | solution.py:553
  16.0 39.9 %collective-permute-start = (bf16[2,256,896]{2,1,0:T(8,128)(2,1)}, bf16[2,256,896]{2,1,0:T(8,128)(2,1)}, u32[]{:S(2)}, u32[]{:S(2)}) collective-permute-start(bf16[2,256,896]{2,1,0:T(8,128)(2,1)} %get-tuple-element.59), channel_id=1, source_target_pairs={{0,1},{1,2},{2,3},{4,5},{5,6},{6,7},{8,9},{9,10},{10,11},{12,13},{... | collective-permute-start | bytes 2752520 | tf_op jit(solution)/shard_map/ppermute | solution.py:553
  33.5 39.1 %collective-permute-start.5 = (bf16[2,32,512]{2,1,0:T(8,128)(2,1)}, bf16[2,32,512]{2,1,0:T(8,128)(2,1)}, u32[]{:S(2)}, u32[]{:S(2)}) collective-permute-start(bf16[2,32,512]{2,1,0:T(8,128)(2,1)} %get-tuple-element.61), channel_id=1, source_target_pairs={{0,1},{1,2},{2,3},{4,5},{5,6},{6,7},{8,9},{9,10},{10,11},{12,13},{... | collective-permute-start | bytes 196616 | tf_op jit(solution)/shard_map/ppermute | solution.py:553
  56.0 16.7 %collective-permute-start.4 = (bf16[2,32,1024]{2,1,0:T(8,128)(2,1)S(1)}, bf16[2,32,1024]{2,1,0:T(8,128)(2,1)S(1)}, u32[]{:S(2)}, u32[]{:S(2)}) collective-permute-start(bf16[2,32,1024]{2,1,0:T(8,128)(2,1)S(1)} %get-tuple-element.62), channel_id=1, source_target_pairs={{4,0},{8,4},{12,8},{16,12},{20,16},{24,20},{28,24},{5,1},{9,5},{13... | collective-permute-start | bytes 393224 | tf_op jit(solution)/shard_map/ppermute | solution.py:553
  64.9 47.3 %all-to-all-start = ((bf16[8,2,256,128]{3,2,1,0:T(8,128)(2,1)}), bf16[8,2,256,128]{3,2,1,0:T(8,128)(2,1)S(1)}, u32[]{:S(2)}, u32[]{:S(2)}) async-start(bf16[8,2,256,128]{3,2,1,0:T(8,128)(2,1)} %shear_tile.6), calls=%async_computation | async-start | bytes 2097152 | tf_op jit(solution)/shard_map/all_to_all | solution.py:670
  70.0 13.5 %collective-permute-start.3 = (bf16[2,32,1024]{2,1,0:T(8,128)(2,1)S(1)}, bf16[2,32,1024]{2,1,0:T(8,128)(2,1)S(1)}, u32[]{:S(2)}, u32[]{:S(2)}) collective-permute-start(bf16[2,32,1024]{2,1,0:T(8,128)(2,1)S(1)} %get-tuple-element.63), channel_id=1, source_target_pairs={{0,4},{4,8},{8,12},{12,16},{16,20},{20,24},{24,28},{1,5},{5,9},{9,... | collective-permute-start | bytes 393224 | tf_op jit(solution)/shard_map/ppermute | solution.py:553
  98.7 18.4 %collective-permute-start.14 = (bf16[1,2,512,128]{3,2,1,0:T(8,128)(2,1)S(1)}, bf16[1,2,512,128]{3,2,1,0:T(8,128)(2,1)S(1)}, u32[]{:S(2)}, u32[]{:S(2)}) collective-permute-start(bf16[1,2,512,128]{3,2,1,0:T(8,128)(2,1)S(1)} %get-tuple-element.48), channel_id=1, source_target_pairs={{0,28},{4,24},{8,20},{12,16},{16,12},{20,8},{24,4},{28,0},{1,29},{... | collective-permute-start | bytes 786440 | tf_op jit(solution)/shard_map/ppermute | solution.py:559
  99.1 18.3 %collective-permute-start.13 = (bf16[1,2,512,128]{3,2,1,0:T(8,128)(2,1)S(1)}, bf16[1,2,512,128]{3,2,1,0:T(8,128)(2,1)S(1)}, u32[]{:S(2)}, u32[]{:S(2)}) collective-permute-start(bf16[1,2,512,128]{3,2,1,0:T(8,128)(2,1)S(1)} %get-tuple-element.49), channel_id=1, source_target_pairs={{0,24},{4,28},{8,16},{12,20},{16,8},{20,12},{24,0},{28,4},{1,25},{... | collective-permute-start | bytes 786440 | tf_op jit(solution)/shard_map/ppermute | solution.py:559
  109.5 10.0 %collective-permute-start.12 = (bf16[1,2,512,128]{3,2,1,0:T(8,128)(2,1)S(1)}, bf16[1,2,512,128]{3,2,1,0:T(8,128)(2,1)}, u32[]{:S(2)}, u32[]{:S(2)}) collective-permute-start(bf16[1,2,512,128]{3,2,1,0:T(8,128)(2,1)S(1)} %get-tuple-element.50), channel_id=1, source_target_pairs={{0,20},{4,16},{8,28},{12,24},{16,4},{20,0},{24,12},{28,8},{1,21},{... | collective-permute-start | bytes 786440 | tf_op jit(solution)/shard_map/ppermute | solution.py:559
  110.9 19.9 %collective-permute-start.11 = (bf16[1,2,512,128]{3,2,1,0:T(8,128)(2,1)S(1)}, bf16[1,2,512,128]{3,2,1,0:T(8,128)(2,1)}, u32[]{:S(2)}, u32[]{:S(2)}) collective-permute-start(bf16[1,2,512,128]{3,2,1,0:T(8,128)(2,1)S(1)} %get-tuple-element.51), channel_id=1, source_target_pairs={{0,16},{4,20},{8,24},{12,28},{16,0},{20,4},{24,8},{28,12},{1,17},{... | collective-permute-start | bytes 786440 | tf_op jit(solution)/shard_map/ppermute | solution.py:559
  111.3 19.5 %collective-permute-start.10 = (bf16[1,2,512,128]{3,2,1,0:T(8,128)(2,1)S(1)}, bf16[1,2,512,128]{3,2,1,0:T(8,128)(2,1)}, u32[]{:S(2)}, u32[]{:S(2)}) collective-permute-start(bf16[1,2,512,128]{3,2,1,0:T(8,128)(2,1)S(1)} %get-tuple-element.52), channel_id=1, source_target_pairs={{0,12},{4,8},{8,4},{12,0},{16,28},{20,24},{24,20},{28,16},{1,13},{... | collective-permute-start | bytes 786440 | tf_op jit(solution)/shard_map/ppermute | solution.py:559
  112.2 48.1 %all-to-all-start.1 = ((bf16[8,2,256,128]{3,2,1,0:T(8,128)(2,1)}), bf16[8,2,256,128]{3,2,1,0:T(8,128)(2,1)}, u32[]{:S(2)}, u32[]{:S(2)}) async-start(bf16[8,2,256,128]{3,2,1,0:T(8,128)(2,1)} %shear_tile.7), calls=%async_computation.1 | async-start | bytes 2097152 | tf_op jit(solution)/shard_map/all_to_all | solution.py:670
  117.1 19.7 %collective-permute-start.9 = (bf16[1,2,512,128]{3,2,1,0:T(8,128)(2,1)S(1)}, bf16[1,2,512,128]{3,2,1,0:T(8,128)(2,1)S(1)}, u32[]{:S(2)}, u32[]{:S(2)}) collective-permute-start(bf16[1,2,512,128]{3,2,1,0:T(8,128)(2,1)S(1)} %get-tuple-element.53), channel_id=1, source_target_pairs={{0,8},{4,12},{8,0},{12,4},{16,24},{20,28},{24,16},{28,20},{1,9},{5... | collective-permute-start | bytes 786440 | tf_op jit(solution)/shard_map/ppermute | solution.py:559
  117.3 19.5 %collective-permute-start.8 = (bf16[1,2,512,128]{3,2,1,0:T(8,128)(2,1)S(1)}, bf16[1,2,512,128]{3,2,1,0:T(8,128)(2,1)S(1)}, u32[]{:S(2)}, u32[]{:S(2)}) collective-permute-start(bf16[1,2,512,128]{3,2,1,0:T(8,128)(2,1)S(1)} %get-tuple-element.54), channel_id=1, source_target_pairs={{0,4},{4,0},{8,12},{12,8},{16,20},{20,16},{24,28},{28,24},{1,5},{5... | collective-permute-start | bytes 786440 | tf_op jit(solution)/shard_map/ppermute | solution.py:559
  153.1 26.4 %collective-permute-start.16 = (bf16[1,2,512,128]{3,2,1,0:T(8,128)(2,1)}, bf16[1,2,512,128]{3,2,1,0:T(8,128)(2,1)S(1)}, u32[]{:S(2)}, u32[]{:S(2)}) collective-permute-start(bf16[1,2,512,128]{3,2,1,0:T(8,128)(2,1)} %get-tuple-element.45), channel_id=1, source_target_pairs={{0,8},{4,12},{8,0},{12,4},{16,24},{20,28},{24,16},{28,20},{1,9},{5... | collective-permute-start | bytes 786440 | tf_op jit(solution)/shard_map/ppermute | solution.py:559
  154.1 26.6 %collective-permute-start.17 = (bf16[1,2,512,128]{3,2,1,0:T(8,128)(2,1)}, bf16[1,2,512,128]{3,2,1,0:T(8,128)(2,1)S(1)}, u32[]{:S(2)}, u32[]{:S(2)}) collective-permute-start(bf16[1,2,512,128]{3,2,1,0:T(8,128)(2,1)} %get-tuple-element.44), channel_id=1, source_target_pairs={{0,12},{4,8},{8,4},{12,0},{16,28},{20,24},{24,20},{28,16},{1,13},{... | collective-permute-start | bytes 786440 | tf_op jit(solution)/shard_map/ppermute | solution.py:559
  155.6 48.4 %collective-permute-start.21 = (bf16[1,2,512,128]{3,2,1,0:T(8,128)(2,1)S(1)}, bf16[1,2,512,128]{3,2,1,0:T(8,128)(2,1)S(1)}, u32[]{:S(2)}, u32[]{:S(2)}) collective-permute-start(bf16[1,2,512,128]{3,2,1,0:T(8,128)(2,1)S(1)} %get-tuple-element.40), channel_id=1, source_target_pairs={{0,28},{4,24},{8,20},{12,16},{16,12},{20,8},{24,4},{28,0},{1,29},{... | collective-permute-start | bytes 786440 | tf_op jit(solution)/shard_map/ppermute | solution.py:559
  157.3 45.7 %collective-permute-start.20 = (bf16[1,2,512,128]{3,2,1,0:T(8,128)(2,1)}, bf16[1,2,512,128]{3,2,1,0:T(8,128)(2,1)}, u32[]{:S(2)}, u32[]{:S(2)}) collective-permute-start(bf16[1,2,512,128]{3,2,1,0:T(8,128)(2,1)} %get-tuple-element.41), channel_id=1, source_target_pairs={{0,24},{4,28},{8,16},{12,20},{16,8},{20,12},{24,0},{28,4},{1,25},{... | collective-permute-start | bytes 786440 | tf_op jit(solution)/shard_map/ppermute | solution.py:559
  158.6 22.3 %collective-permute-start.18 = (bf16[1,2,512,128]{3,2,1,0:T(8,128)(2,1)}, bf16[1,2,512,128]{3,2,1,0:T(8,128)(2,1)}, u32[]{:S(2)}, u32[]{:S(2)}) collective-permute-start(bf16[1,2,512,128]{3,2,1,0:T(8,128)(2,1)} %get-tuple-element.43), channel_id=1, source_target_pairs={{0,16},{4,20},{8,24},{12,28},{16,0},{20,4},{24,8},{28,12},{1,17},{... | collective-permute-start | bytes 786440 | tf_op jit(solution)/shard_map/ppermute | solution.py:559
  172.8 53.3 %all-to-all-start.2 = ((bf16[32,2,128,128]{3,2,1,0:T(8,128)(2,1)}), bf16[32,2,128,128]{3,2,1,0:T(8,128)(2,1)}, u32[]{:S(2)}, u32[]{:S(2)}) async-start(bf16[32,2,128,128]{3,2,1,0:T(8,128)(2,1)} %shear_columns.3), calls=%async_computation.2 | async-start | bytes 4194304 | tf_op jit(solution)/shard_map/all_to_all | solution.py:673
  179.4 23.5 %collective-permute-start.19 = (bf16[1,2,512,128]{3,2,1,0:T(8,128)(2,1)S(1)}, bf16[1,2,512,128]{3,2,1,0:T(8,128)(2,1)S(1)}, u32[]{:S(2)}, u32[]{:S(2)}) collective-permute-start(bf16[1,2,512,128]{3,2,1,0:T(8,128)(2,1)S(1)} %copy-done.11), channel_id=1, source_target_pairs={{0,20},{4,16},{8,28},{12,24},{16,4},{20,0},{24,12},{28,8},{1,21},{... | collective-permute-start | bytes 786440 | tf_op jit(solution)/shard_map/ppermute | solution.py:559
  213.5 48.5 %collective-permute-start.23 = (bf16[7,2,512,128]{3,2,1,0:T(8,128)(2,1)}, bf16[7,2,512,128]{3,2,1,0:T(8,128)(2,1)S(1)}, u32[]{:S(2)}, u32[]{:S(2)}) collective-permute-start(bf16[7,2,512,128]{3,2,1,0:T(8,128)(2,1)} %dynamic-slice_dynamic-update-slice_fusion.5), channel_id=1, source_target_pairs={{1,0},{2,1},{3,2},{5,4},{6,5},{7,6},{9,8},{10,9},{11,10},{13,12},{... | collective-permute-start | bytes 5505032 | tf_op jit(solution)/shard_map/ppermute | solution.py:553
  214.8 47.2 %collective-permute-start.22 = (bf16[7,2,512,128]{3,2,1,0:T(8,128)(2,1)}, bf16[7,2,512,128]{3,2,1,0:T(8,128)(2,1)}, u32[]{:S(2)}, u32[]{:S(2)}) collective-permute-start(bf16[7,2,512,128]{3,2,1,0:T(8,128)(2,1)} %get-tuple-element.26), channel_id=1, source_target_pairs={{0,1},{1,2},{2,3},{4,5},{5,6},{6,7},{8,9},{9,10},{10,11},{12,13},{... | collective-permute-start | bytes 5505032 | tf_op jit(solution)/shard_map/ppermute | solution.py:553
  263.3 57.7 %all-to-all-start.3 = ((bf16[4,2,1088,128]{3,2,1,0:T(8,128)(2,1)}), bf16[4,2,1088,128]{3,2,1,0:T(8,128)(2,1)S(1)}, u32[]{:S(2)}, u32[]{:S(2)}) async-start(bf16[4,2,1088,128]{3,2,1,0:T(8,128)(2,1)} %shear_whole.1), calls=%async_computation.3 | async-start | bytes 4456448 | tf_op jit(solution)/shard_map/all_to_all | solution.py:708
  285.5 6.5 %collective-permute-start.24 = (bf16[8,2,32,128]{3,2,1,0:T(8,128)(2,1)}, bf16[8,2,32,128]{3,2,1,0:T(8,128)(2,1)S(1)}, u32[]{:S(2)}, u32[]{:S(2)}) collective-permute-start(bf16[8,2,32,128]{3,2,1,0:T(8,128)(2,1)} %get-tuple-element.23), channel_id=1, source_target_pairs={{0,4},{4,8},{8,12},{12,16},{16,20},{20,24},{24,28},{1,5},{5,9},{9,... | collective-permute-start | bytes 393224 | tf_op jit(solution)/shard_map/ppermute | solution.py:553
  331.8 23.3 %collective-permute-start.29 = (bf16[1,2,1024,128]{3,2,1,0:T(8,128)(2,1)S(1)}, bf16[1,2,1024,128]{3,2,1,0:T(8,128)(2,1)S(1)}, u32[]{:S(2)}, u32[]{:S(2)}) collective-permute-start(bf16[1,2,1024,128]{3,2,1,0:T(8,128)(2,1)S(1)} %get-tuple-element.18), channel_id=1, source_target_pairs={{4,0},{8,4},{12,8},{16,12},{20,16},{24,20},{28,24},{5,1},{9,5},{13... | collective-permute-start | bytes 1572872 | tf_op jit(solution)/shard_map/ppermute | solution.py:553
  333.8 21.3 %collective-permute-start.28 = (bf16[1,2,1024,128]{3,2,1,0:T(8,128)(2,1)S(1)}, bf16[1,2,1024,128]{3,2,1,0:T(8,128)(2,1)S(1)}, u32[]{:S(2)}, u32[]{:S(2)}) collective-permute-start(bf16[1,2,1024,128]{3,2,1,0:T(8,128)(2,1)S(1)} %get-tuple-element.19), channel_id=1, source_target_pairs={{0,4},{4,8},{8,12},{12,16},{16,20},{20,24},{24,28},{1,5},{5,9},{9,... | collective-permute-start | bytes 1572872 | tf_op jit(solution)/shard_map/ppermute | solution.py:553
  337.2 10.3 %collective-permute-start.27 = (bf16[1,2,512,128]{3,2,1,0:T(8,128)(2,1)S(1)}, bf16[1,2,512,128]{3,2,1,0:T(8,128)(2,1)S(1)}, u32[]{:S(2)}, u32[]{:S(2)}) collective-permute-start(bf16[1,2,512,128]{3,2,1,0:T(8,128)(2,1)S(1)} %get-tuple-element.20), channel_id=1, source_target_pairs={{1,0},{2,1},{3,2},{5,4},{6,5},{7,6},{9,8},{10,9},{11,10},{13,12},{... | collective-permute-start | bytes 786440 | tf_op jit(solution)/shard_map/ppermute | solution.py:553
  338.5 10.7 %collective-permute-start.26 = (bf16[1,2,512,128]{3,2,1,0:T(8,128)(2,1)S(1)}, bf16[1,2,512,128]{3,2,1,0:T(8,128)(2,1)S(1)}, u32[]{:S(2)}, u32[]{:S(2)}) collective-permute-start(bf16[1,2,512,128]{3,2,1,0:T(8,128)(2,1)S(1)} %get-tuple-element.21), channel_id=1, source_target_pairs={{0,1},{1,2},{2,3},{4,5},{5,6},{6,7},{8,9},{9,10},{10,11},{12,13},{... | collective-permute-start | bytes 786440 | tf_op jit(solution)/shard_map/ppermute | solution.py:553
  (32 other events, 504.4 us)

commit v4 on v3

--- a/solution.py
+++ b/solution.py
@@ -553,6 +553,41 @@
     return lax.ppermute(last, axis, up), lax.ppermute(first, axis, down)
 
 
+def after(value, *others):
+    return lax.optimization_barrier((value, others))[0]
+
+
+def ordered_kernel(rank, *refs):
+    count = len(refs) - 2
+    out, arrived = refs[count], refs[count + 1]
+    copies = [
+        pltpu.make_async_copy(refs[s], out.at[pl.ds(s ^ rank[0], 1)], arrived.at[s])
+        for s in range(count)
+    ]
+    for copy in copies:
+        copy.start()
+    for copy in copies:
+        copy.wait()
+
+
+def ordered(pieces, rank):
+    count = len(pieces)
+    shape = (count, *pieces[0].shape[1:])
+    anywhere = pl.BlockSpec(memory_space=pl.ANY)
+    return pl.pallas_call(
+        ordered_kernel,
+        grid_spec=pltpu.PrefetchScalarGridSpec(
+            num_scalar_prefetch=1,
+            grid=(1,),
+            in_specs=[anywhere] * count,
+            out_specs=anywhere,
+            scratch_shapes=[pltpu.SemaphoreType.DMA((count,))],
+        ),
+        out_shape=jax.ShapeDtypeStruct(shape, pieces[0].dtype),
+        name="ordered",
+    )(rank, *pieces)
+
+
 def swapped_shares(slots):
     devices = lax.axis_size("row")
     return [slots[0]] + [
@@ -603,9 +638,6 @@
         rights.append(right)
     wave_a_halos = from_both_sides(wave_a[:, :MARGIN], wave_a[:, -MARGIN:], "row")
     wave_b_halos = from_both_sides(wave_b[:, :MARGIN], wave_b[:, -MARGIN:], "col")
-    lefts[-1], rights[-1], wave_a_halos, wave_b_halos = lax.optimization_barrier(
-        (lefts[-1], rights[-1], wave_a_halos, wave_b_halos)
-    )
 
     base_rows, spare_rows = group_starts(reach - MARGIN - shift_rows, GROUP, BLOCK)
 
@@ -664,10 +696,14 @@
         2,
     ).astype(jnp.bfloat16)
 
-    spread = []
+    spread, sheared = [], ()
     for part in range(PARTS):
-        sheared = first(1, part * part_lines, lefts[part : part + 1], rights[part : part + 1], in_order)
+        left, right = after((lefts[part], rights[part]), sheared)
+        sheared = first(1, part * part_lines, [left], [right], in_order)
         spread.append(lax.all_to_all(sheared, "row", split_axis=0, concat_axis=0, tiled=True))
+    spread, wave_a_halos, wave_b_halos = lax.optimization_barrier(
+        (spread, wave_a_halos, wave_b_halos)
+    )
     place = [[(b, part * part_lines) for b in range(row_devices)] for part in range(PARTS)]
     moved_b = second(1, spread, place, in_order, BLOCK)
     whole = lax.all_to_all(moved_b, ("row", "col"), split_axis=0, concat_axis=0, tiled=True)
@@ -683,13 +719,13 @@
         turned_tables,
     )
 
+    lefts, rights = after((lefts, rights), sheared)
     slots = first(0, 0, lefts, rights, by_rank)
     pieces = swapped_shares([slots[s : s + 1] for s in range(row_devices)])
+    pieces = after(pieces, moved_b)
     moved_a = second(0, pieces, [[(s, 0)] for s in range(row_devices)], by_rank, line_count)
-    pieces = jnp.concatenate(swapped_shares([moved_a[s : s + 1] for s in range(row_devices)]), 0)
-    tile = jnp.concatenate(
-        [lax.dynamic_slice_in_dim(pieces, row_index ^ d, 1, 0) for d in range(row_devices)], 0
-    )
+    pieces = swapped_shares([moved_a[s : s + 1] for s in range(row_devices)])
+    tile = ordered(pieces, by_rank)
     left, right = from_both_sides(tile[:halo], tile[tiles - halo :], "col")
     rotated = shear_tile(
         tile,

time: 367 us -> 418 us (1.14)
  Pallas kernels: 105 us -> 169 us
  starting transfers between devices: 80.9 us -> 66.7 us
  waiting for transfers between devices: 128 us -> 138 us
  local copies, waits for them, and re-layouts: 42 us -> 35.7 us
    pallas_call x0 -> x1, Pallas kernels: none -> 64.7 us  [ordered(): pl.pallas_call(ordered_kernel, grid_spec=pltpu.PrefetchScalarGridSpec(num...]
    ppermute x14, waiting for transfers between devices: 39.3 us -> 53 us  [swapped_shares(): lax.ppermute(slots[s], 'row', [(i, i ^ s) for i in range(devices)])]
    ppermute x16, waiting for transfers between devices: 67 us -> 55.3 us  [from_both_sides(): return (lax.ppermute(last, axis, up), lax.ppermute(first, axis, down))]
    all_to_all x2, waiting for transfers between devices: 0.01 us -> 10.7 us  [on_device(): lax.all_to_all(sheared, 'row', split_axis=0, concat_axis=0, tiled=True)]
    unnamed x77 -> x76, local copies, waits for them, and re-layouts: 17 us -> 9.08 us
    ppermute x16, starting transfers between devices: 44.8 us -> 40 us  [from_both_sides(): return (lax.ppermute(last, axis, up), lax.ppermute(first, axis, down))]
    slice x1 -> x2, local copies, waits for them, and re-layouts: 2.66 us -> 6.84 us  [the longest x1 4.48 us: on_device(): left, right = from_both_sides(tile[:halo], tile[tiles - halo:], 'col')]
  transfers between devices with their start and end apart: 34 -> 34, of which waited for: 13 -> 17; matrix products, arithmetic and copies ran while one was open for 10% -> 6% of each run, Pallas kernels for 25% -> 34%
where the time goes in v4:
time: 418 us; the launch traced here: 416 us
  Pallas kernels  169 us (40%)
  waiting for transfers between devices  138 us (33%)
  starting transfers between devices  66.7 us (16%)
  local copies, waits for them, and re-layouts  35.7 us (9%)
    pallas_call x1, Pallas kernels, ordered(): pl.pallas_call(ordered_kernel, grid_spec=pltpu.PrefetchScalarGridSpec(num...  64.7 us
    ppermute x16, waiting for transfers between devices, from_both_sides(): return (lax.ppermute(last, axis, up), lax.ppermute(first, axis, down))  55.3 us
    ppermute x14, waiting for transfers between devices, swapped_shares(): lax.ppermute(slots[s], 'row', [(i, i ^ s) for i in range(devices)])  53 us
    ppermute x16, starting transfers between devices, from_both_sides(): return (lax.ppermute(last, axis, up), lax.ppermute(first, axis, down))  40 us
    pallas_call x4, Pallas kernels, shear_tile(): pl.pallas_call(kernel, grid_spec=pltpu.PrefetchScalarGridSpec(num_scalar_...  36 us
    pallas_call x2, Pallas kernels, shear_columns(): pl.pallas_call(functools.partial(shear_columns_kernel, front, blocks, len...  25.4 us
    all_to_all x1, waiting for transfers between devices, on_device(): lax.all_to_all(turned, 'col', split_axis=0, concat_axis=0, tiled=True)  18.5 us
    pallas_call x2, Pallas kernels, travel_first(): pl.pallas_call(functools.partial(travel_first_kernel, length, len(halos)...  18.2 us
  transfers between devices with their start and end apart: 34, of which 17 were waited for; matrix products, arithmetic and copies ran while one was open for 6% of the time, Pallas kernels for 34%

profile of v4, /device:TPU:2, one launch (start us, length us, event | category | flops | bytes accessed | tf_op | source)
XLA Modules:
  0.0 415.8 jit_solution(2174554721333559735)
XLA Ops:
  16.6 12.6 %collective-permute-done.refs_0_ = bf16[2,256,896]{2,1,0:T(8,128)(2,1)S(1)} collective-permute-done((bf16[2,256,896]{2,1,0:T(8,128)(2,1)}, bf16[2,256,896]{2,1,0:T(8,128)(2,1)S(1)}, u32[]{:S(2)}, u32[]{:S(2)}) %collective-permute-start) | collective-permute-done | bytes 917536 | tf_op jit(solution)/shard_map/ppermute | solution.py:553
  29.2 7.9 %collective-permute-done.2.refs_1_.refs_2_ = bf16[2,256,896]{2,1,0:T(8,128)(2,1)S(1)} collective-permute-done((bf16[2,256,896]{2,1,0:T(8,128)(2,1)}, bf16[2,256,896]{2,1,0:T(8,128)(2,1)S(1)}, u32[]{:S(2)}, u32[]{:S(2)}) %collective-permute-start.2) | collective-permute-done | bytes 917536 | tf_op jit(solution)/shard_map/ppermute | solution.py:553
  38.1 7.0 %shear_tile.4 = bf16[8,2,256,128]{3,2,1,0:T(8,128)(2,1)} custom-call(s32[16]{0:T(128)} %get-tuple-element.101.base, s32[1]{0:T(128)} %constant.68.clone.1.rank, bf16[2,256,896]{2,1,0:T(8,128)(2,1)} %copy-done.6, bf16[2,256,896]{2,1,0:T(8,128)(2,1)} %copy-done.8, bf16[2,512,1024]{2,1,0:T(8,128)(2,1)} %refs_4_.2, f32[4,1,128]{2,1,0:T(1,128)} %get-tuple-element.97.refs_3_, ...), custom_call_target="tpu_custom_call" | custom-call | tf_op jit(solution)/shard_map/shear_tile/pallas_call | solution.py:189
  45.0 4.3 %all-to-all-start = ((bf16[8,2,256,128]{3,2,1,0:T(8,128)(2,1)}), bf16[8,2,256,128]{3,2,1,0:T(8,128)(2,1)S(1)}, u32[]{:S(2)}, u32[]{:S(2)}) async-start(bf16[8,2,256,128]{3,2,1,0:T(8,128)(2,1)} %shear_tile.4), calls=%async_computation | async-start | bytes 2097152 | tf_op jit(solution)/shard_map/all_to_all | solution.py:703
  62.3 7.0 %shear_tile.5 = bf16[8,2,256,128]{3,2,1,0:T(8,128)(2,1)} custom-call(s32[16]{0:T(128)} %get-tuple-element.102.base, s32[1]{0:T(128)} %constant.68.clone.1.rank, bf16[2,256,896]{2,1,0:T(8,128)(2,1)} %copy-done.7, bf16[2,256,896]{2,1,0:T(8,128)(2,1)} %collective-permute-done.3.refs_1_.refs_3_, bf16[2,512,1024]{2,1,0:T(8,128)(2,1)} %refs_4_.2, ...), custom_call_target="tpu_custom_call" | custom-call | tf_op jit(solution)/shard_map/shear_tile/pallas_call | solution.py:189
  69.3 4.2 %all-to-all-start.1 = ((bf16[8,2,256,128]{3,2,1,0:T(8,128)(2,1)}), bf16[8,2,256,128]{3,2,1,0:T(8,128)(2,1)S(1)}, u32[]{:S(2)}, u32[]{:S(2)}) async-start(bf16[8,2,256,128]{3,2,1,0:T(8,128)(2,1)} %shear_tile.5), calls=%async_computation.1 | async-start | bytes 2097152 | tf_op jit(solution)/shard_map/all_to_all | solution.py:703
  76.7 10.7 %all-to-all-done.1.refs_1_ = bf16[8,2,256,128]{3,2,1,0:T(8,128)(2,1)S(1)} async-done(((bf16[8,2,256,128]{3,2,1,0:T(8,128)(2,1)}), bf16[8,2,256,128]{3,2,1,0:T(8,128)(2,1)S(1)}, u32[]{:S(2)}, u32[]{:S(2)}) %all-to-all-start.1) | async-done | bytes 1048608 | tf_op jit(solution)/shard_map/all_to_all | solution.py:703
  88.4 12.6 %shear_columns.2 = bf16[32,2,128,128]{3,2,1,0:T(8,128)(2,1)} custom-call(s32[1]{0:T(128)} %bitcast.11.base, s32[1]{0:T(128)} %constant.68.clone.1.rank, bf16[8,2,256,128]{3,2,1,0:T(8,128)(2,1)} %copy-done.4, bf16[8,2,256,128]{3,2,1,0:T(8,128)(2,1)} %copy-done.5, s32[1,128]{1,0:T(1,128)} %get-tuple-element.106.refs_2_, f32[1,128]{1,0:T(1,128)} %get-tuple-element.104.refs_3_, ...), custom_call_target="tpu_custom_call" | custom-call | tf_op jit(solution)/shard_map/shear_columns/pallas_call | solution.py:403
  101.0 4.3 %all-to-all-start.2 = ((bf16[32,2,128,128]{3,2,1,0:T(8,128)(2,1)}), bf16[32,2,128,128]{3,2,1,0:T(8,128)(2,1)S(1)}, u32[]{:S(2)}, u32[]{:S(2)}) async-start(bf16[32,2,128,128]{3,2,1,0:T(8,128)(2,1)} %shear_columns.2), calls=%async_computation.2 | async-start | bytes 4194304 | tf_op jit(solution)/shard_map/all_to_all | solution.py:709
  105.8 11.5 %shear_tile.6 = bf16[8,2,512,128]{3,2,1,0:T(8,128)(2,1)} custom-call(s32[32]{0:T(128)} %get-tuple-element.99.base, s32[1]{0:T(128)} %bitcast.1.rank, bf16[2,256,896]{2,1,0:T(8,128)(2,1)} %copy-done.6, bf16[2,256,896]{2,1,0:T(8,128)(2,1)} %copy-done.7, bf16[2,256,896]{2,1,0:T(8,128)(2,1)} %copy-done.8, ...), custom_call_target="tpu_custom_call" | custom-call | tf_op jit(solution)/shard_map/shear_tile/pallas_call | solution.py:189
  124.9 7.6 %collective-permute-done.5.refs_2_ = bf16[1,2,512,128]{3,2,1,0:T(8,128)(2,1)S(1)} collective-permute-done((bf16[1,2,512,128]{3,2,1,0:T(8,128)(2,1)S(1)}, bf16[1,2,512,128]{3,2,1,0:T(8,128)(2,1)S(1)}, u32[]{:S(2)}, u32[]{:S(2)}) %collective-permute-start.5) | collective-permute-done | bytes 262176 | tf_op jit(solution)/shard_map/ppermute | solution.py:594
  134.3 5.5 %collective-permute-done.6.refs_3_ = bf16[1,2,512,128]{3,2,1,0:T(8,128)(2,1)S(1)} collective-permute-done((bf16[1,2,512,128]{3,2,1,0:T(8,128)(2,1)S(1)}, bf16[1,2,512,128]{3,2,1,0:T(8,128)(2,1)S(1)}, u32[]{:S(2)}, u32[]{:S(2)}) %collective-permute-start.6) | collective-permute-done | bytes 262176 | tf_op jit(solution)/shard_map/ppermute | solution.py:594
  139.7 4.7 %collective-permute-done.8.refs_5_ = bf16[1,2,512,128]{3,2,1,0:T(8,128)(2,1)S(1)} collective-permute-done((bf16[1,2,512,128]{3,2,1,0:T(8,128)(2,1)S(1)}, bf16[1,2,512,128]{3,2,1,0:T(8,128)(2,1)S(1)}, u32[]{:S(2)}, u32[]{:S(2)}) %collective-permute-start.8) | collective-permute-done | bytes 262176 | tf_op jit(solution)/shard_map/ppermute | solution.py:594
  144.5 5.9 %collective-permute-done.9.refs_6_ = bf16[1,2,512,128]{3,2,1,0:T(8,128)(2,1)S(1)} collective-permute-done((bf16[1,2,512,128]{3,2,1,0:T(8,128)(2,1)S(1)}, bf16[1,2,512,128]{3,2,1,0:T(8,128)(2,1)S(1)}, u32[]{:S(2)}, u32[]{:S(2)}) %collective-permute-start.9) | collective-permute-done | bytes 262176 | tf_op jit(solution)/shard_map/ppermute | solution.py:594
  150.3 6.7 %collective-permute-done.10.refs_7_ = bf16[1,2,512,128]{3,2,1,0:T(8,128)(2,1)S(1)} collective-permute-done((bf16[1,2,512,128]{3,2,1,0:T(8,128)(2,1)S(1)}, bf16[1,2,512,128]{3,2,1,0:T(8,128)(2,1)S(1)}, u32[]{:S(2)}, u32[]{:S(2)}) %collective-permute-start.10) | collective-permute-done | bytes 262176 | tf_op jit(solution)/shard_map/ppermute | solution.py:594
  157.8 12.7 %shear_columns.3 = bf16[8,2,512,128]{3,2,1,0:T(8,128)(2,1)} custom-call(s32[1]{0:T(128)} %bitcast.3.base, s32[1]{0:T(128)} %bitcast.1.rank, bf16[1,2,512,128]{3,2,1,0:T(8,128)(2,1)} %get-tuple-element.35.refs_0_, bf16[1,2,512,128]{3,2,1,0:T(8,128)(2,1)} %copy-done.20, bf16[1,2,512,128]{3,2,1,0:T(8,128)(2,1)} %copy-done.21, ...), custom_call_target="tpu_custom_call" | custom-call | tf_op jit(solution)/shard_map/shear_columns/pallas_call | solution.py:403
  177.0 5.1 %collective-permute-done.16.refs_2_ = bf16[1,2,512,128]{3,2,1,0:T(8,128)(2,1)S(1)} collective-permute-done((bf16[1,2,512,128]{3,2,1,0:T(8,128)(2,1)S(1)}, bf16[1,2,512,128]{3,2,1,0:T(8,128)(2,1)S(1)}, u32[]{:S(2)}, u32[]{:S(2)}) %collective-permute-start.16) | collective-permute-done | bytes 262176 | tf_op jit(solution)/shard_map/ppermute | solution.py:594
  182.1 4.7 %collective-permute-done.17.refs_3_ = bf16[1,2,512,128]{3,2,1,0:T(8,128)(2,1)S(1)} collective-permute-done((bf16[1,2,512,128]{3,2,1,0:T(8,128)(2,1)S(1)}, bf16[1,2,512,128]{3,2,1,0:T(8,128)(2,1)S(1)}, u32[]{:S(2)}, u32[]{:S(2)}) %collective-permute-start.17) | collective-permute-done | bytes 262176 | tf_op jit(solution)/shard_map/ppermute | solution.py:594
  186.8 12.8 %collective-permute-done.19.refs_5_ = bf16[1,2,512,128]{3,2,1,0:T(8,128)(2,1)S(1)} collective-permute-done((bf16[1,2,512,128]{3,2,1,0:T(8,128)(2,1)S(1)}, bf16[1,2,512,128]{3,2,1,0:T(8,128)(2,1)S(1)}, u32[]{:S(2)}, u32[]{:S(2)}) %collective-permute-start.19) | collective-permute-done | bytes 262176 | tf_op jit(solution)/shard_map/ppermute | solution.py:594
  201.1 64.7 %ordered.1.refs_2_ = bf16[8,2,512,128]{3,2,1,0:T(8,128)(2,1)} custom-call(s32[1]{0:T(128)} %bitcast.1.rank, bf16[1,2,512,128]{3,2,1,0:T(8,128)(2,1)} %get-tuple-element.65.refs_0_, bf16[1,2,512,128]{3,2,1,0:T(8,128)(2,1)} %copy-done.11, bf16[1,2,512,128]{3,2,1,0:T(8,128)(2,1)} %copy-done.12, bf16[1,2,512,128]{3,2,1,0:T(8,128)(2,1)} %copy-done.13, ...), custom_call_target="tpu_custom_call" | custom-call | tf_op jit(solution)/shard_map/ordered/pallas_call | solution.py:577
  265.8 4.5 %fusion.25 = (bf16[7,2,512,128]{3,2,1,0:T(8,128)(2,1)}, bf16[7,2,512,128]{3,2,1,0:T(8,128)(2,1)}) fusion(bf16[8,2,512,128]{3,2,1,0:T(8,128)(2,1)} %ordered.1.refs_2_), kind=kLoop, calls=%fused_computation.73 | loop fusion | bytes 7340032 | tf_op jit(solution)/shard_map/slice | solution.py:729
  270.3 5.0 %collective-permute-start.22 = (bf16[7,2,512,128]{3,2,1,0:T(8,128)(2,1)}, bf16[7,2,512,128]{3,2,1,0:T(8,128)(2,1)}, u32[]{:S(2)}, u32[]{:S(2)}) collective-permute-start(bf16[7,2,512,128]{3,2,1,0:T(8,128)(2,1)} %get-tuple-element.57), channel_id=1, source_target_pairs={{0,1},{1,2},{2,3},{4,5},{5,6},{6,7},{8,9},{9,10},{10,11},{12,13},{... | collective-permute-start | bytes 5505032 | tf_op jit(solution)/shard_map/ppermute | solution.py:553
  279.8 12.8 %shear_whole.1 = bf16[4,2,1088,128]{3,2,1,0:T(8,128)(2,1)} custom-call(s32[8]{0:T(128)} %fusion.15.base, bf16[8,4,2,128,128]{4,3,2,1,0:T(8,128)(2,1)} %bitcast.66, f32[1,128]{1,0:T(1,128)} %fusion.17.offsets, f32[1,128]{1,0:T(1,128)} %fusion.18.fractions, bf16[256,256]{1,0:T(8,128)(2,1)} %constant.84.clone.refs_5_.refs_7_.forward, ...), custom_call_target="tpu_custom_call" | custom-call | tf_op jit(solution)/shard_map/shear_whole/pallas_call | solution.py:297
  292.6 21.6 %collective-permute-done.22.refs_0_ = bf16[7,2,512,128]{3,2,1,0:T(8,128)(2,1)} collective-permute-done((bf16[7,2,512,128]{3,2,1,0:T(8,128)(2,1)}, bf16[7,2,512,128]{3,2,1,0:T(8,128)(2,1)}, u32[]{:S(2)}, u32[]{:S(2)}) %collective-permute-start.22) | collective-permute-done | bytes 1835040 | tf_op jit(solution)/shard_map/ppermute | solution.py:553
  314.2 5.3 %collective-permute-done.23.refs_1_ = bf16[7,2,512,128]{3,2,1,0:T(8,128)(2,1)} collective-permute-done((bf16[7,2,512,128]{3,2,1,0:T(8,128)(2,1)}, bf16[7,2,512,128]{3,2,1,0:T(8,128)(2,1)}, u32[]{:S(2)}, u32[]{:S(2)}) %collective-permute-start.23) | collective-permute-done | bytes 1835040 | tf_op jit(solution)/shard_map/ppermute | solution.py:553
  324.1 10.5 %shear_tile.7.refs_0_ = bf16[8,2,512,128]{3,2,1,0:T(8,128)(2,1)} custom-call(s32[32]{0:T(128)} %get-tuple-element.100.base, s32[1]{0:T(128)} %constant.68.clone.1.rank, bf16[7,2,512,128]{3,2,1,0:T(8,128)(2,1)} %collective-permute-done.22.refs_0_, bf16[7,2,512,128]{3,2,1,0:T(8,128)(2,1)} %collective-permute-done.23.refs_1_, ...), custom_call_target="tpu_custom_call" | custom-call | tf_op jit(solution)/shard_map/shear_tile/pallas_call | solution.py:189
  345.4 10.0 %travel_first.2.body = bf16[8,2,512,128]{3,2,1,0:T(8,128)(2,1)} custom-call(bf16[8,2,512,128]{3,2,1,0:T(8,128)(2,1)} %shear_tile.7.refs_0_, bf16[8,2,32,128]{3,2,1,0:T(8,128)(2,1)} %copy-done.30, bf16[8,2,32,128]{3,2,1,0:T(8,128)(2,1)} %copy-done.31, bf16[2,512,1024]{2,1,0:T(8,128)(2,1)} %refs_3_.1, bf16[2,32,1024]{2,1,0:T(8,128)(2,1)} %copy-done.28, ...), custom_call_target="tpu_custom_call" | custom-call | tf_op jit(solution)/shard_map/travel_first/pallas_call | solution.py:499
  355.3 18.5 %all-to-all-done.3.refs_0_ = bf16[4,2,1088,128]{3,2,1,0:T(8,128)(2,1)S(1)} async-done(((bf16[4,2,1088,128]{3,2,1,0:T(8,128)(2,1)}), bf16[4,2,1088,128]{3,2,1,0:T(8,128)(2,1)S(1)}, u32[]{:S(2)}, u32[]{:S(2)}) %all-to-all-start.3) | async-done | bytes 2228256 | tf_op jit(solution)/shard_map/all_to_all | solution.py:744
  375.2 8.2 %travel_first.3.body = bf16[4,2,1024,128]{3,2,1,0:T(8,128)(2,1)} custom-call(bf16[4,2,1088,128]{3,2,1,0:T(8,128)(2,1)} %copy-done.2, bf16[2,1024,512]{2,1,0:T(8,128)(2,1)} %refs_1_.1, bf16[2,32,512]{2,1,0:T(8,128)(2,1)} %copy-done.33, bf16[2,32,512]{2,1,0:T(8,128)(2,1)} %copy-done.34, bf16[256,384]{1,0:T(8,128)(2,1)} %copy.23.refs_4_), custom_call_target="tpu_custom_call" | custom-call | tf_op jit(solution)/shard_map/travel_first/pallas_call | solution.py:499
  397.6 4.1 collective-permute-done.27.right
  402.5 5.1 %travel_second.2 = bf16[2,512,1024]{2,1,0:T(8,128)(2,1)} custom-call(bf16[1,2,512,128]{3,2,1,0:T(8,128)(2,1)} %copy-done.18, bf16[8,2,512,128]{3,2,1,0:T(8,128)(2,1)} %travel_first.2.body, bf16[1,2,512,128]{3,2,1,0:T(8,128)(2,1)} %copy-done.19, bf16[768,256]{1,0:T(8,128)(2,1)} %get-tuple-element.83.matrix), custom_call_target="tpu_custom_call" | custom-call | tf_op jit(solution)/shard_map/travel_second/pallas_call | solution.py:533
  408.5 7.3 %travel_second.3 = bf16[2,1024,512]{2,1,0:T(8,128)(2,1)} custom-call(bf16[1,2,1024,128]{3,2,1,0:T(8,128)(2,1)} %copy-done.9, bf16[4,2,1024,128]{3,2,1,0:T(8,128)(2,1)} %travel_first.3.body, bf16[1,2,1024,128]{3,2,1,0:T(8,128)(2,1)} %copy-done.10, bf16[768,256]{1,0:T(8,128)(2,1)} %get-tuple-element.82.matrix), custom_call_target="tpu_custom_call" | custom-call | tf_op jit(solution)/shard_map/travel_second/pallas_call | solution.py:533
  (169 shorter events, 87.9 us)
Async XLA Ops:
  4.7 24.5 %collective-permute-start = (bf16[2,256,896]{2,1,0:T(8,128)(2,1)}, bf16[2,256,896]{2,1,0:T(8,128)(2,1)S(1)}, u32[]{:S(2)}, u32[]{:S(2)}) collective-permute-start(bf16[2,256,896]{2,1,0:T(8,128)(2,1)} %get-tuple-element.81), channel_id=1, source_target_pairs={{0,1},{1,2},{2,3},{4,5},{5,6},{6,7},{8,9},{9,10},{10,11},{12,13},{... | collective-permute-start | bytes 2752520 | tf_op jit(solution)/shard_map/ppermute | solution.py:553
  8.2 52.8 %collective-permute-start.1 = (bf16[2,256,896]{2,1,0:T(8,128)(2,1)}, bf16[2,256,896]{2,1,0:T(8,128)(2,1)S(1)}, u32[]{:S(2)}, u32[]{:S(2)}) collective-permute-start(bf16[2,256,896]{2,1,0:T(8,128)(2,1)} %get-tuple-element.80), channel_id=1, source_target_pairs={{0,1},{1,2},{2,3},{4,5},{5,6},{6,7},{8,9},{9,10},{10,11},{12,13},{... | collective-permute-start | bytes 2752520 | tf_op jit(solution)/shard_map/ppermute | solution.py:553
  11.7 25.4 %collective-permute-start.2 = (bf16[2,256,896]{2,1,0:T(8,128)(2,1)}, bf16[2,256,896]{2,1,0:T(8,128)(2,1)S(1)}, u32[]{:S(2)}, u32[]{:S(2)}) collective-permute-start(bf16[2,256,896]{2,1,0:T(8,128)(2,1)} %get-tuple-element.79), channel_id=1, source_target_pairs={{1,0},{2,1},{3,2},{5,4},{6,5},{7,6},{9,8},{10,9},{11,10},{13,12},{... | collective-permute-start | bytes 2752520 | tf_op jit(solution)/shard_map/ppermute | solution.py:553
  13.0 49.3 %collective-permute-start.3 = (bf16[2,256,896]{2,1,0:T(8,128)(2,1)}, bf16[2,256,896]{2,1,0:T(8,128)(2,1)}, u32[]{:S(2)}, u32[]{:S(2)}) collective-permute-start(bf16[2,256,896]{2,1,0:T(8,128)(2,1)} %get-tuple-element.78), channel_id=1, source_target_pairs={{1,0},{2,1},{3,2},{5,4},{6,5},{7,6},{9,8},{10,9},{11,10},{13,12},{... | collective-permute-start | bytes 2752520 | tf_op jit(solution)/shard_map/ppermute | solution.py:553
  45.0 24.3 %all-to-all-start = ((bf16[8,2,256,128]{3,2,1,0:T(8,128)(2,1)}), bf16[8,2,256,128]{3,2,1,0:T(8,128)(2,1)S(1)}, u32[]{:S(2)}, u32[]{:S(2)}) async-start(bf16[8,2,256,128]{3,2,1,0:T(8,128)(2,1)} %shear_tile.4), calls=%async_computation | async-start | bytes 2097152 | tf_op jit(solution)/shard_map/all_to_all | solution.py:703
  50.2 26.4 %collective-permute-start.11 = (bf16[2,32,1024]{2,1,0:T(8,128)(2,1)S(1)}, bf16[2,32,1024]{2,1,0:T(8,128)(2,1)S(1)}, u32[]{:S(2)}, u32[]{:S(2)}) collective-permute-start(bf16[2,32,1024]{2,1,0:T(8,128)(2,1)S(1)} %get-tuple-element.69), channel_id=1, source_target_pairs={{0,4},{4,8},{8,12},{12,16},{16,20},{20,24},{24,28},{1,5},{5,9},{9,... | collective-permute-start | bytes 393224 | tf_op jit(solution)/shard_map/ppermute | solution.py:553
  52.3 24.4 %collective-permute-start.12 = (bf16[2,32,1024]{2,1,0:T(8,128)(2,1)S(1)}, bf16[2,32,1024]{2,1,0:T(8,128)(2,1)S(1)}, u32[]{:S(2)}, u32[]{:S(2)}) collective-permute-start(bf16[2,32,1024]{2,1,0:T(8,128)(2,1)S(1)} %get-tuple-element.68), channel_id=1, source_target_pairs={{4,0},{8,4},{12,8},{16,12},{20,16},{24,20},{28,24},{5,1},{9,5},{13... | collective-permute-start | bytes 393224 | tf_op jit(solution)/shard_map/ppermute | solution.py:553
  56.7 19.9 %collective-permute-start.13 = (bf16[2,32,512]{2,1,0:T(8,128)(2,1)S(1)}, bf16[2,32,512]{2,1,0:T(8,128)(2,1)S(1)}, u32[]{:S(2)}, u32[]{:S(2)}) collective-permute-start(bf16[2,32,512]{2,1,0:T(8,128)(2,1)S(1)} %get-tuple-element.67), channel_id=1, source_target_pairs={{0,1},{1,2},{2,3},{4,5},{5,6},{6,7},{8,9},{9,10},{10,11},{12,13},{... | collective-permute-start | bytes 196616 | tf_op jit(solution)/shard_map/ppermute | solution.py:553
  61.0 15.6 %collective-permute-start.14 = (bf16[2,32,512]{2,1,0:T(8,128)(2,1)S(1)}, bf16[2,32,512]{2,1,0:T(8,128)(2,1)S(1)}, u32[]{:S(2)}, u32[]{:S(2)}) collective-permute-start(bf16[2,32,512]{2,1,0:T(8,128)(2,1)S(1)} %get-tuple-element.66), channel_id=1, source_target_pairs={{1,0},{2,1},{3,2},{5,4},{6,5},{7,6},{9,8},{10,9},{11,10},{13,12},{... | collective-permute-start | bytes 196616 | tf_op jit(solution)/shard_map/ppermute | solution.py:553
  69.3 18.1 %all-to-all-start.1 = ((bf16[8,2,256,128]{3,2,1,0:T(8,128)(2,1)}), bf16[8,2,256,128]{3,2,1,0:T(8,128)(2,1)S(1)}, u32[]{:S(2)}, u32[]{:S(2)}) async-start(bf16[8,2,256,128]{3,2,1,0:T(8,128)(2,1)} %shear_tile.5), calls=%async_computation.1 | async-start | bytes 2097152 | tf_op jit(solution)/shard_map/all_to_all | solution.py:703
  101.0 177.4 %all-to-all-start.2 = ((bf16[32,2,128,128]{3,2,1,0:T(8,128)(2,1)}), bf16[32,2,128,128]{3,2,1,0:T(8,128)(2,1)S(1)}, u32[]{:S(2)}, u32[]{:S(2)}) async-start(bf16[32,2,128,128]{3,2,1,0:T(8,128)(2,1)} %shear_columns.2), calls=%async_computation.2 | async-start | bytes 4194304 | tf_op jit(solution)/shard_map/all_to_all | solution.py:709
  119.9 12.6 %collective-permute-start.5 = (bf16[1,2,512,128]{3,2,1,0:T(8,128)(2,1)S(1)}, bf16[1,2,512,128]{3,2,1,0:T(8,128)(2,1)S(1)}, u32[]{:S(2)}, u32[]{:S(2)}) collective-permute-start(bf16[1,2,512,128]{3,2,1,0:T(8,128)(2,1)S(1)} %get-tuple-element.75), channel_id=1, source_target_pairs={{0,8},{4,12},{8,0},{12,4},{16,24},{20,28},{24,16},{28,20},{1,9},{5... | collective-permute-start | bytes 786440 | tf_op jit(solution)/shard_map/ppermute | solution.py:594
  120.3 19.5 %collective-permute-start.6 = (bf16[1,2,512,128]{3,2,1,0:T(8,128)(2,1)S(1)}, bf16[1,2,512,128]{3,2,1,0:T(8,128)(2,1)S(1)}, u32[]{:S(2)}, u32[]{:S(2)}) collective-permute-start(bf16[1,2,512,128]{3,2,1,0:T(8,128)(2,1)S(1)} %get-tuple-element.74), channel_id=1, source_target_pairs={{0,12},{4,8},{8,4},{12,0},{16,28},{20,24},{24,20},{28,16},{1,13},{... | collective-permute-start | bytes 786440 | tf_op jit(solution)/shard_map/ppermute | solution.py:594
  121.6 18.1 %collective-permute-start.7 = (bf16[1,2,512,128]{3,2,1,0:T(8,128)(2,1)S(1)}, bf16[1,2,512,128]{3,2,1,0:T(8,128)(2,1)S(1)}, u32[]{:S(2)}, u32[]{:S(2)}) collective-permute-start(bf16[1,2,512,128]{3,2,1,0:T(8,128)(2,1)S(1)} %get-tuple-element.73), channel_id=1, source_target_pairs={{0,16},{4,20},{8,24},{12,28},{16,0},{20,4},{24,8},{28,12},{1,17},{... | collective-permute-start | bytes 786440 | tf_op jit(solution)/shard_map/ppermute | solution.py:594
  123.1 21.4 %collective-permute-start.8 = (bf16[1,2,512,128]{3,2,1,0:T(8,128)(2,1)S(1)}, bf16[1,2,512,128]{3,2,1,0:T(8,128)(2,1)S(1)}, u32[]{:S(2)}, u32[]{:S(2)}) collective-permute-start(bf16[1,2,512,128]{3,2,1,0:T(8,128)(2,1)S(1)} %get-tuple-element.72), channel_id=1, source_target_pairs={{0,20},{4,16},{8,28},{12,24},{16,4},{20,0},{24,12},{28,8},{1,21},{... | collective-permute-start | bytes 786440 | tf_op jit(solution)/shard_map/ppermute | solution.py:594
  123.4 26.9 %collective-permute-start.9 = (bf16[1,2,512,128]{3,2,1,0:T(8,128)(2,1)S(1)}, bf16[1,2,512,128]{3,2,1,0:T(8,128)(2,1)S(1)}, u32[]{:S(2)}, u32[]{:S(2)}) collective-permute-start(bf16[1,2,512,128]{3,2,1,0:T(8,128)(2,1)S(1)} %get-tuple-element.71), channel_id=1, source_target_pairs={{0,24},{4,28},{8,16},{12,20},{16,8},{20,12},{24,0},{28,4},{1,25},{... | collective-permute-start | bytes 786440 | tf_op jit(solution)/shard_map/ppermute | solution.py:594
  132.5 24.5 %collective-permute-start.10 = (bf16[1,2,512,128]{3,2,1,0:T(8,128)(2,1)S(1)}, bf16[1,2,512,128]{3,2,1,0:T(8,128)(2,1)S(1)}, u32[]{:S(2)}, u32[]{:S(2)}) collective-permute-start(bf16[1,2,512,128]{3,2,1,0:T(8,128)(2,1)S(1)} %get-tuple-element.70), channel_id=1, source_target_pairs={{0,28},{4,24},{8,20},{12,16},{16,12},{20,8},{24,4},{28,0},{1,29},{... | collective-permute-start | bytes 786440 | tf_op jit(solution)/shard_map/ppermute | solution.py:594
  173.0 9.1 %collective-permute-start.16 = (bf16[1,2,512,128]{3,2,1,0:T(8,128)(2,1)S(1)}, bf16[1,2,512,128]{3,2,1,0:T(8,128)(2,1)S(1)}, u32[]{:S(2)}, u32[]{:S(2)}) collective-permute-start(bf16[1,2,512,128]{3,2,1,0:T(8,128)(2,1)S(1)} %get-tuple-element.63), channel_id=1, source_target_pairs={{0,8},{4,12},{8,0},{12,4},{16,24},{20,28},{24,16},{28,20},{1,9},{5... | collective-permute-start | bytes 786440 | tf_op jit(solution)/shard_map/ppermute | solution.py:594
  173.6 13.2 %collective-permute-start.17 = (bf16[1,2,512,128]{3,2,1,0:T(8,128)(2,1)S(1)}, bf16[1,2,512,128]{3,2,1,0:T(8,128)(2,1)S(1)}, u32[]{:S(2)}, u32[]{:S(2)}) collective-permute-start(bf16[1,2,512,128]{3,2,1,0:T(8,128)(2,1)S(1)} %get-tuple-element.62), channel_id=1, source_target_pairs={{0,12},{4,8},{8,4},{12,0},{16,28},{20,24},{24,20},{28,16},{1,13},{... | collective-permute-start | bytes 786440 | tf_op jit(solution)/shard_map/ppermute | solution.py:594
  174.8 12.0 %collective-permute-start.18 = (bf16[1,2,512,128]{3,2,1,0:T(8,128)(2,1)S(1)}, bf16[1,2,512,128]{3,2,1,0:T(8,128)(2,1)S(1)}, u32[]{:S(2)}, u32[]{:S(2)}) collective-permute-start(bf16[1,2,512,128]{3,2,1,0:T(8,128)(2,1)S(1)} %get-tuple-element.61), channel_id=1, source_target_pairs={{0,16},{4,20},{8,24},{12,28},{16,0},{20,4},{24,8},{28,12},{1,17},{... | collective-permute-start | bytes 786440 | tf_op jit(solution)/shard_map/ppermute | solution.py:594
  175.1 24.5 %collective-permute-start.19 = (bf16[1,2,512,128]{3,2,1,0:T(8,128)(2,1)S(1)}, bf16[1,2,512,128]{3,2,1,0:T(8,128)(2,1)S(1)}, u32[]{:S(2)}, u32[]{:S(2)}) collective-permute-start(bf16[1,2,512,128]{3,2,1,0:T(8,128)(2,1)S(1)} %get-tuple-element.60), channel_id=1, source_target_pairs={{0,20},{4,16},{8,28},{12,24},{16,4},{20,0},{24,12},{28,8},{1,21},{... | collective-permute-start | bytes 786440 | tf_op jit(solution)/shard_map/ppermute | solution.py:594
  176.5 23.1 %collective-permute-start.20 = (bf16[1,2,512,128]{3,2,1,0:T(8,128)(2,1)S(1)}, bf16[1,2,512,128]{3,2,1,0:T(8,128)(2,1)S(1)}, u32[]{:S(2)}, u32[]{:S(2)}) collective-permute-start(bf16[1,2,512,128]{3,2,1,0:T(8,128)(2,1)S(1)} %get-tuple-element.59), channel_id=1, source_target_pairs={{0,24},{4,28},{8,16},{12,20},{16,8},{20,12},{24,0},{28,4},{1,25},{... | collective-permute-start | bytes 786440 | tf_op jit(solution)/shard_map/ppermute | solution.py:594
  182.1 17.5 %collective-permute-start.21 = (bf16[1,2,512,128]{3,2,1,0:T(8,128)(2,1)S(1)}, bf16[1,2,512,128]{3,2,1,0:T(8,128)(2,1)S(1)}, u32[]{:S(2)}, u32[]{:S(2)}) collective-permute-start(bf16[1,2,512,128]{3,2,1,0:T(8,128)(2,1)S(1)} %get-tuple-element.58), channel_id=1, source_target_pairs={{0,28},{4,24},{8,20},{12,16},{16,12},{20,8},{24,4},{28,0},{1,29},{... | collective-permute-start | bytes 786440 | tf_op jit(solution)/shard_map/ppermute | solution.py:594
  270.3 43.9 %collective-permute-start.22 = (bf16[7,2,512,128]{3,2,1,0:T(8,128)(2,1)}, bf16[7,2,512,128]{3,2,1,0:T(8,128)(2,1)}, u32[]{:S(2)}, u32[]{:S(2)}) collective-permute-start(bf16[7,2,512,128]{3,2,1,0:T(8,128)(2,1)} %get-tuple-element.57), channel_id=1, source_target_pairs={{0,1},{1,2},{2,3},{4,5},{5,6},{6,7},{8,9},{9,10},{10,11},{12,13},{... | collective-permute-start | bytes 5505032 | tf_op jit(solution)/shard_map/ppermute | solution.py:553
  275.2 44.3 %collective-permute-start.23 = (bf16[7,2,512,128]{3,2,1,0:T(8,128)(2,1)}, bf16[7,2,512,128]{3,2,1,0:T(8,128)(2,1)}, u32[]{:S(2)}, u32[]{:S(2)}) collective-permute-start(bf16[7,2,512,128]{3,2,1,0:T(8,128)(2,1)} %get-tuple-element.56), channel_id=1, source_target_pairs={{1,0},{2,1},{3,2},{5,4},{6,5},{7,6},{9,8},{10,9},{11,10},{13,12},{... | collective-permute-start | bytes 5505032 | tf_op jit(solution)/shard_map/ppermute | solution.py:553
  319.5 54.4 %all-to-all-start.3 = ((bf16[4,2,1088,128]{3,2,1,0:T(8,128)(2,1)}), bf16[4,2,1088,128]{3,2,1,0:T(8,128)(2,1)S(1)}, u32[]{:S(2)}, u32[]{:S(2)}) async-start(bf16[4,2,1088,128]{3,2,1,0:T(8,128)(2,1)} %shear_whole.1), calls=%async_computation.3 | async-start | bytes 4456448 | tf_op jit(solution)/shard_map/all_to_all | solution.py:744
  336.3 7.3 %collective-permute-start.24 = (bf16[8,2,32,128]{3,2,1,0:T(8,128)(2,1)}, bf16[8,2,32,128]{3,2,1,0:T(8,128)(2,1)S(1)}, u32[]{:S(2)}, u32[]{:S(2)}) collective-permute-start(bf16[8,2,32,128]{3,2,1,0:T(8,128)(2,1)} %get-tuple-element.55), channel_id=1, source_target_pairs={{0,4},{4,8},{8,12},{12,16},{16,20},{20,24},{24,28},{1,5},{5,9},{9,... | collective-permute-start | bytes 393224 | tf_op jit(solution)/shard_map/ppermute | solution.py:553
  338.2 6.5 %collective-permute-start.25 = (bf16[8,2,32,128]{3,2,1,0:T(8,128)(2,1)}, bf16[8,2,32,128]{3,2,1,0:T(8,128)(2,1)S(1)}, u32[]{:S(2)}, u32[]{:S(2)}) collective-permute-start(bf16[8,2,32,128]{3,2,1,0:T(8,128)(2,1)} %get-tuple-element.54), channel_id=1, source_target_pairs={{4,0},{8,4},{12,8},{16,12},{20,16},{24,20},{28,24},{5,1},{9,5},{13... | collective-permute-start | bytes 393224 | tf_op jit(solution)/shard_map/ppermute | solution.py:553
  384.7 22.9 %collective-permute-start.28 = (bf16[1,2,1024,128]{3,2,1,0:T(8,128)(2,1)S(1)}, bf16[1,2,1024,128]{3,2,1,0:T(8,128)(2,1)S(1)}, u32[]{:S(2)}, u32[]{:S(2)}) collective-permute-start(bf16[1,2,1024,128]{3,2,1,0:T(8,128)(2,1)S(1)} %get-tuple-element.51), channel_id=1, source_target_pairs={{0,4},{4,8},{8,12},{12,16},{16,20},{20,24},{24,28},{1,5},{5,9},{9,... | collective-permute-start | bytes 1572872 | tf_op jit(solution)/shard_map/ppermute | solution.py:553
  386.6 21.0 %collective-permute-start.29 = (bf16[1,2,1024,128]{3,2,1,0:T(8,128)(2,1)S(1)}, bf16[1,2,1024,128]{3,2,1,0:T(8,128)(2,1)S(1)}, u32[]{:S(2)}, u32[]{:S(2)}) collective-permute-start(bf16[1,2,1024,128]{3,2,1,0:T(8,128)(2,1)S(1)} %get-tuple-element.50), channel_id=1, source_target_pairs={{4,0},{8,4},{12,8},{16,12},{20,16},{24,20},{28,24},{5,1},{9,5},{13... | collective-permute-start | bytes 1572872 | tf_op jit(solution)/shard_map/ppermute | solution.py:553
  391.3 6.3 %collective-permute-start.26 = (bf16[1,2,512,128]{3,2,1,0:T(8,128)(2,1)S(1)}, bf16[1,2,512,128]{3,2,1,0:T(8,128)(2,1)S(1)}, u32[]{:S(2)}, u32[]{:S(2)}) collective-permute-start(bf16[1,2,512,128]{3,2,1,0:T(8,128)(2,1)S(1)} %get-tuple-element.53), channel_id=1, source_target_pairs={{0,1},{1,2},{2,3},{4,5},{5,6},{6,7},{8,9},{9,10},{10,11},{12,13},{... | collective-permute-start | bytes 786440 | tf_op jit(solution)/shard_map/ppermute | solution.py:553
  392.6 9.1 %collective-permute-start.27 = (bf16[1,2,512,128]{3,2,1,0:T(8,128)(2,1)S(1)}, bf16[1,2,512,128]{3,2,1,0:T(8,128)(2,1)S(1)}, u32[]{:S(2)}, u32[]{:S(2)}) collective-permute-start(bf16[1,2,512,128]{3,2,1,0:T(8,128)(2,1)S(1)} %get-tuple-element.52), channel_id=1, source_target_pairs={{1,0},{2,1},{3,2},{5,4},{6,5},{7,6},{9,8},{10,9},{11,10},{13,12},{... | collective-permute-start | bytes 786440 | tf_op jit(solution)/shard_map/ppermute | solution.py:553
  (40 other events, 601.4 us)

commit v5 on v4

--- a/solution.py
+++ b/solution.py
@@ -558,32 +558,29 @@
 
 
 def ordered_kernel(rank, *refs):
-    count = len(refs) - 2
-    out, arrived = refs[count], refs[count + 1]
-    copies = [
-        pltpu.make_async_copy(refs[s], out.at[pl.ds(s ^ rank[0], 1)], arrived.at[s])
-        for s in range(count)
-    ]
-    for copy in copies:
-        copy.start()
-    for copy in copies:
-        copy.wait()
+    pieces, out = refs[:-1], refs[-1]
+    for s, piece in enumerate(pieces):
+
+        @pl.when(pl.program_id(0) == s)
+        def _():
+            out[...] = piece[...]
 
 
 def ordered(pieces, rank):
     count = len(pieces)
-    shape = (count, *pieces[0].shape[1:])
-    anywhere = pl.BlockSpec(memory_space=pl.ANY)
+    block = pieces[0].shape
+    shape = (count, *block[1:])
+    rest = (0,) * (len(block) - 1)
     return pl.pallas_call(
         ordered_kernel,
         grid_spec=pltpu.PrefetchScalarGridSpec(
             num_scalar_prefetch=1,
-            grid=(1,),
-            in_specs=[anywhere] * count,
-            out_specs=anywhere,
-            scratch_shapes=[pltpu.SemaphoreType.DMA((count,))],
+            grid=(count,),
+            in_specs=[pl.BlockSpec(block, lambda i, rank: (0, *rest))] * count,
+            out_specs=pl.BlockSpec(block, lambda i, rank: (i ^ rank[0], *rest)),
         ),
         out_shape=jax.ShapeDtypeStruct(shape, pieces[0].dtype),
+        compiler_params=pltpu.CompilerParams(vmem_limit_bytes=VMEM_LIMIT),
         name="ordered",
     )(rank, *pieces)
 
@@ -701,9 +698,13 @@
         left, right = after((lefts[part], rights[part]), sheared)
         sheared = first(1, part * part_lines, [left], [right], in_order)
         spread.append(lax.all_to_all(sheared, "row", split_axis=0, concat_axis=0, tiled=True))
-    spread, wave_a_halos, wave_b_halos = lax.optimization_barrier(
-        (spread, wave_a_halos, wave_b_halos)
-    )
+    lefts, rights = after((lefts, rights), sheared)
+    slots = first(0, 0, lefts, rights, by_rank)
+    spread, wave_a_halos, wave_b_halos, slots = lax.optimization_barrier(
+        (spread, wave_a_halos, wave_b_halos, slots)
+    )
+    pieces = swapped_shares([slots[s : s + 1] for s in range(row_devices)])
+
     place = [[(b, part * part_lines) for b in range(row_devices)] for part in range(PARTS)]
     moved_b = second(1, spread, place, in_order, BLOCK)
     whole = lax.all_to_all(moved_b, ("row", "col"), split_axis=0, concat_axis=0, tiled=True)
@@ -719,9 +720,6 @@
         turned_tables,
     )
 
-    lefts, rights = after((lefts, rights), sheared)
-    slots = first(0, 0, lefts, rights, by_rank)
-    pieces = swapped_shares([slots[s : s + 1] for s in range(row_devices)])
     pieces = after(pieces, moved_b)
     moved_a = second(0, pieces, [[(s, 0)] for s in range(row_devices)], by_rank, line_count)
     pieces = swapped_shares([moved_a[s : s + 1] for s in range(row_devices)])

time: 418 us -> 353 us (0.84)
  Pallas kernels: 169 us -> 109 us
  waiting for transfers between devices: 138 us -> 130 us
    pallas_call x1, Pallas kernels: 64.7 us -> 4.54 us  [ordered(): pl.pallas_call(ordered_kernel, grid_spec=pltpu.PrefetchScalarGridSpec(num...]
    all_to_all x2, waiting for transfers between devices: 10.7 us -> 0.01 us  [on_device(): lax.all_to_all(sheared, 'row', split_axis=0, concat_axis=0, tiled=True)]
    ppermute x14, waiting for transfers between devices: 53 us -> 61.7 us  [swapped_shares(): lax.ppermute(slots[s], 'row', [(i, i ^ s) for i in range(devices)])]
    ppermute x16, waiting for transfers between devices: 55.3 us -> 50.5 us  [from_both_sides(): return (lax.ppermute(last, axis, up), lax.ppermute(first, axis, down))]
  transfers between devices with their start and end apart: 34 -> 34, of which waited for: 17 -> 15; matrix products, arithmetic and copies ran while one was open for 6% -> 7% of each run, Pallas kernels for 34% -> 23%
where the time goes in v5:
time: 353 us; the launch traced here: 352 us
  waiting for transfers between devices  130 us (37%)
  Pallas kernels  109 us (31%)
  starting transfers between devices  70.3 us (20%)
  local copies, waits for them, and re-layouts  35.2 us (10%)
    ppermute x14, waiting for transfers between devices, swapped_shares(): lax.ppermute(slots[s], 'row', [(i, i ^ s) for i in range(devices)])  61.7 us
    ppermute x16, waiting for transfers between devices, from_both_sides(): return (lax.ppermute(last, axis, up), lax.ppermute(first, axis, down))  50.5 us
    ppermute x16, starting transfers between devices, from_both_sides(): return (lax.ppermute(last, axis, up), lax.ppermute(first, axis, down))  40.6 us
    pallas_call x4, Pallas kernels, shear_tile(): pl.pallas_call(kernel, grid_spec=pltpu.PrefetchScalarGridSpec(num_scalar_...  36 us
    pallas_call x2, Pallas kernels, shear_columns(): pl.pallas_call(functools.partial(shear_columns_kernel, front, blocks, len...  25.4 us
    all_to_all x1, waiting for transfers between devices, on_device(): lax.all_to_all(turned, 'col', split_axis=0, concat_axis=0, tiled=True)  18.2 us
    pallas_call x2, Pallas kernels, travel_first(): pl.pallas_call(functools.partial(travel_first_kernel, length, len(halos)...  18.2 us
    pallas_call x1, Pallas kernels, shear_whole(): pl.pallas_call(functools.partial(shear_whole_kernel, halo, devices, tiles...  12.8 us
  transfers between devices with their start and end apart: 34, of which 15 were waited for; matrix products, arithmetic and copies ran while one was open for 7% of the time, Pallas kernels for 23%

profile of v5, /device:TPU:2, one launch (start us, length us, event | category | flops | bytes accessed | tf_op | source)
XLA Modules:
  0.0 351.6 jit_solution(5954229854883634227)
XLA Ops:
  0.7 4.0 %fusion.30 = (bf16[2,256,896]{2,1,0:T(8,128)(2,1)}, bf16[2,256,896]{2,1,0:T(8,128)(2,1)}, bf16[2,256,896]{2,1,0:T(8,128)(2,1)}, bf16[2,256,896]{2,1,0:T(8,128)(2,1)}) fusion(bf16[2,512,1024]{2,1,0:T(8,128)(2,1)} %refs_4_.2), kind=kLoop, calls=%fused_computation.78 | loop fusion | bytes 7340032 | tf_op jit(solution)/shard_map/slice | solution.py:633
  9.5 4.6 %collective-permute-start.2 = (bf16[2,256,896]{2,1,0:T(8,128)(2,1)}, bf16[2,256,896]{2,1,0:T(8,128)(2,1)S(1)}, u32[]{:S(2)}, u32[]{:S(2)}) collective-permute-start(bf16[2,256,896]{2,1,0:T(8,128)(2,1)} %get-tuple-element.81), channel_id=1, source_target_pairs={{0,1},{1,2},{2,3},{4,5},{5,6},{6,7},{8,9},{9,10},{10,11},{12,13},{... | collective-permute-start | bytes 2752520 | tf_op jit(solution)/shard_map/ppermute | solution.py:553
  17.7 11.5 %collective-permute-done.refs_0_ = bf16[2,256,896]{2,1,0:T(8,128)(2,1)S(1)} collective-permute-done((bf16[2,256,896]{2,1,0:T(8,128)(2,1)}, bf16[2,256,896]{2,1,0:T(8,128)(2,1)S(1)}, u32[]{:S(2)}, u32[]{:S(2)}) %collective-permute-start) | collective-permute-done | bytes 917536 | tf_op jit(solution)/shard_map/ppermute | solution.py:553
  29.2 4.4 %collective-permute-done.1.refs_1_.refs_2_ = bf16[2,256,896]{2,1,0:T(8,128)(2,1)S(1)} collective-permute-done((bf16[2,256,896]{2,1,0:T(8,128)(2,1)}, bf16[2,256,896]{2,1,0:T(8,128)(2,1)S(1)}, u32[]{:S(2)}, u32[]{:S(2)}) %collective-permute-start.1) | collective-permute-done | bytes 917536 | tf_op jit(solution)/shard_map/ppermute | solution.py:553
  34.5 7.0 %shear_tile.4 = bf16[8,2,256,128]{3,2,1,0:T(8,128)(2,1)} custom-call(s32[16]{0:T(128)} %get-tuple-element.104.base, s32[1]{0:T(128)} %constant.68.clone.1.rank, bf16[2,256,896]{2,1,0:T(8,128)(2,1)} %copy-done.6, bf16[2,256,896]{2,1,0:T(8,128)(2,1)} %copy-done.7, bf16[2,512,1024]{2,1,0:T(8,128)(2,1)} %refs_4_.2, f32[4,1,128]{2,1,0:T(1,128)} %get-tuple-element.99.refs_3_, ...), custom_call_target="tpu_custom_call" | custom-call | tf_op jit(solution)/shard_map/shear_tile/pallas_call | solution.py:189
  41.5 4.3 %all-to-all-start = ((bf16[8,2,256,128]{3,2,1,0:T(8,128)(2,1)}), bf16[8,2,256,128]{3,2,1,0:T(8,128)(2,1)S(1)}, u32[]{:S(2)}, u32[]{:S(2)}) async-start(bf16[8,2,256,128]{3,2,1,0:T(8,128)(2,1)} %shear_tile.4), calls=%async_computation | async-start | bytes 2097152 | tf_op jit(solution)/shard_map/all_to_all | solution.py:700
  59.3 7.0 %shear_tile.5 = bf16[8,2,256,128]{3,2,1,0:T(8,128)(2,1)} custom-call(s32[16]{0:T(128)} %get-tuple-element.103.base, s32[1]{0:T(128)} %constant.68.clone.1.rank, bf16[2,256,896]{2,1,0:T(8,128)(2,1)} %copy-done.8, bf16[2,256,896]{2,1,0:T(8,128)(2,1)} %collective-permute-done.3.refs_1_.refs_3_, bf16[2,512,1024]{2,1,0:T(8,128)(2,1)} %refs_4_.2, ...), custom_call_target="tpu_custom_call" | custom-call | tf_op jit(solution)/shard_map/shear_tile/pallas_call | solution.py:189
  66.3 4.2 %all-to-all-start.1 = ((bf16[8,2,256,128]{3,2,1,0:T(8,128)(2,1)}), bf16[8,2,256,128]{3,2,1,0:T(8,128)(2,1)S(1)}, u32[]{:S(2)}, u32[]{:S(2)}) async-start(bf16[8,2,256,128]{3,2,1,0:T(8,128)(2,1)} %shear_tile.5), calls=%async_computation.1 | async-start | bytes 2097152 | tf_op jit(solution)/shard_map/all_to_all | solution.py:700
  73.6 11.5 %shear_tile.6 = bf16[8,2,512,128]{3,2,1,0:T(8,128)(2,1)} custom-call(s32[32]{0:T(128)} %get-tuple-element.101.base, s32[1]{0:T(128)} %bitcast.1.rank, bf16[2,256,896]{2,1,0:T(8,128)(2,1)} %copy-done.6, bf16[2,256,896]{2,1,0:T(8,128)(2,1)} %copy-done.8, bf16[2,256,896]{2,1,0:T(8,128)(2,1)} %copy-done.7, ...), custom_call_target="tpu_custom_call" | custom-call | tf_op jit(solution)/shard_map/shear_tile/pallas_call | solution.py:189
  86.2 12.6 %shear_columns.2 = bf16[32,2,128,128]{3,2,1,0:T(8,128)(2,1)} custom-call(s32[1]{0:T(128)} %bitcast.11.base, s32[1]{0:T(128)} %constant.68.clone.1.rank, bf16[8,2,256,128]{3,2,1,0:T(8,128)(2,1)} %copy-done.4, bf16[8,2,256,128]{3,2,1,0:T(8,128)(2,1)} %copy-done.5, s32[1,128]{1,0:T(1,128)} %get-tuple-element.108.refs_2_, f32[1,128]{1,0:T(1,128)} %get-tuple-element.106.refs_3_, ...), custom_call_target="tpu_custom_call" | custom-call | tf_op jit(solution)/shard_map/shear_columns/pallas_call | solution.py:403
  98.9 6.1 %all-to-all-start.2 = ((bf16[32,2,128,128]{3,2,1,0:T(8,128)(2,1)}), bf16[32,2,128,128]{3,2,1,0:T(8,128)(2,1)S(1)}, u32[]{:S(2)}, u32[]{:S(2)}) async-start(bf16[32,2,128,128]{3,2,1,0:T(8,128)(2,1)} %shear_columns.2), calls=%async_computation.2 | async-start | bytes 4194304 | tf_op jit(solution)/shard_map/all_to_all | solution.py:710
  112.5 14.3 %collective-permute-done.9.refs_2_ = bf16[1,2,512,128]{3,2,1,0:T(8,128)(2,1)S(1)} collective-permute-done((bf16[1,2,512,128]{3,2,1,0:T(8,128)(2,1)S(1)}, bf16[1,2,512,128]{3,2,1,0:T(8,128)(2,1)S(1)}, u32[]{:S(2)}, u32[]{:S(2)}) %collective-permute-start.9) | collective-permute-done | bytes 262176 | tf_op jit(solution)/shard_map/ppermute | solution.py:591
  128.8 6.7 %collective-permute-done.10.refs_3_ = bf16[1,2,512,128]{3,2,1,0:T(8,128)(2,1)S(1)} collective-permute-done((bf16[1,2,512,128]{3,2,1,0:T(8,128)(2,1)S(1)}, bf16[1,2,512,128]{3,2,1,0:T(8,128)(2,1)S(1)}, u32[]{:S(2)}, u32[]{:S(2)}) %collective-permute-start.10) | collective-permute-done | bytes 262176 | tf_op jit(solution)/shard_map/ppermute | solution.py:591
  135.6 11.4 %collective-permute-done.13.refs_6_ = bf16[1,2,512,128]{3,2,1,0:T(8,128)(2,1)S(1)} collective-permute-done((bf16[1,2,512,128]{3,2,1,0:T(8,128)(2,1)S(1)}, bf16[1,2,512,128]{3,2,1,0:T(8,128)(2,1)S(1)}, u32[]{:S(2)}, u32[]{:S(2)}) %collective-permute-start.13) | collective-permute-done | bytes 262176 | tf_op jit(solution)/shard_map/ppermute | solution.py:591
  147.0 7.1 %collective-permute-done.14.refs_7_ = bf16[1,2,512,128]{3,2,1,0:T(8,128)(2,1)S(1)} collective-permute-done((bf16[1,2,512,128]{3,2,1,0:T(8,128)(2,1)S(1)}, bf16[1,2,512,128]{3,2,1,0:T(8,128)(2,1)S(1)}, u32[]{:S(2)}, u32[]{:S(2)}) %collective-permute-start.14) | collective-permute-done | bytes 262176 | tf_op jit(solution)/shard_map/ppermute | solution.py:591
  154.8 12.8 %shear_columns.3 = bf16[8,2,512,128]{3,2,1,0:T(8,128)(2,1)} custom-call(s32[1]{0:T(128)} %bitcast.3.base, s32[1]{0:T(128)} %bitcast.1.rank, bf16[1,2,512,128]{3,2,1,0:T(8,128)(2,1)} %get-tuple-element.37.refs_0_, bf16[1,2,512,128]{3,2,1,0:T(8,128)(2,1)} %copy-done.20, bf16[1,2,512,128]{3,2,1,0:T(8,128)(2,1)} %copy-done.21, ...), custom_call_target="tpu_custom_call" | custom-call | tf_op jit(solution)/shard_map/shear_columns/pallas_call | solution.py:403
  175.0 4.4 %collective-permute-done.16.refs_2_ = bf16[1,2,512,128]{3,2,1,0:T(8,128)(2,1)S(1)} collective-permute-done((bf16[1,2,512,128]{3,2,1,0:T(8,128)(2,1)S(1)}, bf16[1,2,512,128]{3,2,1,0:T(8,128)(2,1)S(1)}, u32[]{:S(2)}, u32[]{:S(2)}) %collective-permute-start.16) | collective-permute-done | bytes 262176 | tf_op jit(solution)/shard_map/ppermute | solution.py:591
  179.4 4.3 %collective-permute-done.17.refs_3_ = bf16[1,2,512,128]{3,2,1,0:T(8,128)(2,1)S(1)} collective-permute-done((bf16[1,2,512,128]{3,2,1,0:T(8,128)(2,1)S(1)}, bf16[1,2,512,128]{3,2,1,0:T(8,128)(2,1)S(1)}, u32[]{:S(2)}, u32[]{:S(2)}) %collective-permute-start.17) | collective-permute-done | bytes 262176 | tf_op jit(solution)/shard_map/ppermute | solution.py:591
  183.7 13.4 %collective-permute-done.19.refs_5_ = bf16[1,2,512,128]{3,2,1,0:T(8,128)(2,1)S(1)} collective-permute-done((bf16[1,2,512,128]{3,2,1,0:T(8,128)(2,1)S(1)}, bf16[1,2,512,128]{3,2,1,0:T(8,128)(2,1)S(1)}, u32[]{:S(2)}, u32[]{:S(2)}) %collective-permute-start.19) | collective-permute-done | bytes 262176 | tf_op jit(solution)/shard_map/ppermute | solution.py:591
  198.0 4.5 %ordered.1.refs_2_ = bf16[8,2,512,128]{3,2,1,0:T(8,128)(2,1)} custom-call(s32[1]{0:T(128)} %bitcast.1.rank, bf16[1,2,512,128]{3,2,1,0:T(8,128)(2,1)} %get-tuple-element.67.refs_0_, bf16[1,2,512,128]{3,2,1,0:T(8,128)(2,1)} %copy-done.11, bf16[1,2,512,128]{3,2,1,0:T(8,128)(2,1)} %copy-done.12, bf16[1,2,512,128]{3,2,1,0:T(8,128)(2,1)} %copy-done.13, ...), custom_call_target="tpu_custom_call" | custom-call | tf_op jit(solution)/shard_map/ordered/pallas_call | solution.py:574
  202.6 4.5 %fusion.25 = (bf16[7,2,512,128]{3,2,1,0:T(8,128)(2,1)}, bf16[7,2,512,128]{3,2,1,0:T(8,128)(2,1)}) fusion(bf16[8,2,512,128]{3,2,1,0:T(8,128)(2,1)} %ordered.1.refs_2_), kind=kLoop, calls=%fused_computation.73 | loop fusion | bytes 7340032 | tf_op jit(solution)/shard_map/slice | solution.py:727
  207.0 4.4 %collective-permute-start.22 = (bf16[7,2,512,128]{3,2,1,0:T(8,128)(2,1)}, bf16[7,2,512,128]{3,2,1,0:T(8,128)(2,1)}, u32[]{:S(2)}, u32[]{:S(2)}) collective-permute-start(bf16[7,2,512,128]{3,2,1,0:T(8,128)(2,1)} %get-tuple-element.59), channel_id=1, source_target_pairs={{0,1},{1,2},{2,3},{4,5},{5,6},{6,7},{8,9},{9,10},{10,11},{12,13},{... | collective-permute-start | bytes 5505032 | tf_op jit(solution)/shard_map/ppermute | solution.py:553
  216.0 12.8 %shear_whole.1 = bf16[4,2,1088,128]{3,2,1,0:T(8,128)(2,1)} custom-call(s32[8]{0:T(128)} %fusion.15.base, bf16[8,4,2,128,128]{4,3,2,1,0:T(8,128)(2,1)} %bitcast.66, f32[1,128]{1,0:T(1,128)} %fusion.17.offsets, f32[1,128]{1,0:T(1,128)} %fusion.18.fractions, bf16[256,256]{1,0:T(8,128)(2,1)} %constant.84.clone.refs_5_.refs_7_.forward, ...), custom_call_target="tpu_custom_call" | custom-call | tf_op jit(solution)/shard_map/shear_whole/pallas_call | solution.py:297
  228.8 21.3 %collective-permute-done.22.refs_0_ = bf16[7,2,512,128]{3,2,1,0:T(8,128)(2,1)} collective-permute-done((bf16[7,2,512,128]{3,2,1,0:T(8,128)(2,1)}, bf16[7,2,512,128]{3,2,1,0:T(8,128)(2,1)}, u32[]{:S(2)}, u32[]{:S(2)}) %collective-permute-start.22) | collective-permute-done | bytes 1835040 | tf_op jit(solution)/shard_map/ppermute | solution.py:553
  250.1 5.3 %collective-permute-done.23.refs_1_ = bf16[7,2,512,128]{3,2,1,0:T(8,128)(2,1)} collective-permute-done((bf16[7,2,512,128]{3,2,1,0:T(8,128)(2,1)}, bf16[7,2,512,128]{3,2,1,0:T(8,128)(2,1)}, u32[]{:S(2)}, u32[]{:S(2)}) %collective-permute-start.23) | collective-permute-done | bytes 1835040 | tf_op jit(solution)/shard_map/ppermute | solution.py:553
  260.1 10.5 %shear_tile.7.refs_0_ = bf16[8,2,512,128]{3,2,1,0:T(8,128)(2,1)} custom-call(s32[32]{0:T(128)} %get-tuple-element.102.base, s32[1]{0:T(128)} %constant.68.clone.1.rank, bf16[7,2,512,128]{3,2,1,0:T(8,128)(2,1)} %collective-permute-done.22.refs_0_, bf16[7,2,512,128]{3,2,1,0:T(8,128)(2,1)} %collective-permute-done.23.refs_1_, ...), custom_call_target="tpu_custom_call" | custom-call | tf_op jit(solution)/shard_map/shear_tile/pallas_call | solution.py:189
  281.3 10.0 %travel_first.2.body = bf16[8,2,512,128]{3,2,1,0:T(8,128)(2,1)} custom-call(bf16[8,2,512,128]{3,2,1,0:T(8,128)(2,1)} %shear_tile.7.refs_0_, bf16[8,2,32,128]{3,2,1,0:T(8,128)(2,1)} %copy-done.30, bf16[8,2,32,128]{3,2,1,0:T(8,128)(2,1)} %copy-done.31, bf16[2,512,1024]{2,1,0:T(8,128)(2,1)} %refs_3_.1, bf16[2,32,1024]{2,1,0:T(8,128)(2,1)} %copy-done.28, ...), custom_call_target="tpu_custom_call" | custom-call | tf_op jit(solution)/shard_map/travel_first/pallas_call | solution.py:499
  291.3 18.2 %all-to-all-done.3.refs_0_ = bf16[4,2,1088,128]{3,2,1,0:T(8,128)(2,1)S(1)} async-done(((bf16[4,2,1088,128]{3,2,1,0:T(8,128)(2,1)}), bf16[4,2,1088,128]{3,2,1,0:T(8,128)(2,1)S(1)}, u32[]{:S(2)}, u32[]{:S(2)}) %all-to-all-start.3) | async-done | bytes 2228256 | tf_op jit(solution)/shard_map/all_to_all | solution.py:742
  310.8 8.2 %travel_first.3.body = bf16[4,2,1024,128]{3,2,1,0:T(8,128)(2,1)} custom-call(bf16[4,2,1088,128]{3,2,1,0:T(8,128)(2,1)} %copy-done.2, bf16[2,1024,512]{2,1,0:T(8,128)(2,1)} %refs_1_.1, bf16[2,32,512]{2,1,0:T(8,128)(2,1)} %copy-done.33, bf16[2,32,512]{2,1,0:T(8,128)(2,1)} %copy-done.34, bf16[256,384]{1,0:T(8,128)(2,1)} %copy.23.refs_4_), custom_call_target="tpu_custom_call" | custom-call | tf_op jit(solution)/shard_map/travel_first/pallas_call | solution.py:499
  333.4 4.1 %collective-permute-done.27.right = bf16[1,2,512,128]{3,2,1,0:T(8,128)(2,1)S(1)} collective-permute-done((bf16[1,2,512,128]{3,2,1,0:T(8,128)(2,1)S(1)}, bf16[1,2,512,128]{3,2,1,0:T(8,128)(2,1)S(1)}, u32[]{:S(2)}, u32[]{:S(2)}) %collective-permute-start.27) | collective-permute-done | bytes 262176 | tf_op jit(solution)/shard_map/ppermute | solution.py:553
  338.2 5.1 %travel_second.2 = bf16[2,512,1024]{2,1,0:T(8,128)(2,1)} custom-call(bf16[1,2,512,128]{3,2,1,0:T(8,128)(2,1)} %copy-done.18, bf16[8,2,512,128]{3,2,1,0:T(8,128)(2,1)} %travel_first.2.body, bf16[1,2,512,128]{3,2,1,0:T(8,128)(2,1)} %copy-done.19, bf16[768,256]{1,0:T(8,128)(2,1)} %get-tuple-element.85.matrix), custom_call_target="tpu_custom_call" | custom-call | tf_op jit(solution)/shard_map/travel_second/pallas_call | solution.py:533
  344.2 7.3 %travel_second.3 = bf16[2,1024,512]{2,1,0:T(8,128)(2,1)} custom-call(bf16[1,2,1024,128]{3,2,1,0:T(8,128)(2,1)} %copy-done.9, bf16[4,2,1024,128]{3,2,1,0:T(8,128)(2,1)} %travel_first.3.body, bf16[1,2,1024,128]{3,2,1,0:T(8,128)(2,1)} %copy-done.10, bf16[768,256]{1,0:T(8,128)(2,1)} %get-tuple-element.84.matrix), custom_call_target="tpu_custom_call" | custom-call | tf_op jit(solution)/shard_map/travel_second/pallas_call | solution.py:533
  (169 shorter events, 81.3 us)
Async XLA Ops:
  4.6 24.5 %collective-permute-start = (bf16[2,256,896]{2,1,0:T(8,128)(2,1)}, bf16[2,256,896]{2,1,0:T(8,128)(2,1)S(1)}, u32[]{:S(2)}, u32[]{:S(2)}) collective-permute-start(bf16[2,256,896]{2,1,0:T(8,128)(2,1)} %get-tuple-element.83), channel_id=1, source_target_pairs={{0,1},{1,2},{2,3},{4,5},{5,6},{6,7},{8,9},{9,10},{10,11},{12,13},{... | collective-permute-start | bytes 2752520 | tf_op jit(solution)/shard_map/ppermute | solution.py:553
  8.2 25.4 %collective-permute-start.1 = (bf16[2,256,896]{2,1,0:T(8,128)(2,1)}, bf16[2,256,896]{2,1,0:T(8,128)(2,1)S(1)}, u32[]{:S(2)}, u32[]{:S(2)}) collective-permute-start(bf16[2,256,896]{2,1,0:T(8,128)(2,1)} %get-tuple-element.82), channel_id=1, source_target_pairs={{1,0},{2,1},{3,2},{5,4},{6,5},{7,6},{9,8},{10,9},{11,10},{13,12},{... | collective-permute-start | bytes 2752520 | tf_op jit(solution)/shard_map/ppermute | solution.py:553
  9.5 48.5 %collective-permute-start.2 = (bf16[2,256,896]{2,1,0:T(8,128)(2,1)}, bf16[2,256,896]{2,1,0:T(8,128)(2,1)S(1)}, u32[]{:S(2)}, u32[]{:S(2)}) collective-permute-start(bf16[2,256,896]{2,1,0:T(8,128)(2,1)} %get-tuple-element.81), channel_id=1, source_target_pairs={{0,1},{1,2},{2,3},{4,5},{5,6},{6,7},{8,9},{9,10},{10,11},{12,13},{... | collective-permute-start | bytes 2752520 | tf_op jit(solution)/shard_map/ppermute | solution.py:553
  14.1 45.2 %collective-permute-start.3 = (bf16[2,256,896]{2,1,0:T(8,128)(2,1)}, bf16[2,256,896]{2,1,0:T(8,128)(2,1)}, u32[]{:S(2)}, u32[]{:S(2)}) collective-permute-start(bf16[2,256,896]{2,1,0:T(8,128)(2,1)} %get-tuple-element.80), channel_id=1, source_target_pairs={{1,0},{2,1},{3,2},{5,4},{6,5},{7,6},{9,8},{10,9},{11,10},{13,12},{... | collective-permute-start | bytes 2752520 | tf_op jit(solution)/shard_map/ppermute | solution.py:553
  41.5 24.8 %all-to-all-start = ((bf16[8,2,256,128]{3,2,1,0:T(8,128)(2,1)}), bf16[8,2,256,128]{3,2,1,0:T(8,128)(2,1)S(1)}, u32[]{:S(2)}, u32[]{:S(2)}) async-start(bf16[8,2,256,128]{3,2,1,0:T(8,128)(2,1)} %shear_tile.4), calls=%async_computation | async-start | bytes 2097152 | tf_op jit(solution)/shard_map/all_to_all | solution.py:700
  46.7 38.5 %collective-permute-start.4 = (bf16[2,32,1024]{2,1,0:T(8,128)(2,1)S(1)}, bf16[2,32,1024]{2,1,0:T(8,128)(2,1)S(1)}, u32[]{:S(2)}, u32[]{:S(2)}) collective-permute-start(bf16[2,32,1024]{2,1,0:T(8,128)(2,1)S(1)} %get-tuple-element.79), channel_id=1, source_target_pairs={{0,4},{4,8},{8,12},{12,16},{16,20},{20,24},{24,28},{1,5},{5,9},{9,... | collective-permute-start | bytes 393224 | tf_op jit(solution)/shard_map/ppermute | solution.py:553
  48.8 36.4 %collective-permute-start.5 = (bf16[2,32,1024]{2,1,0:T(8,128)(2,1)S(1)}, bf16[2,32,1024]{2,1,0:T(8,128)(2,1)S(1)}, u32[]{:S(2)}, u32[]{:S(2)}) collective-permute-start(bf16[2,32,1024]{2,1,0:T(8,128)(2,1)S(1)} %get-tuple-element.78), channel_id=1, source_target_pairs={{4,0},{8,4},{12,8},{16,12},{20,16},{24,20},{28,24},{5,1},{9,5},{13... | collective-permute-start | bytes 393224 | tf_op jit(solution)/shard_map/ppermute | solution.py:553
  53.2 31.9 %collective-permute-start.6 = (bf16[2,32,512]{2,1,0:T(8,128)(2,1)S(1)}, bf16[2,32,512]{2,1,0:T(8,128)(2,1)S(1)}, u32[]{:S(2)}, u32[]{:S(2)}) collective-permute-start(bf16[2,32,512]{2,1,0:T(8,128)(2,1)S(1)} %get-tuple-element.77), channel_id=1, source_target_pairs={{0,1},{1,2},{2,3},{4,5},{5,6},{6,7},{8,9},{9,10},{10,11},{12,13},{... | collective-permute-start | bytes 196616 | tf_op jit(solution)/shard_map/ppermute | solution.py:553
  58.0 27.2 %collective-permute-start.7 = (bf16[2,32,512]{2,1,0:T(8,128)(2,1)S(1)}, bf16[2,32,512]{2,1,0:T(8,128)(2,1)S(1)}, u32[]{:S(2)}, u32[]{:S(2)}) collective-permute-start(bf16[2,32,512]{2,1,0:T(8,128)(2,1)S(1)} %get-tuple-element.76), channel_id=1, source_target_pairs={{1,0},{2,1},{3,2},{5,4},{6,5},{7,6},{9,8},{10,9},{11,10},{13,12},{... | collective-permute-start | bytes 196616 | tf_op jit(solution)/shard_map/ppermute | solution.py:553
  66.3 18.9 %all-to-all-start.1 = ((bf16[8,2,256,128]{3,2,1,0:T(8,128)(2,1)}), bf16[8,2,256,128]{3,2,1,0:T(8,128)(2,1)S(1)}, u32[]{:S(2)}, u32[]{:S(2)}) async-start(bf16[8,2,256,128]{3,2,1,0:T(8,128)(2,1)} %shear_tile.5), calls=%async_computation.1 | async-start | bytes 2097152 | tf_op jit(solution)/shard_map/all_to_all | solution.py:700
  98.9 115.8 %all-to-all-start.2 = ((bf16[32,2,128,128]{3,2,1,0:T(8,128)(2,1)}), bf16[32,2,128,128]{3,2,1,0:T(8,128)(2,1)S(1)}, u32[]{:S(2)}, u32[]{:S(2)}) async-start(bf16[32,2,128,128]{3,2,1,0:T(8,128)(2,1)} %shear_columns.2), calls=%async_computation.2 | async-start | bytes 4194304 | tf_op jit(solution)/shard_map/all_to_all | solution.py:710
  107.5 19.2 %collective-permute-start.9 = (bf16[1,2,512,128]{3,2,1,0:T(8,128)(2,1)S(1)}, bf16[1,2,512,128]{3,2,1,0:T(8,128)(2,1)S(1)}, u32[]{:S(2)}, u32[]{:S(2)}) collective-permute-start(bf16[1,2,512,128]{3,2,1,0:T(8,128)(2,1)S(1)} %get-tuple-element.73), channel_id=1, source_target_pairs={{0,8},{4,12},{8,0},{12,4},{16,24},{20,28},{24,16},{28,20},{1,9},{5... | collective-permute-start | bytes 786440 | tf_op jit(solution)/shard_map/ppermute | solution.py:591
  107.9 27.6 %collective-permute-start.10 = (bf16[1,2,512,128]{3,2,1,0:T(8,128)(2,1)S(1)}, bf16[1,2,512,128]{3,2,1,0:T(8,128)(2,1)S(1)}, u32[]{:S(2)}, u32[]{:S(2)}) collective-permute-start(bf16[1,2,512,128]{3,2,1,0:T(8,128)(2,1)S(1)} %get-tuple-element.72), channel_id=1, source_target_pairs={{0,12},{4,8},{8,4},{12,0},{16,28},{20,24},{24,20},{28,16},{1,13},{... | collective-permute-start | bytes 786440 | tf_op jit(solution)/shard_map/ppermute | solution.py:591
  109.3 26.3 %collective-permute-start.11 = (bf16[1,2,512,128]{3,2,1,0:T(8,128)(2,1)S(1)}, bf16[1,2,512,128]{3,2,1,0:T(8,128)(2,1)S(1)}, u32[]{:S(2)}, u32[]{:S(2)}) collective-permute-start(bf16[1,2,512,128]{3,2,1,0:T(8,128)(2,1)S(1)} %get-tuple-element.71), channel_id=1, source_target_pairs={{0,16},{4,20},{8,24},{12,28},{16,0},{20,4},{24,8},{28,12},{1,17},{... | collective-permute-start | bytes 786440 | tf_op jit(solution)/shard_map/ppermute | solution.py:591
  110.7 24.8 %collective-permute-start.12 = (bf16[1,2,512,128]{3,2,1,0:T(8,128)(2,1)S(1)}, bf16[1,2,512,128]{3,2,1,0:T(8,128)(2,1)S(1)}, u32[]{:S(2)}, u32[]{:S(2)}) collective-permute-start(bf16[1,2,512,128]{3,2,1,0:T(8,128)(2,1)S(1)} %get-tuple-element.70), channel_id=1, source_target_pairs={{0,20},{4,16},{8,28},{12,24},{16,4},{20,0},{24,12},{28,8},{1,21},{... | collective-permute-start | bytes 786440 | tf_op jit(solution)/shard_map/ppermute | solution.py:591
  111.1 36.0 %collective-permute-start.13 = (bf16[1,2,512,128]{3,2,1,0:T(8,128)(2,1)S(1)}, bf16[1,2,512,128]{3,2,1,0:T(8,128)(2,1)S(1)}, u32[]{:S(2)}, u32[]{:S(2)}) collective-permute-start(bf16[1,2,512,128]{3,2,1,0:T(8,128)(2,1)S(1)} %get-tuple-element.69), channel_id=1, source_target_pairs={{0,24},{4,28},{8,16},{12,20},{16,8},{20,12},{24,0},{28,4},{1,25},{... | collective-permute-start | bytes 786440 | tf_op jit(solution)/shard_map/ppermute | solution.py:591
  126.8 27.3 %collective-permute-start.14 = (bf16[1,2,512,128]{3,2,1,0:T(8,128)(2,1)S(1)}, bf16[1,2,512,128]{3,2,1,0:T(8,128)(2,1)S(1)}, u32[]{:S(2)}, u32[]{:S(2)}) collective-permute-start(bf16[1,2,512,128]{3,2,1,0:T(8,128)(2,1)S(1)} %get-tuple-element.68), channel_id=1, source_target_pairs={{0,28},{4,24},{8,20},{12,16},{16,12},{20,8},{24,4},{28,0},{1,29},{... | collective-permute-start | bytes 786440 | tf_op jit(solution)/shard_map/ppermute | solution.py:591
  170.3 9.1 %collective-permute-start.16 = (bf16[1,2,512,128]{3,2,1,0:T(8,128)(2,1)S(1)}, bf16[1,2,512,128]{3,2,1,0:T(8,128)(2,1)S(1)}, u32[]{:S(2)}, u32[]{:S(2)}) collective-permute-start(bf16[1,2,512,128]{3,2,1,0:T(8,128)(2,1)S(1)} %get-tuple-element.65), channel_id=1, source_target_pairs={{0,8},{4,12},{8,0},{12,4},{16,24},{20,28},{24,16},{28,20},{1,9},{5... | collective-permute-start | bytes 786440 | tf_op jit(solution)/shard_map/ppermute | solution.py:591
  171.4 12.3 %collective-permute-start.17 = (bf16[1,2,512,128]{3,2,1,0:T(8,128)(2,1)S(1)}, bf16[1,2,512,128]{3,2,1,0:T(8,128)(2,1)S(1)}, u32[]{:S(2)}, u32[]{:S(2)}) collective-permute-start(bf16[1,2,512,128]{3,2,1,0:T(8,128)(2,1)S(1)} %get-tuple-element.64), channel_id=1, source_target_pairs={{0,12},{4,8},{8,4},{12,0},{16,28},{20,24},{24,20},{28,16},{1,13},{... | collective-permute-start | bytes 786440 | tf_op jit(solution)/shard_map/ppermute | solution.py:591
  171.9 11.8 %collective-permute-start.18 = (bf16[1,2,512,128]{3,2,1,0:T(8,128)(2,1)S(1)}, bf16[1,2,512,128]{3,2,1,0:T(8,128)(2,1)S(1)}, u32[]{:S(2)}, u32[]{:S(2)}) collective-permute-start(bf16[1,2,512,128]{3,2,1,0:T(8,128)(2,1)S(1)} %get-tuple-element.63), channel_id=1, source_target_pairs={{0,16},{4,20},{8,24},{12,28},{16,0},{20,4},{24,8},{28,12},{1,17},{... | collective-permute-start | bytes 786440 | tf_op jit(solution)/shard_map/ppermute | solution.py:591
  172.4 24.7 %collective-permute-start.19 = (bf16[1,2,512,128]{3,2,1,0:T(8,128)(2,1)S(1)}, bf16[1,2,512,128]{3,2,1,0:T(8,128)(2,1)S(1)}, u32[]{:S(2)}, u32[]{:S(2)}) collective-permute-start(bf16[1,2,512,128]{3,2,1,0:T(8,128)(2,1)S(1)} %get-tuple-element.62), channel_id=1, source_target_pairs={{0,20},{4,16},{8,28},{12,24},{16,4},{20,0},{24,12},{28,8},{1,21},{... | collective-permute-start | bytes 786440 | tf_op jit(solution)/shard_map/ppermute | solution.py:591
  173.8 23.4 %collective-permute-start.20 = (bf16[1,2,512,128]{3,2,1,0:T(8,128)(2,1)S(1)}, bf16[1,2,512,128]{3,2,1,0:T(8,128)(2,1)S(1)}, u32[]{:S(2)}, u32[]{:S(2)}) collective-permute-start(bf16[1,2,512,128]{3,2,1,0:T(8,128)(2,1)S(1)} %get-tuple-element.61), channel_id=1, source_target_pairs={{0,24},{4,28},{8,16},{12,20},{16,8},{20,12},{24,0},{28,4},{1,25},{... | collective-permute-start | bytes 786440 | tf_op jit(solution)/shard_map/ppermute | solution.py:591
  179.4 17.7 %collective-permute-start.21 = (bf16[1,2,512,128]{3,2,1,0:T(8,128)(2,1)S(1)}, bf16[1,2,512,128]{3,2,1,0:T(8,128)(2,1)S(1)}, u32[]{:S(2)}, u32[]{:S(2)}) collective-permute-start(bf16[1,2,512,128]{3,2,1,0:T(8,128)(2,1)S(1)} %get-tuple-element.60), channel_id=1, source_target_pairs={{0,28},{4,24},{8,20},{12,16},{16,12},{20,8},{24,4},{28,0},{1,29},{... | collective-permute-start | bytes 786440 | tf_op jit(solution)/shard_map/ppermute | solution.py:591
  207.0 43.1 %collective-permute-start.22 = (bf16[7,2,512,128]{3,2,1,0:T(8,128)(2,1)}, bf16[7,2,512,128]{3,2,1,0:T(8,128)(2,1)}, u32[]{:S(2)}, u32[]{:S(2)}) collective-permute-start(bf16[7,2,512,128]{3,2,1,0:T(8,128)(2,1)} %get-tuple-element.59), channel_id=1, source_target_pairs={{0,1},{1,2},{2,3},{4,5},{5,6},{6,7},{8,9},{9,10},{10,11},{12,13},{... | collective-permute-start | bytes 5505032 | tf_op jit(solution)/shard_map/ppermute | solution.py:553
  211.5 44.0 %collective-permute-start.23 = (bf16[7,2,512,128]{3,2,1,0:T(8,128)(2,1)}, bf16[7,2,512,128]{3,2,1,0:T(8,128)(2,1)}, u32[]{:S(2)}, u32[]{:S(2)}) collective-permute-start(bf16[7,2,512,128]{3,2,1,0:T(8,128)(2,1)} %get-tuple-element.58), channel_id=1, source_target_pairs={{1,0},{2,1},{3,2},{5,4},{6,5},{7,6},{9,8},{10,9},{11,10},{13,12},{... | collective-permute-start | bytes 5505032 | tf_op jit(solution)/shard_map/ppermute | solution.py:553
  255.4 54.0 %all-to-all-start.3 = ((bf16[4,2,1088,128]{3,2,1,0:T(8,128)(2,1)}), bf16[4,2,1088,128]{3,2,1,0:T(8,128)(2,1)S(1)}, u32[]{:S(2)}, u32[]{:S(2)}) async-start(bf16[4,2,1088,128]{3,2,1,0:T(8,128)(2,1)} %shear_whole.1), calls=%async_computation.3 | async-start | bytes 4456448 | tf_op jit(solution)/shard_map/all_to_all | solution.py:742
  272.3 7.3 %collective-permute-start.24 = (bf16[8,2,32,128]{3,2,1,0:T(8,128)(2,1)}, bf16[8,2,32,128]{3,2,1,0:T(8,128)(2,1)S(1)}, u32[]{:S(2)}, u32[]{:S(2)}) collective-permute-start(bf16[8,2,32,128]{3,2,1,0:T(8,128)(2,1)} %get-tuple-element.57), channel_id=1, source_target_pairs={{0,4},{4,8},{8,12},{12,16},{16,20},{20,24},{24,28},{1,5},{5,9},{9,... | collective-permute-start | bytes 393224 | tf_op jit(solution)/shard_map/ppermute | solution.py:553
  274.2 6.5 %collective-permute-start.25 = (bf16[8,2,32,128]{3,2,1,0:T(8,128)(2,1)}, bf16[8,2,32,128]{3,2,1,0:T(8,128)(2,1)S(1)}, u32[]{:S(2)}, u32[]{:S(2)}) collective-permute-start(bf16[8,2,32,128]{3,2,1,0:T(8,128)(2,1)} %get-tuple-element.56), channel_id=1, source_target_pairs={{4,0},{8,4},{12,8},{16,12},{20,16},{24,20},{28,24},{5,1},{9,5},{13... | collective-permute-start | bytes 393224 | tf_op jit(solution)/shard_map/ppermute | solution.py:553
  320.3 23.0 %collective-permute-start.28 = (bf16[1,2,1024,128]{3,2,1,0:T(8,128)(2,1)S(1)}, bf16[1,2,1024,128]{3,2,1,0:T(8,128)(2,1)S(1)}, u32[]{:S(2)}, u32[]{:S(2)}) collective-permute-start(bf16[1,2,1024,128]{3,2,1,0:T(8,128)(2,1)S(1)} %get-tuple-element.53), channel_id=1, source_target_pairs={{0,4},{4,8},{8,12},{12,16},{16,20},{20,24},{24,28},{1,5},{5,9},{9,... | collective-permute-start | bytes 1572872 | tf_op jit(solution)/shard_map/ppermute | solution.py:553
  322.2 21.1 %collective-permute-start.29 = (bf16[1,2,1024,128]{3,2,1,0:T(8,128)(2,1)S(1)}, bf16[1,2,1024,128]{3,2,1,0:T(8,128)(2,1)S(1)}, u32[]{:S(2)}, u32[]{:S(2)}) collective-permute-start(bf16[1,2,1024,128]{3,2,1,0:T(8,128)(2,1)S(1)} %get-tuple-element.52), channel_id=1, source_target_pairs={{4,0},{8,4},{12,8},{16,12},{20,16},{24,20},{28,24},{5,1},{9,5},{13... | collective-permute-start | bytes 1572872 | tf_op jit(solution)/shard_map/ppermute | solution.py:553
  326.9 6.4 %collective-permute-start.26 = (bf16[1,2,512,128]{3,2,1,0:T(8,128)(2,1)S(1)}, bf16[1,2,512,128]{3,2,1,0:T(8,128)(2,1)S(1)}, u32[]{:S(2)}, u32[]{:S(2)}) collective-permute-start(bf16[1,2,512,128]{3,2,1,0:T(8,128)(2,1)S(1)} %get-tuple-element.55), channel_id=1, source_target_pairs={{0,1},{1,2},{2,3},{4,5},{5,6},{6,7},{8,9},{9,10},{10,11},{12,13},{... | collective-permute-start | bytes 786440 | tf_op jit(solution)/shard_map/ppermute | solution.py:553
  328.2 9.2 %collective-permute-start.27 = (bf16[1,2,512,128]{3,2,1,0:T(8,128)(2,1)S(1)}, bf16[1,2,512,128]{3,2,1,0:T(8,128)(2,1)S(1)}, u32[]{:S(2)}, u32[]{:S(2)}) collective-permute-start(bf16[1,2,512,128]{3,2,1,0:T(8,128)(2,1)S(1)} %get-tuple-element.54), channel_id=1, source_target_pairs={{1,0},{2,1},{3,2},{5,4},{6,5},{7,6},{9,8},{10,9},{11,10},{13,12},{... | collective-permute-start | bytes 786440 | tf_op jit(solution)/shard_map/ppermute | solution.py:553
  (40 other events, 539.3 us)

commit v6 on v5

--- a/solution.py
+++ b/solution.py
@@ -20,6 +20,8 @@
 BINS = WINDOW // 2
 GROUP = 16
 PARTS = 2
+ROWS = 256
+STEPS = 2
 VMEM_LIMIT = 56 * 1024 * 1024
 
 
@@ -86,7 +88,7 @@
                 here = following
         return carry
 
-    lax.fori_loop(0, rows // GROUP, one_group, 0)
+    lax.fori_loop(0, rows // GROUP, one_group, 0, unroll=4)
 
 
 def ramped_lines(shifted, windows, rows, cosine, sine, forward):
@@ -111,11 +113,11 @@
 
 
 def down_lines(vector):
-    return jnp.broadcast_to(vector, (BLOCK, BLOCK)).T
+    return jnp.broadcast_to(vector, (BLOCK, vector.shape[1])).T
 
 
 def line_ramps(fractions, cosine, sine):
-    bins = lane_iota(BLOCK).astype(jnp.float32)
+    bins = lane_iota(fractions.shape[1]).astype(jnp.float32)
     sine[...], cosine[...] = sine_cosine(down_lines(fractions) * bins * (-2.0 * np.pi / WINDOW))
 
 
@@ -163,7 +165,7 @@
     part_lines = lefts[0].shape[-2]
     line_count = parts * part_lines
     tiles = own.shape[2] // BLOCK if wide else own.shape[0]
-    rows = BLOCK
+    rows = min(part_lines, ROWS)
     share = part_lines // rows
     offset = first // rows
     forward, inverse = tables
@@ -184,7 +186,7 @@
     out_spec = pl.BlockSpec((tiles, 2, rows, BLOCK), lambda i, *_: (0, 0, i, 0))
     groups = rows // GROUP
     kernel = functools.partial(
-        shear_tile_kernel, halo, tiles, rows, tiles // 2 if tiles % 2 == 0 else tiles, wide, parts
+        shear_tile_kernel, halo, tiles, rows, tiles // 4 if tiles % 4 == 0 else tiles, wide, parts
     )
     return pl.pallas_call(
         kernel,
@@ -259,15 +261,15 @@
     shift_lines(strip, shifted, base, 0, spare, tiles, step * tiles, rows)
     ramped = ramped_lines(shifted, range(tiles), rows, cosine, sine, forward)
     target = devices - 1 - step
+    result = lax.dot_general(
+        flipped[...], ramped, (((1,), (1,)), ((), ())), preferred_element_type=jnp.float32
+    ).astype(jnp.bfloat16)
     for window in range(tiles):
-        lines = ramped[window * 2 * rows : (window + 1) * 2 * rows]
-        result = lax.dot_general(
-            flipped[...], lines, (((1,), (1,)), ((), ())), preferred_element_type=jnp.float32
-        ).astype(jnp.bfloat16)
         block = tiles - 1 - window
         low = MARGIN + block * BLOCK
         for part in range(2):
-            piece = result[:, part * rows : (part + 1) * rows]
+            lanes = (2 * window + part) * rows
+            piece = result[:, lanes : lanes + rows]
             out[target, part, low : low + BLOCK, :] = piece
             if block == 0:
 
@@ -320,6 +322,7 @@
     offsets, fractions, forward, inverse, out, strip, shifted, cosine, sine = refs
     step = pl.program_id(0)
     per_step = length // BLOCK
+    per_grid = blocks // pl.num_programs(0)
     total = strip.shape[1]
 
     @pl.when(step == 0)
@@ -340,9 +343,8 @@
     row = lax.broadcasted_iota(jnp.int32, (8, BLOCK), 0) + (offset & 7)
     wraps = row >= 8
     index = row & 7
-    block_rows = (step ^ rank[0]) * length
-
-    def one_chunk(chunk):
+
+    def one_chunk(block_rows, chunk):
         begin = pl.multiple_of(base[0] + block_rows + chunk * BLOCK, GROUP)
         for part in range(2):
             value = strip[part, pl.ds(begin, 2 * BLOCK), :].astype(jnp.float32)
@@ -360,15 +362,16 @@
                 jnp.concatenate(moved, 0).astype(jnp.bfloat16)
             )
 
-    for chunk in range(per_step + 1):
-        one_chunk(chunk)
-    ramp_real = jnp.concatenate([cosine[...]] * 2, 1)
-    ramp_imaginary = jnp.concatenate([sine[...]] * 2, 1)
-    for window in range(per_step):
-        low = window * BLOCK
+    def one_block(local, carry):
+        block_rows = ((step * per_grid + local) ^ rank[0]) * length
+        for chunk in range(per_step + 1):
+            one_chunk(block_rows, chunk)
+        windows = [shifted[m * BLOCK : (m + 2) * BLOCK, :] for m in range(per_step)]
         spectrum = jnp.dot(
-            forward[...], shifted[low : low + 2 * BLOCK, :], preferred_element_type=jnp.float32
+            forward[...], jnp.concatenate(windows, 1), preferred_element_type=jnp.float32
         )
+        ramp_real = jnp.concatenate([cosine[...]] * (2 * per_step), 1)
+        ramp_imaginary = jnp.concatenate([sine[...]] * (2 * per_step), 1)
         real, imaginary = spectrum[:BLOCK], spectrum[BLOCK:]
         ramped = jnp.concatenate(
             [
@@ -377,14 +380,18 @@
             ],
             0,
         )
-        result = jnp.dot(inverse[...], ramped, preferred_element_type=jnp.float32).astype(
-            jnp.bfloat16
-        )
-        block, within = low // rows_out, low % rows_out
-        for part in range(2):
-            out[block, part, within : within + BLOCK, :] = result[
-                :, part * BLOCK : (part + 1) * BLOCK
-            ]
+        result = jnp.dot(inverse[...], ramped, preferred_element_type=jnp.float32)
+        result = result.astype(jnp.bfloat16)
+        for window in range(per_step):
+            piece, within = window * BLOCK // rows_out, window * BLOCK % rows_out
+            for part in range(2):
+                lanes = (2 * window + part) * BLOCK
+                out[local * (length // rows_out) + piece, part, within : within + BLOCK, :] = (
+                    result[:, lanes : lanes + BLOCK]
+                )
+        return carry
+
+    lax.fori_loop(0, per_grid, one_block, 0)
 
 
 def shear_columns(owns, place, blocks, front, back, base, rank, spare, fractions, tables, rows_out):
@@ -399,14 +406,16 @@
     )
     full = lambda shape: pl.BlockSpec(shape, lambda i, *_: (0,) * len(shape))
     pieces = blocks * length // rows_out
-    per_step = pieces // blocks
+    steps = STEPS if blocks % STEPS == 0 else 1
     return pl.pallas_call(
         functools.partial(shear_columns_kernel, front, blocks, length, rows_out, place),
         grid_spec=pltpu.PrefetchScalarGridSpec(
             num_scalar_prefetch=2,
-            grid=(blocks,),
+            grid=(steps,),
             in_specs=[full(x.shape) for x in operands],
-            out_specs=pl.BlockSpec((per_step, 2, rows_out, BLOCK), lambda i, *_: (i, 0, 0, 0)),
+            out_specs=pl.BlockSpec(
+                (pieces // steps, 2, rows_out, BLOCK), lambda i, *_: (i, 0, 0, 0)
+            ),
             scratch_shapes=[
                 pltpu.VMEM((2, front + blocks * length + back, BLOCK), jnp.bfloat16),
                 pltpu.VMEM((length + BLOCK, 2 * BLOCK), jnp.bfloat16),
@@ -458,54 +467,59 @@
     )
 
 
-def travel_first_kernel(length, extended, *refs):
+def travel_first_kernel(length, count, extended, *refs):
     if extended:
         body, wave, wave_top, wave_bottom, matrix, out, field = refs
-        top = body.at[0, :, 0:MARGIN]
-        middle = body.at[0, :, MARGIN : MARGIN + length]
-        bottom = body.at[0, :, MARGIN + length :]
     else:
         body, top, bottom, wave, wave_top, wave_bottom, matrix, out, field = refs
-        top, middle, bottom = top.at[0], body.at[0], bottom.at[0]
-    pieces = [(0, MARGIN, top, wave_top, 0)]
-    for first in range(0, length, BLOCK):
-        pieces.append((MARGIN + first, BLOCK, middle, wave, first))
-    pieces.append((MARGIN + length, MARGIN, bottom, wave_bottom, 0))
-    for place, count, value, waves, first in pieces:
-        lines = slice(first, first + count)
-        parts = transmitted(
-            [value[p, lines, :] for p in range(2)], [waves[p, lines, :] for p in range(2)]
-        )
-        for part in range(2):
-            field[part, place : place + count, :] = parts[part]
-    windows = [
-        jnp.concatenate([field[0, m : m + WINDOW, :], field[1, m : m + WINDOW, :]], 0)
-        for m in range(0, length, BLOCK)
-    ]
-    result = jnp.dot(
-        matrix[...], jnp.concatenate(windows, 1), preferred_element_type=jnp.float32
-    ).astype(jnp.bfloat16)
-    for m in range(length // BLOCK):
-        lanes = slice(m * BLOCK, (m + 1) * BLOCK)
-        for part in range(2):
-            out[0, part, lanes, :] = result[part * BLOCK : (part + 1) * BLOCK, lanes]
+    for chunk in range(count):
+        if extended:
+            tops = body.at[chunk, :, 0:MARGIN]
+            middle = body.at[chunk, :, MARGIN : MARGIN + length]
+            bottoms = body.at[chunk, :, MARGIN + length :]
+        else:
+            tops, middle, bottoms = top.at[chunk], body.at[chunk], bottom.at[chunk]
+        pieces = [(0, MARGIN, tops, wave_top, 0)]
+        for first in range(0, length, BLOCK):
+            pieces.append((MARGIN + first, BLOCK, middle, wave, first))
+        pieces.append((MARGIN + length, MARGIN, bottoms, wave_bottom, 0))
+        across = slice(chunk * BLOCK, (chunk + 1) * BLOCK)
+        for place, height, value, waves, first in pieces:
+            lines = slice(first, first + height)
+            parts = transmitted(
+                [value[p, lines, :] for p in range(2)],
+                [waves[p, lines, across] for p in range(2)],
+            )
+            for part in range(2):
+                field[part, place : place + height, across] = parts[part]
+    for m in range(0, length, BLOCK):
+        window = jnp.concatenate([field[0, m : m + WINDOW, :], field[1, m : m + WINDOW, :]], 0)
+        result = jnp.dot(matrix[...], window, preferred_element_type=jnp.float32)
+        result = result.astype(jnp.bfloat16)
+        for chunk in range(count):
+            across = slice(chunk * BLOCK, (chunk + 1) * BLOCK)
+            for part in range(2):
+                out[chunk, part, m : m + BLOCK, :] = result[
+                    part * BLOCK : (part + 1) * BLOCK, across
+                ]
 
 
 def travel_first(body, halos, wave, wave_halos, matrix):
     chunks = body.shape[0]
+    count = chunks // STEPS if chunks % STEPS == 0 else chunks
     length = wave.shape[1]
-    chunk_spec = lambda x: pl.BlockSpec((1, 2, x.shape[2], BLOCK), lambda i: (i, 0, 0, 0))
-    wide_spec = lambda x: pl.BlockSpec((2, x.shape[1], BLOCK), lambda i: (0, 0, i))
+    chunk_spec = lambda x: pl.BlockSpec((count, 2, x.shape[2], BLOCK), lambda i: (i, 0, 0, 0))
+    wide_spec = lambda x: pl.BlockSpec((2, x.shape[1], count * BLOCK), lambda i: (0, 0, i))
     return pl.pallas_call(
-        functools.partial(travel_first_kernel, length, len(halos) == 0),
-        grid=(chunks,),
+        functools.partial(travel_first_kernel, length, count, len(halos) == 0),
+        grid=(chunks // count,),
         in_specs=[chunk_spec(body)]
         + [chunk_spec(x) for x in halos]
         + [wide_spec(x) for x in (wave, *wave_halos)]
         + [pl.BlockSpec(matrix.shape, lambda i: (0, 0))],
-        out_specs=pl.BlockSpec((1, 2, length, BLOCK), lambda i: (i, 0, 0, 0)),
+        out_specs=pl.BlockSpec((count, 2, length, BLOCK), lambda i: (i, 0, 0, 0)),
         out_shape=jax.ShapeDtypeStruct((chunks, 2, length, BLOCK), jnp.bfloat16),
-        scratch_shapes=[pltpu.VMEM((2, length + 2 * MARGIN, BLOCK), jnp.bfloat16)],
+        scratch_shapes=[pltpu.VMEM((2, length + 2 * MARGIN, count * BLOCK), jnp.bfloat16)],
         compiler_params=pltpu.CompilerParams(vmem_limit_bytes=VMEM_LIMIT),
         name="travel_first",
     )(body, *halos, wave, *wave_halos, matrix)
@@ -528,7 +542,7 @@
 
 def travel_second(left, body, right, matrix):
     chunks, _, length, _ = body.shape
-    rows = BLOCK
+    rows = length // STEPS if length % (STEPS * BLOCK) == 0 else length
     edge = pl.BlockSpec((1, 2, rows, BLOCK), lambda i: (0, 0, i, 0))
     return pl.pallas_call(
         functools.partial(travel_second_kernel, chunks, rows),
@@ -557,29 +571,36 @@
     return lax.optimization_barrier((value, others))[0]
 
 
-def ordered_kernel(rank, *refs):
-    pieces, out = refs[:-1], refs[-1]
+def ordered_kernel(halo, rank, *refs):
+    pieces, (out, first, last) = refs[:-3], refs[-3:]
+    count = len(pieces)
     for s, piece in enumerate(pieces):
-
-        @pl.when(pl.program_id(0) == s)
+        place = s ^ rank[0]
+        out[place] = piece[0]
+
+        @pl.when(place < halo)
         def _():
-            out[...] = piece[...]
-
-
-def ordered(pieces, rank):
+            first[place] = piece[0]
+
+        @pl.when(place >= count - halo)
+        def _():
+            last[place - (count - halo)] = piece[0]
+
+
+def ordered(pieces, halo, rank):
     count = len(pieces)
     block = pieces[0].shape
-    shape = (count, *block[1:])
-    rest = (0,) * (len(block) - 1)
+    shapes = [(n, *block[1:]) for n in (count, halo, halo)]
+    full = lambda shape: pl.BlockSpec(shape, lambda i, *_: (0,) * len(shape))
     return pl.pallas_call(
-        ordered_kernel,
+        functools.partial(ordered_kernel, halo),
         grid_spec=pltpu.PrefetchScalarGridSpec(
             num_scalar_prefetch=1,
-            grid=(count,),
-            in_specs=[pl.BlockSpec(block, lambda i, rank: (0, *rest))] * count,
-            out_specs=pl.BlockSpec(block, lambda i, rank: (i ^ rank[0], *rest)),
+            grid=(1,),
+            in_specs=[full(block)] * count,
+            out_specs=[full(shape) for shape in shapes],
         ),
-        out_shape=jax.ShapeDtypeStruct(shape, pieces[0].dtype),
+        out_shape=[jax.ShapeDtypeStruct(shape, pieces[0].dtype) for shape in shapes],
         compiler_params=pltpu.CompilerParams(vmem_limit_bytes=VMEM_LIMIT),
         name="ordered",
     )(rank, *pieces)
@@ -627,14 +648,13 @@
     by_rank = row_index.astype(jnp.int32).reshape(1)
 
     part_lines = line_count // PARTS
-    lefts, rights = [], []
+    lefts, rights, edges = [], [], ()
     for part in range(PARTS):
-        lines = volume_plane[:, part * part_lines : (part + 1) * part_lines]
-        left, right = from_both_sides(lines[:, :, :reach], lines[:, :, width - reach :], "col")
+        lines = after(volume_plane, edges)[:, part * part_lines : (part + 1) * part_lines]
+        edges = (lines[:, :, :reach], lines[:, :, width - reach :])
+        left, right = from_both_sides(*edges, "col")
         lefts.append(left)
         rights.append(right)
-    wave_a_halos = from_both_sides(wave_a[:, :MARGIN], wave_a[:, -MARGIN:], "row")
-    wave_b_halos = from_both_sides(wave_b[:, :MARGIN], wave_b[:, -MARGIN:], "col")
 
     base_rows, spare_rows = group_starts(reach - MARGIN - shift_rows, GROUP, BLOCK)
 
@@ -700,14 +720,19 @@
         spread.append(lax.all_to_all(sheared, "row", split_axis=0, concat_axis=0, tiled=True))
     lefts, rights = after((lefts, rights), sheared)
     slots = first(0, 0, lefts, rights, by_rank)
-    spread, wave_a_halos, wave_b_halos, slots = lax.optimization_barrier(
-        (spread, wave_a_halos, wave_b_halos, slots)
-    )
+    spread = after(spread, slots)
     pieces = swapped_shares([slots[s : s + 1] for s in range(row_devices)])
 
     place = [[(b, part * part_lines) for b in range(row_devices)] for part in range(PARTS)]
     moved_b = second(1, spread, place, in_order, BLOCK)
     whole = lax.all_to_all(moved_b, ("row", "col"), split_axis=0, concat_axis=0, tiled=True)
+    margin_a = after((wave_a[:, :MARGIN], wave_a[:, -MARGIN:]), moved_b)
+    margin_b = after((wave_b[:, :MARGIN], wave_b[:, -MARGIN:]), moved_b)
+    wave_a_halos = from_both_sides(*margin_a, "row")
+    wave_b_halos = from_both_sides(*margin_b, "col")
+    whole, wave_a_halos, wave_b_halos = lax.optimization_barrier(
+        (whole, wave_a_halos, wave_b_halos)
+    )
     whole = whole.reshape(row_devices, column_devices, 2, BLOCK, BLOCK)
     own_lines = lambda x: lax.dynamic_slice_in_dim(x, column_index * BLOCK, BLOCK, 0)
     groups = BLOCK // GROUP
@@ -723,8 +748,8 @@
     pieces = after(pieces, moved_b)
     moved_a = second(0, pieces, [[(s, 0)] for s in range(row_devices)], by_rank, line_count)
     pieces = swapped_shares([moved_a[s : s + 1] for s in range(row_devices)])
-    tile = ordered(pieces, by_rank)
-    left, right = from_both_sides(tile[:halo], tile[tiles - halo :], "col")
+    tile, low, high = ordered(pieces, halo, by_rank)
+    left, right = from_both_sides(low, high, "col")
     rotated = shear_tile(
         tile,
         [left],
@@ -738,7 +763,6 @@
         row_tables,
     )
 
-    turned, left, right = lax.optimization_barrier((turned, left, right))
     turned = lax.all_to_all(turned, "col", split_axis=0, concat_axis=0, tiled=True)
     half_b = travel_first(turned, (), wave_b, wave_b_halos, along_rows[1])
     left, right = from_both_sides(half_b[:1], half_b[-1:], "row")

time: 353 us -> 328 us (0.929)
  Pallas kernels: 109 us -> 88.6 us
  waiting for transfers between devices: 130 us -> 116 us
  starting transfers between devices: 70.3 us -> 81.7 us
    ppermute x14, waiting for transfers between devices: 61.7 us -> 25.5 us  [swapped_shares(): lax.ppermute(slots[s], 'row', [(i, i ^ s) for i in range(devices)])]
    ppermute x16, waiting for transfers between devices: 50.5 us -> 83.8 us  [from_both_sides(): return (lax.ppermute(last, axis, up), lax.ppermute(first, axis, down))]
    all_to_all x1, waiting for transfers between devices: 18.2 us -> 0.01 us  [on_device(): lax.all_to_all(turned, 'col', split_axis=0, concat_axis=0, tiled=True)]
    pallas_call x2, Pallas kernels: 25.4 us -> 16.8 us  [shear_columns(): pl.pallas_call(functools.partial(shear_columns_kernel, front, blocks, len...]
    ppermute x16, starting transfers between devices: 40.6 us -> 47.1 us  [from_both_sides(): return (lax.ppermute(last, axis, up), lax.ppermute(first, axis, down))]
    all_to_all x1, starting transfers between devices: 3.62 us -> 10.1 us  [on_device(): lax.all_to_all(turned, 'col', split_axis=0, concat_axis=0, tiled=True)]
    all_to_all x1, waiting for transfers between devices: 0.01 us -> 5.5 us  [on_device(): lax.all_to_all(moved_b, ('row', 'col'), split_axis=0, concat_axis=0, tile...]
    pallas_call x4, Pallas kernels: 36 us -> 31.9 us  [shear_tile(): pl.pallas_call(kernel, grid_spec=pltpu.PrefetchScalarGridSpec(num_scalar_...]
  transfers between devices with their start and end apart: 34 -> 34, of which waited for: 15 -> 17; matrix products, arithmetic and copies ran while one was open for 7% -> 7% of each run, Pallas kernels for 23% -> 21%
where the time goes in v6:
time: 328 us; the launch traced here: 326 us
  waiting for transfers between devices  116 us (35%)
  Pallas kernels  88.6 us (27%)
  starting transfers between devices  81.7 us (25%)
  local copies, waits for them, and re-layouts  33.4 us (10%)
    ppermute x16, waiting for transfers between devices, from_both_sides(): return (lax.ppermute(last, axis, up), lax.ppermute(first, axis, down))  83.8 us
    ppermute x16, starting transfers between devices, from_both_sides(): return (lax.ppermute(last, axis, up), lax.ppermute(first, axis, down))  47.1 us
    pallas_call x4, Pallas kernels, shear_tile(): pl.pallas_call(kernel, grid_spec=pltpu.PrefetchScalarGridSpec(num_scalar_...  31.9 us
    ppermute x14, waiting for transfers between devices, swapped_shares(): lax.ppermute(slots[s], 'row', [(i, i ^ s) for i in range(devices)])  25.5 us
    pallas_call x2, Pallas kernels, travel_first(): pl.pallas_call(functools.partial(travel_first_kernel, length, count, len(...  16.9 us
    pallas_call x2, Pallas kernels, shear_columns(): pl.pallas_call(functools.partial(shear_columns_kernel, front, blocks, len...  16.8 us
    ppermute x14, starting transfers between devices, swapped_shares(): lax.ppermute(slots[s], 'row', [(i, i ^ s) for i in range(devices)])  10.9 us
    all_to_all x1, starting transfers between devices, on_device(): lax.all_to_all(turned, 'col', split_axis=0, concat_axis=0, tiled=True)  10.1 us
  transfers between devices with their start and end apart: 34, of which 17 were waited for; matrix products, arithmetic and copies ran while one was open for 7% of the time, Pallas kernels for 21%

profile of v6, /device:TPU:2, one launch (start us, length us, event | category | flops | bytes accessed | tf_op | source)
XLA Modules:
  0.0 326.3 jit_solution(12232869371556848762)
XLA Ops:
  10.1 4.6 %collective-permute-start.1 = (bf16[2,256,896]{2,1,0:T(8,128)(2,1)}, bf16[2,256,896]{2,1,0:T(8,128)(2,1)S(1)}, u32[]{:S(2)}, u32[]{:S(2)}) collective-permute-start(bf16[2,256,896]{2,1,0:T(8,128)(2,1)} %get-tuple-element.93), channel_id=1, source_target_pairs={{0,1},{1,2},{2,3},{4,5},{5,6},{6,7},{8,9},{9,10},{10,11},{12,13},{... | collective-permute-start | bytes 2752520 | tf_op jit(solution)/shard_map/ppermute | solution.py:567
  18.3 10.0 %collective-permute-done.refs_0_ = bf16[2,256,896]{2,1,0:T(8,128)(2,1)S(1)} collective-permute-done((bf16[2,256,896]{2,1,0:T(8,128)(2,1)}, bf16[2,256,896]{2,1,0:T(8,128)(2,1)S(1)}, u32[]{:S(2)}, u32[]{:S(2)}) %collective-permute-start) | collective-permute-done | bytes 917536 | tf_op jit(solution)/shard_map/ppermute | solution.py:567
  28.3 4.4 %collective-permute-done.2.refs_1_.refs_2_ = bf16[2,256,896]{2,1,0:T(8,128)(2,1)S(1)} collective-permute-done((bf16[2,256,896]{2,1,0:T(8,128)(2,1)}, bf16[2,256,896]{2,1,0:T(8,128)(2,1)S(1)}, u32[]{:S(2)}, u32[]{:S(2)}) %collective-permute-start.2) | collective-permute-done | bytes 917536 | tf_op jit(solution)/shard_map/ppermute | solution.py:567
  33.6 6.5 %shear_tile.4 = bf16[8,2,256,128]{3,2,1,0:T(8,128)(2,1)} custom-call(s32[16]{0:T(128)} %get-tuple-element.115.base, s32[1]{0:T(128)} %constant.68.clone.1.rank, bf16[2,256,896]{2,1,0:T(8,128)(2,1)} %copy-done.7, bf16[2,256,896]{2,1,0:T(8,128)(2,1)} %copy-done.8, bf16[2,512,1024]{2,1,0:T(8,128)(2,1)} %refs_4_.2, f32[2,1,256]{2,1,0:T(1,128)} %bitcast.61, ...), custom_call_target="tpu_custom_call" | custom-call | tf_op jit(solution)/shard_map/shear_tile/pallas_call | solution.py:191
  40.1 4.3 %all-to-all-start = ((bf16[8,2,256,128]{3,2,1,0:T(8,128)(2,1)}), bf16[8,2,256,128]{3,2,1,0:T(8,128)(2,1)S(1)}, u32[]{:S(2)}, u32[]{:S(2)}) async-start(bf16[8,2,256,128]{3,2,1,0:T(8,128)(2,1)} %shear_tile.4), calls=%async_computation | async-start | bytes 2097152 | tf_op jit(solution)/shard_map/all_to_all | solution.py:720
  46.8 4.2 %collective-permute-done.3.refs_1_.refs_3_ = bf16[2,256,896]{2,1,0:T(8,128)(2,1)} collective-permute-done((bf16[2,256,896]{2,1,0:T(8,128)(2,1)}, bf16[2,256,896]{2,1,0:T(8,128)(2,1)}, u32[]{:S(2)}, u32[]{:S(2)}) %collective-permute-start.3) | collective-permute-done | bytes 917536 | tf_op jit(solution)/shard_map/ppermute | solution.py:567
  51.0 6.5 %shear_tile.5 = bf16[8,2,256,128]{3,2,1,0:T(8,128)(2,1)} custom-call(s32[16]{0:T(128)} %get-tuple-element.116.base, s32[1]{0:T(128)} %constant.68.clone.1.rank, bf16[2,256,896]{2,1,0:T(8,128)(2,1)} %copy-done.9, bf16[2,256,896]{2,1,0:T(8,128)(2,1)} %collective-permute-done.3.refs_1_.refs_3_, bf16[2,512,1024]{2,1,0:T(8,128)(2,1)} %refs_4_.2, ...), custom_call_target="tpu_custom_call" | custom-call | tf_op jit(solution)/shard_map/shear_tile/pallas_call | solution.py:191
  58.3 5.0 %all-to-all-start.1 = ((bf16[8,2,256,128]{3,2,1,0:T(8,128)(2,1)}), bf16[8,2,256,128]{3,2,1,0:T(8,128)(2,1)S(1)}, u32[]{:S(2)}, u32[]{:S(2)}) async-start(bf16[8,2,256,128]{3,2,1,0:T(8,128)(2,1)} %shear_tile.5), calls=%async_computation.1 | async-start | bytes 2097152 | tf_op jit(solution)/shard_map/all_to_all | solution.py:720
  66.4 10.1 %shear_tile.6 = bf16[8,2,512,128]{3,2,1,0:T(8,128)(2,1)} custom-call(s32[32]{0:T(128)} %get-tuple-element.113.base, s32[1]{0:T(128)} %bitcast.1.rank, bf16[2,256,896]{2,1,0:T(8,128)(2,1)} %copy-done.7, bf16[2,256,896]{2,1,0:T(8,128)(2,1)} %copy-done.9, bf16[2,256,896]{2,1,0:T(8,128)(2,1)} %copy-done.8, ...), custom_call_target="tpu_custom_call" | custom-call | tf_op jit(solution)/shard_map/shear_tile/pallas_call | solution.py:191
  78.1 8.4 %shear_columns.2 = bf16[32,2,128,128]{3,2,1,0:T(8,128)(2,1)} custom-call(s32[1]{0:T(128)} %bitcast.11.base, s32[1]{0:T(128)} %constant.68.clone.1.rank, bf16[8,2,256,128]{3,2,1,0:T(8,128)(2,1)} %copy-done.5, bf16[8,2,256,128]{3,2,1,0:T(8,128)(2,1)} %copy-done.6, s32[1,128]{1,0:T(1,128)} %get-tuple-element.120.refs_2_, f32[1,128]{1,0:T(1,128)} %get-tuple-element.118.refs_3_, ...), custom_call_target="tpu_custom_call" | custom-call | tf_op jit(solution)/shard_map/shear_columns/pallas_call | solution.py:410
  86.5 4.3 %all-to-all-start.2 = ((bf16[32,2,128,128]{3,2,1,0:T(8,128)(2,1)}), bf16[32,2,128,128]{3,2,1,0:T(8,128)(2,1)S(1)}, u32[]{:S(2)}, u32[]{:S(2)}) async-start(bf16[32,2,128,128]{3,2,1,0:T(8,128)(2,1)} %shear_columns.2), calls=%async_computation.2 | async-start | bytes 4194304 | tf_op jit(solution)/shard_map/all_to_all | solution.py:728
  108.8 4.0 %collective-permute-done.5.refs_2_ = bf16[1,2,512,128]{3,2,1,0:T(8,128)(2,1)} collective-permute-done((bf16[1,2,512,128]{3,2,1,0:T(8,128)(2,1)}, bf16[1,2,512,128]{3,2,1,0:T(8,128)(2,1)}, u32[]{:S(2)}, u32[]{:S(2)}) %collective-permute-start.5) | collective-permute-done | bytes 262176 | tf_op jit(solution)/shard_map/ppermute | solution.py:612
  113.6 13.4 %collective-permute-done.24.refs_2_ = bf16[2,32,512]{2,1,0:T(8,128)(2,1)S(1)} collective-permute-done((bf16[2,32,512]{2,1,0:T(8,128)(2,1)}, bf16[2,32,512]{2,1,0:T(8,128)(2,1)S(1)}, u32[]{:S(2)}, u32[]{:S(2)}) %collective-permute-start.24) | collective-permute-done | bytes 65568 | tf_op jit(solution)/shard_map/ppermute | solution.py:567
  131.9 5.5 %all-to-all-done.2 = bf16[32,2,128,128]{3,2,1,0:T(8,128)(2,1)S(1)} async-done(((bf16[32,2,128,128]{3,2,1,0:T(8,128)(2,1)}), bf16[32,2,128,128]{3,2,1,0:T(8,128)(2,1)S(1)}, u32[]{:S(2)}, u32[]{:S(2)}) %all-to-all-start.2) | async-done | bytes 2097184 | tf_op jit(solution)/shard_map/all_to_all | solution.py:728
  138.7 9.6 %shear_whole.1 = bf16[4,2,1088,128]{3,2,1,0:T(8,128)(2,1)} custom-call(s32[8]{0:T(128)} %fusion.12.base, bf16[8,4,2,128,128]{4,3,2,1,0:T(8,128)(2,1)} %bitcast.60, f32[1,128]{1,0:T(1,128)} %fusion.14.offsets, f32[1,128]{1,0:T(1,128)} %fusion.15.fractions, bf16[256,256]{1,0:T(8,128)(2,1)} %constant.84.clone.refs_5_.refs_7_.forward, ...), custom_call_target="tpu_custom_call" | custom-call | tf_op jit(solution)/shard_map/shear_whole/pallas_call | solution.py:299
  148.3 10.1 %all-to-all-start.3 = ((bf16[4,2,1088,128]{3,2,1,0:T(8,128)(2,1)}), bf16[4,2,1088,128]{3,2,1,0:T(8,128)(2,1)S(1)}, u32[]{:S(2)}, u32[]{:S(2)}) async-start(bf16[4,2,1088,128]{3,2,1,0:T(8,128)(2,1)} %shear_whole.1), calls=%async_computation.3 | async-start | bytes 4456448 | tf_op jit(solution)/shard_map/all_to_all | solution.py:766
  159.2 8.5 %shear_columns.3 = bf16[8,2,512,128]{3,2,1,0:T(8,128)(2,1)} custom-call(s32[1]{0:T(128)} %bitcast.3.base, s32[1]{0:T(128)} %bitcast.1.rank, bf16[1,2,512,128]{3,2,1,0:T(8,128)(2,1)} %get-tuple-element.44.refs_0_, bf16[1,2,512,128]{3,2,1,0:T(8,128)(2,1)} %collective-permute-done.4.refs_1_, bf16[1,2,512,128]{3,2,1,0:T(8,128)(2,1)} %collective-permute-done.5.refs_2_, ...), custom_call_target="tpu_custom_call" | custom-call | tf_op jit(solution)/shard_map/shear_columns/pallas_call | solution.py:410
  175.1 4.2 %collective-permute-done.12.refs_2_ = bf16[1,2,512,128]{3,2,1,0:T(8,128)(2,1)S(1)} collective-permute-done((bf16[1,2,512,128]{3,2,1,0:T(8,128)(2,1)S(1)}, bf16[1,2,512,128]{3,2,1,0:T(8,128)(2,1)S(1)}, u32[]{:S(2)}, u32[]{:S(2)}) %collective-permute-start.12) | collective-permute-done | bytes 262176 | tf_op jit(solution)/shard_map/ppermute | solution.py:612
  179.6 4.5 %collective-permute-done.13.refs_3_ = bf16[1,2,512,128]{3,2,1,0:T(8,128)(2,1)S(1)} collective-permute-done((bf16[1,2,512,128]{3,2,1,0:T(8,128)(2,1)S(1)}, bf16[1,2,512,128]{3,2,1,0:T(8,128)(2,1)S(1)}, u32[]{:S(2)}, u32[]{:S(2)}) %collective-permute-start.13) | collective-permute-done | bytes 262176 | tf_op jit(solution)/shard_map/ppermute | solution.py:612
  184.0 12.8 %collective-permute-done.15.refs_5_ = bf16[1,2,512,128]{3,2,1,0:T(8,128)(2,1)S(1)} collective-permute-done((bf16[1,2,512,128]{3,2,1,0:T(8,128)(2,1)S(1)}, bf16[1,2,512,128]{3,2,1,0:T(8,128)(2,1)S(1)}, u32[]{:S(2)}, u32[]{:S(2)}) %collective-permute-start.15) | collective-permute-done | bytes 262176 | tf_op jit(solution)/shard_map/ppermute | solution.py:612
  197.7 4.5 %ordered.1 = (bf16[8,2,512,128]{3,2,1,0:T(8,128)(2,1)}, bf16[7,2,512,128]{3,2,1,0:T(8,128)(2,1)}, bf16[7,2,512,128]{3,2,1,0:T(8,128)(2,1)}) custom-call(s32[1]{0:T(128)} %bitcast.1.rank, bf16[1,2,512,128]{3,2,1,0:T(8,128)(2,1)} %get-tuple-element.83.refs_0_, bf16[1,2,512,128]{3,2,1,0:T(8,128)(2,1)} %copy-done.14, bf16[1,2,512,128]{3,2,1,0:T(8,128)(2,1)} %copy-done.15, ...), custom_call_target="tpu_custom_call" | custom-call | tf_op jit(solution)/shard_map/ordered/pallas_call | solution.py:595
  202.2 7.4 %collective-permute-start.18 = (bf16[7,2,512,128]{3,2,1,0:T(8,128)(2,1)}, bf16[7,2,512,128]{3,2,1,0:T(8,128)(2,1)S(1)}, u32[]{:S(2)}, u32[]{:S(2)}) collective-permute-start(bf16[7,2,512,128]{3,2,1,0:T(8,128)(2,1)} %get-tuple-element.52), channel_id=1, source_target_pairs={{0,1},{1,2},{2,3},{4,5},{5,6},{6,7},{8,9},{9,10},{10,11},{12,13},{... | collective-permute-start | bytes 5505032 | tf_op jit(solution)/shard_map/ppermute | solution.py:567
  211.9 37.4 %collective-permute-done.18.refs_0_ = bf16[7,2,512,128]{3,2,1,0:T(8,128)(2,1)S(1)} collective-permute-done((bf16[7,2,512,128]{3,2,1,0:T(8,128)(2,1)}, bf16[7,2,512,128]{3,2,1,0:T(8,128)(2,1)S(1)}, u32[]{:S(2)}, u32[]{:S(2)}) %collective-permute-start.18) | collective-permute-done | bytes 1835040 | tf_op jit(solution)/shard_map/ppermute | solution.py:567
  249.3 4.6 %collective-permute-done.19.refs_1_ = bf16[7,2,512,128]{3,2,1,0:T(8,128)(2,1)S(1)} collective-permute-done((bf16[7,2,512,128]{3,2,1,0:T(8,128)(2,1)}, bf16[7,2,512,128]{3,2,1,0:T(8,128)(2,1)S(1)}, u32[]{:S(2)}, u32[]{:S(2)}) %collective-permute-start.19) | collective-permute-done | bytes 1835040 | tf_op jit(solution)/shard_map/ppermute | solution.py:567
  255.2 8.9 %shear_tile.7.refs_0_ = bf16[8,2,512,128]{3,2,1,0:T(8,128)(2,1)} custom-call(s32[32]{0:T(128)} %get-tuple-element.114.base, s32[1]{0:T(128)} %constant.68.clone.1.rank, bf16[7,2,512,128]{3,2,1,0:T(8,128)(2,1)} %copy-done.10, bf16[7,2,512,128]{3,2,1,0:T(8,128)(2,1)} %copy-done.11, bf16[8,2,512,128]{3,2,1,0:T(8,128)(2,1)} %get-tuple-element.54.refs_2_, ...), custom_call_target="tpu_custom_call" | custom-call | tf_op jit(solution)/shard_map/shear_tile/pallas_call | solution.py:191
  274.9 8.4 %travel_first.2.body = bf16[8,2,512,128]{3,2,1,0:T(8,128)(2,1)} custom-call(bf16[8,2,512,128]{3,2,1,0:T(8,128)(2,1)} %shear_tile.7.refs_0_, bf16[8,2,32,128]{3,2,1,0:T(8,128)(2,1)} %copy-done.25, bf16[8,2,32,128]{3,2,1,0:T(8,128)(2,1)} %copy-done.26, bf16[2,512,1024]{2,1,0:T(8,128)(2,1)} %refs_3_.1, bf16[2,32,1024]{2,1,0:T(8,128)(2,1)} %copy-done.24, ...), custom_call_target="tpu_custom_call" | custom-call | tf_op jit(solution)/shard_map/travel_first/pallas_call | solution.py:513
  284.6 8.5 %travel_first.3.body = bf16[4,2,1024,128]{3,2,1,0:T(8,128)(2,1)} custom-call(bf16[4,2,1088,128]{3,2,1,0:T(8,128)(2,1)} %copy-done.3, bf16[2,1024,512]{2,1,0:T(8,128)(2,1)} %refs_1_.1, bf16[2,32,512]{2,1,0:T(8,128)(2,1)} %copy-done.28, bf16[2,32,512]{2,1,0:T(8,128)(2,1)} %copy-done.29, bf16[256,384]{1,0:T(8,128)(2,1)} %copy.23.refs_4_), custom_call_target="tpu_custom_call" | custom-call | tf_op jit(solution)/shard_map/travel_first/pallas_call | solution.py:513
  294.4 4.4 %collective-permute-start.28 = (bf16[1,2,1024,128]{3,2,1,0:T(8,128)(2,1)S(1)}, bf16[1,2,1024,128]{3,2,1,0:T(8,128)(2,1)S(1)}, u32[]{:S(2)}, u32[]{:S(2)}) collective-permute-start(bf16[1,2,1024,128]{3,2,1,0:T(8,128)(2,1)S(1)} %get-tuple-element.67), channel_id=1, source_target_pairs={{0,4},{4,8},{8,12},{12,16},{16,20},{20,24},{24,28},{1,5},{5,9},{9,... | collective-permute-start | bytes 1572872 | tf_op jit(solution)/shard_map/ppermute | solution.py:567
  307.7 3.9 %collective-permute-done.26.left = bf16[1,2,512,128]{3,2,1,0:T(8,128)(2,1)S(1)} collective-permute-done((bf16[1,2,512,128]{3,2,1,0:T(8,128)(2,1)S(1)}, bf16[1,2,512,128]{3,2,1,0:T(8,128)(2,1)S(1)}, u32[]{:S(2)}, u32[]{:S(2)}) %collective-permute-start.26) | collective-permute-done | bytes 262176 | tf_op jit(solution)/shard_map/ppermute | solution.py:567
  311.6 4.1 %collective-permute-done.27.right = bf16[1,2,512,128]{3,2,1,0:T(8,128)(2,1)S(1)} collective-permute-done((bf16[1,2,512,128]{3,2,1,0:T(8,128)(2,1)S(1)}, bf16[1,2,512,128]{3,2,1,0:T(8,128)(2,1)S(1)}, u32[]{:S(2)}, u32[]{:S(2)}) %collective-permute-start.27) | collective-permute-done | bytes 262176 | tf_op jit(solution)/shard_map/ppermute | solution.py:567
  316.4 4.4 %travel_second.2 = bf16[2,512,1024]{2,1,0:T(8,128)(2,1)} custom-call(bf16[1,2,512,128]{3,2,1,0:T(8,128)(2,1)} %copy-done.21, bf16[8,2,512,128]{3,2,1,0:T(8,128)(2,1)} %travel_first.2.body, bf16[1,2,512,128]{3,2,1,0:T(8,128)(2,1)} %copy-done.22, bf16[768,256]{1,0:T(8,128)(2,1)} %get-tuple-element.97.matrix), custom_call_target="tpu_custom_call" | custom-call | tf_op jit(solution)/shard_map/travel_second/pallas_call | solution.py:547
  321.8 4.4 %travel_second.3 = bf16[2,1024,512]{2,1,0:T(8,128)(2,1)} custom-call(bf16[1,2,1024,128]{3,2,1,0:T(8,128)(2,1)} %copy-done.12, bf16[4,2,1024,128]{3,2,1,0:T(8,128)(2,1)} %travel_first.3.body, bf16[1,2,1024,128]{3,2,1,0:T(8,128)(2,1)} %copy-done.13, bf16[768,256]{1,0:T(8,128)(2,1)} %get-tuple-element.96.matrix), custom_call_target="tpu_custom_call" | custom-call | tf_op jit(solution)/shard_map/travel_second/pallas_call | solution.py:547
  (159 shorter events, 82.3 us)
Async XLA Ops:
  3.7 24.7 %collective-permute-start = (bf16[2,256,896]{2,1,0:T(8,128)(2,1)}, bf16[2,256,896]{2,1,0:T(8,128)(2,1)S(1)}, u32[]{:S(2)}, u32[]{:S(2)}) collective-permute-start(bf16[2,256,896]{2,1,0:T(8,128)(2,1)} %get-tuple-element.95), channel_id=1, source_target_pairs={{0,1},{1,2},{2,3},{4,5},{5,6},{6,7},{8,9},{9,10},{10,11},{12,13},{... | collective-permute-start | bytes 2752520 | tf_op jit(solution)/shard_map/ppermute | solution.py:567
  7.3 25.4 %collective-permute-start.2 = (bf16[2,256,896]{2,1,0:T(8,128)(2,1)}, bf16[2,256,896]{2,1,0:T(8,128)(2,1)S(1)}, u32[]{:S(2)}, u32[]{:S(2)}) collective-permute-start(bf16[2,256,896]{2,1,0:T(8,128)(2,1)} %get-tuple-element.94), channel_id=1, source_target_pairs={{1,0},{2,1},{3,2},{5,4},{6,5},{7,6},{9,8},{10,9},{11,10},{13,12},{... | collective-permute-start | bytes 2752520 | tf_op jit(solution)/shard_map/ppermute | solution.py:567
  10.1 36.7 %collective-permute-start.1 = (bf16[2,256,896]{2,1,0:T(8,128)(2,1)}, bf16[2,256,896]{2,1,0:T(8,128)(2,1)S(1)}, u32[]{:S(2)}, u32[]{:S(2)}) collective-permute-start(bf16[2,256,896]{2,1,0:T(8,128)(2,1)} %get-tuple-element.93), channel_id=1, source_target_pairs={{0,1},{1,2},{2,3},{4,5},{5,6},{6,7},{8,9},{9,10},{10,11},{12,13},{... | collective-permute-start | bytes 2752520 | tf_op jit(solution)/shard_map/ppermute | solution.py:567
  14.7 36.3 %collective-permute-start.3 = (bf16[2,256,896]{2,1,0:T(8,128)(2,1)}, bf16[2,256,896]{2,1,0:T(8,128)(2,1)}, u32[]{:S(2)}, u32[]{:S(2)}) collective-permute-start(bf16[2,256,896]{2,1,0:T(8,128)(2,1)} %get-tuple-element.92), channel_id=1, source_target_pairs={{1,0},{2,1},{3,2},{5,4},{6,5},{7,6},{9,8},{10,9},{11,10},{13,12},{... | collective-permute-start | bytes 2752520 | tf_op jit(solution)/shard_map/ppermute | solution.py:567
  40.1 18.2 %all-to-all-start = ((bf16[8,2,256,128]{3,2,1,0:T(8,128)(2,1)}), bf16[8,2,256,128]{3,2,1,0:T(8,128)(2,1)S(1)}, u32[]{:S(2)}, u32[]{:S(2)}) async-start(bf16[8,2,256,128]{3,2,1,0:T(8,128)(2,1)} %shear_tile.4), calls=%async_computation | async-start | bytes 2097152 | tf_op jit(solution)/shard_map/all_to_all | solution.py:720
  58.3 18.9 %all-to-all-start.1 = ((bf16[8,2,256,128]{3,2,1,0:T(8,128)(2,1)}), bf16[8,2,256,128]{3,2,1,0:T(8,128)(2,1)S(1)}, u32[]{:S(2)}, u32[]{:S(2)}) async-start(bf16[8,2,256,128]{3,2,1,0:T(8,128)(2,1)} %shear_tile.5), calls=%async_computation.1 | async-start | bytes 2097152 | tf_op jit(solution)/shard_map/all_to_all | solution.py:720
  86.5 50.9 %all-to-all-start.2 = ((bf16[32,2,128,128]{3,2,1,0:T(8,128)(2,1)}), bf16[32,2,128,128]{3,2,1,0:T(8,128)(2,1)S(1)}, u32[]{:S(2)}, u32[]{:S(2)}) async-start(bf16[32,2,128,128]{3,2,1,0:T(8,128)(2,1)} %shear_columns.2), calls=%async_computation.2 | async-start | bytes 4194304 | tf_op jit(solution)/shard_map/all_to_all | solution.py:728
  95.0 11.7 %collective-permute-start.4 = (bf16[1,2,512,128]{3,2,1,0:T(8,128)(2,1)}, bf16[1,2,512,128]{3,2,1,0:T(8,128)(2,1)}, u32[]{:S(2)}, u32[]{:S(2)}) collective-permute-start(bf16[1,2,512,128]{3,2,1,0:T(8,128)(2,1)} %get-tuple-element.90), channel_id=1, source_target_pairs={{0,4},{4,0},{8,12},{12,8},{16,20},{20,16},{24,28},{28,24},{1,5},{5... | collective-permute-start | bytes 786440 | tf_op jit(solution)/shard_map/ppermute | solution.py:612
  95.2 17.6 %collective-permute-start.5 = (bf16[1,2,512,128]{3,2,1,0:T(8,128)(2,1)}, bf16[1,2,512,128]{3,2,1,0:T(8,128)(2,1)}, u32[]{:S(2)}, u32[]{:S(2)}) collective-permute-start(bf16[1,2,512,128]{3,2,1,0:T(8,128)(2,1)} %get-tuple-element.89), channel_id=1, source_target_pairs={{0,8},{4,12},{8,0},{12,4},{16,24},{20,28},{24,16},{28,20},{1,9},{5... | collective-permute-start | bytes 786440 | tf_op jit(solution)/shard_map/ppermute | solution.py:612
  97.1 31.3 %collective-permute-start.22 = (bf16[2,32,1024]{2,1,0:T(8,128)(2,1)}, bf16[2,32,1024]{2,1,0:T(8,128)(2,1)S(1)}, u32[]{:S(2)}, u32[]{:S(2)}) collective-permute-start(bf16[2,32,1024]{2,1,0:T(8,128)(2,1)} %get-tuple-element.55), channel_id=1, source_target_pairs={{0,4},{4,8},{8,12},{12,16},{16,20},{20,24},{24,28},{1,5},{5,9},{9,... | collective-permute-start | bytes 393224 | tf_op jit(solution)/shard_map/ppermute | solution.py:567
  99.0 30.4 %collective-permute-start.23 = (bf16[2,32,1024]{2,1,0:T(8,128)(2,1)}, bf16[2,32,1024]{2,1,0:T(8,128)(2,1)}, u32[]{:S(2)}, u32[]{:S(2)}) collective-permute-start(bf16[2,32,1024]{2,1,0:T(8,128)(2,1)} %get-tuple-element.56), channel_id=1, source_target_pairs={{4,0},{8,4},{12,8},{16,12},{20,16},{24,20},{28,24},{5,1},{9,5},{13... | collective-permute-start | bytes 393224 | tf_op jit(solution)/shard_map/ppermute | solution.py:567
  103.2 23.7 %collective-permute-start.24 = (bf16[2,32,512]{2,1,0:T(8,128)(2,1)}, bf16[2,32,512]{2,1,0:T(8,128)(2,1)S(1)}, u32[]{:S(2)}, u32[]{:S(2)}) collective-permute-start(bf16[2,32,512]{2,1,0:T(8,128)(2,1)} %get-tuple-element.57), channel_id=1, source_target_pairs={{0,1},{1,2},{2,3},{4,5},{5,6},{6,7},{8,9},{9,10},{10,11},{12,13},{... | collective-permute-start | bytes 196616 | tf_op jit(solution)/shard_map/ppermute | solution.py:567
  106.8 21.6 %collective-permute-start.25 = (bf16[2,32,512]{2,1,0:T(8,128)(2,1)}, bf16[2,32,512]{2,1,0:T(8,128)(2,1)S(1)}, u32[]{:S(2)}, u32[]{:S(2)}) collective-permute-start(bf16[2,32,512]{2,1,0:T(8,128)(2,1)} %get-tuple-element.58), channel_id=1, source_target_pairs={{1,0},{2,1},{3,2},{5,4},{6,5},{7,6},{9,8},{10,9},{11,10},{13,12},{... | collective-permute-start | bytes 196616 | tf_op jit(solution)/shard_map/ppermute | solution.py:567
  112.8 46.3 %collective-permute-start.6 = (bf16[1,2,512,128]{3,2,1,0:T(8,128)(2,1)S(1)}, bf16[1,2,512,128]{3,2,1,0:T(8,128)(2,1)}, u32[]{:S(2)}, u32[]{:S(2)}) collective-permute-start(bf16[1,2,512,128]{3,2,1,0:T(8,128)(2,1)S(1)} %get-tuple-element.88), channel_id=1, source_target_pairs={{0,12},{4,8},{8,4},{12,0},{16,28},{20,24},{24,20},{28,16},{1,13},{... | collective-permute-start | bytes 786440 | tf_op jit(solution)/shard_map/ppermute | solution.py:612
  126.9 32.2 %collective-permute-start.7 = (bf16[1,2,512,128]{3,2,1,0:T(8,128)(2,1)S(1)}, bf16[1,2,512,128]{3,2,1,0:T(8,128)(2,1)}, u32[]{:S(2)}, u32[]{:S(2)}) collective-permute-start(bf16[1,2,512,128]{3,2,1,0:T(8,128)(2,1)S(1)} %get-tuple-element.87), channel_id=1, source_target_pairs={{0,16},{4,20},{8,24},{12,28},{16,0},{20,4},{24,8},{28,12},{1,17},{... | collective-permute-start | bytes 786440 | tf_op jit(solution)/shard_map/ppermute | solution.py:612
  128.4 30.7 %collective-permute-start.8 = (bf16[1,2,512,128]{3,2,1,0:T(8,128)(2,1)S(1)}, bf16[1,2,512,128]{3,2,1,0:T(8,128)(2,1)}, u32[]{:S(2)}, u32[]{:S(2)}) collective-permute-start(bf16[1,2,512,128]{3,2,1,0:T(8,128)(2,1)S(1)} %get-tuple-element.86), channel_id=1, source_target_pairs={{0,20},{4,16},{8,28},{12,24},{16,4},{20,0},{24,12},{28,8},{1,21},{... | collective-permute-start | bytes 786440 | tf_op jit(solution)/shard_map/ppermute | solution.py:612
  128.4 30.7 %collective-permute-start.9 = (bf16[1,2,512,128]{3,2,1,0:T(8,128)(2,1)S(1)}, bf16[1,2,512,128]{3,2,1,0:T(8,128)(2,1)}, u32[]{:S(2)}, u32[]{:S(2)}) collective-permute-start(bf16[1,2,512,128]{3,2,1,0:T(8,128)(2,1)S(1)} %get-tuple-element.85), channel_id=1, source_target_pairs={{0,24},{4,28},{8,16},{12,20},{16,8},{20,12},{24,0},{28,4},{1,25},{... | collective-permute-start | bytes 786440 | tf_op jit(solution)/shard_map/ppermute | solution.py:612
  129.4 29.8 %collective-permute-start.10 = (bf16[1,2,512,128]{3,2,1,0:T(8,128)(2,1)S(1)}, bf16[1,2,512,128]{3,2,1,0:T(8,128)(2,1)}, u32[]{:S(2)}, u32[]{:S(2)}) collective-permute-start(bf16[1,2,512,128]{3,2,1,0:T(8,128)(2,1)S(1)} %get-tuple-element.84), channel_id=1, source_target_pairs={{0,28},{4,24},{8,20},{12,16},{16,12},{20,8},{24,4},{28,0},{1,29},{... | collective-permute-start | bytes 786440 | tf_op jit(solution)/shard_map/ppermute | solution.py:612
  148.3 135.0 %all-to-all-start.3 = ((bf16[4,2,1088,128]{3,2,1,0:T(8,128)(2,1)}), bf16[4,2,1088,128]{3,2,1,0:T(8,128)(2,1)S(1)}, u32[]{:S(2)}, u32[]{:S(2)}) async-start(bf16[4,2,1088,128]{3,2,1,0:T(8,128)(2,1)} %shear_whole.1), calls=%async_computation.3 | async-start | bytes 4456448 | tf_op jit(solution)/shard_map/all_to_all | solution.py:766
  170.1 9.2 %collective-permute-start.12 = (bf16[1,2,512,128]{3,2,1,0:T(8,128)(2,1)S(1)}, bf16[1,2,512,128]{3,2,1,0:T(8,128)(2,1)S(1)}, u32[]{:S(2)}, u32[]{:S(2)}) collective-permute-start(bf16[1,2,512,128]{3,2,1,0:T(8,128)(2,1)S(1)} %get-tuple-element.81), channel_id=1, source_target_pairs={{0,8},{4,12},{8,0},{12,4},{16,24},{20,28},{24,16},{28,20},{1,9},{5... | collective-permute-start | bytes 786440 | tf_op jit(solution)/shard_map/ppermute | solution.py:612
  170.8 13.2 %collective-permute-start.13 = (bf16[1,2,512,128]{3,2,1,0:T(8,128)(2,1)S(1)}, bf16[1,2,512,128]{3,2,1,0:T(8,128)(2,1)S(1)}, u32[]{:S(2)}, u32[]{:S(2)}) collective-permute-start(bf16[1,2,512,128]{3,2,1,0:T(8,128)(2,1)S(1)} %get-tuple-element.80), channel_id=1, source_target_pairs={{0,12},{4,8},{8,4},{12,0},{16,28},{20,24},{24,20},{28,16},{1,13},{... | collective-permute-start | bytes 786440 | tf_op jit(solution)/shard_map/ppermute | solution.py:612
  172.0 12.0 %collective-permute-start.14 = (bf16[1,2,512,128]{3,2,1,0:T(8,128)(2,1)S(1)}, bf16[1,2,512,128]{3,2,1,0:T(8,128)(2,1)S(1)}, u32[]{:S(2)}, u32[]{:S(2)}) collective-permute-start(bf16[1,2,512,128]{3,2,1,0:T(8,128)(2,1)S(1)} %get-tuple-element.79), channel_id=1, source_target_pairs={{0,16},{4,20},{8,24},{12,28},{16,0},{20,4},{24,8},{28,12},{1,17},{... | collective-permute-start | bytes 786440 | tf_op jit(solution)/shard_map/ppermute | solution.py:612
  173.5 23.4 %collective-permute-start.15 = (bf16[1,2,512,128]{3,2,1,0:T(8,128)(2,1)S(1)}, bf16[1,2,512,128]{3,2,1,0:T(8,128)(2,1)S(1)}, u32[]{:S(2)}, u32[]{:S(2)}) collective-permute-start(bf16[1,2,512,128]{3,2,1,0:T(8,128)(2,1)S(1)} %get-tuple-element.78), channel_id=1, source_target_pairs={{0,20},{4,16},{8,28},{12,24},{16,4},{20,0},{24,12},{28,8},{1,21},{... | collective-permute-start | bytes 786440 | tf_op jit(solution)/shard_map/ppermute | solution.py:612
  173.7 23.1 %collective-permute-start.16 = (bf16[1,2,512,128]{3,2,1,0:T(8,128)(2,1)S(1)}, bf16[1,2,512,128]{3,2,1,0:T(8,128)(2,1)S(1)}, u32[]{:S(2)}, u32[]{:S(2)}) collective-permute-start(bf16[1,2,512,128]{3,2,1,0:T(8,128)(2,1)S(1)} %get-tuple-element.77), channel_id=1, source_target_pairs={{0,24},{4,28},{8,16},{12,20},{16,8},{20,12},{24,0},{28,4},{1,25},{... | collective-permute-start | bytes 786440 | tf_op jit(solution)/shard_map/ppermute | solution.py:612
  179.3 17.5 %collective-permute-start.17 = (bf16[1,2,512,128]{3,2,1,0:T(8,128)(2,1)S(1)}, bf16[1,2,512,128]{3,2,1,0:T(8,128)(2,1)S(1)}, u32[]{:S(2)}, u32[]{:S(2)}) collective-permute-start(bf16[1,2,512,128]{3,2,1,0:T(8,128)(2,1)S(1)} %get-tuple-element.76), channel_id=1, source_target_pairs={{0,28},{4,24},{8,20},{12,16},{16,12},{20,8},{24,4},{28,0},{1,29},{... | collective-permute-start | bytes 786440 | tf_op jit(solution)/shard_map/ppermute | solution.py:612
  202.2 47.1 %collective-permute-start.18 = (bf16[7,2,512,128]{3,2,1,0:T(8,128)(2,1)}, bf16[7,2,512,128]{3,2,1,0:T(8,128)(2,1)S(1)}, u32[]{:S(2)}, u32[]{:S(2)}) collective-permute-start(bf16[7,2,512,128]{3,2,1,0:T(8,128)(2,1)} %get-tuple-element.52), channel_id=1, source_target_pairs={{0,1},{1,2},{2,3},{4,5},{5,6},{6,7},{8,9},{9,10},{10,11},{12,13},{... | collective-permute-start | bytes 5505032 | tf_op jit(solution)/shard_map/ppermute | solution.py:567
  209.6 44.3 %collective-permute-start.19 = (bf16[7,2,512,128]{3,2,1,0:T(8,128)(2,1)}, bf16[7,2,512,128]{3,2,1,0:T(8,128)(2,1)S(1)}, u32[]{:S(2)}, u32[]{:S(2)}) collective-permute-start(bf16[7,2,512,128]{3,2,1,0:T(8,128)(2,1)} %get-tuple-element.53), channel_id=1, source_target_pairs={{1,0},{2,1},{3,2},{5,4},{6,5},{7,6},{9,8},{10,9},{11,10},{13,12},{... | collective-permute-start | bytes 5505032 | tf_op jit(solution)/shard_map/ppermute | solution.py:567
  265.8 7.5 %collective-permute-start.20 = (bf16[8,2,32,128]{3,2,1,0:T(8,128)(2,1)}, bf16[8,2,32,128]{3,2,1,0:T(8,128)(2,1)S(1)}, u32[]{:S(2)}, u32[]{:S(2)}) collective-permute-start(bf16[8,2,32,128]{3,2,1,0:T(8,128)(2,1)} %get-tuple-element.75), channel_id=1, source_target_pairs={{0,4},{4,8},{8,12},{12,16},{16,20},{20,24},{24,28},{1,5},{5,9},{9,... | collective-permute-start | bytes 393224 | tf_op jit(solution)/shard_map/ppermute | solution.py:567
  294.4 26.5 %collective-permute-start.28 = (bf16[1,2,1024,128]{3,2,1,0:T(8,128)(2,1)S(1)}, bf16[1,2,1024,128]{3,2,1,0:T(8,128)(2,1)S(1)}, u32[]{:S(2)}, u32[]{:S(2)}) collective-permute-start(bf16[1,2,1024,128]{3,2,1,0:T(8,128)(2,1)S(1)} %get-tuple-element.67), channel_id=1, source_target_pairs={{0,4},{4,8},{8,12},{12,16},{16,20},{20,24},{24,28},{1,5},{5,9},{9,... | collective-permute-start | bytes 1572872 | tf_op jit(solution)/shard_map/ppermute | solution.py:567
  298.7 22.1 %collective-permute-start.29 = (bf16[1,2,1024,128]{3,2,1,0:T(8,128)(2,1)S(1)}, bf16[1,2,1024,128]{3,2,1,0:T(8,128)(2,1)S(1)}, u32[]{:S(2)}, u32[]{:S(2)}) collective-permute-start(bf16[1,2,1024,128]{3,2,1,0:T(8,128)(2,1)S(1)} %get-tuple-element.66), channel_id=1, source_target_pairs={{4,0},{8,4},{12,8},{16,12},{20,16},{24,20},{28,24},{5,1},{9,5},{13... | collective-permute-start | bytes 1572872 | tf_op jit(solution)/shard_map/ppermute | solution.py:567
  301.7 9.9 %collective-permute-start.26 = (bf16[1,2,512,128]{3,2,1,0:T(8,128)(2,1)S(1)}, bf16[1,2,512,128]{3,2,1,0:T(8,128)(2,1)S(1)}, u32[]{:S(2)}, u32[]{:S(2)}) collective-permute-start(bf16[1,2,512,128]{3,2,1,0:T(8,128)(2,1)S(1)} %get-tuple-element.69), channel_id=1, source_target_pairs={{0,1},{1,2},{2,3},{4,5},{5,6},{6,7},{8,9},{9,10},{10,11},{12,13},{... | collective-permute-start | bytes 786440 | tf_op jit(solution)/shard_map/ppermute | solution.py:567
  305.4 10.3 %collective-permute-start.27 = (bf16[1,2,512,128]{3,2,1,0:T(8,128)(2,1)S(1)}, bf16[1,2,512,128]{3,2,1,0:T(8,128)(2,1)S(1)}, u32[]{:S(2)}, u32[]{:S(2)}) collective-permute-start(bf16[1,2,512,128]{3,2,1,0:T(8,128)(2,1)S(1)} %get-tuple-element.68), channel_id=1, source_target_pairs={{1,0},{2,1},{3,2},{5,4},{6,5},{7,6},{9,8},{10,9},{11,10},{13,12},{... | collective-permute-start | bytes 786440 | tf_op jit(solution)/shard_map/ppermute | solution.py:567
  (35 other events, 376.9 us)

commit v7 on v6

--- a/solution.py
+++ b/solution.py
@@ -121,8 +121,9 @@
     sine[...], cosine[...] = sine_cosine(down_lines(fractions) * bins * (-2.0 * np.pi / WINDOW))
 
 
-def shear_tile_kernel(halo, tiles, rows, batch, wide, parts, base, rank, *refs):
+def shear_tile_kernel(halo, tiles, rows, batch, wide, parts, sent, base, rank, *refs):
     lefts, rights, refs = refs[:parts], refs[parts : 2 * parts], refs[2 * parts :]
+    waves, refs = refs[: int(sent)], refs[int(sent) :]
     own, offsets, fractions, forward, inverse, out = refs[:6]
     strip, shifted, spare, cosine, sine = refs[6:]
     step = pl.program_id(0)
@@ -153,13 +154,20 @@
     line_ramps(fractions[0], cosine, sine)
     shift_lines(strip, shifted, base, step * groups, spare, tiles, 0, rows)
     for first in range(0, tiles, batch):
-        windows = [slot ^ rank[0] for slot in range(first, first + batch)]
+        windows = [slot if sent else slot ^ rank[0] for slot in range(first, first + batch)]
         ramped = ramped_lines(shifted, windows, rows, cosine, sine, forward)
         result = jnp.dot(ramped, inverse[...], preferred_element_type=jnp.float32)
-        out[first : first + batch] = result.astype(jnp.bfloat16).reshape(batch, 2, rows, BLOCK)
-
-
-def shear_tile(own, lefts, rights, first, halo, base, rank, spare, fractions, tables):
+        result = result.astype(jnp.bfloat16).reshape(batch, 2, rows, BLOCK)
+        if sent:
+            for i, window in enumerate(windows):
+                wave = waves[0][:, :, window * BLOCK : (window + 1) * BLOCK]
+                for part, value in enumerate(transmitted(result[i], wave)):
+                    out[window, part] = value
+        else:
+            out[first : first + batch] = result
+
+
+def shear_tile(own, lefts, rights, first, halo, base, rank, spare, fractions, tables, *waves):
     wide = own.ndim == 3
     parts = len(lefts)
     part_lines = lefts[0].shape[-2]
@@ -186,7 +194,14 @@
     out_spec = pl.BlockSpec((tiles, 2, rows, BLOCK), lambda i, *_: (0, 0, i, 0))
     groups = rows // GROUP
     kernel = functools.partial(
-        shear_tile_kernel, halo, tiles, rows, tiles // 4 if tiles % 4 == 0 else tiles, wide, parts
+        shear_tile_kernel,
+        halo,
+        tiles,
+        rows,
+        tiles // 4 if tiles % 4 == 0 else tiles,
+        wide,
+        parts,
+        len(waves) > 0,
     )
     return pl.pallas_call(
         kernel,
@@ -194,6 +209,7 @@
             num_scalar_prefetch=2,
             grid=(line_count // rows,),
             in_specs=halo_specs
+            + [pl.BlockSpec((2, rows, x.shape[2]), lambda i, *_: (0, i + offset, 0)) for x in waves]
             + [piece_spec(own, lambda i: i + offset)]
             + [line_spec] * 2
             + [
@@ -217,6 +233,7 @@
         rank,
         *lefts,
         *rights,
+        *waves,
         own,
         along(spare),
         along(fractions),
@@ -333,9 +350,9 @@
         for own, slots in zip(owns, place):
             count = own.shape[2]
             for i, (slot, within) in enumerate(slots):
-                first = pl.multiple_of(front + (slot ^ rank[0]) * length + within, GROUP)
+                first = front + slot * length + within
                 for part in range(2):
-                    strip[part, pl.ds(first, count), :] = own[i, part]
+                    strip[part, first : first + count, :] = own[i, part]
         bins = lax.broadcasted_iota(jnp.int32, (BLOCK, BLOCK), 0).astype(jnp.float32)
         sine[...], cosine[...] = sine_cosine(bins * fractions[...] * (-2.0 * np.pi / WINDOW))
 
@@ -467,31 +484,29 @@
     )
 
 
-def travel_first_kernel(length, count, extended, *refs):
-    if extended:
+def travel_first_kernel(length, count, sent, *refs):
+    if sent:
+        body, top, bottom, matrix, out, field = refs
+        for chunk in range(count):
+            across = slice(chunk * BLOCK, (chunk + 1) * BLOCK)
+            for part in range(2):
+                field[part, 0:MARGIN, across] = top[chunk, part]
+                field[part, MARGIN : MARGIN + length, across] = body[chunk, part]
+                field[part, MARGIN + length :, across] = bottom[chunk, part]
+    else:
         body, wave, wave_top, wave_bottom, matrix, out, field = refs
-    else:
-        body, top, bottom, wave, wave_top, wave_bottom, matrix, out, field = refs
-    for chunk in range(count):
-        if extended:
-            tops = body.at[chunk, :, 0:MARGIN]
-            middle = body.at[chunk, :, MARGIN : MARGIN + length]
-            bottoms = body.at[chunk, :, MARGIN + length :]
-        else:
-            tops, middle, bottoms = top.at[chunk], body.at[chunk], bottom.at[chunk]
-        pieces = [(0, MARGIN, tops, wave_top, 0)]
-        for first in range(0, length, BLOCK):
-            pieces.append((MARGIN + first, BLOCK, middle, wave, first))
-        pieces.append((MARGIN + length, MARGIN, bottoms, wave_bottom, 0))
-        across = slice(chunk * BLOCK, (chunk + 1) * BLOCK)
-        for place, height, value, waves, first in pieces:
-            lines = slice(first, first + height)
-            parts = transmitted(
-                [value[p, lines, :] for p in range(2)],
-                [waves[p, lines, across] for p in range(2)],
-            )
-            for part in range(2):
-                field[part, place : place + height, across] = parts[part]
+        pieces = [(0, MARGIN, wave_top, 0)]
+        pieces += [(MARGIN + first, BLOCK, wave, first) for first in range(0, length, BLOCK)]
+        pieces += [(MARGIN + length, MARGIN, wave_bottom, 0)]
+        for chunk in range(count):
+            across = slice(chunk * BLOCK, (chunk + 1) * BLOCK)
+            for place, height, waves, first in pieces:
+                parts = transmitted(
+                    [body[chunk, p, place : place + height, :] for p in range(2)],
+                    [waves[p, first : first + height, across] for p in range(2)],
+                )
+                for part in range(2):
+                    field[part, place : place + height, across] = parts[part]
     for m in range(0, length, BLOCK):
         window = jnp.concatenate([field[0, m : m + WINDOW, :], field[1, m : m + WINDOW, :]], 0)
         result = jnp.dot(matrix[...], window, preferred_element_type=jnp.float32)
@@ -504,25 +519,24 @@
                 ]
 
 
-def travel_first(body, halos, wave, wave_halos, matrix):
+def travel_first(body, halos, waves, matrix):
     chunks = body.shape[0]
     count = chunks // STEPS if chunks % STEPS == 0 else chunks
-    length = wave.shape[1]
+    length = body.shape[2] if len(halos) > 0 else body.shape[2] - 2 * MARGIN
     chunk_spec = lambda x: pl.BlockSpec((count, 2, x.shape[2], BLOCK), lambda i: (i, 0, 0, 0))
     wide_spec = lambda x: pl.BlockSpec((2, x.shape[1], count * BLOCK), lambda i: (0, 0, i))
     return pl.pallas_call(
-        functools.partial(travel_first_kernel, length, count, len(halos) == 0),
+        functools.partial(travel_first_kernel, length, count, len(halos) > 0),
         grid=(chunks // count,),
-        in_specs=[chunk_spec(body)]
-        + [chunk_spec(x) for x in halos]
-        + [wide_spec(x) for x in (wave, *wave_halos)]
+        in_specs=[chunk_spec(x) for x in (body, *halos)]
+        + [wide_spec(x) for x in waves]
         + [pl.BlockSpec(matrix.shape, lambda i: (0, 0))],
         out_specs=pl.BlockSpec((count, 2, length, BLOCK), lambda i: (i, 0, 0, 0)),
         out_shape=jax.ShapeDtypeStruct((chunks, 2, length, BLOCK), jnp.bfloat16),
         scratch_shapes=[pltpu.VMEM((2, length + 2 * MARGIN, count * BLOCK), jnp.bfloat16)],
         compiler_params=pltpu.CompilerParams(vmem_limit_bytes=VMEM_LIMIT),
         name="travel_first",
-    )(body, *halos, wave, *wave_halos, matrix)
+    )(body, *halos, *waves, matrix)
 
 
 def travel_second_kernel(chunks, rows, left, body, right, matrix, out):
@@ -719,20 +733,17 @@
         sheared = first(1, part * part_lines, [left], [right], in_order)
         spread.append(lax.all_to_all(sheared, "row", split_axis=0, concat_axis=0, tiled=True))
     lefts, rights = after((lefts, rights), sheared)
-    slots = first(0, 0, lefts, rights, by_rank)
-    spread = after(spread, slots)
-    pieces = swapped_shares([slots[s : s + 1] for s in range(row_devices)])
+    sheared_a = first(0, 0, lefts, rights, in_order)
+    sheared_a = after(sheared_a, spread)
+    spread_a = lax.all_to_all(sheared_a, "row", split_axis=0, concat_axis=0, tiled=True)
+    margin = after((wave_b[:, :MARGIN], wave_b[:, -MARGIN:]), sheared)
+    wave_b_halos = from_both_sides(*margin, "col")
+    spread, wave_b_halos = lax.optimization_barrier((spread, wave_b_halos))
 
     place = [[(b, part * part_lines) for b in range(row_devices)] for part in range(PARTS)]
     moved_b = second(1, spread, place, in_order, BLOCK)
+    moved_b, spread_a = lax.optimization_barrier((moved_b, spread_a))
     whole = lax.all_to_all(moved_b, ("row", "col"), split_axis=0, concat_axis=0, tiled=True)
-    margin_a = after((wave_a[:, :MARGIN], wave_a[:, -MARGIN:]), moved_b)
-    margin_b = after((wave_b[:, :MARGIN], wave_b[:, -MARGIN:]), moved_b)
-    wave_a_halos = from_both_sides(*margin_a, "row")
-    wave_b_halos = from_both_sides(*margin_b, "col")
-    whole, wave_a_halos, wave_b_halos = lax.optimization_barrier(
-        (whole, wave_a_halos, wave_b_halos)
-    )
     whole = whole.reshape(row_devices, column_devices, 2, BLOCK, BLOCK)
     own_lines = lambda x: lax.dynamic_slice_in_dim(x, column_index * BLOCK, BLOCK, 0)
     groups = BLOCK // GROUP
@@ -745,12 +756,13 @@
         turned_tables,
     )
 
-    pieces = after(pieces, moved_b)
-    moved_a = second(0, pieces, [[(s, 0)] for s in range(row_devices)], by_rank, line_count)
+    moved_a = second(
+        0, [spread_a], [[(b, 0) for b in range(row_devices)]], by_rank, line_count
+    )
     pieces = swapped_shares([moved_a[s : s + 1] for s in range(row_devices)])
     tile, low, high = ordered(pieces, halo, by_rank)
     left, right = from_both_sides(low, high, "col")
-    rotated = shear_tile(
+    field_a = shear_tile(
         tile,
         [left],
         [right],
@@ -761,17 +773,20 @@
         spare_rows[0, 1],
         fraction_rows[0, 1],
         row_tables,
-    )
-
+        wave_a,
+    )
+
+    turned = after(turned, (left, right))
     turned = lax.all_to_all(turned, "col", split_axis=0, concat_axis=0, tiled=True)
-    half_b = travel_first(turned, (), wave_b, wave_b_halos, along_rows[1])
+
+    halos = from_both_sides(field_a[:, :, :MARGIN], field_a[:, :, -MARGIN:], "row")
+    half_a = travel_first(field_a, halos, (), along_rows[0])
+    left, right = from_both_sides(half_a[:1], half_a[-1:], "col")
+    exit_a = travel_second(left, half_a, right, along_columns[0])
+
+    half_b = travel_first(turned, (), (wave_b, *wave_b_halos), along_rows[1])
     left, right = from_both_sides(half_b[:1], half_b[-1:], "row")
     exit_b = travel_second(left, half_b, right, along_columns[1])
-
-    halos = from_both_sides(rotated[:, :, :MARGIN], rotated[:, :, -MARGIN:], "row")
-    half_a = travel_first(rotated, halos, wave_a, wave_a_halos, along_rows[0])
-    left, right = from_both_sides(half_a[:1], half_a[-1:], "col")
-    exit_a = travel_second(left, half_a, right, along_columns[0])
     return exit_a, exit_b
 
 

time: 328 us -> 315 us (0.960)
  starting transfers between devices: 81.7 us -> 68.1 us
  waiting for transfers between devices: 116 us -> 123 us
  local copies, waits for them, and re-layouts: 33.4 us -> 28 us
    ppermute x16 -> x14, waiting for transfers between devices: 83.8 us -> 58.5 us  [from_both_sides(): return (lax.ppermute(last, axis, up), lax.ppermute(first, axis, down))]
    all_to_all x1, waiting for transfers between devices: 0.01 us -> 23 us  [on_device(): lax.all_to_all(turned, 'col', split_axis=0, concat_axis=0, tiled=True)]
    ppermute x14 -> x7, waiting for transfers between devices: 25.5 us -> 34.4 us  [swapped_shares(): lax.ppermute(slots[s], 'row', [(i, i ^ s) for i in range(devices)])]
    ppermute x16 -> x14, starting transfers between devices: 47.1 us -> 38.8 us  [from_both_sides(): return (lax.ppermute(last, axis, up), lax.ppermute(first, axis, down))]
    all_to_all x1, starting transfers between devices: 10.1 us -> 3.62 us  [on_device(): lax.all_to_all(turned, 'col', split_axis=0, concat_axis=0, tiled=True)]
    ppermute x14 -> x7, starting transfers between devices: 10.9 us -> 5.21 us  [swapped_shares(): lax.ppermute(slots[s], 'row', [(i, i ^ s) for i in range(devices)])]
    all_to_all x1, waiting for transfers between devices: 5.5 us -> 0.01 us  [on_device(): lax.all_to_all(moved_b, ('row', 'col'), split_axis=0, concat_axis=0, tile...]
    all_to_all x0 -> x1, starting transfers between devices: none -> 5.03 us  [on_device(): lax.all_to_all(sheared_a, 'row', split_axis=0, concat_axis=0, tiled=True)]
  transfers between devices with their start and end apart: 34 -> 26, of which waited for: 17 -> 19; matrix products, arithmetic and copies ran while one was open for 7% -> 6% of each run, Pallas kernels for 21% -> 24%
where the time goes in v7:
time: 315 us; the launch traced here: 312 us
  waiting for transfers between devices  123 us (39%)
  Pallas kernels  87 us (28%)
  starting transfers between devices  68.1 us (22%)
  local copies, waits for them, and re-layouts  28 us (9%)
    ppermute x14, waiting for transfers between devices, from_both_sides(): return (lax.ppermute(last, axis, up), lax.ppermute(first, axis, down))  58.5 us
    ppermute x14, starting transfers between devices, from_both_sides(): return (lax.ppermute(last, axis, up), lax.ppermute(first, axis, down))  38.8 us
    pallas_call x4, Pallas kernels, shear_tile(): pl.pallas_call(kernel, grid_spec=pltpu.PrefetchScalarGridSpec(num_scalar_...  34.9 us
    ppermute x7, waiting for transfers between devices, swapped_shares(): lax.ppermute(slots[s], 'row', [(i, i ^ s) for i in range(devices)])  34.4 us
    all_to_all x1, waiting for transfers between devices, on_device(): lax.all_to_all(turned, 'col', split_axis=0, concat_axis=0, tiled=True)  23 us
    pallas_call x2, Pallas kernels, shear_columns(): pl.pallas_call(functools.partial(shear_columns_kernel, front, blocks, len...  17 us
    pallas_call x2, Pallas kernels, travel_first(): pl.pallas_call(functools.partial(travel_first_kernel, length, count, len(...  12.2 us
    pallas_call x1, Pallas kernels, shear_whole(): pl.pallas_call(functools.partial(shear_whole_kernel, halo, devices, tiles...  9.61 us
  transfers between devices with their start and end apart: 26, of which 19 were waited for; matrix products, arithmetic and copies ran while one was open for 6% of the time, Pallas kernels for 24%

profile of v7, /device:TPU:2, one launch (start us, length us, event | category | flops | bytes accessed | tf_op | source)
XLA Modules:
  0.0 311.9 jit_solution(8623773099976930063)
XLA Ops:
  4.8 4.6 %collective-permute-start = (bf16[2,256,896]{2,1,0:T(8,128)(2,1)S(1)}, bf16[2,256,896]{2,1,0:T(8,128)(2,1)S(1)}, u32[]{:S(2)}, u32[]{:S(2)}) collective-permute-start(bf16[2,256,896]{2,1,0:T(8,128)(2,1)S(1)} %get-tuple-element.67), channel_id=1, source_target_pairs={{0,1},{1,2},{2,3},{4,5},{5,6},{6,7},{8,9},{9,10},{10,11},{12,13},{... | collective-permute-start | bytes 2752520 | tf_op jit(solution)/shard_map/ppermute | solution.py:581
  12.2 5.5 %collective-permute-start.2 = (bf16[2,256,896]{2,1,0:T(8,128)(2,1)}, bf16[2,256,896]{2,1,0:T(8,128)(2,1)}, u32[]{:S(2)}, u32[]{:S(2)}) collective-permute-start(bf16[2,256,896]{2,1,0:T(8,128)(2,1)} %get-tuple-element.65), channel_id=1, source_target_pairs={{0,1},{1,2},{2,3},{4,5},{5,6},{6,7},{8,9},{9,10},{10,11},{12,13},{... | collective-permute-start | bytes 2752520 | tf_op jit(solution)/shard_map/ppermute | solution.py:581
  20.0 8.9 %collective-permute-done.1.refs_1_.refs_2_ = bf16[2,256,896]{2,1,0:T(8,128)(2,1)S(1)} collective-permute-done((bf16[2,256,896]{2,1,0:T(8,128)(2,1)}, bf16[2,256,896]{2,1,0:T(8,128)(2,1)S(1)}, u32[]{:S(2)}, u32[]{:S(2)}) %collective-permute-start.1) | collective-permute-done | bytes 917536 | tf_op jit(solution)/shard_map/ppermute | solution.py:581
  31.0 6.5 %shear_tile.4 = bf16[8,2,256,128]{3,2,1,0:T(8,128)(2,1)} custom-call(s32[16]{0:T(128)} %get-tuple-element.88.base, s32[1]{0:T(128)} %constant.68.clone.1.rank, bf16[2,256,896]{2,1,0:T(8,128)(2,1)} %copy-done.8, bf16[2,256,896]{2,1,0:T(8,128)(2,1)} %copy-done.7, bf16[2,512,1024]{2,1,0:T(8,128)(2,1)} %refs_4_.3, f32[2,1,256]{2,1,0:T(1,128)} %bitcast.63, ...), custom_call_target="tpu_custom_call" | custom-call | tf_op jit(solution)/shard_map/shear_tile/pallas_call | solution.py:206
  37.5 4.3 %all-to-all-start = ((bf16[8,2,256,128]{3,2,1,0:T(8,128)(2,1)}), bf16[8,2,256,128]{3,2,1,0:T(8,128)(2,1)S(1)}, u32[]{:S(2)}, u32[]{:S(2)}) async-start(bf16[8,2,256,128]{3,2,1,0:T(8,128)(2,1)} %shear_tile.4), calls=%async_computation | async-start | bytes 2097152 | tf_op jit(solution)/shard_map/all_to_all | solution.py:734
  41.7 5.7 %collective-permute-done.3.refs_1_.refs_3_ = bf16[2,256,896]{2,1,0:T(8,128)(2,1)} collective-permute-done((bf16[2,256,896]{2,1,0:T(8,128)(2,1)}, bf16[2,256,896]{2,1,0:T(8,128)(2,1)}, u32[]{:S(2)}, u32[]{:S(2)}) %collective-permute-start.3) | collective-permute-done | bytes 917536 | tf_op jit(solution)/shard_map/ppermute | solution.py:581
  48.4 6.5 %shear_tile.5 = bf16[8,2,256,128]{3,2,1,0:T(8,128)(2,1)} custom-call(s32[16]{0:T(128)} %get-tuple-element.87.base, s32[1]{0:T(128)} %constant.68.clone.1.rank, bf16[2,256,896]{2,1,0:T(8,128)(2,1)} %collective-permute-done.2.refs_0_.refs_1_, bf16[2,256,896]{2,1,0:T(8,128)(2,1)} %collective-permute-done.3.refs_1_.refs_3_, bf16[2,512,1024]{2,1,0:T(8,128)(2,1)} %refs_4_.3, ...), custom_call_target="tpu_custom_call" | custom-call | tf_op jit(solution)/shard_map/shear_tile/pallas_call | solution.py:206
  55.6 5.0 %all-to-all-start.1 = ((bf16[8,2,256,128]{3,2,1,0:T(8,128)(2,1)}), bf16[8,2,256,128]{3,2,1,0:T(8,128)(2,1)S(1)}, u32[]{:S(2)}, u32[]{:S(2)}) async-start(bf16[8,2,256,128]{3,2,1,0:T(8,128)(2,1)} %shear_tile.5), calls=%async_computation.1 | async-start | bytes 2097152 | tf_op jit(solution)/shard_map/all_to_all | solution.py:734
  61.2 10.1 %shear_tile.6 = bf16[8,2,512,128]{3,2,1,0:T(8,128)(2,1)} custom-call(s32[32]{0:T(128)} %get-tuple-element.85.base, s32[1]{0:T(128)} %constant.68.clone.1.rank, bf16[2,256,896]{2,1,0:T(8,128)(2,1)} %copy-done.8, bf16[2,256,896]{2,1,0:T(8,128)(2,1)} %collective-permute-done.2.refs_0_.refs_1_, bf16[2,256,896]{2,1,0:T(8,128)(2,1)} %copy-done.7, ...), custom_call_target="tpu_custom_call" | custom-call | tf_op jit(solution)/shard_map/shear_tile/pallas_call | solution.py:206
  75.5 5.0 %all-to-all-start.2 = ((bf16[8,2,512,128]{3,2,1,0:T(8,128)(2,1)}), bf16[8,2,512,128]{3,2,1,0:T(8,128)(2,1)S(1)}, u32[]{:S(2)}, u32[]{:S(2)}) async-start(bf16[8,2,512,128]{3,2,1,0:T(8,128)(2,1)} %shear_tile.6), calls=%async_computation.2 | async-start | bytes 4194304 | tf_op jit(solution)/shard_map/all_to_all | solution.py:738
  84.1 4.4 %collective-permute-start.4 = (bf16[2,32,512]{2,1,0:T(8,128)(2,1)S(1)}, bf16[2,32,512]{2,1,0:T(8,128)(2,1)S(1)}, u32[]{:S(2)}, u32[]{:S(2)}) collective-permute-start(bf16[2,32,512]{2,1,0:T(8,128)(2,1)S(1)} %get-tuple-element.29), channel_id=1, source_target_pairs={{0,1},{1,2},{2,3},{4,5},{5,6},{6,7},{8,9},{9,10},{10,11},{12,13},{... | collective-permute-start | bytes 196616 | tf_op jit(solution)/shard_map/ppermute | solution.py:581
  94.7 8.4 %shear_columns.2 = bf16[32,2,128,128]{3,2,1,0:T(8,128)(2,1)} custom-call(s32[1]{0:T(128)} %bitcast.4.base, s32[1]{0:T(128)} %constant.68.clone.1.rank, bf16[8,2,256,128]{3,2,1,0:T(8,128)(2,1)} %copy-done.5, bf16[8,2,256,128]{3,2,1,0:T(8,128)(2,1)} %copy-done.6, s32[1,128]{1,0:T(1,128)} %get-tuple-element.92.refs_2_, f32[1,128]{1,0:T(1,128)} %get-tuple-element.90.refs_3_, ...), custom_call_target="tpu_custom_call" | custom-call | tf_op jit(solution)/shard_map/shear_columns/pallas_call | solution.py:427
  107.0 6.2 %all-to-all-start.3 = ((bf16[32,2,128,128]{3,2,1,0:T(8,128)(2,1)}), bf16[32,2,128,128]{3,2,1,0:T(8,128)(2,1)S(1)}, u32[]{:S(2)}, u32[]{:S(2)}) async-start(bf16[32,2,128,128]{3,2,1,0:T(8,128)(2,1)} %shear_columns.2), calls=%async_computation.3 | async-start | bytes 4194304 | tf_op jit(solution)/shard_map/all_to_all | solution.py:746
  114.0 8.5 %shear_columns.3 = bf16[8,2,512,128]{3,2,1,0:T(8,128)(2,1)} custom-call(s32[1]{0:T(128)} %bitcast.3.base, s32[1]{0:T(128)} %bitcast.1.rank, bf16[8,2,512,128]{3,2,1,0:T(8,128)(2,1)} %copy-done.4, s32[1,128]{1,0:T(1,128)} %get-tuple-element.91.refs_1_, f32[1,128]{1,0:T(1,128)} %get-tuple-element.89.refs_2_, bf16[256,256]{1,0:T(8,128)(2,1)} %constant.86.clone.refs_4_.refs_3_, ...), custom_call_target="tpu_custom_call" | custom-call | tf_op jit(solution)/shard_map/shear_columns/pallas_call | solution.py:427
  129.4 10.5 %collective-permute-done.12.refs_7_ = bf16[1,2,512,128]{3,2,1,0:T(8,128)(2,1)S(1)} collective-permute-done((bf16[1,2,512,128]{3,2,1,0:T(8,128)(2,1)S(1)}, bf16[1,2,512,128]{3,2,1,0:T(8,128)(2,1)S(1)}, u32[]{:S(2)}, u32[]{:S(2)}) %collective-permute-start.12) | collective-permute-done | bytes 262176 | tf_op jit(solution)/shard_map/ppermute | solution.py:626
  140.7 8.9 %collective-permute-done.11.refs_6_ = bf16[1,2,512,128]{3,2,1,0:T(8,128)(2,1)S(1)} collective-permute-done((bf16[1,2,512,128]{3,2,1,0:T(8,128)(2,1)S(1)}, bf16[1,2,512,128]{3,2,1,0:T(8,128)(2,1)S(1)}, u32[]{:S(2)}, u32[]{:S(2)}) %collective-permute-start.11) | collective-permute-done | bytes 262176 | tf_op jit(solution)/shard_map/ppermute | solution.py:626
  149.6 5.8 %collective-permute-done.10.refs_5_ = bf16[1,2,512,128]{3,2,1,0:T(8,128)(2,1)S(1)} collective-permute-done((bf16[1,2,512,128]{3,2,1,0:T(8,128)(2,1)S(1)}, bf16[1,2,512,128]{3,2,1,0:T(8,128)(2,1)S(1)}, u32[]{:S(2)}, u32[]{:S(2)}) %collective-permute-start.10) | collective-permute-done | bytes 262176 | tf_op jit(solution)/shard_map/ppermute | solution.py:626
  155.3 7.7 %collective-permute-done.9.refs_4_ = bf16[1,2,512,128]{3,2,1,0:T(8,128)(2,1)S(1)} collective-permute-done((bf16[1,2,512,128]{3,2,1,0:T(8,128)(2,1)S(1)}, bf16[1,2,512,128]{3,2,1,0:T(8,128)(2,1)S(1)}, u32[]{:S(2)}, u32[]{:S(2)}) %collective-permute-start.9) | collective-permute-done | bytes 262176 | tf_op jit(solution)/shard_map/ppermute | solution.py:626
  165.3 4.5 %ordered.1 = (bf16[8,2,512,128]{3,2,1,0:T(8,128)(2,1)}, bf16[7,2,512,128]{3,2,1,0:T(8,128)(2,1)}, bf16[7,2,512,128]{3,2,1,0:T(8,128)(2,1)}) custom-call(s32[1]{0:T(128)} %bitcast.1.rank, bf16[1,2,512,128]{3,2,1,0:T(8,128)(2,1)} %get-tuple-element.61.refs_0_, bf16[1,2,512,128]{3,2,1,0:T(8,128)(2,1)} %copy-done.17, bf16[1,2,512,128]{3,2,1,0:T(8,128)(2,1)} %copy-done.16, ...), custom_call_target="tpu_custom_call" | custom-call | tf_op jit(solution)/shard_map/ordered/pallas_call | solution.py:609
  169.8 4.3 %collective-permute-start.13 = (bf16[7,2,512,128]{3,2,1,0:T(8,128)(2,1)}, bf16[7,2,512,128]{3,2,1,0:T(8,128)(2,1)}, u32[]{:S(2)}, u32[]{:S(2)}) collective-permute-start(bf16[7,2,512,128]{3,2,1,0:T(8,128)(2,1)} %get-tuple-element.39), channel_id=1, source_target_pairs={{0,1},{1,2},{2,3},{4,5},{5,6},{6,7},{8,9},{9,10},{10,11},{12,13},{... | collective-permute-start | bytes 5505032 | tf_op jit(solution)/shard_map/ppermute | solution.py:581
  178.3 9.6 %shear_whole.1 = bf16[4,2,1088,128]{3,2,1,0:T(8,128)(2,1)} custom-call(s32[8]{0:T(128)} %fusion.12.base, bf16[8,4,2,128,128]{4,3,2,1,0:T(8,128)(2,1)} %bitcast.60, f32[1,128]{1,0:T(1,128)} %fusion.14.offsets, f32[1,128]{1,0:T(1,128)} %fusion.15.fractions, bf16[256,256]{1,0:T(8,128)(2,1)} %constant.84.clone.refs_5_.refs_7_.refs_6_.forward, ...), custom_call_target="tpu_custom_call" | custom-call | tf_op jit(solution)/shard_map/shear_whole/pallas_call | solution.py:316
  188.0 24.5 %collective-permute-done.13.refs_0_ = bf16[7,2,512,128]{3,2,1,0:T(8,128)(2,1)} collective-permute-done((bf16[7,2,512,128]{3,2,1,0:T(8,128)(2,1)}, bf16[7,2,512,128]{3,2,1,0:T(8,128)(2,1)}, u32[]{:S(2)}, u32[]{:S(2)}) %collective-permute-start.13) | collective-permute-done | bytes 1835040 | tf_op jit(solution)/shard_map/ppermute | solution.py:581
  212.5 5.6 %collective-permute-done.14.refs_1_ = bf16[7,2,512,128]{3,2,1,0:T(8,128)(2,1)} collective-permute-done((bf16[7,2,512,128]{3,2,1,0:T(8,128)(2,1)}, bf16[7,2,512,128]{3,2,1,0:T(8,128)(2,1)}, u32[]{:S(2)}, u32[]{:S(2)}) %collective-permute-start.14) | collective-permute-done | bytes 1835040 | tf_op jit(solution)/shard_map/ppermute | solution.py:581
  218.1 3.6 %all-to-all-start.4 = ((bf16[4,2,1088,128]{3,2,1,0:T(8,128)(2,1)}), bf16[4,2,1088,128]{3,2,1,0:T(8,128)(2,1)S(1)}, u32[]{:S(2)}, u32[]{:S(2)}) async-start(bf16[4,2,1088,128]{3,2,1,0:T(8,128)(2,1)} %shear_whole.1), calls=%async_computation.4 | async-start | bytes 4456448 | tf_op jit(solution)/shard_map/all_to_all | solution.py:780
  222.8 11.8 %shear_tile.7.refs_0_ = bf16[8,2,512,128]{3,2,1,0:T(8,128)(2,1)} custom-call(s32[32]{0:T(128)} %get-tuple-element.86.base, s32[1]{0:T(128)} %constant.68.clone.1.rank, bf16[7,2,512,128]{3,2,1,0:T(8,128)(2,1)} %collective-permute-done.13.refs_0_, bf16[7,2,512,128]{3,2,1,0:T(8,128)(2,1)} %collective-permute-done.14.refs_1_, bf16[2,512,1024]{2,1,0:T(8,128)(2,1)} %refs_2_.5, ...), custom_call_target="tpu_custom_call" | custom-call | tf_op jit(solution)/shard_map/shear_tile/pallas_call | solution.py:206
  245.3 3.8 %travel_first.2.body = bf16[8,2,512,128]{3,2,1,0:T(8,128)(2,1)} custom-call(bf16[8,2,512,128]{3,2,1,0:T(8,128)(2,1)} %shear_tile.7.refs_0_, bf16[8,2,32,128]{3,2,1,0:T(8,128)(2,1)} %copy-done.22, bf16[8,2,32,128]{3,2,1,0:T(8,128)(2,1)} %copy-done.21, bf16[256,384]{1,0:T(8,128)(2,1)} %copy.22.refs_3_), custom_call_target="tpu_custom_call" | custom-call | tf_op jit(solution)/shard_map/travel_first/pallas_call | solution.py:528
  249.1 23.0 %all-to-all-done.4.refs_0_ = bf16[4,2,1088,128]{3,2,1,0:T(8,128)(2,1)S(1)} async-done(((bf16[4,2,1088,128]{3,2,1,0:T(8,128)(2,1)}), bf16[4,2,1088,128]{3,2,1,0:T(8,128)(2,1)S(1)}, u32[]{:S(2)}, u32[]{:S(2)}) %all-to-all-start.4) | async-done | bytes 2228256 | tf_op jit(solution)/shard_map/all_to_all | solution.py:780
  273.5 8.4 %travel_first.3.body = bf16[4,2,1024,128]{3,2,1,0:T(8,128)(2,1)} custom-call(bf16[4,2,1088,128]{3,2,1,0:T(8,128)(2,1)} %copy-done.2, bf16[2,1024,512]{2,1,0:T(8,128)(2,1)} %refs_1_.1, bf16[2,32,512]{2,1,0:T(8,128)(2,1)} %copy-done.24, bf16[2,32,512]{2,1,0:T(8,128)(2,1)} %copy-done.25, bf16[256,384]{1,0:T(8,128)(2,1)} %copy.23.refs_4_), custom_call_target="tpu_custom_call" | custom-call | tf_op jit(solution)/shard_map/travel_first/pallas_call | solution.py:528
  290.2 4.6 %collective-permute-start.17 = (bf16[1,2,512,128]{3,2,1,0:T(8,128)(2,1)S(1)}, bf16[1,2,512,128]{3,2,1,0:T(8,128)(2,1)S(1)}, u32[]{:S(2)}, u32[]{:S(2)}) collective-permute-start(bf16[1,2,512,128]{3,2,1,0:T(8,128)(2,1)S(1)} %get-tuple-element.51), channel_id=1, source_target_pairs={{0,1},{1,2},{2,3},{4,5},{5,6},{6,7},{8,9},{9,10},{10,11},{12,13},{... | collective-permute-start | bytes 786440 | tf_op jit(solution)/shard_map/ppermute | solution.py:581
  295.7 4.0 %collective-permute-done.18.right = bf16[1,2,512,128]{3,2,1,0:T(8,128)(2,1)S(1)} collective-permute-done((bf16[1,2,512,128]{3,2,1,0:T(8,128)(2,1)S(1)}, bf16[1,2,512,128]{3,2,1,0:T(8,128)(2,1)S(1)}, u32[]{:S(2)}, u32[]{:S(2)}) %collective-permute-start.18) | collective-permute-done | bytes 262176 | tf_op jit(solution)/shard_map/ppermute | solution.py:581
  302.0 4.4 %travel_second.2 = bf16[2,512,1024]{2,1,0:T(8,128)(2,1)} custom-call(bf16[1,2,512,128]{3,2,1,0:T(8,128)(2,1)} %copy-done.19, bf16[8,2,512,128]{3,2,1,0:T(8,128)(2,1)} %travel_first.2.body, bf16[1,2,512,128]{3,2,1,0:T(8,128)(2,1)} %copy-done.18, bf16[768,256]{1,0:T(8,128)(2,1)} %get-tuple-element.69.matrix), custom_call_target="tpu_custom_call" | custom-call | tf_op jit(solution)/shard_map/travel_second/pallas_call | solution.py:561
  307.4 4.4 %travel_second.3 = bf16[2,1024,512]{2,1,0:T(8,128)(2,1)} custom-call(bf16[1,2,1024,128]{3,2,1,0:T(8,128)(2,1)} %copy-done.10, bf16[4,2,1024,128]{3,2,1,0:T(8,128)(2,1)} %travel_first.3.body, bf16[1,2,1024,128]{3,2,1,0:T(8,128)(2,1)} %copy-done.9, bf16[768,256]{1,0:T(8,128)(2,1)} %get-tuple-element.68.matrix), custom_call_target="tpu_custom_call" | custom-call | tf_op jit(solution)/shard_map/travel_second/pallas_call | solution.py:561
  (133 shorter events, 70.3 us)
Async XLA Ops:
  0.6 80.7 %copy-start = (f32[2,1024]{1,0:T(2,128)S(1)}, f32[2,1024]{1,0:T(2,128)}, u32[]{:S(2)}) copy-start(f32[2,1024]{1,0:T(2,128)} %param.22) | copy-start | bytes 24580
  3.4 25.5 %collective-permute-start.1 = (bf16[2,256,896]{2,1,0:T(8,128)(2,1)}, bf16[2,256,896]{2,1,0:T(8,128)(2,1)S(1)}, u32[]{:S(2)}, u32[]{:S(2)}) collective-permute-start(bf16[2,256,896]{2,1,0:T(8,128)(2,1)} %get-tuple-element.66), channel_id=1, source_target_pairs={{1,0},{2,1},{3,2},{5,4},{6,5},{7,6},{9,8},{10,9},{11,10},{13,12},{... | collective-permute-start | bytes 2752520 | tf_op jit(solution)/shard_map/ppermute | solution.py:581
  4.8 25.3 %collective-permute-start = (bf16[2,256,896]{2,1,0:T(8,128)(2,1)S(1)}, bf16[2,256,896]{2,1,0:T(8,128)(2,1)S(1)}, u32[]{:S(2)}, u32[]{:S(2)}) collective-permute-start(bf16[2,256,896]{2,1,0:T(8,128)(2,1)S(1)} %get-tuple-element.67), channel_id=1, source_target_pairs={{0,1},{1,2},{2,3},{4,5},{5,6},{6,7},{8,9},{9,10},{10,11},{12,13},{... | collective-permute-start | bytes 2752520 | tf_op jit(solution)/shard_map/ppermute | solution.py:581
  10.9 36.5 %collective-permute-start.3 = (bf16[2,256,896]{2,1,0:T(8,128)(2,1)}, bf16[2,256,896]{2,1,0:T(8,128)(2,1)}, u32[]{:S(2)}, u32[]{:S(2)}) collective-permute-start(bf16[2,256,896]{2,1,0:T(8,128)(2,1)} %get-tuple-element.64), channel_id=1, source_target_pairs={{1,0},{2,1},{3,2},{5,4},{6,5},{7,6},{9,8},{10,9},{11,10},{13,12},{... | collective-permute-start | bytes 2752520 | tf_op jit(solution)/shard_map/ppermute | solution.py:581
  12.2 36.2 %collective-permute-start.2 = (bf16[2,256,896]{2,1,0:T(8,128)(2,1)}, bf16[2,256,896]{2,1,0:T(8,128)(2,1)}, u32[]{:S(2)}, u32[]{:S(2)}) collective-permute-start(bf16[2,256,896]{2,1,0:T(8,128)(2,1)} %get-tuple-element.65), channel_id=1, source_target_pairs={{0,1},{1,2},{2,3},{4,5},{5,6},{6,7},{8,9},{9,10},{10,11},{12,13},{... | collective-permute-start | bytes 2752520 | tf_op jit(solution)/shard_map/ppermute | solution.py:581
  37.5 18.2 %all-to-all-start = ((bf16[8,2,256,128]{3,2,1,0:T(8,128)(2,1)}), bf16[8,2,256,128]{3,2,1,0:T(8,128)(2,1)S(1)}, u32[]{:S(2)}, u32[]{:S(2)}) async-start(bf16[8,2,256,128]{3,2,1,0:T(8,128)(2,1)} %shear_tile.4), calls=%async_computation | async-start | bytes 2097152 | tf_op jit(solution)/shard_map/all_to_all | solution.py:734
  55.6 15.6 %copy-start.5 = (bf16[8,2,256,128]{3,2,1,0:T(8,128)(2,1)}, bf16[8,2,256,128]{3,2,1,0:T(8,128)(2,1)S(1)}, u32[]{:S(2)}) copy-start(bf16[8,2,256,128]{3,2,1,0:T(8,128)(2,1)S(1)} %all-to-all-done.refs_0_) | copy-start | bytes 3145732
  55.6 18.9 %all-to-all-start.1 = ((bf16[8,2,256,128]{3,2,1,0:T(8,128)(2,1)}), bf16[8,2,256,128]{3,2,1,0:T(8,128)(2,1)S(1)}, u32[]{:S(2)}, u32[]{:S(2)}) async-start(bf16[8,2,256,128]{3,2,1,0:T(8,128)(2,1)} %shear_tile.5), calls=%async_computation.1 | async-start | bytes 2097152 | tf_op jit(solution)/shard_map/all_to_all | solution.py:734
  75.5 30.2 %all-to-all-start.2 = ((bf16[8,2,512,128]{3,2,1,0:T(8,128)(2,1)}), bf16[8,2,512,128]{3,2,1,0:T(8,128)(2,1)S(1)}, u32[]{:S(2)}, u32[]{:S(2)}) async-start(bf16[8,2,512,128]{3,2,1,0:T(8,128)(2,1)} %shear_tile.6), calls=%async_computation.2 | async-start | bytes 4194304 | tf_op jit(solution)/shard_map/all_to_all | solution.py:738
  84.1 7.0 %collective-permute-start.4 = (bf16[2,32,512]{2,1,0:T(8,128)(2,1)S(1)}, bf16[2,32,512]{2,1,0:T(8,128)(2,1)S(1)}, u32[]{:S(2)}, u32[]{:S(2)}) collective-permute-start(bf16[2,32,512]{2,1,0:T(8,128)(2,1)S(1)} %get-tuple-element.29), channel_id=1, source_target_pairs={{0,1},{1,2},{2,3},{4,5},{5,6},{6,7},{8,9},{9,10},{10,11},{12,13},{... | collective-permute-start | bytes 196616 | tf_op jit(solution)/shard_map/ppermute | solution.py:581
  88.5 6.2 %collective-permute-start.5 = (bf16[2,32,512]{2,1,0:T(8,128)(2,1)S(1)}, bf16[2,32,512]{2,1,0:T(8,128)(2,1)S(1)}, u32[]{:S(2)}, u32[]{:S(2)}) collective-permute-start(bf16[2,32,512]{2,1,0:T(8,128)(2,1)S(1)} %get-tuple-element.30), channel_id=1, source_target_pairs={{1,0},{2,1},{3,2},{5,4},{6,5},{7,6},{9,8},{10,9},{11,10},{13,12},{... | collective-permute-start | bytes 196616 | tf_op jit(solution)/shard_map/ppermute | solution.py:581
  107.0 70.0 %all-to-all-start.3 = ((bf16[32,2,128,128]{3,2,1,0:T(8,128)(2,1)}), bf16[32,2,128,128]{3,2,1,0:T(8,128)(2,1)S(1)}, u32[]{:S(2)}, u32[]{:S(2)}) async-start(bf16[32,2,128,128]{3,2,1,0:T(8,128)(2,1)} %shear_columns.2), calls=%async_computation.3 | async-start | bytes 4194304 | tf_op jit(solution)/shard_map/all_to_all | solution.py:746
  124.9 15.0 %collective-permute-start.12 = (bf16[1,2,512,128]{3,2,1,0:T(8,128)(2,1)S(1)}, bf16[1,2,512,128]{3,2,1,0:T(8,128)(2,1)S(1)}, u32[]{:S(2)}, u32[]{:S(2)}) collective-permute-start(bf16[1,2,512,128]{3,2,1,0:T(8,128)(2,1)S(1)} %get-tuple-element.54), channel_id=1, source_target_pairs={{0,28},{4,24},{8,20},{12,16},{16,12},{20,8},{24,4},{28,0},{1,29},{... | collective-permute-start | bytes 786440 | tf_op jit(solution)/shard_map/ppermute | solution.py:626
  126.2 23.4 %collective-permute-start.11 = (bf16[1,2,512,128]{3,2,1,0:T(8,128)(2,1)S(1)}, bf16[1,2,512,128]{3,2,1,0:T(8,128)(2,1)S(1)}, u32[]{:S(2)}, u32[]{:S(2)}) collective-permute-start(bf16[1,2,512,128]{3,2,1,0:T(8,128)(2,1)S(1)} %get-tuple-element.55), channel_id=1, source_target_pairs={{0,24},{4,28},{8,16},{12,20},{16,8},{20,12},{24,0},{28,4},{1,25},{... | collective-permute-start | bytes 786440 | tf_op jit(solution)/shard_map/ppermute | solution.py:626
  127.6 27.7 %collective-permute-start.10 = (bf16[1,2,512,128]{3,2,1,0:T(8,128)(2,1)S(1)}, bf16[1,2,512,128]{3,2,1,0:T(8,128)(2,1)S(1)}, u32[]{:S(2)}, u32[]{:S(2)}) collective-permute-start(bf16[1,2,512,128]{3,2,1,0:T(8,128)(2,1)S(1)} %get-tuple-element.56), channel_id=1, source_target_pairs={{0,20},{4,16},{8,28},{12,24},{16,4},{20,0},{24,12},{28,8},{1,21},{... | collective-permute-start | bytes 786440 | tf_op jit(solution)/shard_map/ppermute | solution.py:626
  128.8 34.3 %collective-permute-start.9 = (bf16[1,2,512,128]{3,2,1,0:T(8,128)(2,1)S(1)}, bf16[1,2,512,128]{3,2,1,0:T(8,128)(2,1)S(1)}, u32[]{:S(2)}, u32[]{:S(2)}) collective-permute-start(bf16[1,2,512,128]{3,2,1,0:T(8,128)(2,1)S(1)} %get-tuple-element.57), channel_id=1, source_target_pairs={{0,16},{4,20},{8,24},{12,28},{16,0},{20,4},{24,8},{28,12},{1,17},{... | collective-permute-start | bytes 786440 | tf_op jit(solution)/shard_map/ppermute | solution.py:626
  129.3 33.8 %collective-permute-start.8 = (bf16[1,2,512,128]{3,2,1,0:T(8,128)(2,1)S(1)}, bf16[1,2,512,128]{3,2,1,0:T(8,128)(2,1)S(1)}, u32[]{:S(2)}, u32[]{:S(2)}) collective-permute-start(bf16[1,2,512,128]{3,2,1,0:T(8,128)(2,1)S(1)} %get-tuple-element.58), channel_id=1, source_target_pairs={{0,12},{4,8},{8,4},{12,0},{16,28},{20,24},{24,20},{28,16},{1,13},{... | collective-permute-start | bytes 786440 | tf_op jit(solution)/shard_map/ppermute | solution.py:626
  140.0 24.6 %copy-start.11 = (bf16[1,2,512,128]{3,2,1,0:T(8,128)(2,1)}, bf16[1,2,512,128]{3,2,1,0:T(8,128)(2,1)S(1)}, u32[]{:S(2)}) copy-start(bf16[1,2,512,128]{3,2,1,0:T(8,128)(2,1)S(1)} %collective-permute-done.12.refs_7_) | copy-start | bytes 786436
  140.0 24.6 %collective-permute-start.7 = (bf16[1,2,512,128]{3,2,1,0:T(8,128)(2,1)S(1)}, bf16[1,2,512,128]{3,2,1,0:T(8,128)(2,1)S(1)}, u32[]{:S(2)}, u32[]{:S(2)}) collective-permute-start(bf16[1,2,512,128]{3,2,1,0:T(8,128)(2,1)S(1)} %get-tuple-element.59), channel_id=1, source_target_pairs={{0,8},{4,12},{8,0},{12,4},{16,24},{20,28},{24,16},{28,20},{1,9},{5... | collective-permute-start | bytes 786440 | tf_op jit(solution)/shard_map/ppermute | solution.py:626
  149.6 15.0 %collective-permute-start.6 = (bf16[1,2,512,128]{3,2,1,0:T(8,128)(2,1)S(1)}, bf16[1,2,512,128]{3,2,1,0:T(8,128)(2,1)S(1)}, u32[]{:S(2)}, u32[]{:S(2)}) collective-permute-start(bf16[1,2,512,128]{3,2,1,0:T(8,128)(2,1)S(1)} %get-tuple-element.60), channel_id=1, source_target_pairs={{0,4},{4,0},{8,12},{12,8},{16,20},{20,16},{24,28},{28,24},{1,5},{5... | collective-permute-start | bytes 786440 | tf_op jit(solution)/shard_map/ppermute | solution.py:626
  169.8 42.7 %collective-permute-start.13 = (bf16[7,2,512,128]{3,2,1,0:T(8,128)(2,1)}, bf16[7,2,512,128]{3,2,1,0:T(8,128)(2,1)}, u32[]{:S(2)}, u32[]{:S(2)}) collective-permute-start(bf16[7,2,512,128]{3,2,1,0:T(8,128)(2,1)} %get-tuple-element.39), channel_id=1, source_target_pairs={{0,1},{1,2},{2,3},{4,5},{5,6},{6,7},{8,9},{9,10},{10,11},{12,13},{... | collective-permute-start | bytes 5505032 | tf_op jit(solution)/shard_map/ppermute | solution.py:581
  174.1 44.0 %collective-permute-start.14 = (bf16[7,2,512,128]{3,2,1,0:T(8,128)(2,1)}, bf16[7,2,512,128]{3,2,1,0:T(8,128)(2,1)}, u32[]{:S(2)}, u32[]{:S(2)}) collective-permute-start(bf16[7,2,512,128]{3,2,1,0:T(8,128)(2,1)} %get-tuple-element.40), channel_id=1, source_target_pairs={{1,0},{2,1},{3,2},{5,4},{6,5},{7,6},{9,8},{10,9},{11,10},{13,12},{... | collective-permute-start | bytes 5505032 | tf_op jit(solution)/shard_map/ppermute | solution.py:581
  188.0 33.8 %copy-start.28 = (f32[2]{0:T(128)S(1)}, f32[2]{0:T(128)}, u32[]{:S(2)}) copy-start(f32[2]{0:T(128)} %param.23) | copy-start | bytes 28
  188.0 34.0 %copy-start.20 = (f32[192,256,1,1]{1,0,2,3:T(8,128)S(1)}, f32[192,256,1,1]{1,0,2,3:T(8,128)}, u32[]{:S(2)}) copy-start(f32[192,256,1,1]{1,0,2,3:T(8,128)} %constant.93) | copy-start | bytes 589828
  188.0 34.0 %copy-start.23 = (f32[256,128]{1,0:T(8,128)S(1)}, f32[256,128]{1,0:T(8,128)}, u32[]{:S(2)}) copy-start(f32[256,128]{1,0:T(8,128)} %constant.89.clone) | copy-start | bytes 393220
  218.1 54.0 %all-to-all-start.4 = ((bf16[4,2,1088,128]{3,2,1,0:T(8,128)(2,1)}), bf16[4,2,1088,128]{3,2,1,0:T(8,128)(2,1)S(1)}, u32[]{:S(2)}, u32[]{:S(2)}) async-start(bf16[4,2,1088,128]{3,2,1,0:T(8,128)(2,1)} %shear_whole.1), calls=%async_computation.4 | async-start | bytes 4456448 | tf_op jit(solution)/shard_map/all_to_all | solution.py:780
  236.2 6.0 %collective-permute-start.16 = (bf16[8,2,32,128]{3,2,1,0:T(8,128)(2,1)}, bf16[8,2,32,128]{3,2,1,0:T(8,128)(2,1)S(1)}, u32[]{:S(2)}, u32[]{:S(2)}) collective-permute-start(bf16[8,2,32,128]{3,2,1,0:T(8,128)(2,1)} %get-tuple-element.52), channel_id=1, source_target_pairs={{4,0},{8,4},{12,8},{16,12},{20,16},{24,20},{28,24},{5,1},{9,5},{13... | collective-permute-start | bytes 393224 | tf_op jit(solution)/shard_map/ppermute | solution.py:581
  238.2 6.5 %collective-permute-start.15 = (bf16[8,2,32,128]{3,2,1,0:T(8,128)(2,1)}, bf16[8,2,32,128]{3,2,1,0:T(8,128)(2,1)S(1)}, u32[]{:S(2)}, u32[]{:S(2)}) collective-permute-start(bf16[8,2,32,128]{3,2,1,0:T(8,128)(2,1)} %get-tuple-element.53), channel_id=1, source_target_pairs={{0,4},{4,8},{8,12},{12,16},{16,20},{20,24},{24,28},{1,5},{5,9},{9,... | collective-permute-start | bytes 393224 | tf_op jit(solution)/shard_map/ppermute | solution.py:581
  283.2 23.2 %collective-permute-start.20 = (bf16[1,2,1024,128]{3,2,1,0:T(8,128)(2,1)S(1)}, bf16[1,2,1024,128]{3,2,1,0:T(8,128)(2,1)S(1)}, u32[]{:S(2)}, u32[]{:S(2)}) collective-permute-start(bf16[1,2,1024,128]{3,2,1,0:T(8,128)(2,1)S(1)} %get-tuple-element.48), channel_id=1, source_target_pairs={{4,0},{8,4},{12,8},{16,12},{20,16},{24,20},{28,24},{5,1},{9,5},{13... | collective-permute-start | bytes 1572872 | tf_op jit(solution)/shard_map/ppermute | solution.py:581
  285.4 21.1 %collective-permute-start.19 = (bf16[1,2,1024,128]{3,2,1,0:T(8,128)(2,1)S(1)}, bf16[1,2,1024,128]{3,2,1,0:T(8,128)(2,1)S(1)}, u32[]{:S(2)}, u32[]{:S(2)}) collective-permute-start(bf16[1,2,1024,128]{3,2,1,0:T(8,128)(2,1)S(1)} %get-tuple-element.49), channel_id=1, source_target_pairs={{0,4},{4,8},{8,12},{12,16},{16,20},{20,24},{24,28},{1,5},{5,9},{9,... | collective-permute-start | bytes 1572872 | tf_op jit(solution)/shard_map/ppermute | solution.py:581
  288.9 10.9 %collective-permute-start.18 = (bf16[1,2,512,128]{3,2,1,0:T(8,128)(2,1)S(1)}, bf16[1,2,512,128]{3,2,1,0:T(8,128)(2,1)S(1)}, u32[]{:S(2)}, u32[]{:S(2)}) collective-permute-start(bf16[1,2,512,128]{3,2,1,0:T(8,128)(2,1)S(1)} %get-tuple-element.50), channel_id=1, source_target_pairs={{1,0},{2,1},{3,2},{5,4},{6,5},{7,6},{9,8},{10,9},{11,10},{13,12},{... | collective-permute-start | bytes 786440 | tf_op jit(solution)/shard_map/ppermute | solution.py:581
  290.2 11.2 %collective-permute-start.17 = (bf16[1,2,512,128]{3,2,1,0:T(8,128)(2,1)S(1)}, bf16[1,2,512,128]{3,2,1,0:T(8,128)(2,1)S(1)}, u32[]{:S(2)}, u32[]{:S(2)}) collective-permute-start(bf16[1,2,512,128]{3,2,1,0:T(8,128)(2,1)S(1)} %get-tuple-element.51), channel_id=1, source_target_pairs={{0,1},{1,2},{2,3},{4,5},{5,6},{6,7},{8,9},{9,10},{10,11},{12,13},{... | collective-permute-start | bytes 786440 | tf_op jit(solution)/shard_map/ppermute | solution.py:581
  (23 other events, 101.8 us)

commit v8 on v7

--- a/solution.py
+++ b/solution.py
@@ -350,9 +350,9 @@
         for own, slots in zip(owns, place):
             count = own.shape[2]
             for i, (slot, within) in enumerate(slots):
-                first = front + slot * length + within
+                first = pl.multiple_of(front + (slot ^ rank[0]) * length + within, GROUP)
                 for part in range(2):
-                    strip[part, first : first + count, :] = own[i, part]
+                    strip[part, pl.ds(first, count), :] = own[i, part]
         bins = lax.broadcasted_iota(jnp.int32, (BLOCK, BLOCK), 0).astype(jnp.float32)
         sine[...], cosine[...] = sine_cosine(bins * fractions[...] * (-2.0 * np.pi / WINDOW))
 
@@ -733,16 +733,13 @@
         sheared = first(1, part * part_lines, [left], [right], in_order)
         spread.append(lax.all_to_all(sheared, "row", split_axis=0, concat_axis=0, tiled=True))
     lefts, rights = after((lefts, rights), sheared)
-    sheared_a = first(0, 0, lefts, rights, in_order)
-    sheared_a = after(sheared_a, spread)
-    spread_a = lax.all_to_all(sheared_a, "row", split_axis=0, concat_axis=0, tiled=True)
-    margin = after((wave_b[:, :MARGIN], wave_b[:, -MARGIN:]), sheared)
-    wave_b_halos = from_both_sides(*margin, "col")
-    spread, wave_b_halos = lax.optimization_barrier((spread, wave_b_halos))
+    slots = first(0, 0, lefts, rights, by_rank)
+    shares = [slots[s : s + 1] for s in range(row_devices)]
+    spread, shares = lax.optimization_barrier((spread, shares))
+    pieces = swapped_shares(shares)
 
     place = [[(b, part * part_lines) for b in range(row_devices)] for part in range(PARTS)]
     moved_b = second(1, spread, place, in_order, BLOCK)
-    moved_b, spread_a = lax.optimization_barrier((moved_b, spread_a))
     whole = lax.all_to_all(moved_b, ("row", "col"), split_axis=0, concat_axis=0, tiled=True)
     whole = whole.reshape(row_devices, column_devices, 2, BLOCK, BLOCK)
     own_lines = lambda x: lax.dynamic_slice_in_dim(x, column_index * BLOCK, BLOCK, 0)
@@ -756,12 +753,20 @@
         turned_tables,
     )
 
-    moved_a = second(
-        0, [spread_a], [[(b, 0) for b in range(row_devices)]], by_rank, line_count
-    )
+    pieces = after(pieces, moved_b)
+    moved_a = second(0, pieces, [[(s, 0)] for s in range(row_devices)], by_rank, line_count)
     pieces = swapped_shares([moved_a[s : s + 1] for s in range(row_devices)])
     tile, low, high = ordered(pieces, halo, by_rank)
     left, right = from_both_sides(low, high, "col")
+
+    margin = after((wave_b[:, :MARGIN], wave_b[:, -MARGIN:]), turned)
+    wave_b_halos = from_both_sides(*margin, "col")
+    turned = lax.all_to_all(turned, "col", split_axis=0, concat_axis=0, tiled=True)
+    half_b = travel_first(turned, (), (wave_b, *wave_b_halos), along_rows[1])
+    low, high = from_both_sides(half_b[:1], half_b[-1:], "row")
+    exit_b = travel_second(low, half_b, high, along_columns[1])
+
+    left, right = after((left, right), exit_b)
     field_a = shear_tile(
         tile,
         [left],
@@ -775,18 +780,10 @@
         row_tables,
         wave_a,
     )
-
-    turned = after(turned, (left, right))
-    turned = lax.all_to_all(turned, "col", split_axis=0, concat_axis=0, tiled=True)
-
     halos = from_both_sides(field_a[:, :, :MARGIN], field_a[:, :, -MARGIN:], "row")
     half_a = travel_first(field_a, halos, (), along_rows[0])
-    left, right = from_both_sides(half_a[:1], half_a[-1:], "col")
-    exit_a = travel_second(left, half_a, right, along_columns[0])
-
-    half_b = travel_first(turned, (), (wave_b, *wave_b_halos), along_rows[1])
-    left, right = from_both_sides(half_b[:1], half_b[-1:], "row")
-    exit_b = travel_second(left, half_b, right, along_columns[1])
+    low, high = from_both_sides(half_a[:1], half_a[-1:], "col")
+    exit_a = travel_second(low, half_a, high, along_columns[0])
     return exit_a, exit_b
 
 

time: 315 us -> 354 us (1.12)
  waiting for transfers between devices: 123 us -> 155 us
  starting transfers between devices: 68.1 us -> 72 us
    all_to_all x1, waiting for transfers between devices: 0.01 us -> 44.8 us  [on_device(): lax.all_to_all(moved_b, ('row', 'col'), split_axis=0, concat_axis=0, tile...]
    all_to_all x1, waiting for transfers between devices: 23 us -> 0.01 us  [on_device(): lax.all_to_all(turned, 'col', split_axis=0, concat_axis=0, tiled=True)]
    ppermute x7 -> x14, waiting for transfers between devices: 34.4 us -> 43.1 us  [swapped_shares(): lax.ppermute(slots[s], 'row', [(i, i ^ s) for i in range(devices)])]
    ppermute x14, waiting for transfers between devices: 58.5 us -> 65.8 us  [from_both_sides(): return (lax.ppermute(last, axis, up), lax.ppermute(first, axis, down))]
    ppermute x7 -> x14, starting transfers between devices: 5.21 us -> 10.4 us  [swapped_shares(): lax.ppermute(slots[s], 'row', [(i, i ^ s) for i in range(devices)])]
    all_to_all x1 -> x0, starting transfers between devices: 5.03 us -> none  [on_device(): lax.all_to_all(sheared_a, 'row', split_axis=0, concat_axis=0, tiled=True)]
    unnamed x58 -> x74, local copies, waits for them, and re-layouts: 9.04 us -> 9.22 us
  transfers between devices with their start and end apart: 26 -> 32, of which waited for: 19 -> 20; matrix products, arithmetic and copies ran while one was open for 6% -> 6% of each run, Pallas kernels for 24% -> 14%
where the time goes in v8:
time: 354 us; the launch traced here: 350 us
  waiting for transfers between devices  155 us (44%)
  Pallas kernels  86.9 us (25%)
  starting transfers between devices  72 us (20%)
  local copies, waits for them, and re-layouts  30.5 us (9%)
    ppermute x14, waiting for transfers between devices, from_both_sides(): return (lax.ppermute(last, axis, up), lax.ppermute(first, axis, down))  65.8 us
    all_to_all x1, waiting for transfers between devices, on_device(): lax.all_to_all(moved_b, ('row', 'col'), split_axis=0, concat_axis=0, tile...  44.8 us
    ppermute x14, waiting for transfers between devices, swapped_shares(): lax.ppermute(slots[s], 'row', [(i, i ^ s) for i in range(devices)])  43.1 us
    ppermute x14, starting transfers between devices, from_both_sides(): return (lax.ppermute(last, axis, up), lax.ppermute(first, axis, down))  40.9 us
    pallas_call x4, Pallas kernels, shear_tile(): pl.pallas_call(kernel, grid_spec=pltpu.PrefetchScalarGridSpec(num_scalar_...  34.9 us
    pallas_call x2, Pallas kernels, shear_columns(): pl.pallas_call(functools.partial(shear_columns_kernel, front, blocks, len...  16.8 us
    pallas_call x2, Pallas kernels, travel_first(): pl.pallas_call(functools.partial(travel_first_kernel, length, count, len(...  12.3 us
    ppermute x14, starting transfers between devices, swapped_shares(): lax.ppermute(slots[s], 'row', [(i, i ^ s) for i in range(devices)])  10.4 us
  transfers between devices with their start and end apart: 32, of which 20 were waited for; matrix products, arithmetic and copies ran while one was open for 6% of the time, Pallas kernels for 14%

profile of v8, /device:TPU:2, one launch (start us, length us, event | category | flops | bytes accessed | tf_op | source)
XLA Modules:
  0.0 350.2 jit_solution(12121698740105750481)
XLA Ops:
  5.1 4.6 %collective-permute-start = (bf16[2,256,896]{2,1,0:T(8,128)(2,1)}, bf16[2,256,896]{2,1,0:T(8,128)(2,1)S(1)}, u32[]{:S(2)}, u32[]{:S(2)}) collective-permute-start(bf16[2,256,896]{2,1,0:T(8,128)(2,1)} %get-tuple-element.99), channel_id=1, source_target_pairs={{0,1},{1,2},{2,3},{4,5},{5,6},{6,7},{8,9},{9,10},{10,11},{12,13},{... | collective-permute-start | bytes 2752520 | tf_op jit(solution)/shard_map/ppermute | solution.py:581
  12.5 5.5 %collective-permute-start.2 = (bf16[2,256,896]{2,1,0:T(8,128)(2,1)}, bf16[2,256,896]{2,1,0:T(8,128)(2,1)}, u32[]{:S(2)}, u32[]{:S(2)}) collective-permute-start(bf16[2,256,896]{2,1,0:T(8,128)(2,1)} %get-tuple-element.97), channel_id=1, source_target_pairs={{0,1},{1,2},{2,3},{4,5},{5,6},{6,7},{8,9},{9,10},{10,11},{12,13},{... | collective-permute-start | bytes 2752520 | tf_op jit(solution)/shard_map/ppermute | solution.py:581
  20.3 8.8 %collective-permute-done.1.refs_1_.refs_2_ = bf16[2,256,896]{2,1,0:T(8,128)(2,1)S(1)} collective-permute-done((bf16[2,256,896]{2,1,0:T(8,128)(2,1)}, bf16[2,256,896]{2,1,0:T(8,128)(2,1)S(1)}, u32[]{:S(2)}, u32[]{:S(2)}) %collective-permute-start.1) | collective-permute-done | bytes 917536 | tf_op jit(solution)/shard_map/ppermute | solution.py:581
  31.7 6.5 %shear_tile.4 = bf16[8,2,256,128]{3,2,1,0:T(8,128)(2,1)} custom-call(s32[16]{0:T(128)} %get-tuple-element.120.base, s32[1]{0:T(128)} %constant.68.clone.1.rank, bf16[2,256,896]{2,1,0:T(8,128)(2,1)} %copy-done.8, bf16[2,256,896]{2,1,0:T(8,128)(2,1)} %copy-done.7, bf16[2,512,1024]{2,1,0:T(8,128)(2,1)} %refs_4_.2, f32[2,1,256]{2,1,0:T(1,128)} %bitcast.63, ...), custom_call_target="tpu_custom_call" | custom-call | tf_op jit(solution)/shard_map/shear_tile/pallas_call | solution.py:206
  38.1 4.3 %all-to-all-start = ((bf16[8,2,256,128]{3,2,1,0:T(8,128)(2,1)}), bf16[8,2,256,128]{3,2,1,0:T(8,128)(2,1)S(1)}, u32[]{:S(2)}, u32[]{:S(2)}) async-start(bf16[8,2,256,128]{3,2,1,0:T(8,128)(2,1)} %shear_tile.4), calls=%async_computation | async-start | bytes 2097152 | tf_op jit(solution)/shard_map/all_to_all | solution.py:734
  49.0 6.5 %shear_tile.5 = bf16[8,2,256,128]{3,2,1,0:T(8,128)(2,1)} custom-call(s32[16]{0:T(128)} %get-tuple-element.119.base, s32[1]{0:T(128)} %constant.68.clone.1.rank, bf16[2,256,896]{2,1,0:T(8,128)(2,1)} %collective-permute-done.2.refs_0_.refs_1_, bf16[2,256,896]{2,1,0:T(8,128)(2,1)} %copy-done.9, bf16[2,512,1024]{2,1,0:T(8,128)(2,1)} %refs_4_.2, ...), custom_call_target="tpu_custom_call" | custom-call | tf_op jit(solution)/shard_map/shear_tile/pallas_call | solution.py:206
  56.3 5.0 %all-to-all-start.1 = ((bf16[8,2,256,128]{3,2,1,0:T(8,128)(2,1)}), bf16[8,2,256,128]{3,2,1,0:T(8,128)(2,1)S(1)}, u32[]{:S(2)}, u32[]{:S(2)}) async-start(bf16[8,2,256,128]{3,2,1,0:T(8,128)(2,1)} %shear_tile.5), calls=%async_computation.1 | async-start | bytes 2097152 | tf_op jit(solution)/shard_map/all_to_all | solution.py:734
  63.2 10.1 %shear_tile.6 = bf16[8,2,512,128]{3,2,1,0:T(8,128)(2,1)} custom-call(s32[32]{0:T(128)} %get-tuple-element.117.base, s32[1]{0:T(128)} %bitcast.1.rank, bf16[2,256,896]{2,1,0:T(8,128)(2,1)} %copy-done.8, bf16[2,256,896]{2,1,0:T(8,128)(2,1)} %collective-permute-done.2.refs_0_.refs_1_, bf16[2,256,896]{2,1,0:T(8,128)(2,1)} %copy-done.7, ...), custom_call_target="tpu_custom_call" | custom-call | tf_op jit(solution)/shard_map/shear_tile/pallas_call | solution.py:206
  76.8 8.4 %shear_columns.2 = bf16[32,2,128,128]{3,2,1,0:T(8,128)(2,1)} custom-call(s32[1]{0:T(128)} %bitcast.11.base, s32[1]{0:T(128)} %constant.68.clone.1.rank, bf16[8,2,256,128]{3,2,1,0:T(8,128)(2,1)} %copy-done.5, bf16[8,2,256,128]{3,2,1,0:T(8,128)(2,1)} %copy-done.6, s32[1,128]{1,0:T(1,128)} %get-tuple-element.124.refs_2_, f32[1,128]{1,0:T(1,128)} %get-tuple-element.122.refs_3_, ...), custom_call_target="tpu_custom_call" | custom-call | tf_op jit(solution)/shard_map/shear_columns/pallas_call | solution.py:427
  85.2 6.9 %all-to-all-start.2 = ((bf16[32,2,128,128]{3,2,1,0:T(8,128)(2,1)}), bf16[32,2,128,128]{3,2,1,0:T(8,128)(2,1)S(1)}, u32[]{:S(2)}, u32[]{:S(2)}) async-start(bf16[32,2,128,128]{3,2,1,0:T(8,128)(2,1)} %shear_columns.2), calls=%async_computation.2 | async-start | bytes 4194304 | tf_op jit(solution)/shard_map/all_to_all | solution.py:743
  93.8 44.8 %all-to-all-done.2 = bf16[32,2,128,128]{3,2,1,0:T(8,128)(2,1)S(1)} async-done(((bf16[32,2,128,128]{3,2,1,0:T(8,128)(2,1)}), bf16[32,2,128,128]{3,2,1,0:T(8,128)(2,1)S(1)}, u32[]{:S(2)}, u32[]{:S(2)}) %all-to-all-start.2) | async-done | bytes 2097184 | tf_op jit(solution)/shard_map/all_to_all | solution.py:743
  140.0 9.6 %shear_whole.1 = bf16[4,2,1088,128]{3,2,1,0:T(8,128)(2,1)} custom-call(s32[8]{0:T(128)} %fusion.12.base, bf16[8,4,2,128,128]{4,3,2,1,0:T(8,128)(2,1)} %bitcast.60, f32[1,128]{1,0:T(1,128)} %fusion.14.offsets, f32[1,128]{1,0:T(1,128)} %fusion.15.fractions, bf16[256,256]{1,0:T(8,128)(2,1)} %constant.84.clone.refs_5_.refs_7_.forward.refs_6_, ...), custom_call_target="tpu_custom_call" | custom-call | tf_op jit(solution)/shard_map/shear_whole/pallas_call | solution.py:316
  149.6 4.6 %all-to-all-start.3 = ((bf16[4,2,1088,128]{3,2,1,0:T(8,128)(2,1)}), bf16[4,2,1088,128]{3,2,1,0:T(8,128)(2,1)S(1)}, u32[]{:S(2)}, u32[]{:S(2)}) async-start(bf16[4,2,1088,128]{3,2,1,0:T(8,128)(2,1)} %shear_whole.1), calls=%async_computation.3 | async-start | bytes 4456448 | tf_op jit(solution)/shard_map/all_to_all | solution.py:764
  160.1 5.1 %collective-permute-done.5.refs_2_ = bf16[1,2,512,128]{3,2,1,0:T(8,128)(2,1)S(1)} collective-permute-done((bf16[1,2,512,128]{3,2,1,0:T(8,128)(2,1)}, bf16[1,2,512,128]{3,2,1,0:T(8,128)(2,1)S(1)}, u32[]{:S(2)}, u32[]{:S(2)}) %collective-permute-start.5) | collective-permute-done | bytes 262176 | tf_op jit(solution)/shard_map/ppermute | solution.py:626
  169.1 13.7 %collective-permute-done.8.refs_5_ = bf16[1,2,512,128]{3,2,1,0:T(8,128)(2,1)S(1)} collective-permute-done((bf16[1,2,512,128]{3,2,1,0:T(8,128)(2,1)S(1)}, bf16[1,2,512,128]{3,2,1,0:T(8,128)(2,1)S(1)}, u32[]{:S(2)}, u32[]{:S(2)}) %collective-permute-start.8) | collective-permute-done | bytes 262176 | tf_op jit(solution)/shard_map/ppermute | solution.py:626
  183.7 8.4 %shear_columns.3 = bf16[8,2,512,128]{3,2,1,0:T(8,128)(2,1)} custom-call(s32[1]{0:T(128)} %bitcast.3.base, s32[1]{0:T(128)} %bitcast.1.rank, bf16[1,2,512,128]{3,2,1,0:T(8,128)(2,1)} %get-tuple-element.55.refs_0_, bf16[1,2,512,128]{3,2,1,0:T(8,128)(2,1)} %copy-done.21, bf16[1,2,512,128]{3,2,1,0:T(8,128)(2,1)} %copy-done.22, ...), custom_call_target="tpu_custom_call" | custom-call | tf_op jit(solution)/shard_map/shear_columns/pallas_call | solution.py:427
  199.1 4.5 %collective-permute-done.17.refs_7_ = bf16[1,2,512,128]{3,2,1,0:T(8,128)(2,1)S(1)} collective-permute-done((bf16[1,2,512,128]{3,2,1,0:T(8,128)(2,1)S(1)}, bf16[1,2,512,128]{3,2,1,0:T(8,128)(2,1)S(1)}, u32[]{:S(2)}, u32[]{:S(2)}) %collective-permute-start.17) | collective-permute-done | bytes 262176 | tf_op jit(solution)/shard_map/ppermute | solution.py:626
  203.6 6.7 %collective-permute-done.16.refs_6_ = bf16[1,2,512,128]{3,2,1,0:T(8,128)(2,1)S(1)} collective-permute-done((bf16[1,2,512,128]{3,2,1,0:T(8,128)(2,1)S(1)}, bf16[1,2,512,128]{3,2,1,0:T(8,128)(2,1)S(1)}, u32[]{:S(2)}, u32[]{:S(2)}) %collective-permute-start.16) | collective-permute-done | bytes 262176 | tf_op jit(solution)/shard_map/ppermute | solution.py:626
  211.0 4.3 %collective-permute-done.15.refs_5_ = bf16[1,2,512,128]{3,2,1,0:T(8,128)(2,1)S(1)} collective-permute-done((bf16[1,2,512,128]{3,2,1,0:T(8,128)(2,1)S(1)}, bf16[1,2,512,128]{3,2,1,0:T(8,128)(2,1)S(1)}, u32[]{:S(2)}, u32[]{:S(2)}) %collective-permute-start.15) | collective-permute-done | bytes 262176 | tf_op jit(solution)/shard_map/ppermute | solution.py:626
  215.3 5.6 %collective-permute-done.14.refs_4_ = bf16[1,2,512,128]{3,2,1,0:T(8,128)(2,1)S(1)} collective-permute-done((bf16[1,2,512,128]{3,2,1,0:T(8,128)(2,1)S(1)}, bf16[1,2,512,128]{3,2,1,0:T(8,128)(2,1)S(1)}, u32[]{:S(2)}, u32[]{:S(2)}) %collective-permute-start.14) | collective-permute-done | bytes 262176 | tf_op jit(solution)/shard_map/ppermute | solution.py:626
  221.9 4.5 %ordered.1 = (bf16[8,2,512,128]{3,2,1,0:T(8,128)(2,1)}, bf16[7,2,512,128]{3,2,1,0:T(8,128)(2,1)}, bf16[7,2,512,128]{3,2,1,0:T(8,128)(2,1)}) custom-call(s32[1]{0:T(128)} %bitcast.1.rank, bf16[1,2,512,128]{3,2,1,0:T(8,128)(2,1)} %get-tuple-element.87.refs_0_, bf16[1,2,512,128]{3,2,1,0:T(8,128)(2,1)} %copy-done.18, bf16[1,2,512,128]{3,2,1,0:T(8,128)(2,1)} %copy-done.17, ...), custom_call_target="tpu_custom_call" | custom-call | tf_op jit(solution)/shard_map/ordered/pallas_call | solution.py:609
  226.3 4.8 %collective-permute-start.18 = (bf16[7,2,512,128]{3,2,1,0:T(8,128)(2,1)}, bf16[7,2,512,128]{3,2,1,0:T(8,128)(2,1)}, u32[]{:S(2)}, u32[]{:S(2)}) collective-permute-start(bf16[7,2,512,128]{3,2,1,0:T(8,128)(2,1)} %get-tuple-element.63), channel_id=1, source_target_pairs={{0,1},{1,2},{2,3},{4,5},{5,6},{6,7},{8,9},{9,10},{10,11},{12,13},{... | collective-permute-start | bytes 5505032 | tf_op jit(solution)/shard_map/ppermute | solution.py:581
  233.4 4.6 %collective-permute-start.20 = (bf16[2,32,512]{2,1,0:T(8,128)(2,1)S(1)}, bf16[2,32,512]{2,1,0:T(8,128)(2,1)S(1)}, u32[]{:S(2)}, u32[]{:S(2)}) collective-permute-start(bf16[2,32,512]{2,1,0:T(8,128)(2,1)S(1)} %get-tuple-element.65), channel_id=1, source_target_pairs={{0,1},{1,2},{2,3},{4,5},{5,6},{6,7},{8,9},{9,10},{10,11},{12,13},{... | collective-permute-start | bytes 196616 | tf_op jit(solution)/shard_map/ppermute | solution.py:581
  240.1 30.8 %collective-permute-done.20.refs_2_ = bf16[2,32,512]{2,1,0:T(8,128)(2,1)S(1)} collective-permute-done((bf16[2,32,512]{2,1,0:T(8,128)(2,1)S(1)}, bf16[2,32,512]{2,1,0:T(8,128)(2,1)S(1)}, u32[]{:S(2)}, u32[]{:S(2)}) %collective-permute-start.20) | collective-permute-done | bytes 65568 | tf_op jit(solution)/shard_map/ppermute | solution.py:581
  270.9 5.4 %collective-permute-done.21.refs_3_ = bf16[2,32,512]{2,1,0:T(8,128)(2,1)S(1)} collective-permute-done((bf16[2,32,512]{2,1,0:T(8,128)(2,1)S(1)}, bf16[2,32,512]{2,1,0:T(8,128)(2,1)S(1)}, u32[]{:S(2)}, u32[]{:S(2)}) %collective-permute-start.21) | collective-permute-done | bytes 65568 | tf_op jit(solution)/shard_map/ppermute | solution.py:581
  278.3 8.4 %travel_first.2.body = bf16[4,2,1024,128]{3,2,1,0:T(8,128)(2,1)} custom-call(bf16[4,2,1088,128]{3,2,1,0:T(8,128)(2,1)} %copy-done.3, bf16[2,1024,512]{2,1,0:T(8,128)(2,1)} %refs_1_.1, bf16[2,32,512]{2,1,0:T(8,128)(2,1)} %copy-done.32, bf16[2,32,512]{2,1,0:T(8,128)(2,1)} %copy-done.33, bf16[256,384]{1,0:T(8,128)(2,1)} %copy.22.refs_4_), custom_call_target="tpu_custom_call" | custom-call | tf_op jit(solution)/shard_map/travel_first/pallas_call | solution.py:528
  293.5 5.8 %collective-permute-done.23.right = bf16[1,2,1024,128]{3,2,1,0:T(8,128)(2,1)S(1)} collective-permute-done((bf16[1,2,1024,128]{3,2,1,0:T(8,128)(2,1)S(1)}, bf16[1,2,1024,128]{3,2,1,0:T(8,128)(2,1)S(1)}, u32[]{:S(2)}, u32[]{:S(2)}) %collective-permute-start.23) | collective-permute-done | bytes 524320 | tf_op jit(solution)/shard_map/ppermute | solution.py:581
  301.3 4.4 %travel_second.2 = bf16[2,1024,512]{2,1,0:T(8,128)(2,1)} custom-call(bf16[1,2,1024,128]{3,2,1,0:T(8,128)(2,1)} %copy-done.11, bf16[4,2,1024,128]{3,2,1,0:T(8,128)(2,1)} %travel_first.2.body, bf16[1,2,1024,128]{3,2,1,0:T(8,128)(2,1)} %copy-done.10, bf16[768,256]{1,0:T(8,128)(2,1)} %get-tuple-element.101.matrix), custom_call_target="tpu_custom_call" | custom-call | tf_op jit(solution)/shard_map/travel_second/pallas_call | solution.py:561
  305.7 11.8 %shear_tile.7.refs_0_ = bf16[8,2,512,128]{3,2,1,0:T(8,128)(2,1)} custom-call(s32[32]{0:T(128)} %get-tuple-element.118.base, s32[1]{0:T(128)} %constant.68.clone.1.rank, bf16[7,2,512,128]{3,2,1,0:T(8,128)(2,1)} %collective-permute-done.18.refs_0_, bf16[7,2,512,128]{3,2,1,0:T(8,128)(2,1)} %collective-permute-done.19.refs_1_, bf16[2,512,1024]{2,1,0:T(8,128)(2,1)} %refs_2_.5, ...), custom_call_target="tpu_custom_call" | custom-call | tf_op jit(solution)/shard_map/shear_tile/pallas_call | solution.py:206
  334.6 4.6 %collective-permute-start.26 = (bf16[1,2,512,128]{3,2,1,0:T(8,128)(2,1)S(1)}, bf16[1,2,512,128]{3,2,1,0:T(8,128)(2,1)S(1)}, u32[]{:S(2)}, u32[]{:S(2)}) collective-permute-start(bf16[1,2,512,128]{3,2,1,0:T(8,128)(2,1)S(1)} %get-tuple-element.73), channel_id=1, source_target_pairs={{0,1},{1,2},{2,3},{4,5},{5,6},{6,7},{8,9},{9,10},{10,11},{12,13},{... | collective-permute-start | bytes 786440 | tf_op jit(solution)/shard_map/ppermute | solution.py:581
  339.1 4.2 %collective-permute-done.27.right = bf16[1,2,512,128]{3,2,1,0:T(8,128)(2,1)S(1)} collective-permute-done((bf16[1,2,512,128]{3,2,1,0:T(8,128)(2,1)S(1)}, bf16[1,2,512,128]{3,2,1,0:T(8,128)(2,1)S(1)}, u32[]{:S(2)}, u32[]{:S(2)}) %collective-permute-start.27) | collective-permute-done | bytes 262176 | tf_op jit(solution)/shard_map/ppermute | solution.py:581
  345.8 4.4 %travel_second.3 = bf16[2,512,1024]{2,1,0:T(8,128)(2,1)} custom-call(bf16[1,2,512,128]{3,2,1,0:T(8,128)(2,1)} %copy-done.20, bf16[8,2,512,128]{3,2,1,0:T(8,128)(2,1)} %travel_first.3.body, bf16[1,2,512,128]{3,2,1,0:T(8,128)(2,1)} %copy-done.19, bf16[768,256]{1,0:T(8,128)(2,1)} %get-tuple-element.100.matrix), custom_call_target="tpu_custom_call" | custom-call | tf_op jit(solution)/shard_map/travel_second/pallas_call | solution.py:561
  (162 shorter events, 80.5 us)
Async XLA Ops:
  3.7 25.5 %collective-permute-start.1 = (bf16[2,256,896]{2,1,0:T(8,128)(2,1)}, bf16[2,256,896]{2,1,0:T(8,128)(2,1)S(1)}, u32[]{:S(2)}, u32[]{:S(2)}) collective-permute-start(bf16[2,256,896]{2,1,0:T(8,128)(2,1)} %get-tuple-element.98), channel_id=1, source_target_pairs={{1,0},{2,1},{3,2},{5,4},{6,5},{7,6},{9,8},{10,9},{11,10},{13,12},{... | collective-permute-start | bytes 2752520 | tf_op jit(solution)/shard_map/ppermute | solution.py:581
  5.1 25.6 %collective-permute-start = (bf16[2,256,896]{2,1,0:T(8,128)(2,1)}, bf16[2,256,896]{2,1,0:T(8,128)(2,1)S(1)}, u32[]{:S(2)}, u32[]{:S(2)}) collective-permute-start(bf16[2,256,896]{2,1,0:T(8,128)(2,1)} %get-tuple-element.99), channel_id=1, source_target_pairs={{0,1},{1,2},{2,3},{4,5},{5,6},{6,7},{8,9},{9,10},{10,11},{12,13},{... | collective-permute-start | bytes 2752520 | tf_op jit(solution)/shard_map/ppermute | solution.py:581
  11.2 36.4 %collective-permute-start.3 = (bf16[2,256,896]{2,1,0:T(8,128)(2,1)}, bf16[2,256,896]{2,1,0:T(8,128)(2,1)S(1)}, u32[]{:S(2)}, u32[]{:S(2)}) collective-permute-start(bf16[2,256,896]{2,1,0:T(8,128)(2,1)} %get-tuple-element.96), channel_id=1, source_target_pairs={{1,0},{2,1},{3,2},{5,4},{6,5},{7,6},{9,8},{10,9},{11,10},{13,12},{... | collective-permute-start | bytes 2752520 | tf_op jit(solution)/shard_map/ppermute | solution.py:581
  12.5 36.4 %collective-permute-start.2 = (bf16[2,256,896]{2,1,0:T(8,128)(2,1)}, bf16[2,256,896]{2,1,0:T(8,128)(2,1)}, u32[]{:S(2)}, u32[]{:S(2)}) collective-permute-start(bf16[2,256,896]{2,1,0:T(8,128)(2,1)} %get-tuple-element.97), channel_id=1, source_target_pairs={{0,1},{1,2},{2,3},{4,5},{5,6},{6,7},{8,9},{9,10},{10,11},{12,13},{... | collective-permute-start | bytes 2752520 | tf_op jit(solution)/shard_map/ppermute | solution.py:581
  38.1 18.2 %all-to-all-start = ((bf16[8,2,256,128]{3,2,1,0:T(8,128)(2,1)}), bf16[8,2,256,128]{3,2,1,0:T(8,128)(2,1)S(1)}, u32[]{:S(2)}, u32[]{:S(2)}) async-start(bf16[8,2,256,128]{3,2,1,0:T(8,128)(2,1)} %shear_tile.4), calls=%async_computation | async-start | bytes 2097152 | tf_op jit(solution)/shard_map/all_to_all | solution.py:734
  56.3 19.5 %all-to-all-start.1 = ((bf16[8,2,256,128]{3,2,1,0:T(8,128)(2,1)}), bf16[8,2,256,128]{3,2,1,0:T(8,128)(2,1)S(1)}, u32[]{:S(2)}, u32[]{:S(2)}) async-start(bf16[8,2,256,128]{3,2,1,0:T(8,128)(2,1)} %shear_tile.5), calls=%async_computation.1 | async-start | bytes 2097152 | tf_op jit(solution)/shard_map/all_to_all | solution.py:734
  85.2 53.5 %all-to-all-start.2 = ((bf16[32,2,128,128]{3,2,1,0:T(8,128)(2,1)}), bf16[32,2,128,128]{3,2,1,0:T(8,128)(2,1)S(1)}, u32[]{:S(2)}, u32[]{:S(2)}) async-start(bf16[32,2,128,128]{3,2,1,0:T(8,128)(2,1)} %shear_columns.2), calls=%async_computation.2 | async-start | bytes 4194304 | tf_op jit(solution)/shard_map/all_to_all | solution.py:743
  149.6 126.8 %all-to-all-start.3 = ((bf16[4,2,1088,128]{3,2,1,0:T(8,128)(2,1)}), bf16[4,2,1088,128]{3,2,1,0:T(8,128)(2,1)S(1)}, u32[]{:S(2)}, u32[]{:S(2)}) async-start(bf16[4,2,1088,128]{3,2,1,0:T(8,128)(2,1)} %shear_whole.1), calls=%async_computation.3 | async-start | bytes 4456448 | tf_op jit(solution)/shard_map/all_to_all | solution.py:764
  154.1 5.2 %collective-permute-start.4 = (bf16[1,2,512,128]{3,2,1,0:T(8,128)(2,1)}, bf16[1,2,512,128]{3,2,1,0:T(8,128)(2,1)S(1)}, u32[]{:S(2)}, u32[]{:S(2)}) collective-permute-start(bf16[1,2,512,128]{3,2,1,0:T(8,128)(2,1)} %get-tuple-element.46), channel_id=1, source_target_pairs={{0,4},{4,0},{8,12},{12,8},{16,20},{20,16},{24,28},{28,24},{1,5},{5... | collective-permute-start | bytes 786440 | tf_op jit(solution)/shard_map/ppermute | solution.py:626
  155.8 9.4 %collective-permute-start.5 = (bf16[1,2,512,128]{3,2,1,0:T(8,128)(2,1)}, bf16[1,2,512,128]{3,2,1,0:T(8,128)(2,1)S(1)}, u32[]{:S(2)}, u32[]{:S(2)}) collective-permute-start(bf16[1,2,512,128]{3,2,1,0:T(8,128)(2,1)} %get-tuple-element.47), channel_id=1, source_target_pairs={{0,8},{4,12},{8,0},{12,4},{16,24},{20,28},{24,16},{28,20},{1,9},{5... | collective-permute-start | bytes 786440 | tf_op jit(solution)/shard_map/ppermute | solution.py:626
  155.8 13.2 %collective-permute-start.6 = (bf16[1,2,512,128]{3,2,1,0:T(8,128)(2,1)S(1)}, bf16[1,2,512,128]{3,2,1,0:T(8,128)(2,1)S(1)}, u32[]{:S(2)}, u32[]{:S(2)}) collective-permute-start(bf16[1,2,512,128]{3,2,1,0:T(8,128)(2,1)S(1)} %get-tuple-element.48), channel_id=1, source_target_pairs={{0,12},{4,8},{8,4},{12,0},{16,28},{20,24},{24,20},{28,16},{1,13},{... | collective-permute-start | bytes 786440 | tf_op jit(solution)/shard_map/ppermute | solution.py:626
  157.2 11.8 %collective-permute-start.7 = (bf16[1,2,512,128]{3,2,1,0:T(8,128)(2,1)S(1)}, bf16[1,2,512,128]{3,2,1,0:T(8,128)(2,1)S(1)}, u32[]{:S(2)}, u32[]{:S(2)}) collective-permute-start(bf16[1,2,512,128]{3,2,1,0:T(8,128)(2,1)S(1)} %get-tuple-element.49), channel_id=1, source_target_pairs={{0,16},{4,20},{8,24},{12,28},{16,0},{20,4},{24,8},{28,12},{1,17},{... | collective-permute-start | bytes 786440 | tf_op jit(solution)/shard_map/ppermute | solution.py:626
  157.8 25.0 %collective-permute-start.8 = (bf16[1,2,512,128]{3,2,1,0:T(8,128)(2,1)S(1)}, bf16[1,2,512,128]{3,2,1,0:T(8,128)(2,1)S(1)}, u32[]{:S(2)}, u32[]{:S(2)}) collective-permute-start(bf16[1,2,512,128]{3,2,1,0:T(8,128)(2,1)S(1)} %get-tuple-element.50), channel_id=1, source_target_pairs={{0,20},{4,16},{8,28},{12,24},{16,4},{20,0},{24,12},{28,8},{1,21},{... | collective-permute-start | bytes 786440 | tf_op jit(solution)/shard_map/ppermute | solution.py:626
  159.3 23.4 %collective-permute-start.9 = (bf16[1,2,512,128]{3,2,1,0:T(8,128)(2,1)S(1)}, bf16[1,2,512,128]{3,2,1,0:T(8,128)(2,1)S(1)}, u32[]{:S(2)}, u32[]{:S(2)}) collective-permute-start(bf16[1,2,512,128]{3,2,1,0:T(8,128)(2,1)S(1)} %get-tuple-element.51), channel_id=1, source_target_pairs={{0,24},{4,28},{8,16},{12,20},{16,8},{20,12},{24,0},{28,4},{1,25},{... | collective-permute-start | bytes 786440 | tf_op jit(solution)/shard_map/ppermute | solution.py:626
  165.2 17.6 %collective-permute-start.10 = (bf16[1,2,512,128]{3,2,1,0:T(8,128)(2,1)S(1)}, bf16[1,2,512,128]{3,2,1,0:T(8,128)(2,1)S(1)}, u32[]{:S(2)}, u32[]{:S(2)}) collective-permute-start(bf16[1,2,512,128]{3,2,1,0:T(8,128)(2,1)S(1)} %get-tuple-element.52), channel_id=1, source_target_pairs={{0,28},{4,24},{8,20},{12,16},{16,12},{20,8},{24,4},{28,0},{1,29},{... | collective-permute-start | bytes 786440 | tf_op jit(solution)/shard_map/ppermute | solution.py:626
  194.5 9.1 %collective-permute-start.17 = (bf16[1,2,512,128]{3,2,1,0:T(8,128)(2,1)S(1)}, bf16[1,2,512,128]{3,2,1,0:T(8,128)(2,1)S(1)}, u32[]{:S(2)}, u32[]{:S(2)}) collective-permute-start(bf16[1,2,512,128]{3,2,1,0:T(8,128)(2,1)S(1)} %get-tuple-element.80), channel_id=1, source_target_pairs={{0,28},{4,24},{8,20},{12,16},{16,12},{20,8},{24,4},{28,0},{1,29},{... | collective-permute-start | bytes 786440 | tf_op jit(solution)/shard_map/ppermute | solution.py:626
  195.1 15.2 %collective-permute-start.16 = (bf16[1,2,512,128]{3,2,1,0:T(8,128)(2,1)S(1)}, bf16[1,2,512,128]{3,2,1,0:T(8,128)(2,1)S(1)}, u32[]{:S(2)}, u32[]{:S(2)}) collective-permute-start(bf16[1,2,512,128]{3,2,1,0:T(8,128)(2,1)S(1)} %get-tuple-element.81), channel_id=1, source_target_pairs={{0,24},{4,28},{8,16},{12,20},{16,8},{20,12},{24,0},{28,4},{1,25},{... | collective-permute-start | bytes 786440 | tf_op jit(solution)/shard_map/ppermute | solution.py:626
  197.6 17.7 %collective-permute-start.15 = (bf16[1,2,512,128]{3,2,1,0:T(8,128)(2,1)S(1)}, bf16[1,2,512,128]{3,2,1,0:T(8,128)(2,1)S(1)}, u32[]{:S(2)}, u32[]{:S(2)}) collective-permute-start(bf16[1,2,512,128]{3,2,1,0:T(8,128)(2,1)S(1)} %get-tuple-element.82), channel_id=1, source_target_pairs={{0,20},{4,16},{8,28},{12,24},{16,4},{20,0},{24,12},{28,8},{1,21},{... | collective-permute-start | bytes 786440 | tf_op jit(solution)/shard_map/ppermute | solution.py:626
  197.7 23.2 %collective-permute-start.14 = (bf16[1,2,512,128]{3,2,1,0:T(8,128)(2,1)S(1)}, bf16[1,2,512,128]{3,2,1,0:T(8,128)(2,1)S(1)}, u32[]{:S(2)}, u32[]{:S(2)}) collective-permute-start(bf16[1,2,512,128]{3,2,1,0:T(8,128)(2,1)S(1)} %get-tuple-element.83), channel_id=1, source_target_pairs={{0,16},{4,20},{8,24},{12,28},{16,0},{20,4},{24,8},{28,12},{1,17},{... | collective-permute-start | bytes 786440 | tf_op jit(solution)/shard_map/ppermute | solution.py:626
  199.1 21.8 %collective-permute-start.13 = (bf16[1,2,512,128]{3,2,1,0:T(8,128)(2,1)S(1)}, bf16[1,2,512,128]{3,2,1,0:T(8,128)(2,1)S(1)}, u32[]{:S(2)}, u32[]{:S(2)}) collective-permute-start(bf16[1,2,512,128]{3,2,1,0:T(8,128)(2,1)S(1)} %get-tuple-element.84), channel_id=1, source_target_pairs={{0,12},{4,8},{8,4},{12,0},{16,28},{20,24},{24,20},{28,16},{1,13},{... | collective-permute-start | bytes 786440 | tf_op jit(solution)/shard_map/ppermute | solution.py:626
  203.6 17.3 %collective-permute-start.12 = (bf16[1,2,512,128]{3,2,1,0:T(8,128)(2,1)S(1)}, bf16[1,2,512,128]{3,2,1,0:T(8,128)(2,1)S(1)}, u32[]{:S(2)}, u32[]{:S(2)}) collective-permute-start(bf16[1,2,512,128]{3,2,1,0:T(8,128)(2,1)S(1)} %get-tuple-element.85), channel_id=1, source_target_pairs={{0,8},{4,12},{8,0},{12,4},{16,24},{20,28},{24,16},{28,20},{1,9},{5... | collective-permute-start | bytes 786440 | tf_op jit(solution)/shard_map/ppermute | solution.py:626
  210.3 10.7 %collective-permute-start.11 = (bf16[1,2,512,128]{3,2,1,0:T(8,128)(2,1)S(1)}, bf16[1,2,512,128]{3,2,1,0:T(8,128)(2,1)S(1)}, u32[]{:S(2)}, u32[]{:S(2)}) collective-permute-start(bf16[1,2,512,128]{3,2,1,0:T(8,128)(2,1)S(1)} %get-tuple-element.86), channel_id=1, source_target_pairs={{0,4},{4,0},{8,12},{12,8},{16,20},{20,16},{24,28},{28,24},{1,5},{5... | collective-permute-start | bytes 786440 | tf_op jit(solution)/shard_map/ppermute | solution.py:626
  226.3 79.4 %collective-permute-start.18 = (bf16[7,2,512,128]{3,2,1,0:T(8,128)(2,1)}, bf16[7,2,512,128]{3,2,1,0:T(8,128)(2,1)}, u32[]{:S(2)}, u32[]{:S(2)}) collective-permute-start(bf16[7,2,512,128]{3,2,1,0:T(8,128)(2,1)} %get-tuple-element.63), channel_id=1, source_target_pairs={{0,1},{1,2},{2,3},{4,5},{5,6},{6,7},{8,9},{9,10},{10,11},{12,13},{... | collective-permute-start | bytes 5505032 | tf_op jit(solution)/shard_map/ppermute | solution.py:581
  231.1 74.6 %collective-permute-start.19 = (bf16[7,2,512,128]{3,2,1,0:T(8,128)(2,1)}, bf16[7,2,512,128]{3,2,1,0:T(8,128)(2,1)}, u32[]{:S(2)}, u32[]{:S(2)}) collective-permute-start(bf16[7,2,512,128]{3,2,1,0:T(8,128)(2,1)} %get-tuple-element.64), channel_id=1, source_target_pairs={{1,0},{2,1},{3,2},{5,4},{6,5},{7,6},{9,8},{10,9},{11,10},{13,12},{... | collective-permute-start | bytes 5505032 | tf_op jit(solution)/shard_map/ppermute | solution.py:581
  233.4 37.5 %collective-permute-start.20 = (bf16[2,32,512]{2,1,0:T(8,128)(2,1)S(1)}, bf16[2,32,512]{2,1,0:T(8,128)(2,1)S(1)}, u32[]{:S(2)}, u32[]{:S(2)}) collective-permute-start(bf16[2,32,512]{2,1,0:T(8,128)(2,1)S(1)} %get-tuple-element.65), channel_id=1, source_target_pairs={{0,1},{1,2},{2,3},{4,5},{5,6},{6,7},{8,9},{9,10},{10,11},{12,13},{... | collective-permute-start | bytes 196616 | tf_op jit(solution)/shard_map/ppermute | solution.py:581
  238.0 38.4 %collective-permute-start.21 = (bf16[2,32,512]{2,1,0:T(8,128)(2,1)S(1)}, bf16[2,32,512]{2,1,0:T(8,128)(2,1)S(1)}, u32[]{:S(2)}, u32[]{:S(2)}) collective-permute-start(bf16[2,32,512]{2,1,0:T(8,128)(2,1)S(1)} %get-tuple-element.66), channel_id=1, source_target_pairs={{1,0},{2,1},{3,2},{5,4},{6,5},{7,6},{9,8},{10,9},{11,10},{13,12},{... | collective-permute-start | bytes 196616 | tf_op jit(solution)/shard_map/ppermute | solution.py:581
  288.0 11.2 %collective-permute-start.23 = (bf16[1,2,1024,128]{3,2,1,0:T(8,128)(2,1)S(1)}, bf16[1,2,1024,128]{3,2,1,0:T(8,128)(2,1)S(1)}, u32[]{:S(2)}, u32[]{:S(2)}) collective-permute-start(bf16[1,2,1024,128]{3,2,1,0:T(8,128)(2,1)S(1)} %get-tuple-element.76), channel_id=1, source_target_pairs={{4,0},{8,4},{12,8},{16,12},{20,16},{24,20},{28,24},{5,1},{9,5},{13... | collective-permute-start | bytes 1572872 | tf_op jit(solution)/shard_map/ppermute | solution.py:581
  290.0 10.5 %collective-permute-start.22 = (bf16[1,2,1024,128]{3,2,1,0:T(8,128)(2,1)S(1)}, bf16[1,2,1024,128]{3,2,1,0:T(8,128)(2,1)S(1)}, u32[]{:S(2)}, u32[]{:S(2)}) collective-permute-start(bf16[1,2,1024,128]{3,2,1,0:T(8,128)(2,1)S(1)} %get-tuple-element.77), channel_id=1, source_target_pairs={{0,4},{4,8},{8,12},{12,16},{16,20},{20,24},{24,28},{1,5},{5,9},{9,... | collective-permute-start | bytes 1572872 | tf_op jit(solution)/shard_map/ppermute | solution.py:581
  318.5 6.8 %collective-permute-start.25 = (bf16[8,2,32,128]{3,2,1,0:T(8,128)(2,1)S(1)}, bf16[8,2,32,128]{3,2,1,0:T(8,128)(2,1)S(1)}, u32[]{:S(2)}, u32[]{:S(2)}) collective-permute-start(bf16[8,2,32,128]{3,2,1,0:T(8,128)(2,1)S(1)} %get-tuple-element.74), channel_id=1, source_target_pairs={{4,0},{8,4},{12,8},{16,12},{20,16},{24,20},{28,24},{5,1},{9,5},{13... | collective-permute-start | bytes 393224 | tf_op jit(solution)/shard_map/ppermute | solution.py:581
  321.3 6.3 %collective-permute-start.24 = (bf16[8,2,32,128]{3,2,1,0:T(8,128)(2,1)S(1)}, bf16[8,2,32,128]{3,2,1,0:T(8,128)(2,1)S(1)}, u32[]{:S(2)}, u32[]{:S(2)}) collective-permute-start(bf16[8,2,32,128]{3,2,1,0:T(8,128)(2,1)S(1)} %get-tuple-element.75), channel_id=1, source_target_pairs={{0,4},{4,8},{8,12},{12,16},{16,20},{20,24},{24,28},{1,5},{5,9},{9,... | collective-permute-start | bytes 393224 | tf_op jit(solution)/shard_map/ppermute | solution.py:581
  333.3 10.1 %collective-permute-start.27 = (bf16[1,2,512,128]{3,2,1,0:T(8,128)(2,1)S(1)}, bf16[1,2,512,128]{3,2,1,0:T(8,128)(2,1)S(1)}, u32[]{:S(2)}, u32[]{:S(2)}) collective-permute-start(bf16[1,2,512,128]{3,2,1,0:T(8,128)(2,1)S(1)} %get-tuple-element.72), channel_id=1, source_target_pairs={{1,0},{2,1},{3,2},{5,4},{6,5},{7,6},{9,8},{10,9},{11,10},{13,12},{... | collective-permute-start | bytes 786440 | tf_op jit(solution)/shard_map/ppermute | solution.py:581
  334.6 10.6 %collective-permute-start.26 = (bf16[1,2,512,128]{3,2,1,0:T(8,128)(2,1)S(1)}, bf16[1,2,512,128]{3,2,1,0:T(8,128)(2,1)S(1)}, u32[]{:S(2)}, u32[]{:S(2)}) collective-permute-start(bf16[1,2,512,128]{3,2,1,0:T(8,128)(2,1)S(1)} %get-tuple-element.73), channel_id=1, source_target_pairs={{0,1},{1,2},{2,3},{4,5},{5,6},{6,7},{8,9},{9,10},{10,11},{12,13},{... | collective-permute-start | bytes 786440 | tf_op jit(solution)/shard_map/ppermute | solution.py:581
  (37 other events, 275.7 us)

commit v9 on v8

--- a/solution.py
+++ b/solution.py
@@ -167,11 +167,11 @@
             out[first : first + batch] = result
 
 
-def shear_tile(own, lefts, rights, first, halo, base, rank, spare, fractions, tables, *waves):
+def shear_tile(own, lefts, rights, first, lines, halo, base, rank, spare, fractions, tables, *waves):
     wide = own.ndim == 3
     parts = len(lefts)
-    part_lines = lefts[0].shape[-2]
-    line_count = parts * part_lines
+    line_count = lines
+    part_lines = line_count // parts
     tiles = own.shape[2] // BLOCK if wide else own.shape[0]
     rows = min(part_lines, ROWS)
     share = part_lines // rows
@@ -666,9 +666,17 @@
     for part in range(PARTS):
         lines = after(volume_plane, edges)[:, part * part_lines : (part + 1) * part_lines]
         edges = (lines[:, :, :reach], lines[:, :, width - reach :])
+        if part == PARTS - 1:
+            fill = ((0, 0), (0, 0), (0, reach - line_count))
+            margins = (wave_b[:, :MARGIN], wave_b[:, -MARGIN:])
+            edges = [
+                jnp.concatenate([edge, jnp.pad(margin, fill)], 1)
+                for edge, margin in zip(edges, margins)
+            ]
         left, right = from_both_sides(*edges, "col")
         lefts.append(left)
         rights.append(right)
+    wave_b_halos = [x[-1][:, part_lines:, :line_count] for x in (lefts, rights)]
 
     base_rows, spare_rows = group_starts(reach - MARGIN - shift_rows, GROUP, BLOCK)
 
@@ -684,6 +692,7 @@
             lefts,
             rights,
             begin,
+            len(lefts) * part_lines,
             halo,
             base_rows[view, 0],
             rank,
@@ -741,6 +750,9 @@
     place = [[(b, part * part_lines) for b in range(row_devices)] for part in range(PARTS)]
     moved_b = second(1, spread, place, in_order, BLOCK)
     whole = lax.all_to_all(moved_b, ("row", "col"), split_axis=0, concat_axis=0, tiled=True)
+    pieces = after(pieces, moved_b)
+    moved_a = second(0, pieces, [[(s, 0)] for s in range(row_devices)], by_rank, line_count)
+    moved_a, whole = lax.optimization_barrier((moved_a, whole))
     whole = whole.reshape(row_devices, column_devices, 2, BLOCK, BLOCK)
     own_lines = lambda x: lax.dynamic_slice_in_dim(x, column_index * BLOCK, BLOCK, 0)
     groups = BLOCK // GROUP
@@ -753,14 +765,10 @@
         turned_tables,
     )
 
-    pieces = after(pieces, moved_b)
-    moved_a = second(0, pieces, [[(s, 0)] for s in range(row_devices)], by_rank, line_count)
     pieces = swapped_shares([moved_a[s : s + 1] for s in range(row_devices)])
     tile, low, high = ordered(pieces, halo, by_rank)
     left, right = from_both_sides(low, high, "col")
 
-    margin = after((wave_b[:, :MARGIN], wave_b[:, -MARGIN:]), turned)
-    wave_b_halos = from_both_sides(*margin, "col")
     turned = lax.all_to_all(turned, "col", split_axis=0, concat_axis=0, tiled=True)
     half_b = travel_first(turned, (), (wave_b, *wave_b_halos), along_rows[1])
     low, high = from_both_sides(half_b[:1], half_b[-1:], "row")
@@ -772,6 +780,7 @@
         [left],
         [right],
         0,
+        line_count,
         halo,
         base_rows[0, 1],
         in_order,
@@ -1035,7 +1044,7 @@
         fits = (
             rows == BLOCK * lax.axis_size("col")
             and width == BLOCK * lax.axis_size("row")
-            and width >= SHIFT_X + MARGIN
+            and width >= -(-(SHIFT_X + MARGIN) // BLOCK) * BLOCK >= rows
         )
         chosen = on_device if fits else general_on_device
         return chosen(volume_plane, *rest)

time: 354 us -> 303 us (0.86)
  waiting for transfers between devices: 155 us -> 110 us
  starting transfers between devices: 72 us -> 64.4 us
    all_to_all x1, waiting for transfers between devices: 44.8 us -> 0.01 us  [on_device(): lax.all_to_all(moved_b, ('row', 'col'), split_axis=0, concat_axis=0, tile...]
    ppermute x14 -> x12, waiting for transfers between devices: 65.8 us -> 42.6 us  [from_both_sides(): return (lax.ppermute(last, axis, up), lax.ppermute(first, axis, down))]
    ppermute x14, waiting for transfers between devices: 43.1 us -> 60.2 us  [swapped_shares(): lax.ppermute(slots[s], 'row', [(i, i ^ s) for i in range(devices)])]
    ppermute x14 -> x12, starting transfers between devices: 40.9 us -> 32.2 us  [from_both_sides(): return (lax.ppermute(last, axis, up), lax.ppermute(first, axis, down))]
    all_to_all x1, waiting for transfers between devices: 0.01 us -> 7.22 us  [on_device(): lax.all_to_all(turned, 'col', split_axis=0, concat_axis=0, tiled=True)]
    unnamed x74 -> x62, local copies, waits for them, and re-layouts: 9.22 us -> 8.15 us
  transfers between devices with their start and end apart: 32 -> 30, of which waited for: 20 -> 18; matrix products, arithmetic and copies ran while one was open for 6% -> 8% of each run, Pallas kernels for 14% -> 16%
where the time goes in v9:
time: 303 us; the launch traced here: 301 us
  waiting for transfers between devices  110 us (36%)
  Pallas kernels  86.9 us (29%)
  starting transfers between devices  64.4 us (21%)
  local copies, waits for them, and re-layouts  31.3 us (10%)
  other arithmetic  5.26 us (2%)
    ppermute x14, waiting for transfers between devices, swapped_shares(): lax.ppermute(slots[s], 'row', [(i, i ^ s) for i in range(devices)])  60.2 us
    ppermute x12, waiting for transfers between devices, from_both_sides(): return (lax.ppermute(last, axis, up), lax.ppermute(first, axis, down))  42.6 us
    pallas_call x4, Pallas kernels, shear_tile(): pl.pallas_call(kernel, grid_spec=pltpu.PrefetchScalarGridSpec(num_scalar_...  34.8 us
    ppermute x12, starting transfers between devices, from_both_sides(): return (lax.ppermute(last, axis, up), lax.ppermute(first, axis, down))  32.2 us
    pallas_call x2, Pallas kernels, shear_columns(): pl.pallas_call(functools.partial(shear_columns_kernel, front, blocks, len...  16.8 us
    ppermute x14, starting transfers between devices, swapped_shares(): lax.ppermute(slots[s], 'row', [(i, i ^ s) for i in range(devices)])  13 us
    pallas_call x2, Pallas kernels, travel_first(): pl.pallas_call(functools.partial(travel_first_kernel, length, count, len(...  12.3 us
    pallas_call x1, Pallas kernels, shear_whole(): pl.pallas_call(functools.partial(shear_whole_kernel, halo, devices, tiles...  9.6 us
  transfers between devices with their start and end apart: 30, of which 18 were waited for; matrix products, arithmetic and copies ran while one was open for 8% of the time, Pallas kernels for 16%

profile of v9, /device:TPU:2, one launch (start us, length us, event | category | flops | bytes accessed | tf_op | source)
XLA Modules:
  0.0 301.0 jit_solution(18274145476547149981)
XLA Ops:
  5.0 5.5 %collective-permute-start = (bf16[2,256,896]{2,1,0:T(8,128)(2,1)}, bf16[2,256,896]{2,1,0:T(8,128)(2,1)}, u32[]{:S(2)}, u32[]{:S(2)}) collective-permute-start(bf16[2,256,896]{2,1,0:T(8,128)(2,1)} %get-tuple-element.99), channel_id=1, source_target_pairs={{0,1},{1,2},{2,3},{4,5},{5,6},{6,7},{8,9},{9,10},{10,11},{12,13},{... | collective-permute-start | bytes 2752520 | tf_op jit(solution)/shard_map/ppermute | solution.py:581
  19.9 9.1 %collective-permute-done.1.refs_1_.refs_2_ = bf16[2,256,896]{2,1,0:T(8,128)(2,1)S(1)} collective-permute-done((bf16[2,256,896]{2,1,0:T(8,128)(2,1)}, bf16[2,256,896]{2,1,0:T(8,128)(2,1)S(1)}, u32[]{:S(2)}, u32[]{:S(2)}) %collective-permute-start.1) | collective-permute-done | bytes 917536 | tf_op jit(solution)/shard_map/ppermute | solution.py:581
  30.6 6.5 %shear_tile.4 = bf16[8,2,256,128]{3,2,1,0:T(8,128)(2,1)} custom-call(s32[16]{0:T(128)} %get-tuple-element.120.base, s32[1]{0:T(128)} %constant.69.clone.1.rank, bf16[2,256,896]{2,1,0:T(8,128)(2,1)} %collective-permute-done.refs_0_, bf16[2,256,896]{2,1,0:T(8,128)(2,1)} %copy-done.9, bf16[2,512,1024]{2,1,0:T(8,128)(2,1)} %refs_4_.2, f32[2,1,256]{2,1,0:T(1,128)} %bitcast.63, ...), custom_call_target="tpu_custom_call" | custom-call | tf_op jit(solution)/shard_map/shear_tile/pallas_call | solution.py:206
  37.1 4.3 %all-to-all-start = ((bf16[8,2,256,128]{3,2,1,0:T(8,128)(2,1)}), bf16[8,2,256,128]{3,2,1,0:T(8,128)(2,1)S(1)}, u32[]{:S(2)}, u32[]{:S(2)}) async-start(bf16[8,2,256,128]{3,2,1,0:T(8,128)(2,1)} %shear_tile.4), calls=%async_computation | async-start | bytes 2097152 | tf_op jit(solution)/shard_map/all_to_all | solution.py:743
  44.1 7.2 %collective-permute-done.2.refs_0_.refs_1_ = bf16[2,288,896]{2,1,0:T(8,128)(2,1)S(1)} collective-permute-done((bf16[2,288,896]{2,1,0:T(8,128)(2,1)}, bf16[2,288,896]{2,1,0:T(8,128)(2,1)S(1)}, u32[]{:S(2)}, u32[]{:S(2)}) %collective-permute-start.2) | collective-permute-done | bytes 1032224 | tf_op jit(solution)/shard_map/ppermute | solution.py:581
  52.6 6.5 %shear_tile.5 = bf16[8,2,256,128]{3,2,1,0:T(8,128)(2,1)} custom-call(s32[16]{0:T(128)} %get-tuple-element.119.base, s32[1]{0:T(128)} %constant.69.clone.1.rank, bf16[2,288,896]{2,1,0:T(8,128)(2,1)} %copy-done.5, bf16[2,288,896]{2,1,0:T(8,128)(2,1)} %copy-done.6, bf16[2,512,1024]{2,1,0:T(8,128)(2,1)} %refs_4_.2, f32[2,1,256]{2,1,0:T(1,128)} %bitcast.64, ...), custom_call_target="tpu_custom_call" | custom-call | tf_op jit(solution)/shard_map/shear_tile/pallas_call | solution.py:206
  59.1 4.3 %all-to-all-start.1 = ((bf16[8,2,256,128]{3,2,1,0:T(8,128)(2,1)}), bf16[8,2,256,128]{3,2,1,0:T(8,128)(2,1)S(1)}, u32[]{:S(2)}, u32[]{:S(2)}) async-start(bf16[8,2,256,128]{3,2,1,0:T(8,128)(2,1)} %shear_tile.5), calls=%async_computation.1 | async-start | bytes 2097152 | tf_op jit(solution)/shard_map/all_to_all | solution.py:743
  65.2 10.1 %shear_tile.6 = bf16[8,2,512,128]{3,2,1,0:T(8,128)(2,1)} custom-call(s32[32]{0:T(128)} %get-tuple-element.117.base, s32[1]{0:T(128)} %bitcast.1.rank, bf16[2,256,896]{2,1,0:T(8,128)(2,1)} %collective-permute-done.refs_0_, bf16[2,288,896]{2,1,0:T(8,128)(2,1)} %copy-done.5, bf16[2,256,896]{2,1,0:T(8,128)(2,1)} %copy-done.9, bf16[2,288,896]{2,1,0:T(8,128)(2,1)} %copy-done.6, ...), custom_call_target="tpu_custom_call" | custom-call | tf_op jit(solution)/shard_map/shear_tile/pallas_call | solution.py:206
  79.1 8.4 %shear_columns.2 = bf16[32,2,128,128]{3,2,1,0:T(8,128)(2,1)} custom-call(s32[1]{0:T(128)} %bitcast.11.base, s32[1]{0:T(128)} %constant.69.clone.1.rank, bf16[8,2,256,128]{3,2,1,0:T(8,128)(2,1)} %copy-done.7, bf16[8,2,256,128]{3,2,1,0:T(8,128)(2,1)} %copy-done.8, s32[1,128]{1,0:T(1,128)} %get-tuple-element.124.refs_2_, f32[1,128]{1,0:T(1,128)} %get-tuple-element.122.refs_3_, ...), custom_call_target="tpu_custom_call" | custom-call | tf_op jit(solution)/shard_map/shear_columns/pallas_call | solution.py:427
  87.4 6.9 %all-to-all-start.2 = ((bf16[32,2,128,128]{3,2,1,0:T(8,128)(2,1)}), bf16[32,2,128,128]{3,2,1,0:T(8,128)(2,1)S(1)}, u32[]{:S(2)}, u32[]{:S(2)}) async-start(bf16[32,2,128,128]{3,2,1,0:T(8,128)(2,1)} %shear_columns.2), calls=%async_computation.2 | async-start | bytes 4194304 | tf_op jit(solution)/shard_map/all_to_all | solution.py:752
  99.6 17.0 %collective-permute-done.5.refs_2_ = bf16[1,2,512,128]{3,2,1,0:T(8,128)(2,1)} collective-permute-done((bf16[1,2,512,128]{3,2,1,0:T(8,128)(2,1)}, bf16[1,2,512,128]{3,2,1,0:T(8,128)(2,1)}, u32[]{:S(2)}, u32[]{:S(2)}) %collective-permute-start.5) | collective-permute-done | bytes 262176 | tf_op jit(solution)/shard_map/ppermute | solution.py:626
  120.1 5.0 %collective-permute-done.6.refs_3_ = bf16[1,2,512,128]{3,2,1,0:T(8,128)(2,1)} collective-permute-done((bf16[1,2,512,128]{3,2,1,0:T(8,128)(2,1)}, bf16[1,2,512,128]{3,2,1,0:T(8,128)(2,1)}, u32[]{:S(2)}, u32[]{:S(2)}) %collective-permute-start.6) | collective-permute-done | bytes 262176 | tf_op jit(solution)/shard_map/ppermute | solution.py:626
  125.1 11.5 %collective-permute-done.9.refs_6_ = bf16[1,2,512,128]{3,2,1,0:T(8,128)(2,1)} collective-permute-done((bf16[1,2,512,128]{3,2,1,0:T(8,128)(2,1)S(1)}, bf16[1,2,512,128]{3,2,1,0:T(8,128)(2,1)}, u32[]{:S(2)}, u32[]{:S(2)}) %collective-permute-start.9) | collective-permute-done | bytes 262176 | tf_op jit(solution)/shard_map/ppermute | solution.py:626
  136.6 7.1 %collective-permute-done.10.refs_7_ = bf16[1,2,512,128]{3,2,1,0:T(8,128)(2,1)} collective-permute-done((bf16[1,2,512,128]{3,2,1,0:T(8,128)(2,1)S(1)}, bf16[1,2,512,128]{3,2,1,0:T(8,128)(2,1)}, u32[]{:S(2)}, u32[]{:S(2)}) %collective-permute-start.10) | collective-permute-done | bytes 262176 | tf_op jit(solution)/shard_map/ppermute | solution.py:626
  143.7 8.4 %shear_columns.3 = bf16[8,2,512,128]{3,2,1,0:T(8,128)(2,1)} custom-call(s32[1]{0:T(128)} %bitcast.3.base, s32[1]{0:T(128)} %bitcast.1.rank, bf16[1,2,512,128]{3,2,1,0:T(8,128)(2,1)} %get-tuple-element.55.refs_0_, bf16[1,2,512,128]{3,2,1,0:T(8,128)(2,1)} %collective-permute-done.4.refs_1_, bf16[1,2,512,128]{3,2,1,0:T(8,128)(2,1)} %collective-permute-done.5.refs_2_, ...), custom_call_target="tpu_custom_call" | custom-call | tf_op jit(solution)/shard_map/shear_columns/pallas_call | solution.py:427
  153.4 9.6 %shear_whole.1 = bf16[4,2,1088,128]{3,2,1,0:T(8,128)(2,1)} custom-call(s32[8]{0:T(128)} %fusion.16.base, bf16[8,4,2,128,128]{4,3,2,1,0:T(8,128)(2,1)} %bitcast.60, f32[1,128]{1,0:T(1,128)} %fusion.18.offsets, f32[1,128]{1,0:T(1,128)} %fusion.19.fractions, bf16[256,256]{1,0:T(8,128)(2,1)} %constant.86.clone.refs_5_.refs_7_.forward.refs_6_, ...), custom_call_target="tpu_custom_call" | custom-call | tf_op jit(solution)/shard_map/shear_whole/pallas_call | solution.py:316
  163.0 3.9 %all-to-all-start.3 = ((bf16[4,2,1088,128]{3,2,1,0:T(8,128)(2,1)}), bf16[4,2,1088,128]{3,2,1,0:T(8,128)(2,1)S(1)}, u32[]{:S(2)}, u32[]{:S(2)}) async-start(bf16[4,2,1088,128]{3,2,1,0:T(8,128)(2,1)} %shear_whole.1), calls=%async_computation.3 | async-start | bytes 4456448 | tf_op jit(solution)/shard_map/all_to_all | solution.py:772
  174.6 4.1 %collective-permute-done.17.refs_7_ = bf16[1,2,512,128]{3,2,1,0:T(8,128)(2,1)S(1)} collective-permute-done((bf16[1,2,512,128]{3,2,1,0:T(8,128)(2,1)S(1)}, bf16[1,2,512,128]{3,2,1,0:T(8,128)(2,1)S(1)}, u32[]{:S(2)}, u32[]{:S(2)}) %collective-permute-start.17) | collective-permute-done | bytes 262176 | tf_op jit(solution)/shard_map/ppermute | solution.py:626
  180.0 4.7 %collective-permute-done.16.refs_6_ = bf16[1,2,512,128]{3,2,1,0:T(8,128)(2,1)S(1)} collective-permute-done((bf16[1,2,512,128]{3,2,1,0:T(8,128)(2,1)S(1)}, bf16[1,2,512,128]{3,2,1,0:T(8,128)(2,1)S(1)}, u32[]{:S(2)}, u32[]{:S(2)}) %collective-permute-start.16) | collective-permute-done | bytes 262176 | tf_op jit(solution)/shard_map/ppermute | solution.py:626
  184.8 5.2 %collective-permute-done.15.refs_5_ = bf16[1,2,512,128]{3,2,1,0:T(8,128)(2,1)S(1)} collective-permute-done((bf16[1,2,512,128]{3,2,1,0:T(8,128)(2,1)S(1)}, bf16[1,2,512,128]{3,2,1,0:T(8,128)(2,1)S(1)}, u32[]{:S(2)}, u32[]{:S(2)}) %collective-permute-start.15) | collective-permute-done | bytes 262176 | tf_op jit(solution)/shard_map/ppermute | solution.py:626
  190.0 5.6 %collective-permute-done.14.refs_4_ = bf16[1,2,512,128]{3,2,1,0:T(8,128)(2,1)S(1)} collective-permute-done((bf16[1,2,512,128]{3,2,1,0:T(8,128)(2,1)S(1)}, bf16[1,2,512,128]{3,2,1,0:T(8,128)(2,1)S(1)}, u32[]{:S(2)}, u32[]{:S(2)}) %collective-permute-start.14) | collective-permute-done | bytes 262176 | tf_op jit(solution)/shard_map/ppermute | solution.py:626
  196.6 4.5 %ordered.1 = (bf16[8,2,512,128]{3,2,1,0:T(8,128)(2,1)}, bf16[7,2,512,128]{3,2,1,0:T(8,128)(2,1)}, bf16[7,2,512,128]{3,2,1,0:T(8,128)(2,1)}) custom-call(s32[1]{0:T(128)} %bitcast.1.rank, bf16[1,2,512,128]{3,2,1,0:T(8,128)(2,1)} %get-tuple-element.85.refs_0_, bf16[1,2,512,128]{3,2,1,0:T(8,128)(2,1)} %copy-done.21, bf16[1,2,512,128]{3,2,1,0:T(8,128)(2,1)} %copy-done.20, ...), custom_call_target="tpu_custom_call" | custom-call | tf_op jit(solution)/shard_map/ordered/pallas_call | solution.py:609
  201.1 5.1 %collective-permute-start.18 = (bf16[7,2,512,128]{3,2,1,0:T(8,128)(2,1)}, bf16[7,2,512,128]{3,2,1,0:T(8,128)(2,1)}, u32[]{:S(2)}, u32[]{:S(2)}) collective-permute-start(bf16[7,2,512,128]{3,2,1,0:T(8,128)(2,1)} %get-tuple-element.64), channel_id=1, source_target_pairs={{0,1},{1,2},{2,3},{4,5},{5,6},{6,7},{8,9},{9,10},{10,11},{12,13},{... | collective-permute-start | bytes 5505032 | tf_op jit(solution)/shard_map/ppermute | solution.py:581
  212.1 7.2 %all-to-all-done.3.refs_0_ = bf16[4,2,1088,128]{3,2,1,0:T(8,128)(2,1)S(1)} async-done(((bf16[4,2,1088,128]{3,2,1,0:T(8,128)(2,1)}), bf16[4,2,1088,128]{3,2,1,0:T(8,128)(2,1)S(1)}, u32[]{:S(2)}, u32[]{:S(2)}) %all-to-all-start.3) | async-done | bytes 2228256 | tf_op jit(solution)/shard_map/all_to_all | solution.py:772
  220.7 8.4 %travel_first.2.body = bf16[4,2,1024,128]{3,2,1,0:T(8,128)(2,1)} custom-call(bf16[4,2,1088,128]{3,2,1,0:T(8,128)(2,1)} %copy-done.3, bf16[2,1024,512]{2,1,0:T(8,128)(2,1)} %refs_1_.1, bf16[2,32,512]{2,1,0:T(8,128)(2,1)} %slice.270.refs_2_, bf16[2,32,512]{2,1,0:T(8,128)(2,1)} %slice.271.refs_3_, bf16[256,384]{1,0:T(8,128)(2,1)} %copy.22.refs_4_), custom_call_target="tpu_custom_call" | custom-call | tf_op jit(solution)/shard_map/travel_first/pallas_call | solution.py:528
  236.0 5.8 %collective-permute-done.21.right = bf16[1,2,1024,128]{3,2,1,0:T(8,128)(2,1)S(1)} collective-permute-done((bf16[1,2,1024,128]{3,2,1,0:T(8,128)(2,1)S(1)}, bf16[1,2,1024,128]{3,2,1,0:T(8,128)(2,1)S(1)}, u32[]{:S(2)}, u32[]{:S(2)}) %collective-permute-start.21) | collective-permute-done | bytes 524320 | tf_op jit(solution)/shard_map/ppermute | solution.py:581
  243.6 4.4 %travel_second.2 = bf16[2,1024,512]{2,1,0:T(8,128)(2,1)} custom-call(bf16[1,2,1024,128]{3,2,1,0:T(8,128)(2,1)} %copy-done.11, bf16[4,2,1024,128]{3,2,1,0:T(8,128)(2,1)} %travel_first.2.body, bf16[1,2,1024,128]{3,2,1,0:T(8,128)(2,1)} %copy-done.10, bf16[768,256]{1,0:T(8,128)(2,1)} %get-tuple-element.101.matrix), custom_call_target="tpu_custom_call" | custom-call | tf_op jit(solution)/shard_map/travel_second/pallas_call | solution.py:561
  248.1 9.7 %collective-permute-done.19.refs_1_ = bf16[7,2,512,128]{3,2,1,0:T(8,128)(2,1)} collective-permute-done((bf16[7,2,512,128]{3,2,1,0:T(8,128)(2,1)}, bf16[7,2,512,128]{3,2,1,0:T(8,128)(2,1)}, u32[]{:S(2)}, u32[]{:S(2)}) %collective-permute-start.19) | collective-permute-done | bytes 1835040 | tf_op jit(solution)/shard_map/ppermute | solution.py:581
  257.8 11.8 %shear_tile.7.refs_0_ = bf16[8,2,512,128]{3,2,1,0:T(8,128)(2,1)} custom-call(s32[32]{0:T(128)} %get-tuple-element.118.base, s32[1]{0:T(128)} %constant.69.clone.1.rank, bf16[7,2,512,128]{3,2,1,0:T(8,128)(2,1)} %collective-permute-done.18.refs_0_, bf16[7,2,512,128]{3,2,1,0:T(8,128)(2,1)} %collective-permute-done.19.refs_1_, bf16[2,512,1024]{2,1,0:T(8,128)(2,1)} %refs_2_.5, ...), custom_call_target="tpu_custom_call" | custom-call | tf_op jit(solution)/shard_map/shear_tile/pallas_call | solution.py:206
  280.3 3.9 %travel_first.3.body = bf16[8,2,512,128]{3,2,1,0:T(8,128)(2,1)} custom-call(bf16[8,2,512,128]{3,2,1,0:T(8,128)(2,1)} %shear_tile.7.refs_0_, bf16[8,2,32,128]{3,2,1,0:T(8,128)(2,1)} %copy-done.26, bf16[8,2,32,128]{3,2,1,0:T(8,128)(2,1)} %copy-done.25, bf16[256,384]{1,0:T(8,128)(2,1)} %copy.23.refs_3_), custom_call_target="tpu_custom_call" | custom-call | tf_op jit(solution)/shard_map/travel_first/pallas_call | solution.py:528
  286.6 4.6 %collective-permute-start.24 = (bf16[1,2,512,128]{3,2,1,0:T(8,128)(2,1)S(1)}, bf16[1,2,512,128]{3,2,1,0:T(8,128)(2,1)S(1)}, u32[]{:S(2)}, u32[]{:S(2)}) collective-permute-start(bf16[1,2,512,128]{3,2,1,0:T(8,128)(2,1)S(1)} %get-tuple-element.73), channel_id=1, source_target_pairs={{0,1},{1,2},{2,3},{4,5},{5,6},{6,7},{8,9},{9,10},{10,11},{12,13},{... | collective-permute-start | bytes 786440 | tf_op jit(solution)/shard_map/ppermute | solution.py:581
  296.6 4.4 %travel_second.3 = bf16[2,512,1024]{2,1,0:T(8,128)(2,1)} custom-call(bf16[1,2,512,128]{3,2,1,0:T(8,128)(2,1)} %copy-done.23, bf16[8,2,512,128]{3,2,1,0:T(8,128)(2,1)} %travel_first.3.body, bf16[1,2,512,128]{3,2,1,0:T(8,128)(2,1)} %copy-done.22, bf16[768,256]{1,0:T(8,128)(2,1)} %get-tuple-element.100.matrix), custom_call_target="tpu_custom_call" | custom-call | tf_op jit(solution)/shard_map/travel_second/pallas_call | solution.py:561
  (150 shorter events, 78.1 us)
Async XLA Ops:
  0.6 42.8 %copy-start = (f32[2,1024]{1,0:T(2,128)S(1)}, f32[2,1024]{1,0:T(2,128)}, u32[]{:S(2)}) copy-start(f32[2,1024]{1,0:T(2,128)} %param.22) | copy-start | bytes 24580
  3.7 25.3 %collective-permute-start.1 = (bf16[2,256,896]{2,1,0:T(8,128)(2,1)}, bf16[2,256,896]{2,1,0:T(8,128)(2,1)S(1)}, u32[]{:S(2)}, u32[]{:S(2)}) collective-permute-start(bf16[2,256,896]{2,1,0:T(8,128)(2,1)} %get-tuple-element.98), channel_id=1, source_target_pairs={{1,0},{2,1},{3,2},{5,4},{6,5},{7,6},{9,8},{10,9},{11,10},{13,12},{... | collective-permute-start | bytes 2752520 | tf_op jit(solution)/shard_map/ppermute | solution.py:581
  5.0 25.6 %collective-permute-start = (bf16[2,256,896]{2,1,0:T(8,128)(2,1)}, bf16[2,256,896]{2,1,0:T(8,128)(2,1)}, u32[]{:S(2)}, u32[]{:S(2)}) collective-permute-start(bf16[2,256,896]{2,1,0:T(8,128)(2,1)} %get-tuple-element.99), channel_id=1, source_target_pairs={{0,1},{1,2},{2,3},{4,5},{5,6},{6,7},{8,9},{9,10},{10,11},{12,13},{... | collective-permute-start | bytes 2752520 | tf_op jit(solution)/shard_map/ppermute | solution.py:581
  12.7 38.6 %collective-permute-start.2 = (bf16[2,288,896]{2,1,0:T(8,128)(2,1)}, bf16[2,288,896]{2,1,0:T(8,128)(2,1)S(1)}, u32[]{:S(2)}, u32[]{:S(2)}) collective-permute-start(bf16[2,288,896]{2,1,0:T(8,128)(2,1)} %fusion.2), channel_id=1, source_target_pairs={{0,1},{1,2},{2,3},{4,5},{5,6},{6,7},{8,9},{9,10},{10,11},{12,13},{... | collective-permute-start | bytes 3096584 | tf_op jit(solution)/shard_map/ppermute | solution.py:581
  16.4 34.9 %collective-permute-start.3 = (bf16[2,288,896]{2,1,0:T(8,128)(2,1)}, bf16[2,288,896]{2,1,0:T(8,128)(2,1)S(1)}, u32[]{:S(2)}, u32[]{:S(2)}) collective-permute-start(bf16[2,288,896]{2,1,0:T(8,128)(2,1)} %fusion.3), channel_id=1, source_target_pairs={{1,0},{2,1},{3,2},{5,4},{6,5},{7,6},{9,8},{10,9},{11,10},{13,12},{... | collective-permute-start | bytes 3096584 | tf_op jit(solution)/shard_map/ppermute | solution.py:581
  37.1 22.0 %all-to-all-start = ((bf16[8,2,256,128]{3,2,1,0:T(8,128)(2,1)}), bf16[8,2,256,128]{3,2,1,0:T(8,128)(2,1)S(1)}, u32[]{:S(2)}, u32[]{:S(2)}) async-start(bf16[8,2,256,128]{3,2,1,0:T(8,128)(2,1)} %shear_tile.4), calls=%async_computation | async-start | bytes 2097152 | tf_op jit(solution)/shard_map/all_to_all | solution.py:743
  59.1 19.0 %all-to-all-start.1 = ((bf16[8,2,256,128]{3,2,1,0:T(8,128)(2,1)}), bf16[8,2,256,128]{3,2,1,0:T(8,128)(2,1)S(1)}, u32[]{:S(2)}, u32[]{:S(2)}) async-start(bf16[8,2,256,128]{3,2,1,0:T(8,128)(2,1)} %shear_tile.5), calls=%async_computation.1 | async-start | bytes 2097152 | tf_op jit(solution)/shard_map/all_to_all | solution.py:743
  87.4 64.6 %all-to-all-start.2 = ((bf16[32,2,128,128]{3,2,1,0:T(8,128)(2,1)}), bf16[32,2,128,128]{3,2,1,0:T(8,128)(2,1)S(1)}, u32[]{:S(2)}, u32[]{:S(2)}) async-start(bf16[32,2,128,128]{3,2,1,0:T(8,128)(2,1)} %shear_columns.2), calls=%async_computation.2 | async-start | bytes 4194304 | tf_op jit(solution)/shard_map/all_to_all | solution.py:752
  94.4 3.7 %collective-permute-start.4 = (bf16[1,2,512,128]{3,2,1,0:T(8,128)(2,1)}, bf16[1,2,512,128]{3,2,1,0:T(8,128)(2,1)}, u32[]{:S(2)}, u32[]{:S(2)}) collective-permute-start(bf16[1,2,512,128]{3,2,1,0:T(8,128)(2,1)} %get-tuple-element.46), channel_id=1, source_target_pairs={{0,4},{4,0},{8,12},{12,8},{16,20},{20,16},{24,28},{28,24},{1,5},{5... | collective-permute-start | bytes 786440 | tf_op jit(solution)/shard_map/ppermute | solution.py:626
  94.6 22.0 %collective-permute-start.5 = (bf16[1,2,512,128]{3,2,1,0:T(8,128)(2,1)}, bf16[1,2,512,128]{3,2,1,0:T(8,128)(2,1)}, u32[]{:S(2)}, u32[]{:S(2)}) collective-permute-start(bf16[1,2,512,128]{3,2,1,0:T(8,128)(2,1)} %get-tuple-element.47), channel_id=1, source_target_pairs={{0,8},{4,12},{8,0},{12,4},{16,24},{20,28},{24,16},{28,20},{1,9},{5... | collective-permute-start | bytes 786440 | tf_op jit(solution)/shard_map/ppermute | solution.py:626
  95.0 30.1 %collective-permute-start.6 = (bf16[1,2,512,128]{3,2,1,0:T(8,128)(2,1)}, bf16[1,2,512,128]{3,2,1,0:T(8,128)(2,1)}, u32[]{:S(2)}, u32[]{:S(2)}) collective-permute-start(bf16[1,2,512,128]{3,2,1,0:T(8,128)(2,1)} %get-tuple-element.48), channel_id=1, source_target_pairs={{0,12},{4,8},{8,4},{12,0},{16,28},{20,24},{24,20},{28,16},{1,13},{... | collective-permute-start | bytes 786440 | tf_op jit(solution)/shard_map/ppermute | solution.py:626
  96.3 28.8 %collective-permute-start.7 = (bf16[1,2,512,128]{3,2,1,0:T(8,128)(2,1)S(1)}, bf16[1,2,512,128]{3,2,1,0:T(8,128)(2,1)}, u32[]{:S(2)}, u32[]{:S(2)}) collective-permute-start(bf16[1,2,512,128]{3,2,1,0:T(8,128)(2,1)S(1)} %copy-done.14), channel_id=1, source_target_pairs={{0,16},{4,20},{8,24},{12,28},{16,0},{20,4},{24,8},{28,12},{1,17},{... | collective-permute-start | bytes 786440 | tf_op jit(solution)/shard_map/ppermute | solution.py:626
  97.8 27.3 %collective-permute-start.8 = (bf16[1,2,512,128]{3,2,1,0:T(8,128)(2,1)S(1)}, bf16[1,2,512,128]{3,2,1,0:T(8,128)(2,1)}, u32[]{:S(2)}, u32[]{:S(2)}) collective-permute-start(bf16[1,2,512,128]{3,2,1,0:T(8,128)(2,1)S(1)} %copy-done.13), channel_id=1, source_target_pairs={{0,20},{4,16},{8,28},{12,24},{16,4},{20,0},{24,12},{28,8},{1,21},{... | collective-permute-start | bytes 786440 | tf_op jit(solution)/shard_map/ppermute | solution.py:626
  98.1 38.4 %collective-permute-start.9 = (bf16[1,2,512,128]{3,2,1,0:T(8,128)(2,1)S(1)}, bf16[1,2,512,128]{3,2,1,0:T(8,128)(2,1)}, u32[]{:S(2)}, u32[]{:S(2)}) collective-permute-start(bf16[1,2,512,128]{3,2,1,0:T(8,128)(2,1)S(1)} %copy-done.12), channel_id=1, source_target_pairs={{0,24},{4,28},{8,16},{12,20},{16,8},{20,12},{24,0},{28,4},{1,25},{... | collective-permute-start | bytes 786440 | tf_op jit(solution)/shard_map/ppermute | solution.py:626
  116.6 27.1 %collective-permute-start.10 = (bf16[1,2,512,128]{3,2,1,0:T(8,128)(2,1)S(1)}, bf16[1,2,512,128]{3,2,1,0:T(8,128)(2,1)}, u32[]{:S(2)}, u32[]{:S(2)}) collective-permute-start(bf16[1,2,512,128]{3,2,1,0:T(8,128)(2,1)S(1)} %get-tuple-element.52), channel_id=1, source_target_pairs={{0,28},{4,24},{8,20},{12,16},{16,12},{20,8},{24,4},{28,0},{1,29},{... | collective-permute-start | bytes 786440 | tf_op jit(solution)/shard_map/ppermute | solution.py:626
  163.0 56.3 %all-to-all-start.3 = ((bf16[4,2,1088,128]{3,2,1,0:T(8,128)(2,1)}), bf16[4,2,1088,128]{3,2,1,0:T(8,128)(2,1)S(1)}, u32[]{:S(2)}, u32[]{:S(2)}) async-start(bf16[4,2,1088,128]{3,2,1,0:T(8,128)(2,1)} %shear_whole.1), calls=%async_computation.3 | async-start | bytes 4456448 | tf_op jit(solution)/shard_map/all_to_all | solution.py:772
  169.3 38.2 %copy-start.27 = (f32[256,128]{1,0:T(8,128)S(1)}, f32[256,128]{1,0:T(8,128)}, u32[]{:S(2)}) copy-start(f32[256,128]{1,0:T(8,128)} %constant.91.clone) | copy-start | bytes 393220
  169.3 9.4 %collective-permute-start.17 = (bf16[1,2,512,128]{3,2,1,0:T(8,128)(2,1)S(1)}, bf16[1,2,512,128]{3,2,1,0:T(8,128)(2,1)S(1)}, u32[]{:S(2)}, u32[]{:S(2)}) collective-permute-start(bf16[1,2,512,128]{3,2,1,0:T(8,128)(2,1)S(1)} %get-tuple-element.78), channel_id=1, source_target_pairs={{0,28},{4,24},{8,20},{12,16},{16,12},{20,8},{24,4},{28,0},{1,29},{... | collective-permute-start | bytes 786440 | tf_op jit(solution)/shard_map/ppermute | solution.py:626
  170.2 14.4 %collective-permute-start.16 = (bf16[1,2,512,128]{3,2,1,0:T(8,128)(2,1)S(1)}, bf16[1,2,512,128]{3,2,1,0:T(8,128)(2,1)S(1)}, u32[]{:S(2)}, u32[]{:S(2)}) collective-permute-start(bf16[1,2,512,128]{3,2,1,0:T(8,128)(2,1)S(1)} %get-tuple-element.79), channel_id=1, source_target_pairs={{0,24},{4,28},{8,16},{12,20},{16,8},{20,12},{24,0},{28,4},{1,25},{... | collective-permute-start | bytes 786440 | tf_op jit(solution)/shard_map/ppermute | solution.py:626
  171.9 18.1 %collective-permute-start.15 = (bf16[1,2,512,128]{3,2,1,0:T(8,128)(2,1)S(1)}, bf16[1,2,512,128]{3,2,1,0:T(8,128)(2,1)S(1)}, u32[]{:S(2)}, u32[]{:S(2)}) collective-permute-start(bf16[1,2,512,128]{3,2,1,0:T(8,128)(2,1)S(1)} %get-tuple-element.80), channel_id=1, source_target_pairs={{0,20},{4,16},{8,28},{12,24},{16,4},{20,0},{24,12},{28,8},{1,21},{... | collective-permute-start | bytes 786440 | tf_op jit(solution)/shard_map/ppermute | solution.py:626
  172.2 23.5 %collective-permute-start.14 = (bf16[1,2,512,128]{3,2,1,0:T(8,128)(2,1)S(1)}, bf16[1,2,512,128]{3,2,1,0:T(8,128)(2,1)S(1)}, u32[]{:S(2)}, u32[]{:S(2)}) collective-permute-start(bf16[1,2,512,128]{3,2,1,0:T(8,128)(2,1)S(1)} %get-tuple-element.81), channel_id=1, source_target_pairs={{0,16},{4,20},{8,24},{12,28},{16,0},{20,4},{24,8},{28,12},{1,17},{... | collective-permute-start | bytes 786440 | tf_op jit(solution)/shard_map/ppermute | solution.py:626
  173.7 22.0 %collective-permute-start.13 = (bf16[1,2,512,128]{3,2,1,0:T(8,128)(2,1)S(1)}, bf16[1,2,512,128]{3,2,1,0:T(8,128)(2,1)S(1)}, u32[]{:S(2)}, u32[]{:S(2)}) collective-permute-start(bf16[1,2,512,128]{3,2,1,0:T(8,128)(2,1)S(1)} %get-tuple-element.82), channel_id=1, source_target_pairs={{0,12},{4,8},{8,4},{12,0},{16,28},{20,24},{24,20},{28,16},{1,13},{... | collective-permute-start | bytes 786440 | tf_op jit(solution)/shard_map/ppermute | solution.py:626
  178.7 17.0 %collective-permute-start.12 = (bf16[1,2,512,128]{3,2,1,0:T(8,128)(2,1)S(1)}, bf16[1,2,512,128]{3,2,1,0:T(8,128)(2,1)S(1)}, u32[]{:S(2)}, u32[]{:S(2)}) collective-permute-start(bf16[1,2,512,128]{3,2,1,0:T(8,128)(2,1)S(1)} %get-tuple-element.83), channel_id=1, source_target_pairs={{0,8},{4,12},{8,0},{12,4},{16,24},{20,28},{24,16},{28,20},{1,9},{5... | collective-permute-start | bytes 786440 | tf_op jit(solution)/shard_map/ppermute | solution.py:626
  184.7 11.0 %collective-permute-start.11 = (bf16[1,2,512,128]{3,2,1,0:T(8,128)(2,1)S(1)}, bf16[1,2,512,128]{3,2,1,0:T(8,128)(2,1)S(1)}, u32[]{:S(2)}, u32[]{:S(2)}) collective-permute-start(bf16[1,2,512,128]{3,2,1,0:T(8,128)(2,1)S(1)} %get-tuple-element.84), channel_id=1, source_target_pairs={{0,4},{4,0},{8,12},{12,8},{16,20},{20,16},{24,28},{28,24},{1,5},{5... | collective-permute-start | bytes 786440 | tf_op jit(solution)/shard_map/ppermute | solution.py:626
  201.1 46.9 %collective-permute-start.18 = (bf16[7,2,512,128]{3,2,1,0:T(8,128)(2,1)}, bf16[7,2,512,128]{3,2,1,0:T(8,128)(2,1)}, u32[]{:S(2)}, u32[]{:S(2)}) collective-permute-start(bf16[7,2,512,128]{3,2,1,0:T(8,128)(2,1)} %get-tuple-element.64), channel_id=1, source_target_pairs={{0,1},{1,2},{2,3},{4,5},{5,6},{6,7},{8,9},{9,10},{10,11},{12,13},{... | collective-permute-start | bytes 5505032 | tf_op jit(solution)/shard_map/ppermute | solution.py:581
  206.2 51.5 %collective-permute-start.19 = (bf16[7,2,512,128]{3,2,1,0:T(8,128)(2,1)}, bf16[7,2,512,128]{3,2,1,0:T(8,128)(2,1)}, u32[]{:S(2)}, u32[]{:S(2)}) collective-permute-start(bf16[7,2,512,128]{3,2,1,0:T(8,128)(2,1)} %get-tuple-element.65), channel_id=1, source_target_pairs={{1,0},{2,1},{3,2},{5,4},{6,5},{7,6},{9,8},{10,9},{11,10},{13,12},{... | collective-permute-start | bytes 5505032 | tf_op jit(solution)/shard_map/ppermute | solution.py:581
  230.4 11.4 %collective-permute-start.21 = (bf16[1,2,1024,128]{3,2,1,0:T(8,128)(2,1)S(1)}, bf16[1,2,1024,128]{3,2,1,0:T(8,128)(2,1)S(1)}, u32[]{:S(2)}, u32[]{:S(2)}) collective-permute-start(bf16[1,2,1024,128]{3,2,1,0:T(8,128)(2,1)S(1)} %get-tuple-element.76), channel_id=1, source_target_pairs={{4,0},{8,4},{12,8},{16,12},{20,16},{24,20},{28,24},{5,1},{9,5},{13... | collective-permute-start | bytes 1572872 | tf_op jit(solution)/shard_map/ppermute | solution.py:581
  232.3 10.5 %collective-permute-start.20 = (bf16[1,2,1024,128]{3,2,1,0:T(8,128)(2,1)S(1)}, bf16[1,2,1024,128]{3,2,1,0:T(8,128)(2,1)S(1)}, u32[]{:S(2)}, u32[]{:S(2)}) collective-permute-start(bf16[1,2,1024,128]{3,2,1,0:T(8,128)(2,1)S(1)} %get-tuple-element.77), channel_id=1, source_target_pairs={{0,4},{4,8},{8,12},{12,16},{16,20},{20,24},{24,28},{1,5},{5,9},{9,... | collective-permute-start | bytes 1572872 | tf_op jit(solution)/shard_map/ppermute | solution.py:581
  270.6 5.6 %collective-permute-start.23 = (bf16[8,2,32,128]{3,2,1,0:T(8,128)(2,1)S(1)}, bf16[8,2,32,128]{3,2,1,0:T(8,128)(2,1)S(1)}, u32[]{:S(2)}, u32[]{:S(2)}) collective-permute-start(bf16[8,2,32,128]{3,2,1,0:T(8,128)(2,1)S(1)} %get-tuple-element.74), channel_id=1, source_target_pairs={{4,0},{8,4},{12,8},{16,12},{20,16},{24,20},{28,24},{5,1},{9,5},{13... | collective-permute-start | bytes 393224 | tf_op jit(solution)/shard_map/ppermute | solution.py:581
  273.4 6.3 %collective-permute-start.22 = (bf16[8,2,32,128]{3,2,1,0:T(8,128)(2,1)S(1)}, bf16[8,2,32,128]{3,2,1,0:T(8,128)(2,1)S(1)}, u32[]{:S(2)}, u32[]{:S(2)}) collective-permute-start(bf16[8,2,32,128]{3,2,1,0:T(8,128)(2,1)S(1)} %get-tuple-element.75), channel_id=1, source_target_pairs={{0,4},{4,8},{8,12},{12,16},{16,20},{20,24},{24,28},{1,5},{5,9},{9,... | collective-permute-start | bytes 393224 | tf_op jit(solution)/shard_map/ppermute | solution.py:581
  285.3 9.4 %collective-permute-start.25 = (bf16[1,2,512,128]{3,2,1,0:T(8,128)(2,1)S(1)}, bf16[1,2,512,128]{3,2,1,0:T(8,128)(2,1)S(1)}, u32[]{:S(2)}, u32[]{:S(2)}) collective-permute-start(bf16[1,2,512,128]{3,2,1,0:T(8,128)(2,1)S(1)} %get-tuple-element.72), channel_id=1, source_target_pairs={{1,0},{2,1},{3,2},{5,4},{6,5},{7,6},{9,8},{10,9},{11,10},{13,12},{... | collective-permute-start | bytes 786440 | tf_op jit(solution)/shard_map/ppermute | solution.py:581
  286.6 9.3 %collective-permute-start.24 = (bf16[1,2,512,128]{3,2,1,0:T(8,128)(2,1)S(1)}, bf16[1,2,512,128]{3,2,1,0:T(8,128)(2,1)S(1)}, u32[]{:S(2)}, u32[]{:S(2)}) collective-permute-start(bf16[1,2,512,128]{3,2,1,0:T(8,128)(2,1)S(1)} %get-tuple-element.73), channel_id=1, source_target_pairs={{0,1},{1,2},{2,3},{4,5},{5,6},{6,7},{8,9},{9,10},{10,11},{12,13},{... | collective-permute-start | bytes 786440 | tf_op jit(solution)/shard_map/ppermute | solution.py:581
  (29 other events, 170.2 us)

commit v10 on v9

--- a/solution.py
+++ b/solution.py
@@ -350,9 +350,9 @@
         for own, slots in zip(owns, place):
             count = own.shape[2]
             for i, (slot, within) in enumerate(slots):
-                first = pl.multiple_of(front + (slot ^ rank[0]) * length + within, GROUP)
+                first = front + slot * length + within
                 for part in range(2):
-                    strip[part, pl.ds(first, count), :] = own[i, part]
+                    strip[part, first : first + count, :] = own[i, part]
         bins = lax.broadcasted_iota(jnp.int32, (BLOCK, BLOCK), 0).astype(jnp.float32)
         sine[...], cosine[...] = sine_cosine(bins * fractions[...] * (-2.0 * np.pi / WINDOW))
 
@@ -736,23 +736,30 @@
         2,
     ).astype(jnp.bfloat16)
 
-    spread, sheared = [], ()
+    across_rows = lambda x: lax.all_to_all(x, "row", split_axis=0, concat_axis=0, tiled=True)
+
+    spread_a, sheared = [], ()
     for part in range(PARTS):
         left, right = after((lefts[part], rights[part]), sheared)
-        sheared = first(1, part * part_lines, [left], [right], in_order)
-        spread.append(lax.all_to_all(sheared, "row", split_axis=0, concat_axis=0, tiled=True))
+        sheared = first(0, part * part_lines, [left], [right], in_order)
+        spread_a.append(across_rows(sheared))
     lefts, rights = after((lefts, rights), sheared)
-    slots = first(0, 0, lefts, rights, by_rank)
-    shares = [slots[s : s + 1] for s in range(row_devices)]
-    spread, shares = lax.optimization_barrier((spread, shares))
-    pieces = swapped_shares(shares)
-
+    sheared_b = after(first(1, 0, lefts, rights, in_order), spread_a)
+    spread_b = across_rows(sheared_b)
+
+    spread_a = after(spread_a, sheared_b)
     place = [[(b, part * part_lines) for b in range(row_devices)] for part in range(PARTS)]
-    moved_b = second(1, spread, place, in_order, BLOCK)
+    moved_a = second(0, spread_a, place, by_rank, line_count)
+    pieces = swapped_shares([moved_a[s : s + 1] for s in range(row_devices)])
+    spread_b, early = lax.optimization_barrier((spread_b, pieces[1:5]))
+    pieces[1:5] = early
+    place = [[(b, 0) for b in range(row_devices)]]
+    moved_b = second(1, [spread_b], place, in_order, BLOCK)
     whole = lax.all_to_all(moved_b, ("row", "col"), split_axis=0, concat_axis=0, tiled=True)
-    pieces = after(pieces, moved_b)
-    moved_a = second(0, pieces, [[(s, 0)] for s in range(row_devices)], by_rank, line_count)
-    moved_a, whole = lax.optimization_barrier((moved_a, whole))
+
+    tile, low, high = ordered(pieces, halo, by_rank)
+    left, right = from_both_sides(low, high, "col")
+
     whole = whole.reshape(row_devices, column_devices, 2, BLOCK, BLOCK)
     own_lines = lambda x: lax.dynamic_slice_in_dim(x, column_index * BLOCK, BLOCK, 0)
     groups = BLOCK // GROUP
@@ -764,17 +771,8 @@
         own_lines(fraction_rows[1, 1]),
         turned_tables,
     )
-
-    pieces = swapped_shares([moved_a[s : s + 1] for s in range(row_devices)])
-    tile, low, high = ordered(pieces, halo, by_rank)
-    left, right = from_both_sides(low, high, "col")
-
     turned = lax.all_to_all(turned, "col", split_axis=0, concat_axis=0, tiled=True)
-    half_b = travel_first(turned, (), (wave_b, *wave_b_halos), along_rows[1])
-    low, high = from_both_sides(half_b[:1], half_b[-1:], "row")
-    exit_b = travel_second(low, half_b, high, along_columns[1])
-
-    left, right = after((left, right), exit_b)
+
     field_a = shear_tile(
         tile,
         [left],
@@ -793,6 +791,11 @@
     half_a = travel_first(field_a, halos, (), along_rows[0])
     low, high = from_both_sides(half_a[:1], half_a[-1:], "col")
     exit_a = travel_second(low, half_a, high, along_columns[0])
+
+    turned = after(turned, exit_a)
+    half_b = travel_first(turned, (), (wave_b, *wave_b_halos), along_rows[1])
+    low, high = from_both_sides(half_b[:1], half_b[-1:], "row")
+    exit_b = travel_second(low, half_b, high, along_columns[1])
     return exit_a, exit_b
 
 

time: 303 us -> 369 us (1.22); the launches traced: 301 us -> 363 us
  waiting for transfers between devices: 110 us -> 167 us
  starting transfers between devices: 64.4 us -> 68.9 us
    all_to_all x1, waiting for transfers between devices: 0.01 us -> 44.8 us  [on_device(): lax.all_to_all(moved_b, ('row', 'col'), split_axis=0, concat_axis=0, tile...]
    ppermute x12, waiting for transfers between devices: 42.6 us -> 85.2 us  [from_both_sides(): return (lax.ppermute(last, axis, up), lax.ppermute(first, axis, down))]
    ppermute x14 -> x7, waiting for transfers between devices: 60.2 us -> 34.2 us  [swapped_shares(): lax.ppermute(slots[s], 'row', [(i, i ^ s) for i in range(devices)])]
    all_to_all x1, waiting for transfers between devices: 7.22 us -> 0.01 us  [on_device(): lax.all_to_all(turned, 'col', split_axis=0, concat_axis=0, tiled=True)]
    ppermute x14 -> x7, starting transfers between devices: 13 us -> 7.38 us  [swapped_shares(): lax.ppermute(slots[s], 'row', [(i, i ^ s) for i in range(devices)])]
    all_to_all x2 -> x3, starting transfers between devices: 8.51 us -> 13.5 us  [on_device(): lax.all_to_all(x, 'row', split_axis=0, concat_axis=0, tiled=True)]
    ppermute x12, starting transfers between devices: 32.2 us -> 36.2 us  [from_both_sides(): return (lax.ppermute(last, axis, up), lax.ppermute(first, axis, down))]
    unnamed x62 -> x56, local copies, waits for them, and re-layouts: 8.15 us -> 9.9 us
  transfers between devices with their start and end apart: 30 -> 24, of which waited for: 18 -> 16; matrix products, arithmetic and copies ran while one was open for 8% -> 7% of each run, Pallas kernels for 16% -> 15%
where the time goes in v10:
time: 369 us; the launch traced here: 363 us
  waiting for transfers between devices  167 us (45%)
  Pallas kernels  86.9 us (24%)
  starting transfers between devices  68.9 us (19%)
  local copies, waits for them, and re-layouts  31.9 us (9%)
  other arithmetic  5.37 us (1%)
    ppermute x12, waiting for transfers between devices, from_both_sides(): return (lax.ppermute(last, axis, up), lax.ppermute(first, axis, down))  85.2 us
    all_to_all x1, waiting for transfers between devices, on_device(): lax.all_to_all(moved_b, ('row', 'col'), split_axis=0, concat_axis=0, tile...  44.8 us
    ppermute x12, starting transfers between devices, from_both_sides(): return (lax.ppermute(last, axis, up), lax.ppermute(first, axis, down))  36.2 us
    pallas_call x4, Pallas kernels, shear_tile(): pl.pallas_call(kernel, grid_spec=pltpu.PrefetchScalarGridSpec(num_scalar_...  34.8 us
    ppermute x7, waiting for transfers between devices, swapped_shares(): lax.ppermute(slots[s], 'row', [(i, i ^ s) for i in range(devices)])  34.2 us
    pallas_call x2, Pallas kernels, shear_columns(): pl.pallas_call(functools.partial(shear_columns_kernel, front, blocks, len...  16.9 us
    all_to_all x3, starting transfers between devices, on_device(): lax.all_to_all(x, 'row', split_axis=0, concat_axis=0, tiled=True)  13.5 us
    pallas_call x2, Pallas kernels, travel_first(): pl.pallas_call(functools.partial(travel_first_kernel, length, count, len(...  12.3 us
  transfers between devices with their start and end apart: 24, of which 16 were waited for; matrix products, arithmetic and copies ran while one was open for 7% of the time, Pallas kernels for 15%

profile of v10, /device:TPU:2, one launch (start us, length us, event | category | flops | bytes accessed | tf_op | source)
XLA Modules:
  0.0 362.8 jit_solution(11822126096196266514)
XLA Ops:
  5.0 5.5 %collective-permute-start = (bf16[2,256,896]{2,1,0:T(8,128)(2,1)}, bf16[2,256,896]{2,1,0:T(8,128)(2,1)}, u32[]{:S(2)}, u32[]{:S(2)}) collective-permute-start(bf16[2,256,896]{2,1,0:T(8,128)(2,1)} %get-tuple-element.65), channel_id=1, source_target_pairs={{0,1},{1,2},{2,3},{4,5},{5,6},{6,7},{8,9},{9,10},{10,11},{12,13},{... | collective-permute-start | bytes 2752520 | tf_op jit(solution)/shard_map/ppermute | solution.py:581
  19.9 9.0 %collective-permute-done.1.refs_1_.refs_2_ = bf16[2,256,896]{2,1,0:T(8,128)(2,1)S(1)} collective-permute-done((bf16[2,256,896]{2,1,0:T(8,128)(2,1)}, bf16[2,256,896]{2,1,0:T(8,128)(2,1)S(1)}, u32[]{:S(2)}, u32[]{:S(2)}) %collective-permute-start.1) | collective-permute-done | bytes 917536 | tf_op jit(solution)/shard_map/ppermute | solution.py:581
  30.6 6.4 %shear_tile.4 = bf16[8,2,256,128]{3,2,1,0:T(8,128)(2,1)} custom-call(s32[16]{0:T(128)} %get-tuple-element.86.base, s32[1]{0:T(128)} %constant.69.clone.1.rank, bf16[2,256,896]{2,1,0:T(8,128)(2,1)} %collective-permute-done.refs_0_, bf16[2,256,896]{2,1,0:T(8,128)(2,1)} %copy-done.10, bf16[2,512,1024]{2,1,0:T(8,128)(2,1)} %refs_4_.3, f32[2,1,256]{2,1,0:T(1,128)} %bitcast.63, ...), custom_call_target="tpu_custom_call" | custom-call | tf_op jit(solution)/shard_map/shear_tile/pallas_call | solution.py:206
  37.0 4.3 %all-to-all-start = ((bf16[8,2,256,128]{3,2,1,0:T(8,128)(2,1)}), bf16[8,2,256,128]{3,2,1,0:T(8,128)(2,1)S(1)}, u32[]{:S(2)}, u32[]{:S(2)}) async-start(bf16[8,2,256,128]{3,2,1,0:T(8,128)(2,1)} %shear_tile.4), calls=%async_computation | async-start | bytes 2097152 | tf_op jit(solution)/shard_map/all_to_all | solution.py:739
  41.3 9.9 %collective-permute-done.2.refs_0_.refs_1_ = bf16[2,288,896]{2,1,0:T(8,128)(2,1)S(1)} collective-permute-done((bf16[2,288,896]{2,1,0:T(8,128)(2,1)}, bf16[2,288,896]{2,1,0:T(8,128)(2,1)S(1)}, u32[]{:S(2)}, u32[]{:S(2)}) %collective-permute-start.2) | collective-permute-done | bytes 1032224 | tf_op jit(solution)/shard_map/ppermute | solution.py:581
  52.6 6.5 %shear_tile.5 = bf16[8,2,256,128]{3,2,1,0:T(8,128)(2,1)} custom-call(s32[16]{0:T(128)} %get-tuple-element.85.base, s32[1]{0:T(128)} %constant.69.clone.1.rank, bf16[2,288,896]{2,1,0:T(8,128)(2,1)} %copy-done.6, bf16[2,288,896]{2,1,0:T(8,128)(2,1)} %copy-done.7, bf16[2,512,1024]{2,1,0:T(8,128)(2,1)} %refs_4_.3, f32[2,1,256]{2,1,0:T(1,128)} %bitcast.64, ...), custom_call_target="tpu_custom_call" | custom-call | tf_op jit(solution)/shard_map/shear_tile/pallas_call | solution.py:206
  59.1 4.3 %all-to-all-start.1 = ((bf16[8,2,256,128]{3,2,1,0:T(8,128)(2,1)}), bf16[8,2,256,128]{3,2,1,0:T(8,128)(2,1)S(1)}, u32[]{:S(2)}, u32[]{:S(2)}) async-start(bf16[8,2,256,128]{3,2,1,0:T(8,128)(2,1)} %shear_tile.5), calls=%async_computation.1 | async-start | bytes 2097152 | tf_op jit(solution)/shard_map/all_to_all | solution.py:739
  64.7 10.1 %shear_tile.6 = bf16[8,2,512,128]{3,2,1,0:T(8,128)(2,1)} custom-call(s32[32]{0:T(128)} %get-tuple-element.83.base, s32[1]{0:T(128)} %constant.69.clone.1.rank, bf16[2,256,896]{2,1,0:T(8,128)(2,1)} %collective-permute-done.refs_0_, bf16[2,288,896]{2,1,0:T(8,128)(2,1)} %copy-done.6, bf16[2,256,896]{2,1,0:T(8,128)(2,1)} %copy-done.10, ...), custom_call_target="tpu_custom_call" | custom-call | tf_op jit(solution)/shard_map/shear_tile/pallas_call | solution.py:206
  78.3 5.0 %all-to-all-start.2 = ((bf16[8,2,512,128]{3,2,1,0:T(8,128)(2,1)}), bf16[8,2,512,128]{3,2,1,0:T(8,128)(2,1)S(1)}, u32[]{:S(2)}, u32[]{:S(2)}) async-start(bf16[8,2,512,128]{3,2,1,0:T(8,128)(2,1)} %shear_tile.6), calls=%async_computation.2 | async-start | bytes 4194304 | tf_op jit(solution)/shard_map/all_to_all | solution.py:739
  86.5 8.4 %shear_columns.2 = bf16[8,2,512,128]{3,2,1,0:T(8,128)(2,1)} custom-call(s32[1]{0:T(128)} %bitcast.3.base, s32[1]{0:T(128)} %bitcast.1.rank, bf16[8,2,256,128]{3,2,1,0:T(8,128)(2,1)} %copy-done.8, bf16[8,2,256,128]{3,2,1,0:T(8,128)(2,1)} %copy-done.9, s32[1,128]{1,0:T(1,128)} %get-tuple-element.90.refs_2_, f32[1,128]{1,0:T(1,128)} %get-tuple-element.88.refs_3_, ...), custom_call_target="tpu_custom_call" | custom-call | tf_op jit(solution)/shard_map/shear_columns/pallas_call | solution.py:427
  101.3 12.7 %collective-permute-done.7.refs_4_ = bf16[1,2,512,128]{3,2,1,0:T(8,128)(2,1)S(1)} collective-permute-done((bf16[1,2,512,128]{3,2,1,0:T(8,128)(2,1)S(1)}, bf16[1,2,512,128]{3,2,1,0:T(8,128)(2,1)S(1)}, u32[]{:S(2)}, u32[]{:S(2)}) %collective-permute-start.7) | collective-permute-done | bytes 262176 | tf_op jit(solution)/shard_map/ppermute | solution.py:626
  114.1 4.6 %collective-permute-done.5.refs_2_ = bf16[1,2,512,128]{3,2,1,0:T(8,128)(2,1)S(1)} collective-permute-done((bf16[1,2,512,128]{3,2,1,0:T(8,128)(2,1)S(1)}, bf16[1,2,512,128]{3,2,1,0:T(8,128)(2,1)S(1)}, u32[]{:S(2)}, u32[]{:S(2)}) %collective-permute-start.5) | collective-permute-done | bytes 262176 | tf_op jit(solution)/shard_map/ppermute | solution.py:626
  120.0 8.5 %shear_columns.3 = bf16[32,2,128,128]{3,2,1,0:T(8,128)(2,1)} custom-call(s32[1]{0:T(128)} %bitcast.25.base, s32[1]{0:T(128)} %constant.69.clone.1.rank, bf16[8,2,512,128]{3,2,1,0:T(8,128)(2,1)} %copy-done.4, s32[1,128]{1,0:T(1,128)} %get-tuple-element.89.refs_1_, f32[1,128]{1,0:T(1,128)} %get-tuple-element.87.refs_2_, ...), custom_call_target="tpu_custom_call" | custom-call | tf_op jit(solution)/shard_map/shear_columns/pallas_call | solution.py:427
  128.5 7.2 %all-to-all-start.3 = ((bf16[32,2,128,128]{3,2,1,0:T(8,128)(2,1)}), bf16[32,2,128,128]{3,2,1,0:T(8,128)(2,1)S(1)}, u32[]{:S(2)}, u32[]{:S(2)}) async-start(bf16[32,2,128,128]{3,2,1,0:T(8,128)(2,1)} %shear_columns.3), calls=%async_computation.3 | async-start | bytes 4194304 | tf_op jit(solution)/shard_map/all_to_all | solution.py:758
  137.4 44.8 %all-to-all-done.3 = bf16[32,2,128,128]{3,2,1,0:T(8,128)(2,1)S(1)} async-done(((bf16[32,2,128,128]{3,2,1,0:T(8,128)(2,1)}), bf16[32,2,128,128]{3,2,1,0:T(8,128)(2,1)S(1)}, u32[]{:S(2)}, u32[]{:S(2)}) %all-to-all-start.3) | async-done | bytes 2097184 | tf_op jit(solution)/shard_map/all_to_all | solution.py:758
  183.5 9.6 %shear_whole.1 = bf16[4,2,1088,128]{3,2,1,0:T(8,128)(2,1)} custom-call(s32[8]{0:T(128)} %fusion.16.base, bf16[8,4,2,128,128]{4,3,2,1,0:T(8,128)(2,1)} %bitcast.60, f32[1,128]{1,0:T(1,128)} %fusion.18.offsets, f32[1,128]{1,0:T(1,128)} %fusion.19.fractions, bf16[256,256]{1,0:T(8,128)(2,1)} %constant.86.clone.refs_5_.refs_7_.refs_6_.forward, ...), custom_call_target="tpu_custom_call" | custom-call | tf_op jit(solution)/shard_map/shear_whole/pallas_call | solution.py:316
  193.2 4.6 %all-to-all-start.4 = ((bf16[4,2,1088,128]{3,2,1,0:T(8,128)(2,1)}), bf16[4,2,1088,128]{3,2,1,0:T(8,128)(2,1)S(1)}, u32[]{:S(2)}, u32[]{:S(2)}) async-start(bf16[4,2,1088,128]{3,2,1,0:T(8,128)(2,1)} %shear_whole.1), calls=%async_computation.4 | async-start | bytes 4456448 | tf_op jit(solution)/shard_map/all_to_all | solution.py:774
  201.8 4.9 %collective-permute-done.10.refs_7_ = bf16[1,2,512,128]{3,2,1,0:T(8,128)(2,1)S(1)} collective-permute-done((bf16[1,2,512,128]{3,2,1,0:T(8,128)(2,1)}, bf16[1,2,512,128]{3,2,1,0:T(8,128)(2,1)S(1)}, u32[]{:S(2)}, u32[]{:S(2)}) %collective-permute-start.10) | collective-permute-done | bytes 262176 | tf_op jit(solution)/shard_map/ppermute | solution.py:626
  206.7 6.5 %collective-permute-done.9.refs_6_ = bf16[1,2,512,128]{3,2,1,0:T(8,128)(2,1)S(1)} collective-permute-done((bf16[1,2,512,128]{3,2,1,0:T(8,128)(2,1)S(1)}, bf16[1,2,512,128]{3,2,1,0:T(8,128)(2,1)S(1)}, u32[]{:S(2)}, u32[]{:S(2)}) %collective-permute-start.9) | collective-permute-done | bytes 262176 | tf_op jit(solution)/shard_map/ppermute | solution.py:626
  213.3 5.5 %collective-permute-done.8.refs_5_ = bf16[1,2,512,128]{3,2,1,0:T(8,128)(2,1)S(1)} collective-permute-done((bf16[1,2,512,128]{3,2,1,0:T(8,128)(2,1)S(1)}, bf16[1,2,512,128]{3,2,1,0:T(8,128)(2,1)S(1)}, u32[]{:S(2)}, u32[]{:S(2)}) %collective-permute-start.8) | collective-permute-done | bytes 262176 | tf_op jit(solution)/shard_map/ppermute | solution.py:626
  219.5 4.5 %ordered.1 = (bf16[8,2,512,128]{3,2,1,0:T(8,128)(2,1)}, bf16[7,2,512,128]{3,2,1,0:T(8,128)(2,1)}, bf16[7,2,512,128]{3,2,1,0:T(8,128)(2,1)}) custom-call(s32[1]{0:T(128)} %bitcast.1.rank, bf16[1,2,512,128]{3,2,1,0:T(8,128)(2,1)} %get-tuple-element.59.refs_0_, bf16[1,2,512,128]{3,2,1,0:T(8,128)(2,1)} %collective-permute-done.4.refs_1_, ...), custom_call_target="tpu_custom_call" | custom-call | tf_op jit(solution)/shard_map/ordered/pallas_call | solution.py:609
  224.0 4.0 %collective-permute-start.11 = (bf16[7,2,512,128]{3,2,1,0:T(8,128)(2,1)}, bf16[7,2,512,128]{3,2,1,0:T(8,128)(2,1)S(1)}, u32[]{:S(2)}, u32[]{:S(2)}) collective-permute-start(bf16[7,2,512,128]{3,2,1,0:T(8,128)(2,1)} %get-tuple-element.39), channel_id=1, source_target_pairs={{0,1},{1,2},{2,3},{4,5},{5,6},{6,7},{8,9},{9,10},{10,11},{12,13},{... | collective-permute-start | bytes 5505032 | tf_op jit(solution)/shard_map/ppermute | solution.py:581
  230.3 43.4 %collective-permute-done.11.refs_0_ = bf16[7,2,512,128]{3,2,1,0:T(8,128)(2,1)S(1)} collective-permute-done((bf16[7,2,512,128]{3,2,1,0:T(8,128)(2,1)}, bf16[7,2,512,128]{3,2,1,0:T(8,128)(2,1)S(1)}, u32[]{:S(2)}, u32[]{:S(2)}) %collective-permute-start.11) | collective-permute-done | bytes 1835040 | tf_op jit(solution)/shard_map/ppermute | solution.py:581
  273.7 9.0 %collective-permute-done.12.refs_1_ = bf16[7,2,512,128]{3,2,1,0:T(8,128)(2,1)S(1)} collective-permute-done((bf16[7,2,512,128]{3,2,1,0:T(8,128)(2,1)}, bf16[7,2,512,128]{3,2,1,0:T(8,128)(2,1)S(1)}, u32[]{:S(2)}, u32[]{:S(2)}) %collective-permute-start.12) | collective-permute-done | bytes 1835040 | tf_op jit(solution)/shard_map/ppermute | solution.py:581
  283.9 11.8 %shear_tile.7.refs_0_ = bf16[8,2,512,128]{3,2,1,0:T(8,128)(2,1)} custom-call(s32[32]{0:T(128)} %get-tuple-element.84.base, s32[1]{0:T(128)} %constant.69.clone.1.rank, bf16[7,2,512,128]{3,2,1,0:T(8,128)(2,1)} %copy-done.11, bf16[7,2,512,128]{3,2,1,0:T(8,128)(2,1)} %copy-done.12, bf16[2,512,1024]{2,1,0:T(8,128)(2,1)} %refs_2_.5, ...), custom_call_target="tpu_custom_call" | custom-call | tf_op jit(solution)/shard_map/shear_tile/pallas_call | solution.py:206
  302.7 3.2 collective-permute-done.13.refs_1_
  306.5 3.8 %travel_first.2.body = bf16[8,2,512,128]{3,2,1,0:T(8,128)(2,1)} custom-call(bf16[8,2,512,128]{3,2,1,0:T(8,128)(2,1)} %shear_tile.7.refs_0_, bf16[8,2,32,128]{3,2,1,0:T(8,128)(2,1)} %copy-done.23, bf16[8,2,32,128]{3,2,1,0:T(8,128)(2,1)} %copy-done.22, bf16[256,384]{1,0:T(8,128)(2,1)} %copy.22.refs_3_), custom_call_target="tpu_custom_call" | custom-call | tf_op jit(solution)/shard_map/travel_first/pallas_call | solution.py:528
  313.5 10.4 %collective-permute-start.15 = (bf16[1,2,512,128]{3,2,1,0:T(8,128)(2,1)}, bf16[1,2,512,128]{3,2,1,0:T(8,128)(2,1)}, u32[]{:S(2)}, u32[]{:S(2)}) collective-permute-start(bf16[1,2,512,128]{3,2,1,0:T(8,128)(2,1)} %get-tuple-element.49), channel_id=1, source_target_pairs={{0,1},{1,2},{2,3},{4,5},{5,6},{6,7},{8,9},{9,10},{10,11},{12,13},{... | collective-permute-start | bytes 786440 | tf_op jit(solution)/shard_map/ppermute | solution.py:581
  329.6 4.4 %travel_second.2 = bf16[2,512,1024]{2,1,0:T(8,128)(2,1)} custom-call(bf16[1,2,512,128]{3,2,1,0:T(8,128)(2,1)} %collective-permute-done.15.left, bf16[8,2,512,128]{3,2,1,0:T(8,128)(2,1)} %travel_first.2.body, bf16[1,2,512,128]{3,2,1,0:T(8,128)(2,1)} %collective-permute-done.16.right, bf16[768,256]{1,0:T(8,128)(2,1)} %get-tuple-element.67.matrix), custom_call_target="tpu_custom_call" | custom-call | tf_op jit(solution)/shard_map/travel_second/pallas_call | solution.py:561
  335.4 8.4 %travel_first.3.body = bf16[4,2,1024,128]{3,2,1,0:T(8,128)(2,1)} custom-call(bf16[4,2,1088,128]{3,2,1,0:T(8,128)(2,1)} %copy-done.3, bf16[2,1024,512]{2,1,0:T(8,128)(2,1)} %refs_1_.1, bf16[2,32,512]{2,1,0:T(8,128)(2,1)} %slice.247.refs_2_, bf16[2,32,512]{2,1,0:T(8,128)(2,1)} %slice.248.refs_3_, bf16[256,384]{1,0:T(8,128)(2,1)} %copy.23.refs_4_), custom_call_target="tpu_custom_call" | custom-call | tf_op jit(solution)/shard_map/travel_first/pallas_call | solution.py:528
  349.5 5.8 %collective-permute-done.18.right = bf16[1,2,1024,128]{3,2,1,0:T(8,128)(2,1)S(1)} collective-permute-done((bf16[1,2,1024,128]{3,2,1,0:T(8,128)(2,1)S(1)}, bf16[1,2,1024,128]{3,2,1,0:T(8,128)(2,1)S(1)}, u32[]{:S(2)}, u32[]{:S(2)}) %collective-permute-start.18) | collective-permute-done | bytes 524320 | tf_op jit(solution)/shard_map/ppermute | solution.py:581
  358.4 4.4 %travel_second.3 = bf16[2,1024,512]{2,1,0:T(8,128)(2,1)} custom-call(bf16[1,2,1024,128]{3,2,1,0:T(8,128)(2,1)} %copy-done.14, bf16[4,2,1024,128]{3,2,1,0:T(8,128)(2,1)} %travel_first.3.body, bf16[1,2,1024,128]{3,2,1,0:T(8,128)(2,1)} %copy-done.13, bf16[768,256]{1,0:T(8,128)(2,1)} %get-tuple-element.66.matrix), custom_call_target="tpu_custom_call" | custom-call | tf_op jit(solution)/shard_map/travel_second/pallas_call | solution.py:561
  (131 shorter events, 69.0 us)
Async XLA Ops:
  0.6 84.0 %copy-start = (f32[2,1024]{1,0:T(2,128)S(1)}, f32[2,1024]{1,0:T(2,128)}, u32[]{:S(2)}) copy-start(f32[2,1024]{1,0:T(2,128)} %param.22) | copy-start | bytes 24580
  3.7 25.3 %collective-permute-start.1 = (bf16[2,256,896]{2,1,0:T(8,128)(2,1)}, bf16[2,256,896]{2,1,0:T(8,128)(2,1)S(1)}, u32[]{:S(2)}, u32[]{:S(2)}) collective-permute-start(bf16[2,256,896]{2,1,0:T(8,128)(2,1)} %get-tuple-element.64), channel_id=1, source_target_pairs={{1,0},{2,1},{3,2},{5,4},{6,5},{7,6},{9,8},{10,9},{11,10},{13,12},{... | collective-permute-start | bytes 2752520 | tf_op jit(solution)/shard_map/ppermute | solution.py:581
  5.0 25.6 %collective-permute-start = (bf16[2,256,896]{2,1,0:T(8,128)(2,1)}, bf16[2,256,896]{2,1,0:T(8,128)(2,1)}, u32[]{:S(2)}, u32[]{:S(2)}) collective-permute-start(bf16[2,256,896]{2,1,0:T(8,128)(2,1)} %get-tuple-element.65), channel_id=1, source_target_pairs={{0,1},{1,2},{2,3},{4,5},{5,6},{6,7},{8,9},{9,10},{10,11},{12,13},{... | collective-permute-start | bytes 2752520 | tf_op jit(solution)/shard_map/ppermute | solution.py:581
  12.7 38.6 %collective-permute-start.2 = (bf16[2,288,896]{2,1,0:T(8,128)(2,1)}, bf16[2,288,896]{2,1,0:T(8,128)(2,1)S(1)}, u32[]{:S(2)}, u32[]{:S(2)}) collective-permute-start(bf16[2,288,896]{2,1,0:T(8,128)(2,1)} %fusion.2), channel_id=1, source_target_pairs={{0,1},{1,2},{2,3},{4,5},{5,6},{6,7},{8,9},{9,10},{10,11},{12,13},{... | collective-permute-start | bytes 3096584 | tf_op jit(solution)/shard_map/ppermute | solution.py:581
  16.4 34.9 %collective-permute-start.3 = (bf16[2,288,896]{2,1,0:T(8,128)(2,1)}, bf16[2,288,896]{2,1,0:T(8,128)(2,1)S(1)}, u32[]{:S(2)}, u32[]{:S(2)}) collective-permute-start(bf16[2,288,896]{2,1,0:T(8,128)(2,1)} %fusion.3), channel_id=1, source_target_pairs={{1,0},{2,1},{3,2},{5,4},{6,5},{7,6},{9,8},{10,9},{11,10},{13,12},{... | collective-permute-start | bytes 3096584 | tf_op jit(solution)/shard_map/ppermute | solution.py:581
  37.0 22.1 %all-to-all-start = ((bf16[8,2,256,128]{3,2,1,0:T(8,128)(2,1)}), bf16[8,2,256,128]{3,2,1,0:T(8,128)(2,1)S(1)}, u32[]{:S(2)}, u32[]{:S(2)}) async-start(bf16[8,2,256,128]{3,2,1,0:T(8,128)(2,1)} %shear_tile.4), calls=%async_computation | async-start | bytes 2097152 | tf_op jit(solution)/shard_map/all_to_all | solution.py:739
  59.1 15.7 %copy-start.8 = (bf16[8,2,256,128]{3,2,1,0:T(8,128)(2,1)}, bf16[8,2,256,128]{3,2,1,0:T(8,128)(2,1)S(1)}, u32[]{:S(2)}) copy-start(bf16[8,2,256,128]{3,2,1,0:T(8,128)(2,1)S(1)} %all-to-all-done.refs_0_) | copy-start | bytes 3145732
  59.1 18.2 %all-to-all-start.1 = ((bf16[8,2,256,128]{3,2,1,0:T(8,128)(2,1)}), bf16[8,2,256,128]{3,2,1,0:T(8,128)(2,1)S(1)}, u32[]{:S(2)}, u32[]{:S(2)}) async-start(bf16[8,2,256,128]{3,2,1,0:T(8,128)(2,1)} %shear_tile.5), calls=%async_computation.1 | async-start | bytes 2097152 | tf_op jit(solution)/shard_map/all_to_all | solution.py:739
  78.3 40.4 %all-to-all-start.2 = ((bf16[8,2,512,128]{3,2,1,0:T(8,128)(2,1)}), bf16[8,2,512,128]{3,2,1,0:T(8,128)(2,1)S(1)}, u32[]{:S(2)}, u32[]{:S(2)}) async-start(bf16[8,2,512,128]{3,2,1,0:T(8,128)(2,1)} %shear_tile.6), calls=%async_computation.2 | async-start | bytes 4194304 | tf_op jit(solution)/shard_map/all_to_all | solution.py:739
  97.4 16.7 %collective-permute-start.7 = (bf16[1,2,512,128]{3,2,1,0:T(8,128)(2,1)S(1)}, bf16[1,2,512,128]{3,2,1,0:T(8,128)(2,1)S(1)}, u32[]{:S(2)}, u32[]{:S(2)}) collective-permute-start(bf16[1,2,512,128]{3,2,1,0:T(8,128)(2,1)S(1)} %get-tuple-element.55), channel_id=1, source_target_pairs={{0,16},{4,20},{8,24},{12,28},{16,0},{20,4},{24,8},{28,12},{1,17},{... | collective-permute-start | bytes 786440 | tf_op jit(solution)/shard_map/ppermute | solution.py:626
  98.9 15.2 %collective-permute-start.6 = (bf16[1,2,512,128]{3,2,1,0:T(8,128)(2,1)S(1)}, bf16[1,2,512,128]{3,2,1,0:T(8,128)(2,1)S(1)}, u32[]{:S(2)}, u32[]{:S(2)}) collective-permute-start(bf16[1,2,512,128]{3,2,1,0:T(8,128)(2,1)S(1)} %get-tuple-element.56), channel_id=1, source_target_pairs={{0,12},{4,8},{8,4},{12,0},{16,28},{20,24},{24,20},{28,16},{1,13},{... | collective-permute-start | bytes 786440 | tf_op jit(solution)/shard_map/ppermute | solution.py:626
  98.9 19.7 %collective-permute-start.5 = (bf16[1,2,512,128]{3,2,1,0:T(8,128)(2,1)S(1)}, bf16[1,2,512,128]{3,2,1,0:T(8,128)(2,1)S(1)}, u32[]{:S(2)}, u32[]{:S(2)}) collective-permute-start(bf16[1,2,512,128]{3,2,1,0:T(8,128)(2,1)S(1)} %get-tuple-element.57), channel_id=1, source_target_pairs={{0,8},{4,12},{8,0},{12,4},{16,24},{20,28},{24,16},{28,20},{1,9},{5... | collective-permute-start | bytes 786440 | tf_op jit(solution)/shard_map/ppermute | solution.py:626
  100.4 18.3 %collective-permute-start.4 = (bf16[1,2,512,128]{3,2,1,0:T(8,128)(2,1)S(1)}, bf16[1,2,512,128]{3,2,1,0:T(8,128)(2,1)}, u32[]{:S(2)}, u32[]{:S(2)}) collective-permute-start(bf16[1,2,512,128]{3,2,1,0:T(8,128)(2,1)S(1)} %get-tuple-element.58), channel_id=1, source_target_pairs={{0,4},{4,0},{8,12},{12,8},{16,20},{20,16},{24,28},{28,24},{1,5},{5... | collective-permute-start | bytes 786440 | tf_op jit(solution)/shard_map/ppermute | solution.py:626
  114.0 79.1 %copy-start.15 = (bf16[1,2,512,128]{3,2,1,0:T(8,128)(2,1)}, bf16[1,2,512,128]{3,2,1,0:T(8,128)(2,1)S(1)}, u32[]{:S(2)}) copy-start(bf16[1,2,512,128]{3,2,1,0:T(8,128)(2,1)S(1)} %collective-permute-done.7.refs_4_) | copy-start | bytes 786436
  114.1 79.1 %copy-start.16 = (bf16[1,2,512,128]{3,2,1,0:T(8,128)(2,1)}, bf16[1,2,512,128]{3,2,1,0:T(8,128)(2,1)S(1)}, u32[]{:S(2)}) copy-start(bf16[1,2,512,128]{3,2,1,0:T(8,128)(2,1)S(1)} %collective-permute-done.6.refs_3_) | copy-start | bytes 786436
  118.6 74.5 %copy-start.17 = (bf16[1,2,512,128]{3,2,1,0:T(8,128)(2,1)}, bf16[1,2,512,128]{3,2,1,0:T(8,128)(2,1)S(1)}, u32[]{:S(2)}) copy-start(bf16[1,2,512,128]{3,2,1,0:T(8,128)(2,1)S(1)} %collective-permute-done.5.refs_2_) | copy-start | bytes 786436
  128.5 53.7 %all-to-all-start.3 = ((bf16[32,2,128,128]{3,2,1,0:T(8,128)(2,1)}), bf16[32,2,128,128]{3,2,1,0:T(8,128)(2,1)S(1)}, u32[]{:S(2)}, u32[]{:S(2)}) async-start(bf16[32,2,128,128]{3,2,1,0:T(8,128)(2,1)} %shear_columns.3), calls=%async_computation.3 | async-start | bytes 4194304 | tf_op jit(solution)/shard_map/all_to_all | solution.py:758
  193.2 140.9 %all-to-all-start.4 = ((bf16[4,2,1088,128]{3,2,1,0:T(8,128)(2,1)}), bf16[4,2,1088,128]{3,2,1,0:T(8,128)(2,1)S(1)}, u32[]{:S(2)}, u32[]{:S(2)}) async-start(bf16[4,2,1088,128]{3,2,1,0:T(8,128)(2,1)} %shear_whole.1), calls=%async_computation.4 | async-start | bytes 4456448 | tf_op jit(solution)/shard_map/all_to_all | solution.py:774
  197.8 31.5 %copy-start.27 = (f32[2]{0:T(128)S(1)}, f32[2]{0:T(128)}, u32[]{:S(2)}) copy-start(f32[2]{0:T(128)} %param.23) | copy-start | bytes 28
  197.8 31.7 %copy-start.21 = (f32[192,256,1,1]{1,0,2,3:T(8,128)S(1)}, f32[192,256,1,1]{1,0,2,3:T(8,128)}, u32[]{:S(2)}) copy-start(f32[192,256,1,1]{1,0,2,3:T(8,128)} %constant.99) | copy-start | bytes 589828
  197.8 31.7 %copy-start.24 = (f32[256,128]{1,0:T(8,128)S(1)}, f32[256,128]{1,0:T(8,128)}, u32[]{:S(2)}) copy-start(f32[256,128]{1,0:T(8,128)} %constant.91.clone) | copy-start | bytes 393220
  197.8 9.0 %collective-permute-start.10 = (bf16[1,2,512,128]{3,2,1,0:T(8,128)(2,1)}, bf16[1,2,512,128]{3,2,1,0:T(8,128)(2,1)S(1)}, u32[]{:S(2)}, u32[]{:S(2)}) collective-permute-start(bf16[1,2,512,128]{3,2,1,0:T(8,128)(2,1)} %get-tuple-element.52), channel_id=1, source_target_pairs={{0,28},{4,24},{8,20},{12,16},{16,12},{20,8},{24,4},{28,0},{1,29},{... | collective-permute-start | bytes 786440 | tf_op jit(solution)/shard_map/ppermute | solution.py:626
  199.7 13.6 %collective-permute-start.9 = (bf16[1,2,512,128]{3,2,1,0:T(8,128)(2,1)S(1)}, bf16[1,2,512,128]{3,2,1,0:T(8,128)(2,1)S(1)}, u32[]{:S(2)}, u32[]{:S(2)}) collective-permute-start(bf16[1,2,512,128]{3,2,1,0:T(8,128)(2,1)S(1)} %get-tuple-element.53), channel_id=1, source_target_pairs={{0,24},{4,28},{8,16},{12,20},{16,8},{20,12},{24,0},{28,4},{1,25},{... | collective-permute-start | bytes 786440 | tf_op jit(solution)/shard_map/ppermute | solution.py:626
  201.8 17.0 %collective-permute-start.8 = (bf16[1,2,512,128]{3,2,1,0:T(8,128)(2,1)S(1)}, bf16[1,2,512,128]{3,2,1,0:T(8,128)(2,1)S(1)}, u32[]{:S(2)}, u32[]{:S(2)}) collective-permute-start(bf16[1,2,512,128]{3,2,1,0:T(8,128)(2,1)S(1)} %get-tuple-element.54), channel_id=1, source_target_pairs={{0,20},{4,16},{8,28},{12,24},{16,4},{20,0},{24,12},{28,8},{1,21},{... | collective-permute-start | bytes 786440 | tf_op jit(solution)/shard_map/ppermute | solution.py:626
  224.0 49.7 %collective-permute-start.11 = (bf16[7,2,512,128]{3,2,1,0:T(8,128)(2,1)}, bf16[7,2,512,128]{3,2,1,0:T(8,128)(2,1)S(1)}, u32[]{:S(2)}, u32[]{:S(2)}) collective-permute-start(bf16[7,2,512,128]{3,2,1,0:T(8,128)(2,1)} %get-tuple-element.39), channel_id=1, source_target_pairs={{0,1},{1,2},{2,3},{4,5},{5,6},{6,7},{8,9},{9,10},{10,11},{12,13},{... | collective-permute-start | bytes 5505032 | tf_op jit(solution)/shard_map/ppermute | solution.py:581
  228.0 54.7 %collective-permute-start.12 = (bf16[7,2,512,128]{3,2,1,0:T(8,128)(2,1)}, bf16[7,2,512,128]{3,2,1,0:T(8,128)(2,1)S(1)}, u32[]{:S(2)}, u32[]{:S(2)}) collective-permute-start(bf16[7,2,512,128]{3,2,1,0:T(8,128)(2,1)} %get-tuple-element.40), channel_id=1, source_target_pairs={{1,0},{2,1},{3,2},{5,4},{6,5},{7,6},{9,8},{10,9},{11,10},{13,12},{... | collective-permute-start | bytes 5505032 | tf_op jit(solution)/shard_map/ppermute | solution.py:581
  297.4 5.2 %collective-permute-start.14 = (bf16[8,2,32,128]{3,2,1,0:T(8,128)(2,1)}, bf16[8,2,32,128]{3,2,1,0:T(8,128)(2,1)S(1)}, u32[]{:S(2)}, u32[]{:S(2)}) collective-permute-start(bf16[8,2,32,128]{3,2,1,0:T(8,128)(2,1)} %get-tuple-element.50), channel_id=1, source_target_pairs={{4,0},{8,4},{12,8},{16,12},{20,16},{24,20},{28,24},{5,1},{9,5},{13... | collective-permute-start | bytes 393224 | tf_op jit(solution)/shard_map/ppermute | solution.py:581
  299.3 6.5 %collective-permute-start.13 = (bf16[8,2,32,128]{3,2,1,0:T(8,128)(2,1)}, bf16[8,2,32,128]{3,2,1,0:T(8,128)(2,1)S(1)}, u32[]{:S(2)}, u32[]{:S(2)}) collective-permute-start(bf16[8,2,32,128]{3,2,1,0:T(8,128)(2,1)} %get-tuple-element.51), channel_id=1, source_target_pairs={{0,4},{4,8},{8,12},{12,16},{16,20},{20,24},{24,28},{1,5},{5,9},{9,... | collective-permute-start | bytes 393224 | tf_op jit(solution)/shard_map/ppermute | solution.py:581
  312.2 16.5 %collective-permute-start.16 = (bf16[1,2,512,128]{3,2,1,0:T(8,128)(2,1)}, bf16[1,2,512,128]{3,2,1,0:T(8,128)(2,1)}, u32[]{:S(2)}, u32[]{:S(2)}) collective-permute-start(bf16[1,2,512,128]{3,2,1,0:T(8,128)(2,1)} %get-tuple-element.48), channel_id=1, source_target_pairs={{1,0},{2,1},{3,2},{5,4},{6,5},{7,6},{9,8},{10,9},{11,10},{13,12},{... | collective-permute-start | bytes 786440 | tf_op jit(solution)/shard_map/ppermute | solution.py:581
  313.5 16.1 %collective-permute-start.15 = (bf16[1,2,512,128]{3,2,1,0:T(8,128)(2,1)}, bf16[1,2,512,128]{3,2,1,0:T(8,128)(2,1)}, u32[]{:S(2)}, u32[]{:S(2)}) collective-permute-start(bf16[1,2,512,128]{3,2,1,0:T(8,128)(2,1)} %get-tuple-element.49), channel_id=1, source_target_pairs={{0,1},{1,2},{2,3},{4,5},{5,6},{6,7},{8,9},{9,10},{10,11},{12,13},{... | collective-permute-start | bytes 786440 | tf_op jit(solution)/shard_map/ppermute | solution.py:581
  345.1 10.2 %collective-permute-start.18 = (bf16[1,2,1024,128]{3,2,1,0:T(8,128)(2,1)S(1)}, bf16[1,2,1024,128]{3,2,1,0:T(8,128)(2,1)S(1)}, u32[]{:S(2)}, u32[]{:S(2)}) collective-permute-start(bf16[1,2,1024,128]{3,2,1,0:T(8,128)(2,1)S(1)} %get-tuple-element.46), channel_id=1, source_target_pairs={{4,0},{8,4},{12,8},{16,12},{20,16},{24,20},{28,24},{5,1},{9,5},{13... | collective-permute-start | bytes 1572872 | tf_op jit(solution)/shard_map/ppermute | solution.py:581
  347.0 10.5 %collective-permute-start.17 = (bf16[1,2,1024,128]{3,2,1,0:T(8,128)(2,1)S(1)}, bf16[1,2,1024,128]{3,2,1,0:T(8,128)(2,1)S(1)}, u32[]{:S(2)}, u32[]{:S(2)}) collective-permute-start(bf16[1,2,1024,128]{3,2,1,0:T(8,128)(2,1)S(1)} %get-tuple-element.47), channel_id=1, source_target_pairs={{0,4},{4,8},{8,12},{12,16},{16,20},{20,24},{24,28},{1,5},{5,9},{9,... | collective-permute-start | bytes 1572872 | tf_op jit(solution)/shard_map/ppermute | solution.py:581
  (20 other events, 73.0 us)

commit v11 on v9

--- a/solution.py
+++ b/solution.py
@@ -744,15 +744,13 @@
     lefts, rights = after((lefts, rights), sheared)
     slots = first(0, 0, lefts, rights, by_rank)
     shares = [slots[s : s + 1] for s in range(row_devices)]
-    spread, shares = lax.optimization_barrier((spread, shares))
+    spread = after(spread, shares)
     pieces = swapped_shares(shares)
 
     place = [[(b, part * part_lines) for b in range(row_devices)] for part in range(PARTS)]
     moved_b = second(1, spread, place, in_order, BLOCK)
     whole = lax.all_to_all(moved_b, ("row", "col"), split_axis=0, concat_axis=0, tiled=True)
-    pieces = after(pieces, moved_b)
-    moved_a = second(0, pieces, [[(s, 0)] for s in range(row_devices)], by_rank, line_count)
-    moved_a, whole = lax.optimization_barrier((moved_a, whole))
+    whole = after(whole, pieces)
     whole = whole.reshape(row_devices, column_devices, 2, BLOCK, BLOCK)
     own_lines = lambda x: lax.dynamic_slice_in_dim(x, column_index * BLOCK, BLOCK, 0)
     groups = BLOCK // GROUP
@@ -765,12 +763,15 @@
         turned_tables,
     )
 
+    sent = lax.all_to_all(turned, "col", split_axis=0, concat_axis=0, tiled=True)
+
+    pieces = after(pieces, turned)
+    moved_a = second(0, pieces, [[(s, 0)] for s in range(row_devices)], by_rank, line_count)
     pieces = swapped_shares([moved_a[s : s + 1] for s in range(row_devices)])
     tile, low, high = ordered(pieces, halo, by_rank)
     left, right = from_both_sides(low, high, "col")
 
-    turned = lax.all_to_all(turned, "col", split_axis=0, concat_axis=0, tiled=True)
-    half_b = travel_first(turned, (), (wave_b, *wave_b_halos), along_rows[1])
+    half_b = travel_first(sent, (), (wave_b, *wave_b_halos), along_rows[1])
     low, high = from_both_sides(half_b[:1], half_b[-1:], "row")
     exit_b = travel_second(low, half_b, high, along_columns[1])
 

time: 303 us -> 296 us (0.977)
  waiting for transfers between devices: 110 us -> 102 us
    all_to_all x1, waiting for transfers between devices: 7.22 us -> 0.01 us  [on_device(): lax.all_to_all(turned, 'col', split_axis=0, concat_axis=0, tiled=True)]
  transfers between devices with their start and end apart: 30 -> 30, of which waited for: 18 -> 19; matrix products, arithmetic and copies ran while one was open for 8% -> 8% of each run, Pallas kernels for 16% -> 17%
where the time goes in v11:
time: 296 us; the launch traced here: 293 us
  waiting for transfers between devices  102 us (34%)
  Pallas kernels  86.9 us (29%)
  starting transfers between devices  64.5 us (22%)
  local copies, waits for them, and re-layouts  31.3 us (11%)
  other arithmetic  5.27 us (2%)
    ppermute x14, waiting for transfers between devices, swapped_shares(): lax.ppermute(slots[s], 'row', [(i, i ^ s) for i in range(devices)])  60.6 us
    ppermute x12, waiting for transfers between devices, from_both_sides(): return (lax.ppermute(last, axis, up), lax.ppermute(first, axis, down))  41.7 us
    pallas_call x4, Pallas kernels, shear_tile(): pl.pallas_call(kernel, grid_spec=pltpu.PrefetchScalarGridSpec(num_scalar_...  34.9 us
    ppermute x12, starting transfers between devices, from_both_sides(): return (lax.ppermute(last, axis, up), lax.ppermute(first, axis, down))  31.9 us
    pallas_call x2, Pallas kernels, shear_columns(): pl.pallas_call(functools.partial(shear_columns_kernel, front, blocks, len...  16.8 us
    ppermute x14, starting transfers between devices, swapped_shares(): lax.ppermute(slots[s], 'row', [(i, i ^ s) for i in range(devices)])  12.8 us
    pallas_call x2, Pallas kernels, travel_first(): pl.pallas_call(functools.partial(travel_first_kernel, length, count, len(...  12.3 us
    pallas_call x1, Pallas kernels, shear_whole(): pl.pallas_call(functools.partial(shear_whole_kernel, halo, devices, tiles...  9.6 us
  transfers between devices with their start and end apart: 30, of which 19 were waited for; matrix products, arithmetic and copies ran while one was open for 8% of the time, Pallas kernels for 17%

profile of v11, /device:TPU:2, one launch (start us, length us, event | category | flops | bytes accessed | tf_op | source)
XLA Modules:
  0.0 293.3 jit_solution(4131325215440236168)
XLA Ops:
  5.0 5.5 %collective-permute-start = (bf16[2,256,896]{2,1,0:T(8,128)(2,1)}, bf16[2,256,896]{2,1,0:T(8,128)(2,1)}, u32[]{:S(2)}, u32[]{:S(2)}) collective-permute-start(bf16[2,256,896]{2,1,0:T(8,128)(2,1)} %get-tuple-element.81), channel_id=1, source_target_pairs={{0,1},{1,2},{2,3},{4,5},{5,6},{6,7},{8,9},{9,10},{10,11},{12,13},{... | collective-permute-start | bytes 2752520 | tf_op jit(solution)/shard_map/ppermute | solution.py:581
  19.9 9.1 %collective-permute-done.2.refs_1_.refs_2_ = bf16[2,256,896]{2,1,0:T(8,128)(2,1)S(1)} collective-permute-done((bf16[2,256,896]{2,1,0:T(8,128)(2,1)}, bf16[2,256,896]{2,1,0:T(8,128)(2,1)S(1)}, u32[]{:S(2)}, u32[]{:S(2)}) %collective-permute-start.2) | collective-permute-done | bytes 917536 | tf_op jit(solution)/shard_map/ppermute | solution.py:581
  30.6 6.5 %shear_tile.4 = bf16[8,2,256,128]{3,2,1,0:T(8,128)(2,1)} custom-call(s32[16]{0:T(128)} %get-tuple-element.101.base, s32[1]{0:T(128)} %constant.69.clone.1.rank, bf16[2,256,896]{2,1,0:T(8,128)(2,1)} %collective-permute-done.refs_0_, bf16[2,256,896]{2,1,0:T(8,128)(2,1)} %copy-done.9, bf16[2,512,1024]{2,1,0:T(8,128)(2,1)} %refs_4_.2, f32[2,1,256]{2,1,0:T(1,128)} %bitcast.63, ...), custom_call_target="tpu_custom_call" | custom-call | tf_op jit(solution)/shard_map/shear_tile/pallas_call | solution.py:206
  37.1 4.3 %all-to-all-start = ((bf16[8,2,256,128]{3,2,1,0:T(8,128)(2,1)}), bf16[8,2,256,128]{3,2,1,0:T(8,128)(2,1)S(1)}, u32[]{:S(2)}, u32[]{:S(2)}) async-start(bf16[8,2,256,128]{3,2,1,0:T(8,128)(2,1)} %shear_tile.4), calls=%async_computation | async-start | bytes 2097152 | tf_op jit(solution)/shard_map/all_to_all | solution.py:743
  44.0 7.3 %collective-permute-done.1.refs_0_.refs_1_ = bf16[2,288,896]{2,1,0:T(8,128)(2,1)S(1)} collective-permute-done((bf16[2,288,896]{2,1,0:T(8,128)(2,1)}, bf16[2,288,896]{2,1,0:T(8,128)(2,1)S(1)}, u32[]{:S(2)}, u32[]{:S(2)}) %collective-permute-start.1) | collective-permute-done | bytes 1032224 | tf_op jit(solution)/shard_map/ppermute | solution.py:581
  52.6 6.5 %shear_tile.5 = bf16[8,2,256,128]{3,2,1,0:T(8,128)(2,1)} custom-call(s32[16]{0:T(128)} %get-tuple-element.102.base, s32[1]{0:T(128)} %constant.69.clone.1.rank, bf16[2,288,896]{2,1,0:T(8,128)(2,1)} %copy-done.5, bf16[2,288,896]{2,1,0:T(8,128)(2,1)} %copy-done.6, bf16[2,512,1024]{2,1,0:T(8,128)(2,1)} %refs_4_.2, f32[2,1,256]{2,1,0:T(1,128)} %bitcast.64, ...), custom_call_target="tpu_custom_call" | custom-call | tf_op jit(solution)/shard_map/shear_tile/pallas_call | solution.py:206
  59.1 4.3 %all-to-all-start.1 = ((bf16[8,2,256,128]{3,2,1,0:T(8,128)(2,1)}), bf16[8,2,256,128]{3,2,1,0:T(8,128)(2,1)S(1)}, u32[]{:S(2)}, u32[]{:S(2)}) async-start(bf16[8,2,256,128]{3,2,1,0:T(8,128)(2,1)} %shear_tile.5), calls=%async_computation.1 | async-start | bytes 2097152 | tf_op jit(solution)/shard_map/all_to_all | solution.py:743
  65.2 10.1 %shear_tile.6 = bf16[8,2,512,128]{3,2,1,0:T(8,128)(2,1)} custom-call(s32[32]{0:T(128)} %get-tuple-element.99.base, s32[1]{0:T(128)} %bitcast.1.rank, bf16[2,256,896]{2,1,0:T(8,128)(2,1)} %collective-permute-done.refs_0_, bf16[2,288,896]{2,1,0:T(8,128)(2,1)} %copy-done.5, bf16[2,256,896]{2,1,0:T(8,128)(2,1)} %copy-done.9, bf16[2,288,896]{2,1,0:T(8,128)(2,1)} %copy-done.6, ...), custom_call_target="tpu_custom_call" | custom-call | tf_op jit(solution)/shard_map/shear_tile/pallas_call | solution.py:206
  79.1 8.4 %shear_columns.2 = bf16[32,2,128,128]{3,2,1,0:T(8,128)(2,1)} custom-call(s32[1]{0:T(128)} %bitcast.12.base, s32[1]{0:T(128)} %constant.69.clone.1.rank, bf16[8,2,256,128]{3,2,1,0:T(8,128)(2,1)} %copy-done.7, bf16[8,2,256,128]{3,2,1,0:T(8,128)(2,1)} %copy-done.8, s32[1,128]{1,0:T(1,128)} %get-tuple-element.106.refs_2_, f32[1,128]{1,0:T(1,128)} %get-tuple-element.104.refs_3_, ...), custom_call_target="tpu_custom_call" | custom-call | tf_op jit(solution)/shard_map/shear_columns/pallas_call | solution.py:427
  87.5 7.0 %all-to-all-start.2 = ((bf16[32,2,128,128]{3,2,1,0:T(8,128)(2,1)}), bf16[32,2,128,128]{3,2,1,0:T(8,128)(2,1)S(1)}, u32[]{:S(2)}, u32[]{:S(2)}) async-start(bf16[32,2,128,128]{3,2,1,0:T(8,128)(2,1)} %shear_columns.2), calls=%async_computation.2 | async-start | bytes 4194304 | tf_op jit(solution)/shard_map/all_to_all | solution.py:752
  99.0 21.3 %collective-permute-done.10.refs_7_ = bf16[1,2,512,128]{3,2,1,0:T(8,128)(2,1)} collective-permute-done((bf16[1,2,512,128]{3,2,1,0:T(8,128)(2,1)}, bf16[1,2,512,128]{3,2,1,0:T(8,128)(2,1)}, u32[]{:S(2)}, u32[]{:S(2)}) %collective-permute-start.10) | collective-permute-done | bytes 262176 | tf_op jit(solution)/shard_map/ppermute | solution.py:626
  122.2 7.9 %collective-permute-done.9.refs_6_ = bf16[1,2,512,128]{3,2,1,0:T(8,128)(2,1)} collective-permute-done((bf16[1,2,512,128]{3,2,1,0:T(8,128)(2,1)}, bf16[1,2,512,128]{3,2,1,0:T(8,128)(2,1)}, u32[]{:S(2)}, u32[]{:S(2)}) %collective-permute-start.9) | collective-permute-done | bytes 262176 | tf_op jit(solution)/shard_map/ppermute | solution.py:626
  133.6 7.8 %collective-permute-done.7.refs_4_ = bf16[1,2,512,128]{3,2,1,0:T(8,128)(2,1)} collective-permute-done((bf16[1,2,512,128]{3,2,1,0:T(8,128)(2,1)S(1)}, bf16[1,2,512,128]{3,2,1,0:T(8,128)(2,1)}, u32[]{:S(2)}, u32[]{:S(2)}) %collective-permute-start.7) | collective-permute-done | bytes 262176 | tf_op jit(solution)/shard_map/ppermute | solution.py:626
  144.8 9.6 %shear_whole.1 = bf16[4,2,1088,128]{3,2,1,0:T(8,128)(2,1)} custom-call(s32[8]{0:T(128)} %fusion.16.base, bf16[8,4,2,128,128]{4,3,2,1,0:T(8,128)(2,1)} %bitcast.60, f32[1,128]{1,0:T(1,128)} %fusion.18.offsets, f32[1,128]{1,0:T(1,128)} %fusion.19.fractions, bf16[256,256]{1,0:T(8,128)(2,1)} %constant.86.clone.refs_5_.refs_7_.forward.refs_6_, ...), custom_call_target="tpu_custom_call" | custom-call | tf_op jit(solution)/shard_map/shear_whole/pallas_call | solution.py:316
  154.4 4.4 %all-to-all-start.3 = ((bf16[4,2,1088,128]{3,2,1,0:T(8,128)(2,1)}), bf16[4,2,1088,128]{3,2,1,0:T(8,128)(2,1)S(1)}, u32[]{:S(2)}, u32[]{:S(2)}) async-start(bf16[4,2,1088,128]{3,2,1,0:T(8,128)(2,1)} %shear_whole.1), calls=%async_computation.3 | async-start | bytes 4456448 | tf_op jit(solution)/shard_map/all_to_all | solution.py:766
  159.4 8.5 %shear_columns.3 = bf16[8,2,512,128]{3,2,1,0:T(8,128)(2,1)} custom-call(s32[1]{0:T(128)} %bitcast.3.base, s32[1]{0:T(128)} %bitcast.1.rank, bf16[1,2,512,128]{3,2,1,0:T(8,128)(2,1)} %get-tuple-element.39.refs_0_, bf16[1,2,512,128]{3,2,1,0:T(8,128)(2,1)} %collective-permute-done.4.refs_1_, bf16[1,2,512,128]{3,2,1,0:T(8,128)(2,1)} %collective-permute-done.5.refs_2_, ...), custom_call_target="tpu_custom_call" | custom-call | tf_op jit(solution)/shard_map/shear_columns/pallas_call | solution.py:427
  175.1 4.7 %collective-permute-done.17.refs_7_ = bf16[1,2,512,128]{3,2,1,0:T(8,128)(2,1)S(1)} collective-permute-done((bf16[1,2,512,128]{3,2,1,0:T(8,128)(2,1)S(1)}, bf16[1,2,512,128]{3,2,1,0:T(8,128)(2,1)S(1)}, u32[]{:S(2)}, u32[]{:S(2)}) %collective-permute-start.17) | collective-permute-done | bytes 262176 | tf_op jit(solution)/shard_map/ppermute | solution.py:626
  181.1 4.0 %collective-permute-done.16.refs_6_ = bf16[1,2,512,128]{3,2,1,0:T(8,128)(2,1)S(1)} collective-permute-done((bf16[1,2,512,128]{3,2,1,0:T(8,128)(2,1)S(1)}, bf16[1,2,512,128]{3,2,1,0:T(8,128)(2,1)S(1)}, u32[]{:S(2)}, u32[]{:S(2)}) %collective-permute-start.16) | collective-permute-done | bytes 262176 | tf_op jit(solution)/shard_map/ppermute | solution.py:626
  185.4 5.3 %collective-permute-done.15.refs_5_ = bf16[1,2,512,128]{3,2,1,0:T(8,128)(2,1)S(1)} collective-permute-done((bf16[1,2,512,128]{3,2,1,0:T(8,128)(2,1)S(1)}, bf16[1,2,512,128]{3,2,1,0:T(8,128)(2,1)S(1)}, u32[]{:S(2)}, u32[]{:S(2)}) %collective-permute-start.15) | collective-permute-done | bytes 262176 | tf_op jit(solution)/shard_map/ppermute | solution.py:626
  190.7 5.7 %collective-permute-done.14.refs_4_ = bf16[1,2,512,128]{3,2,1,0:T(8,128)(2,1)S(1)} collective-permute-done((bf16[1,2,512,128]{3,2,1,0:T(8,128)(2,1)S(1)}, bf16[1,2,512,128]{3,2,1,0:T(8,128)(2,1)S(1)}, u32[]{:S(2)}, u32[]{:S(2)}) %collective-permute-start.14) | collective-permute-done | bytes 262176 | tf_op jit(solution)/shard_map/ppermute | solution.py:626
  197.4 4.5 %ordered.1 = (bf16[8,2,512,128]{3,2,1,0:T(8,128)(2,1)}, bf16[7,2,512,128]{3,2,1,0:T(8,128)(2,1)}, bf16[7,2,512,128]{3,2,1,0:T(8,128)(2,1)}) custom-call(s32[1]{0:T(128)} %bitcast.1.rank, bf16[1,2,512,128]{3,2,1,0:T(8,128)(2,1)} %get-tuple-element.67.refs_0_, bf16[1,2,512,128]{3,2,1,0:T(8,128)(2,1)} %copy-done.21, bf16[1,2,512,128]{3,2,1,0:T(8,128)(2,1)} %copy-done.20, ...), custom_call_target="tpu_custom_call" | custom-call | tf_op jit(solution)/shard_map/ordered/pallas_call | solution.py:609
  201.9 5.2 %collective-permute-start.18 = (bf16[7,2,512,128]{3,2,1,0:T(8,128)(2,1)}, bf16[7,2,512,128]{3,2,1,0:T(8,128)(2,1)}, u32[]{:S(2)}, u32[]{:S(2)}) collective-permute-start(bf16[7,2,512,128]{3,2,1,0:T(8,128)(2,1)} %get-tuple-element.47), channel_id=1, source_target_pairs={{0,1},{1,2},{2,3},{4,5},{5,6},{6,7},{8,9},{9,10},{10,11},{12,13},{... | collective-permute-start | bytes 5505032 | tf_op jit(solution)/shard_map/ppermute | solution.py:581
  214.3 8.4 %travel_first.2.body = bf16[4,2,1024,128]{3,2,1,0:T(8,128)(2,1)} custom-call(bf16[4,2,1088,128]{3,2,1,0:T(8,128)(2,1)} %copy-done.3, bf16[2,1024,512]{2,1,0:T(8,128)(2,1)} %refs_1_.1, bf16[2,32,512]{2,1,0:T(8,128)(2,1)} %slice.278.refs_2_, bf16[2,32,512]{2,1,0:T(8,128)(2,1)} %slice.279.refs_3_, bf16[256,384]{1,0:T(8,128)(2,1)} %copy.22.refs_4_), custom_call_target="tpu_custom_call" | custom-call | tf_op jit(solution)/shard_map/travel_first/pallas_call | solution.py:528
  229.7 5.2 %collective-permute-done.21.right = bf16[1,2,1024,128]{3,2,1,0:T(8,128)(2,1)S(1)} collective-permute-done((bf16[1,2,1024,128]{3,2,1,0:T(8,128)(2,1)S(1)}, bf16[1,2,1024,128]{3,2,1,0:T(8,128)(2,1)S(1)}, u32[]{:S(2)}, u32[]{:S(2)}) %collective-permute-start.21) | collective-permute-done | bytes 524320 | tf_op jit(solution)/shard_map/ppermute | solution.py:581
  237.5 4.4 %travel_second.2 = bf16[2,1024,512]{2,1,0:T(8,128)(2,1)} custom-call(bf16[1,2,1024,128]{3,2,1,0:T(8,128)(2,1)} %copy-done.11, bf16[4,2,1024,128]{3,2,1,0:T(8,128)(2,1)} %travel_first.2.body, bf16[1,2,1024,128]{3,2,1,0:T(8,128)(2,1)} %copy-done.10, bf16[768,256]{1,0:T(8,128)(2,1)} %get-tuple-element.83.matrix), custom_call_target="tpu_custom_call" | custom-call | tf_op jit(solution)/shard_map/travel_second/pallas_call | solution.py:561
  241.9 3.7 %collective-permute-done.18.refs_0_ = bf16[7,2,512,128]{3,2,1,0:T(8,128)(2,1)} collective-permute-done((bf16[7,2,512,128]{3,2,1,0:T(8,128)(2,1)}, bf16[7,2,512,128]{3,2,1,0:T(8,128)(2,1)}, u32[]{:S(2)}, u32[]{:S(2)}) %collective-permute-start.18) | collective-permute-done | bytes 1835040 | tf_op jit(solution)/shard_map/ppermute | solution.py:581
  245.7 5.3 %collective-permute-done.19.refs_1_ = bf16[7,2,512,128]{3,2,1,0:T(8,128)(2,1)} collective-permute-done((bf16[7,2,512,128]{3,2,1,0:T(8,128)(2,1)}, bf16[7,2,512,128]{3,2,1,0:T(8,128)(2,1)}, u32[]{:S(2)}, u32[]{:S(2)}) %collective-permute-start.19) | collective-permute-done | bytes 1835040 | tf_op jit(solution)/shard_map/ppermute | solution.py:581
  251.0 11.8 %shear_tile.7.refs_0_ = bf16[8,2,512,128]{3,2,1,0:T(8,128)(2,1)} custom-call(s32[32]{0:T(128)} %get-tuple-element.100.base, s32[1]{0:T(128)} %constant.69.clone.1.rank, bf16[7,2,512,128]{3,2,1,0:T(8,128)(2,1)} %collective-permute-done.18.refs_0_, bf16[7,2,512,128]{3,2,1,0:T(8,128)(2,1)} %collective-permute-done.19.refs_1_, bf16[2,512,1024]{2,1,0:T(8,128)(2,1)} %refs_2_.5, ...), custom_call_target="tpu_custom_call" | custom-call | tf_op jit(solution)/shard_map/shear_tile/pallas_call | solution.py:206
  272.7 3.9 %travel_first.3.body = bf16[8,2,512,128]{3,2,1,0:T(8,128)(2,1)} custom-call(bf16[8,2,512,128]{3,2,1,0:T(8,128)(2,1)} %shear_tile.7.refs_0_, bf16[8,2,32,128]{3,2,1,0:T(8,128)(2,1)} %copy-done.26, bf16[8,2,32,128]{3,2,1,0:T(8,128)(2,1)} %copy-done.25, bf16[256,384]{1,0:T(8,128)(2,1)} %copy.23.refs_3_), custom_call_target="tpu_custom_call" | custom-call | tf_op jit(solution)/shard_map/travel_first/pallas_call | solution.py:528
  278.9 4.6 %collective-permute-start.24 = (bf16[1,2,512,128]{3,2,1,0:T(8,128)(2,1)S(1)}, bf16[1,2,512,128]{3,2,1,0:T(8,128)(2,1)S(1)}, u32[]{:S(2)}, u32[]{:S(2)}) collective-permute-start(bf16[1,2,512,128]{3,2,1,0:T(8,128)(2,1)S(1)} %get-tuple-element.55), channel_id=1, source_target_pairs={{0,1},{1,2},{2,3},{4,5},{5,6},{6,7},{8,9},{9,10},{10,11},{12,13},{... | collective-permute-start | bytes 786440 | tf_op jit(solution)/shard_map/ppermute | solution.py:581
  283.5 3.5 %collective-permute-done.25.right = bf16[1,2,512,128]{3,2,1,0:T(8,128)(2,1)S(1)} collective-permute-done((bf16[1,2,512,128]{3,2,1,0:T(8,128)(2,1)S(1)}, bf16[1,2,512,128]{3,2,1,0:T(8,128)(2,1)S(1)}, u32[]{:S(2)}, u32[]{:S(2)}) %collective-permute-start.25) | collective-permute-done | bytes 262176 | tf_op jit(solution)/shard_map/ppermute | solution.py:581
  288.9 4.4 %travel_second.3 = bf16[2,512,1024]{2,1,0:T(8,128)(2,1)} custom-call(bf16[1,2,512,128]{3,2,1,0:T(8,128)(2,1)} %copy-done.23, bf16[8,2,512,128]{3,2,1,0:T(8,128)(2,1)} %travel_first.3.body, bf16[1,2,512,128]{3,2,1,0:T(8,128)(2,1)} %copy-done.22, bf16[768,256]{1,0:T(8,128)(2,1)} %get-tuple-element.82.matrix), custom_call_target="tpu_custom_call" | custom-call | tf_op jit(solution)/shard_map/travel_second/pallas_call | solution.py:561
  (150 shorter events, 78.1 us)
Async XLA Ops:
  0.6 42.8 %copy-start = (f32[2,1024]{1,0:T(2,128)S(1)}, f32[2,1024]{1,0:T(2,128)}, u32[]{:S(2)}) copy-start(f32[2,1024]{1,0:T(2,128)} %param.22) | copy-start | bytes 24580
  3.7 25.3 %collective-permute-start.2 = (bf16[2,256,896]{2,1,0:T(8,128)(2,1)}, bf16[2,256,896]{2,1,0:T(8,128)(2,1)S(1)}, u32[]{:S(2)}, u32[]{:S(2)}) collective-permute-start(bf16[2,256,896]{2,1,0:T(8,128)(2,1)} %get-tuple-element.80), channel_id=1, source_target_pairs={{1,0},{2,1},{3,2},{5,4},{6,5},{7,6},{9,8},{10,9},{11,10},{13,12},{... | collective-permute-start | bytes 2752520 | tf_op jit(solution)/shard_map/ppermute | solution.py:581
  5.0 25.6 %collective-permute-start = (bf16[2,256,896]{2,1,0:T(8,128)(2,1)}, bf16[2,256,896]{2,1,0:T(8,128)(2,1)}, u32[]{:S(2)}, u32[]{:S(2)}) collective-permute-start(bf16[2,256,896]{2,1,0:T(8,128)(2,1)} %get-tuple-element.81), channel_id=1, source_target_pairs={{0,1},{1,2},{2,3},{4,5},{5,6},{6,7},{8,9},{9,10},{10,11},{12,13},{... | collective-permute-start | bytes 2752520 | tf_op jit(solution)/shard_map/ppermute | solution.py:581
  12.7 38.6 %collective-permute-start.1 = (bf16[2,288,896]{2,1,0:T(8,128)(2,1)}, bf16[2,288,896]{2,1,0:T(8,128)(2,1)S(1)}, u32[]{:S(2)}, u32[]{:S(2)}) collective-permute-start(bf16[2,288,896]{2,1,0:T(8,128)(2,1)} %fusion.2), channel_id=1, source_target_pairs={{0,1},{1,2},{2,3},{4,5},{5,6},{6,7},{8,9},{9,10},{10,11},{12,13},{... | collective-permute-start | bytes 3096584 | tf_op jit(solution)/shard_map/ppermute | solution.py:581
  16.4 34.9 %collective-permute-start.3 = (bf16[2,288,896]{2,1,0:T(8,128)(2,1)}, bf16[2,288,896]{2,1,0:T(8,128)(2,1)S(1)}, u32[]{:S(2)}, u32[]{:S(2)}) collective-permute-start(bf16[2,288,896]{2,1,0:T(8,128)(2,1)} %fusion.3), channel_id=1, source_target_pairs={{1,0},{2,1},{3,2},{5,4},{6,5},{7,6},{9,8},{10,9},{11,10},{13,12},{... | collective-permute-start | bytes 3096584 | tf_op jit(solution)/shard_map/ppermute | solution.py:581
  37.1 22.0 %all-to-all-start = ((bf16[8,2,256,128]{3,2,1,0:T(8,128)(2,1)}), bf16[8,2,256,128]{3,2,1,0:T(8,128)(2,1)S(1)}, u32[]{:S(2)}, u32[]{:S(2)}) async-start(bf16[8,2,256,128]{3,2,1,0:T(8,128)(2,1)} %shear_tile.4), calls=%async_computation | async-start | bytes 2097152 | tf_op jit(solution)/shard_map/all_to_all | solution.py:743
  59.1 19.0 %all-to-all-start.1 = ((bf16[8,2,256,128]{3,2,1,0:T(8,128)(2,1)}), bf16[8,2,256,128]{3,2,1,0:T(8,128)(2,1)S(1)}, u32[]{:S(2)}, u32[]{:S(2)}) async-start(bf16[8,2,256,128]{3,2,1,0:T(8,128)(2,1)} %shear_tile.5), calls=%async_computation.1 | async-start | bytes 2097152 | tf_op jit(solution)/shard_map/all_to_all | solution.py:743
  87.5 56.0 %all-to-all-start.2 = ((bf16[32,2,128,128]{3,2,1,0:T(8,128)(2,1)}), bf16[32,2,128,128]{3,2,1,0:T(8,128)(2,1)S(1)}, u32[]{:S(2)}, u32[]{:S(2)}) async-start(bf16[32,2,128,128]{3,2,1,0:T(8,128)(2,1)} %shear_columns.2), calls=%async_computation.2 | async-start | bytes 4194304 | tf_op jit(solution)/shard_map/all_to_all | solution.py:752
  94.4 25.8 %collective-permute-start.10 = (bf16[1,2,512,128]{3,2,1,0:T(8,128)(2,1)}, bf16[1,2,512,128]{3,2,1,0:T(8,128)(2,1)}, u32[]{:S(2)}, u32[]{:S(2)}) collective-permute-start(bf16[1,2,512,128]{3,2,1,0:T(8,128)(2,1)} %get-tuple-element.68), channel_id=1, source_target_pairs={{0,28},{4,24},{8,20},{12,16},{16,12},{20,8},{24,4},{28,0},{1,29},{... | collective-permute-start | bytes 786440 | tf_op jit(solution)/shard_map/ppermute | solution.py:626
  95.7 34.4 %collective-permute-start.9 = (bf16[1,2,512,128]{3,2,1,0:T(8,128)(2,1)}, bf16[1,2,512,128]{3,2,1,0:T(8,128)(2,1)}, u32[]{:S(2)}, u32[]{:S(2)}) collective-permute-start(bf16[1,2,512,128]{3,2,1,0:T(8,128)(2,1)} %get-tuple-element.69), channel_id=1, source_target_pairs={{0,24},{4,28},{8,16},{12,20},{16,8},{20,12},{24,0},{28,4},{1,25},{... | collective-permute-start | bytes 786440 | tf_op jit(solution)/shard_map/ppermute | solution.py:626
  97.2 36.4 %collective-permute-start.8 = (bf16[1,2,512,128]{3,2,1,0:T(8,128)(2,1)}, bf16[1,2,512,128]{3,2,1,0:T(8,128)(2,1)}, u32[]{:S(2)}, u32[]{:S(2)}) collective-permute-start(bf16[1,2,512,128]{3,2,1,0:T(8,128)(2,1)} %get-tuple-element.70), channel_id=1, source_target_pairs={{0,20},{4,16},{8,28},{12,24},{16,4},{20,0},{24,12},{28,8},{1,21},{... | collective-permute-start | bytes 786440 | tf_op jit(solution)/shard_map/ppermute | solution.py:626
  98.3 43.0 %collective-permute-start.7 = (bf16[1,2,512,128]{3,2,1,0:T(8,128)(2,1)S(1)}, bf16[1,2,512,128]{3,2,1,0:T(8,128)(2,1)}, u32[]{:S(2)}, u32[]{:S(2)}) collective-permute-start(bf16[1,2,512,128]{3,2,1,0:T(8,128)(2,1)S(1)} %copy-done.14), channel_id=1, source_target_pairs={{0,16},{4,20},{8,24},{12,28},{16,0},{20,4},{24,8},{28,12},{1,17},{... | collective-permute-start | bytes 786440 | tf_op jit(solution)/shard_map/ppermute | solution.py:626
  98.9 42.4 %collective-permute-start.6 = (bf16[1,2,512,128]{3,2,1,0:T(8,128)(2,1)S(1)}, bf16[1,2,512,128]{3,2,1,0:T(8,128)(2,1)}, u32[]{:S(2)}, u32[]{:S(2)}) collective-permute-start(bf16[1,2,512,128]{3,2,1,0:T(8,128)(2,1)S(1)} %copy-done.13), channel_id=1, source_target_pairs={{0,12},{4,8},{8,4},{12,0},{16,28},{20,24},{24,20},{28,16},{1,13},{... | collective-permute-start | bytes 786440 | tf_op jit(solution)/shard_map/ppermute | solution.py:626
  120.3 23.2 %collective-permute-start.5 = (bf16[1,2,512,128]{3,2,1,0:T(8,128)(2,1)S(1)}, bf16[1,2,512,128]{3,2,1,0:T(8,128)(2,1)}, u32[]{:S(2)}, u32[]{:S(2)}) collective-permute-start(bf16[1,2,512,128]{3,2,1,0:T(8,128)(2,1)S(1)} %copy-done.12), channel_id=1, source_target_pairs={{0,8},{4,12},{8,0},{12,4},{16,24},{20,28},{24,16},{28,20},{1,9},{5... | collective-permute-start | bytes 786440 | tf_op jit(solution)/shard_map/ppermute | solution.py:626
  130.2 13.3 %collective-permute-start.4 = (bf16[1,2,512,128]{3,2,1,0:T(8,128)(2,1)S(1)}, bf16[1,2,512,128]{3,2,1,0:T(8,128)(2,1)}, u32[]{:S(2)}, u32[]{:S(2)}) collective-permute-start(bf16[1,2,512,128]{3,2,1,0:T(8,128)(2,1)S(1)} %get-tuple-element.74), channel_id=1, source_target_pairs={{0,4},{4,0},{8,12},{12,8},{16,20},{20,16},{24,28},{28,24},{1,5},{5... | collective-permute-start | bytes 786440 | tf_op jit(solution)/shard_map/ppermute | solution.py:626
  154.4 58.6 %all-to-all-start.3 = ((bf16[4,2,1088,128]{3,2,1,0:T(8,128)(2,1)}), bf16[4,2,1088,128]{3,2,1,0:T(8,128)(2,1)S(1)}, u32[]{:S(2)}, u32[]{:S(2)}) async-start(bf16[4,2,1088,128]{3,2,1,0:T(8,128)(2,1)} %shear_whole.1), calls=%async_computation.3 | async-start | bytes 4456448 | tf_op jit(solution)/shard_map/all_to_all | solution.py:766
  170.3 38.2 %copy-start.27 = (f32[256,128]{1,0:T(8,128)S(1)}, f32[256,128]{1,0:T(8,128)}, u32[]{:S(2)}) copy-start(f32[256,128]{1,0:T(8,128)} %constant.91.clone) | copy-start | bytes 393220
  170.3 9.6 %collective-permute-start.17 = (bf16[1,2,512,128]{3,2,1,0:T(8,128)(2,1)S(1)}, bf16[1,2,512,128]{3,2,1,0:T(8,128)(2,1)S(1)}, u32[]{:S(2)}, u32[]{:S(2)}) collective-permute-start(bf16[1,2,512,128]{3,2,1,0:T(8,128)(2,1)S(1)} %get-tuple-element.60), channel_id=1, source_target_pairs={{0,28},{4,24},{8,20},{12,16},{16,12},{20,8},{24,4},{28,0},{1,29},{... | collective-permute-start | bytes 786440 | tf_op jit(solution)/shard_map/ppermute | solution.py:626
  171.5 13.6 %collective-permute-start.16 = (bf16[1,2,512,128]{3,2,1,0:T(8,128)(2,1)S(1)}, bf16[1,2,512,128]{3,2,1,0:T(8,128)(2,1)S(1)}, u32[]{:S(2)}, u32[]{:S(2)}) collective-permute-start(bf16[1,2,512,128]{3,2,1,0:T(8,128)(2,1)S(1)} %get-tuple-element.61), channel_id=1, source_target_pairs={{0,24},{4,28},{8,16},{12,20},{16,8},{20,12},{24,0},{28,4},{1,25},{... | collective-permute-start | bytes 786440 | tf_op jit(solution)/shard_map/ppermute | solution.py:626
  172.5 18.2 %collective-permute-start.15 = (bf16[1,2,512,128]{3,2,1,0:T(8,128)(2,1)S(1)}, bf16[1,2,512,128]{3,2,1,0:T(8,128)(2,1)S(1)}, u32[]{:S(2)}, u32[]{:S(2)}) collective-permute-start(bf16[1,2,512,128]{3,2,1,0:T(8,128)(2,1)S(1)} %get-tuple-element.62), channel_id=1, source_target_pairs={{0,20},{4,16},{8,28},{12,24},{16,4},{20,0},{24,12},{28,8},{1,21},{... | collective-permute-start | bytes 786440 | tf_op jit(solution)/shard_map/ppermute | solution.py:626
  174.2 22.2 %collective-permute-start.14 = (bf16[1,2,512,128]{3,2,1,0:T(8,128)(2,1)S(1)}, bf16[1,2,512,128]{3,2,1,0:T(8,128)(2,1)S(1)}, u32[]{:S(2)}, u32[]{:S(2)}) collective-permute-start(bf16[1,2,512,128]{3,2,1,0:T(8,128)(2,1)S(1)} %get-tuple-element.63), channel_id=1, source_target_pairs={{0,16},{4,20},{8,24},{12,28},{16,0},{20,4},{24,8},{28,12},{1,17},{... | collective-permute-start | bytes 786440 | tf_op jit(solution)/shard_map/ppermute | solution.py:626
  174.7 21.8 %collective-permute-start.13 = (bf16[1,2,512,128]{3,2,1,0:T(8,128)(2,1)S(1)}, bf16[1,2,512,128]{3,2,1,0:T(8,128)(2,1)S(1)}, u32[]{:S(2)}, u32[]{:S(2)}) collective-permute-start(bf16[1,2,512,128]{3,2,1,0:T(8,128)(2,1)S(1)} %get-tuple-element.64), channel_id=1, source_target_pairs={{0,12},{4,8},{8,4},{12,0},{16,28},{20,24},{24,20},{28,16},{1,13},{... | collective-permute-start | bytes 786440 | tf_op jit(solution)/shard_map/ppermute | solution.py:626
  179.9 16.6 %collective-permute-start.12 = (bf16[1,2,512,128]{3,2,1,0:T(8,128)(2,1)S(1)}, bf16[1,2,512,128]{3,2,1,0:T(8,128)(2,1)S(1)}, u32[]{:S(2)}, u32[]{:S(2)}) collective-permute-start(bf16[1,2,512,128]{3,2,1,0:T(8,128)(2,1)S(1)} %get-tuple-element.65), channel_id=1, source_target_pairs={{0,8},{4,12},{8,0},{12,4},{16,24},{20,28},{24,16},{28,20},{1,9},{5... | collective-permute-start | bytes 786440 | tf_op jit(solution)/shard_map/ppermute | solution.py:626
  185.1 11.4 %collective-permute-start.11 = (bf16[1,2,512,128]{3,2,1,0:T(8,128)(2,1)S(1)}, bf16[1,2,512,128]{3,2,1,0:T(8,128)(2,1)S(1)}, u32[]{:S(2)}, u32[]{:S(2)}) collective-permute-start(bf16[1,2,512,128]{3,2,1,0:T(8,128)(2,1)S(1)} %get-tuple-element.66), channel_id=1, source_target_pairs={{0,4},{4,0},{8,12},{12,8},{16,20},{20,16},{24,28},{28,24},{1,5},{5... | collective-permute-start | bytes 786440 | tf_op jit(solution)/shard_map/ppermute | solution.py:626
  201.9 43.7 %collective-permute-start.18 = (bf16[7,2,512,128]{3,2,1,0:T(8,128)(2,1)}, bf16[7,2,512,128]{3,2,1,0:T(8,128)(2,1)}, u32[]{:S(2)}, u32[]{:S(2)}) collective-permute-start(bf16[7,2,512,128]{3,2,1,0:T(8,128)(2,1)} %get-tuple-element.47), channel_id=1, source_target_pairs={{0,1},{1,2},{2,3},{4,5},{5,6},{6,7},{8,9},{9,10},{10,11},{12,13},{... | collective-permute-start | bytes 5505032 | tf_op jit(solution)/shard_map/ppermute | solution.py:581
  207.1 43.9 %collective-permute-start.19 = (bf16[7,2,512,128]{3,2,1,0:T(8,128)(2,1)}, bf16[7,2,512,128]{3,2,1,0:T(8,128)(2,1)}, u32[]{:S(2)}, u32[]{:S(2)}) collective-permute-start(bf16[7,2,512,128]{3,2,1,0:T(8,128)(2,1)} %get-tuple-element.48), channel_id=1, source_target_pairs={{1,0},{2,1},{3,2},{5,4},{6,5},{7,6},{9,8},{10,9},{11,10},{13,12},{... | collective-permute-start | bytes 5505032 | tf_op jit(solution)/shard_map/ppermute | solution.py:581
  224.1 10.9 %collective-permute-start.21 = (bf16[1,2,1024,128]{3,2,1,0:T(8,128)(2,1)S(1)}, bf16[1,2,1024,128]{3,2,1,0:T(8,128)(2,1)S(1)}, u32[]{:S(2)}, u32[]{:S(2)}) collective-permute-start(bf16[1,2,1024,128]{3,2,1,0:T(8,128)(2,1)S(1)} %get-tuple-element.58), channel_id=1, source_target_pairs={{4,0},{8,4},{12,8},{16,12},{20,16},{24,20},{28,24},{5,1},{9,5},{13... | collective-permute-start | bytes 1572872 | tf_op jit(solution)/shard_map/ppermute | solution.py:581
  226.2 10.5 %collective-permute-start.20 = (bf16[1,2,1024,128]{3,2,1,0:T(8,128)(2,1)S(1)}, bf16[1,2,1024,128]{3,2,1,0:T(8,128)(2,1)S(1)}, u32[]{:S(2)}, u32[]{:S(2)}) collective-permute-start(bf16[1,2,1024,128]{3,2,1,0:T(8,128)(2,1)S(1)} %get-tuple-element.59), channel_id=1, source_target_pairs={{0,4},{4,8},{8,12},{12,16},{16,20},{20,24},{24,28},{1,5},{5,9},{9,... | collective-permute-start | bytes 1572872 | tf_op jit(solution)/shard_map/ppermute | solution.py:581
  263.8 5.2 %collective-permute-start.23 = (bf16[8,2,32,128]{3,2,1,0:T(8,128)(2,1)S(1)}, bf16[8,2,32,128]{3,2,1,0:T(8,128)(2,1)S(1)}, u32[]{:S(2)}, u32[]{:S(2)}) collective-permute-start(bf16[8,2,32,128]{3,2,1,0:T(8,128)(2,1)S(1)} %get-tuple-element.56), channel_id=1, source_target_pairs={{4,0},{8,4},{12,8},{16,12},{20,16},{24,20},{28,24},{5,1},{9,5},{13... | collective-permute-start | bytes 393224 | tf_op jit(solution)/shard_map/ppermute | solution.py:581
  265.7 6.3 %collective-permute-start.22 = (bf16[8,2,32,128]{3,2,1,0:T(8,128)(2,1)S(1)}, bf16[8,2,32,128]{3,2,1,0:T(8,128)(2,1)S(1)}, u32[]{:S(2)}, u32[]{:S(2)}) collective-permute-start(bf16[8,2,32,128]{3,2,1,0:T(8,128)(2,1)S(1)} %get-tuple-element.57), channel_id=1, source_target_pairs={{0,4},{4,8},{8,12},{12,16},{16,20},{20,24},{24,28},{1,5},{5,9},{9,... | collective-permute-start | bytes 393224 | tf_op jit(solution)/shard_map/ppermute | solution.py:581
  277.6 9.4 %collective-permute-start.25 = (bf16[1,2,512,128]{3,2,1,0:T(8,128)(2,1)S(1)}, bf16[1,2,512,128]{3,2,1,0:T(8,128)(2,1)S(1)}, u32[]{:S(2)}, u32[]{:S(2)}) collective-permute-start(bf16[1,2,512,128]{3,2,1,0:T(8,128)(2,1)S(1)} %get-tuple-element.54), channel_id=1, source_target_pairs={{1,0},{2,1},{3,2},{5,4},{6,5},{7,6},{9,8},{10,9},{11,10},{13,12},{... | collective-permute-start | bytes 786440 | tf_op jit(solution)/shard_map/ppermute | solution.py:581
  278.9 9.3 %collective-permute-start.24 = (bf16[1,2,512,128]{3,2,1,0:T(8,128)(2,1)S(1)}, bf16[1,2,512,128]{3,2,1,0:T(8,128)(2,1)S(1)}, u32[]{:S(2)}, u32[]{:S(2)}) collective-permute-start(bf16[1,2,512,128]{3,2,1,0:T(8,128)(2,1)S(1)} %get-tuple-element.55), channel_id=1, source_target_pairs={{0,1},{1,2},{2,3},{4,5},{5,6},{6,7},{8,9},{9,10},{10,11},{12,13},{... | collective-permute-start | bytes 786440 | tf_op jit(solution)/shard_map/ppermute | solution.py:581
  (29 other events, 195.2 us)

commit v12 on v11

--- a/solution.py
+++ b/solution.py
@@ -486,7 +486,7 @@
 
 def travel_first_kernel(length, count, sent, *refs):
     if sent:
-        body, top, bottom, matrix, out, field = refs
+        body, top, bottom, matrix, out, low, high, field = refs
         for chunk in range(count):
             across = slice(chunk * BLOCK, (chunk + 1) * BLOCK)
             for part in range(2):
@@ -494,7 +494,7 @@
                 field[part, MARGIN : MARGIN + length, across] = body[chunk, part]
                 field[part, MARGIN + length :, across] = bottom[chunk, part]
     else:
-        body, wave, wave_top, wave_bottom, matrix, out, field = refs
+        body, wave, wave_top, wave_bottom, matrix, out, low, high, field = refs
         pieces = [(0, MARGIN, wave_top, 0)]
         pieces += [(MARGIN + first, BLOCK, wave, first) for first in range(0, length, BLOCK)]
         pieces += [(MARGIN + length, MARGIN, wave_bottom, 0)]
@@ -518,6 +518,20 @@
                     part * BLOCK : (part + 1) * BLOCK, across
                 ]
 
+    def outermost(chunk, edge, first):
+        for part in range(2):
+            for m in range(0, length, BLOCK):
+                turned = out[chunk, part, m : m + BLOCK, :].astype(jnp.float32).T
+                edge[part, :, m : m + BLOCK] = turned[first : first + MARGIN].astype(jnp.bfloat16)
+
+    @pl.when(pl.program_id(0) == 0)
+    def _():
+        outermost(0, low, 0)
+
+    @pl.when(pl.program_id(0) == pl.num_programs(0) - 1)
+    def _():
+        outermost(count - 1, high, BLOCK - MARGIN)
+
 
 def travel_first(body, halos, waves, matrix):
     chunks = body.shape[0]
@@ -531,8 +545,10 @@
         in_specs=[chunk_spec(x) for x in (body, *halos)]
         + [wide_spec(x) for x in waves]
         + [pl.BlockSpec(matrix.shape, lambda i: (0, 0))],
-        out_specs=pl.BlockSpec((count, 2, length, BLOCK), lambda i: (i, 0, 0, 0)),
-        out_shape=jax.ShapeDtypeStruct((chunks, 2, length, BLOCK), jnp.bfloat16),
+        out_specs=[pl.BlockSpec((count, 2, length, BLOCK), lambda i: (i, 0, 0, 0))]
+        + [pl.BlockSpec((2, MARGIN, length), lambda i: (0, 0, 0))] * 2,
+        out_shape=[jax.ShapeDtypeStruct((chunks, 2, length, BLOCK), jnp.bfloat16)]
+        + [jax.ShapeDtypeStruct((2, MARGIN, length), jnp.bfloat16)] * 2,
         scratch_shapes=[pltpu.VMEM((2, length + 2 * MARGIN, count * BLOCK), jnp.bfloat16)],
         compiler_params=pltpu.CompilerParams(vmem_limit_bytes=VMEM_LIMIT),
         name="travel_first",
@@ -540,7 +556,14 @@
 
 
 def travel_second_kernel(chunks, rows, left, body, right, matrix, out):
-    parts = [[left[0, p]] + [body[m, p] for m in range(chunks)] + [right[0, p]] for p in range(2)]
+    empty = jnp.zeros((BLOCK - MARGIN, rows), jnp.float32)
+    upright = lambda *pieces: jnp.concatenate(pieces, 0).T.astype(jnp.bfloat16)
+    parts = [
+        [upright(empty, left[p].astype(jnp.float32))]
+        + [body[m, p] for m in range(chunks)]
+        + [upright(right[p].astype(jnp.float32), empty)]
+        for p in range(2)
+    ]
     windows = [
         jnp.concatenate(parts[0][m : m + 3] + parts[1][m : m + 3], 1) for m in range(chunks)
     ]
@@ -557,7 +580,7 @@
 def travel_second(left, body, right, matrix):
     chunks, _, length, _ = body.shape
     rows = length // STEPS if length % (STEPS * BLOCK) == 0 else length
-    edge = pl.BlockSpec((1, 2, rows, BLOCK), lambda i: (0, 0, i, 0))
+    edge = pl.BlockSpec((2, MARGIN, rows), lambda i: (0, 0, i))
     return pl.pallas_call(
         functools.partial(travel_second_kernel, chunks, rows),
         grid=(length // rows,),
@@ -771,8 +794,8 @@
     tile, low, high = ordered(pieces, halo, by_rank)
     left, right = from_both_sides(low, high, "col")
 
-    half_b = travel_first(sent, (), (wave_b, *wave_b_halos), along_rows[1])
-    low, high = from_both_sides(half_b[:1], half_b[-1:], "row")
+    half_b, low, high = travel_first(sent, (), (wave_b, *wave_b_halos), along_rows[1])
+    low, high = from_both_sides(low, high, "row")
     exit_b = travel_second(low, half_b, high, along_columns[1])
 
     left, right = after((left, right), exit_b)
@@ -791,8 +814,8 @@
         wave_a,
     )
     halos = from_both_sides(field_a[:, :, :MARGIN], field_a[:, :, -MARGIN:], "row")
-    half_a = travel_first(field_a, halos, (), along_rows[0])
-    low, high = from_both_sides(half_a[:1], half_a[-1:], "col")
+    half_a, low, high = travel_first(field_a, halos, (), along_rows[0])
+    low, high = from_both_sides(low, high, "col")
     exit_a = travel_second(low, half_a, high, along_columns[0])
     return exit_a, exit_b
 

time: 296 us -> 293 us (0.990)
  transfers between devices with their start and end apart: 30 -> 30, of which waited for: 19 -> 18; matrix products, arithmetic and copies ran while one was open for 8% -> 8% of each run, Pallas kernels for 17% -> 17%
where the time goes in v12:
time: 293 us; the launch traced here: 290 us
  waiting for transfers between devices  103 us (35%)
  Pallas kernels  87.3 us (30%)
  starting transfers between devices  63.2 us (22%)
  local copies, waits for them, and re-layouts  28.7 us (10%)
  other arithmetic  5.27 us (2%)
    ppermute x14, waiting for transfers between devices, swapped_shares(): lax.ppermute(slots[s], 'row', [(i, i ^ s) for i in range(devices)])  60.7 us
    ppermute x12, waiting for transfers between devices, from_both_sides(): return (lax.ppermute(last, axis, up), lax.ppermute(first, axis, down))  42.1 us
    pallas_call x4, Pallas kernels, shear_tile(): pl.pallas_call(kernel, grid_spec=pltpu.PrefetchScalarGridSpec(num_scalar_...  34.9 us
    ppermute x12, starting transfers between devices, from_both_sides(): return (lax.ppermute(last, axis, up), lax.ppermute(first, axis, down))  30.6 us
    pallas_call x2, Pallas kernels, shear_columns(): pl.pallas_call(functools.partial(shear_columns_kernel, front, blocks, len...  16.8 us
    ppermute x14, starting transfers between devices, swapped_shares(): lax.ppermute(slots[s], 'row', [(i, i ^ s) for i in range(devices)])  12.7 us
    pallas_call x2, Pallas kernels, travel_first(): pl.pallas_call(functools.partial(travel_first_kernel, length, count, len(...  12.7 us
    pallas_call x1, Pallas kernels, shear_whole(): pl.pallas_call(functools.partial(shear_whole_kernel, halo, devices, tiles...  9.6 us
  transfers between devices with their start and end apart: 30, of which 18 were waited for; matrix products, arithmetic and copies ran while one was open for 8% of the time, Pallas kernels for 17%

profile of v12, /device:TPU:2, one launch (start us, length us, event | category | flops | bytes accessed | tf_op | source)
XLA Modules:
  0.0 290.3 jit_solution(3835996262396281939)
XLA Ops:
  5.0 5.5 %collective-permute-start = (bf16[2,256,896]{2,1,0:T(8,128)(2,1)}, bf16[2,256,896]{2,1,0:T(8,128)(2,1)}, u32[]{:S(2)}, u32[]{:S(2)}) collective-permute-start(bf16[2,256,896]{2,1,0:T(8,128)(2,1)} %get-tuple-element.89), channel_id=1, source_target_pairs={{0,1},{1,2},{2,3},{4,5},{5,6},{6,7},{8,9},{9,10},{10,11},{12,13},{... | collective-permute-start | bytes 2752520 | tf_op jit(solution)/shard_map/ppermute | solution.py:604
  19.9 9.1 %collective-permute-done.2.refs_1_.refs_2_ = bf16[2,256,896]{2,1,0:T(8,128)(2,1)S(1)} collective-permute-done((bf16[2,256,896]{2,1,0:T(8,128)(2,1)}, bf16[2,256,896]{2,1,0:T(8,128)(2,1)S(1)}, u32[]{:S(2)}, u32[]{:S(2)}) %collective-permute-start.2) | collective-permute-done | bytes 917536 | tf_op jit(solution)/shard_map/ppermute | solution.py:604
  30.6 6.5 %shear_tile.4 = bf16[8,2,256,128]{3,2,1,0:T(8,128)(2,1)} custom-call(s32[16]{0:T(128)} %get-tuple-element.109.base, s32[1]{0:T(128)} %constant.69.clone.1.rank, bf16[2,256,896]{2,1,0:T(8,128)(2,1)} %collective-permute-done.refs_0_, bf16[2,256,896]{2,1,0:T(8,128)(2,1)} %copy-done.9, bf16[2,512,1024]{2,1,0:T(8,128)(2,1)} %refs_4_.2, f32[2,1,256]{2,1,0:T(1,128)} %bitcast.63, ...), custom_call_target="tpu_custom_call" | custom-call | tf_op jit(solution)/shard_map/shear_tile/pallas_call | solution.py:206
  37.1 4.3 %all-to-all-start = ((bf16[8,2,256,128]{3,2,1,0:T(8,128)(2,1)}), bf16[8,2,256,128]{3,2,1,0:T(8,128)(2,1)S(1)}, u32[]{:S(2)}, u32[]{:S(2)}) async-start(bf16[8,2,256,128]{3,2,1,0:T(8,128)(2,1)} %shear_tile.4), calls=%async_computation | async-start | bytes 2097152 | tf_op jit(solution)/shard_map/all_to_all | solution.py:766
  44.0 7.3 %collective-permute-done.1.refs_0_.refs_1_ = bf16[2,288,896]{2,1,0:T(8,128)(2,1)S(1)} collective-permute-done((bf16[2,288,896]{2,1,0:T(8,128)(2,1)}, bf16[2,288,896]{2,1,0:T(8,128)(2,1)S(1)}, u32[]{:S(2)}, u32[]{:S(2)}) %collective-permute-start.1) | collective-permute-done | bytes 1032224 | tf_op jit(solution)/shard_map/ppermute | solution.py:604
  52.6 6.5 %shear_tile.5 = bf16[8,2,256,128]{3,2,1,0:T(8,128)(2,1)} custom-call(s32[16]{0:T(128)} %get-tuple-element.110.base, s32[1]{0:T(128)} %constant.69.clone.1.rank, bf16[2,288,896]{2,1,0:T(8,128)(2,1)} %copy-done.5, bf16[2,288,896]{2,1,0:T(8,128)(2,1)} %copy-done.6, bf16[2,512,1024]{2,1,0:T(8,128)(2,1)} %refs_4_.2, f32[2,1,256]{2,1,0:T(1,128)} %bitcast.64, ...), custom_call_target="tpu_custom_call" | custom-call | tf_op jit(solution)/shard_map/shear_tile/pallas_call | solution.py:206
  59.1 4.3 %all-to-all-start.1 = ((bf16[8,2,256,128]{3,2,1,0:T(8,128)(2,1)}), bf16[8,2,256,128]{3,2,1,0:T(8,128)(2,1)S(1)}, u32[]{:S(2)}, u32[]{:S(2)}) async-start(bf16[8,2,256,128]{3,2,1,0:T(8,128)(2,1)} %shear_tile.5), calls=%async_computation.1 | async-start | bytes 2097152 | tf_op jit(solution)/shard_map/all_to_all | solution.py:766
  65.2 10.1 %shear_tile.6 = bf16[8,2,512,128]{3,2,1,0:T(8,128)(2,1)} custom-call(s32[32]{0:T(128)} %get-tuple-element.107.base, s32[1]{0:T(128)} %bitcast.1.rank, bf16[2,256,896]{2,1,0:T(8,128)(2,1)} %collective-permute-done.refs_0_, bf16[2,288,896]{2,1,0:T(8,128)(2,1)} %copy-done.5, bf16[2,256,896]{2,1,0:T(8,128)(2,1)} %copy-done.9, bf16[2,288,896]{2,1,0:T(8,128)(2,1)} %copy-done.6, ...), custom_call_target="tpu_custom_call" | custom-call | tf_op jit(solution)/shard_map/shear_tile/pallas_call | solution.py:206
  79.1 8.4 %shear_columns.2 = bf16[32,2,128,128]{3,2,1,0:T(8,128)(2,1)} custom-call(s32[1]{0:T(128)} %bitcast.12.base, s32[1]{0:T(128)} %constant.69.clone.1.rank, bf16[8,2,256,128]{3,2,1,0:T(8,128)(2,1)} %copy-done.7, bf16[8,2,256,128]{3,2,1,0:T(8,128)(2,1)} %copy-done.8, s32[1,128]{1,0:T(1,128)} %get-tuple-element.114.refs_2_, f32[1,128]{1,0:T(1,128)} %get-tuple-element.112.refs_3_, ...), custom_call_target="tpu_custom_call" | custom-call | tf_op jit(solution)/shard_map/shear_columns/pallas_call | solution.py:427
  87.5 6.9 %all-to-all-start.2 = ((bf16[32,2,128,128]{3,2,1,0:T(8,128)(2,1)}), bf16[32,2,128,128]{3,2,1,0:T(8,128)(2,1)S(1)}, u32[]{:S(2)}, u32[]{:S(2)}) async-start(bf16[32,2,128,128]{3,2,1,0:T(8,128)(2,1)} %shear_columns.2), calls=%async_computation.2 | async-start | bytes 4194304 | tf_op jit(solution)/shard_map/all_to_all | solution.py:775
  99.0 21.3 %collective-permute-done.10.refs_7_ = bf16[1,2,512,128]{3,2,1,0:T(8,128)(2,1)} collective-permute-done((bf16[1,2,512,128]{3,2,1,0:T(8,128)(2,1)}, bf16[1,2,512,128]{3,2,1,0:T(8,128)(2,1)}, u32[]{:S(2)}, u32[]{:S(2)}) %collective-permute-start.10) | collective-permute-done | bytes 262176 | tf_op jit(solution)/shard_map/ppermute | solution.py:649
  122.2 7.9 %collective-permute-done.9.refs_6_ = bf16[1,2,512,128]{3,2,1,0:T(8,128)(2,1)} collective-permute-done((bf16[1,2,512,128]{3,2,1,0:T(8,128)(2,1)}, bf16[1,2,512,128]{3,2,1,0:T(8,128)(2,1)}, u32[]{:S(2)}, u32[]{:S(2)}) %collective-permute-start.9) | collective-permute-done | bytes 262176 | tf_op jit(solution)/shard_map/ppermute | solution.py:649
  133.6 7.8 %collective-permute-done.7.refs_4_ = bf16[1,2,512,128]{3,2,1,0:T(8,128)(2,1)} collective-permute-done((bf16[1,2,512,128]{3,2,1,0:T(8,128)(2,1)S(1)}, bf16[1,2,512,128]{3,2,1,0:T(8,128)(2,1)}, u32[]{:S(2)}, u32[]{:S(2)}) %collective-permute-start.7) | collective-permute-done | bytes 262176 | tf_op jit(solution)/shard_map/ppermute | solution.py:649
  144.8 9.6 %shear_whole.1 = bf16[4,2,1088,128]{3,2,1,0:T(8,128)(2,1)} custom-call(s32[8]{0:T(128)} %fusion.16.base, bf16[8,4,2,128,128]{4,3,2,1,0:T(8,128)(2,1)} %bitcast.60, f32[1,128]{1,0:T(1,128)} %fusion.18.offsets, f32[1,128]{1,0:T(1,128)} %fusion.19.fractions, bf16[256,256]{1,0:T(8,128)(2,1)} %constant.86.clone.refs_5_.refs_7_.forward.refs_6_, ...), custom_call_target="tpu_custom_call" | custom-call | tf_op jit(solution)/shard_map/shear_whole/pallas_call | solution.py:316
  154.4 4.4 %all-to-all-start.3 = ((bf16[4,2,1088,128]{3,2,1,0:T(8,128)(2,1)}), bf16[4,2,1088,128]{3,2,1,0:T(8,128)(2,1)S(1)}, u32[]{:S(2)}, u32[]{:S(2)}) async-start(bf16[4,2,1088,128]{3,2,1,0:T(8,128)(2,1)} %shear_whole.1), calls=%async_computation.3 | async-start | bytes 4456448 | tf_op jit(solution)/shard_map/all_to_all | solution.py:789
  159.4 8.5 %shear_columns.3 = bf16[8,2,512,128]{3,2,1,0:T(8,128)(2,1)} custom-call(s32[1]{0:T(128)} %bitcast.3.base, s32[1]{0:T(128)} %bitcast.1.rank, bf16[1,2,512,128]{3,2,1,0:T(8,128)(2,1)} %get-tuple-element.45.refs_0_, bf16[1,2,512,128]{3,2,1,0:T(8,128)(2,1)} %collective-permute-done.4.refs_1_, bf16[1,2,512,128]{3,2,1,0:T(8,128)(2,1)} %collective-permute-done.5.refs_2_, ...), custom_call_target="tpu_custom_call" | custom-call | tf_op jit(solution)/shard_map/shear_columns/pallas_call | solution.py:427
  175.1 4.8 %collective-permute-done.17.refs_7_ = bf16[1,2,512,128]{3,2,1,0:T(8,128)(2,1)S(1)} collective-permute-done((bf16[1,2,512,128]{3,2,1,0:T(8,128)(2,1)S(1)}, bf16[1,2,512,128]{3,2,1,0:T(8,128)(2,1)S(1)}, u32[]{:S(2)}, u32[]{:S(2)}) %collective-permute-start.17) | collective-permute-done | bytes 262176 | tf_op jit(solution)/shard_map/ppermute | solution.py:649
  181.1 4.0 %collective-permute-done.16.refs_6_ = bf16[1,2,512,128]{3,2,1,0:T(8,128)(2,1)S(1)} collective-permute-done((bf16[1,2,512,128]{3,2,1,0:T(8,128)(2,1)S(1)}, bf16[1,2,512,128]{3,2,1,0:T(8,128)(2,1)S(1)}, u32[]{:S(2)}, u32[]{:S(2)}) %collective-permute-start.16) | collective-permute-done | bytes 262176 | tf_op jit(solution)/shard_map/ppermute | solution.py:649
  185.3 5.5 %collective-permute-done.15.refs_5_ = bf16[1,2,512,128]{3,2,1,0:T(8,128)(2,1)S(1)} collective-permute-done((bf16[1,2,512,128]{3,2,1,0:T(8,128)(2,1)S(1)}, bf16[1,2,512,128]{3,2,1,0:T(8,128)(2,1)S(1)}, u32[]{:S(2)}, u32[]{:S(2)}) %collective-permute-start.15) | collective-permute-done | bytes 262176 | tf_op jit(solution)/shard_map/ppermute | solution.py:649
  190.7 5.7 %collective-permute-done.14.refs_4_ = bf16[1,2,512,128]{3,2,1,0:T(8,128)(2,1)S(1)} collective-permute-done((bf16[1,2,512,128]{3,2,1,0:T(8,128)(2,1)S(1)}, bf16[1,2,512,128]{3,2,1,0:T(8,128)(2,1)S(1)}, u32[]{:S(2)}, u32[]{:S(2)}) %collective-permute-start.14) | collective-permute-done | bytes 262176 | tf_op jit(solution)/shard_map/ppermute | solution.py:649
  197.4 4.5 %ordered.1 = (bf16[8,2,512,128]{3,2,1,0:T(8,128)(2,1)}, bf16[7,2,512,128]{3,2,1,0:T(8,128)(2,1)}, bf16[7,2,512,128]{3,2,1,0:T(8,128)(2,1)}) custom-call(s32[1]{0:T(128)} %bitcast.1.rank, bf16[1,2,512,128]{3,2,1,0:T(8,128)(2,1)} %get-tuple-element.75.refs_0_, bf16[1,2,512,128]{3,2,1,0:T(8,128)(2,1)} %copy-done.19, bf16[1,2,512,128]{3,2,1,0:T(8,128)(2,1)} %copy-done.18, ...), custom_call_target="tpu_custom_call" | custom-call | tf_op jit(solution)/shard_map/ordered/pallas_call | solution.py:632
  201.9 5.2 %collective-permute-start.18 = (bf16[7,2,512,128]{3,2,1,0:T(8,128)(2,1)}, bf16[7,2,512,128]{3,2,1,0:T(8,128)(2,1)}, u32[]{:S(2)}, u32[]{:S(2)}) collective-permute-start(bf16[7,2,512,128]{3,2,1,0:T(8,128)(2,1)} %get-tuple-element.53), channel_id=1, source_target_pairs={{0,1},{1,2},{2,3},{4,5},{5,6},{6,7},{8,9},{9,10},{10,11},{12,13},{... | collective-permute-start | bytes 5505032 | tf_op jit(solution)/shard_map/ppermute | solution.py:604
  214.6 8.5 %travel_first.2 = (bf16[4,2,1024,128]{3,2,1,0:T(8,128)(2,1)}, bf16[2,32,1024]{2,1,0:T(8,128)(2,1)}, bf16[2,32,1024]{2,1,0:T(8,128)(2,1)}) custom-call(bf16[4,2,1088,128]{3,2,1,0:T(8,128)(2,1)} %copy-done.3, bf16[2,1024,512]{2,1,0:T(8,128)(2,1)} %refs_1_.1, bf16[2,32,512]{2,1,0:T(8,128)(2,1)} %slice.262.refs_2_, bf16[2,32,512]{2,1,0:T(8,128)(2,1)} %slice.263.refs_3_, ...), custom_call_target="tpu_custom_call" | custom-call | tf_op jit(solution)/shard_map/travel_first/pallas_call | solution.py:542
  225.1 3.9 %collective-permute-start.21 = (bf16[2,32,1024]{2,1,0:T(8,128)(2,1)}, bf16[2,32,1024]{2,1,0:T(8,128)(2,1)S(1)}, u32[]{:S(2)}, u32[]{:S(2)}) collective-permute-start(bf16[2,32,1024]{2,1,0:T(8,128)(2,1)} %get-tuple-element.57), channel_id=1, source_target_pairs={{4,0},{8,4},{12,8},{16,12},{20,16},{24,20},{28,24},{5,1},{9,5},{13... | collective-permute-start | bytes 393224 | tf_op jit(solution)/shard_map/ppermute | solution.py:604
  232.2 4.4 %travel_second.2 = bf16[2,1024,512]{2,1,0:T(8,128)(2,1)} custom-call(bf16[2,32,1024]{2,1,0:T(8,128)(2,1)} %copy-done.22, bf16[4,2,1024,128]{3,2,1,0:T(8,128)(2,1)} %get-tuple-element.56.body, bf16[2,32,1024]{2,1,0:T(8,128)(2,1)} %copy-done.24, bf16[768,256]{1,0:T(8,128)(2,1)} %get-tuple-element.91.matrix), custom_call_target="tpu_custom_call" | custom-call | tf_op jit(solution)/shard_map/travel_second/pallas_call | solution.py:584
  236.6 9.0 %collective-permute-done.18.refs_0_ = bf16[7,2,512,128]{3,2,1,0:T(8,128)(2,1)} collective-permute-done((bf16[7,2,512,128]{3,2,1,0:T(8,128)(2,1)}, bf16[7,2,512,128]{3,2,1,0:T(8,128)(2,1)}, u32[]{:S(2)}, u32[]{:S(2)}) %collective-permute-start.18) | collective-permute-done | bytes 1835040 | tf_op jit(solution)/shard_map/ppermute | solution.py:604
  245.6 5.3 %collective-permute-done.19.refs_1_ = bf16[7,2,512,128]{3,2,1,0:T(8,128)(2,1)} collective-permute-done((bf16[7,2,512,128]{3,2,1,0:T(8,128)(2,1)}, bf16[7,2,512,128]{3,2,1,0:T(8,128)(2,1)}, u32[]{:S(2)}, u32[]{:S(2)}) %collective-permute-start.19) | collective-permute-done | bytes 1835040 | tf_op jit(solution)/shard_map/ppermute | solution.py:604
  251.0 11.8 %shear_tile.7.refs_0_ = bf16[8,2,512,128]{3,2,1,0:T(8,128)(2,1)} custom-call(s32[32]{0:T(128)} %get-tuple-element.108.base, s32[1]{0:T(128)} %constant.69.clone.1.rank, bf16[7,2,512,128]{3,2,1,0:T(8,128)(2,1)} %collective-permute-done.18.refs_0_, bf16[7,2,512,128]{3,2,1,0:T(8,128)(2,1)} %collective-permute-done.19.refs_1_, bf16[2,512,1024]{2,1,0:T(8,128)(2,1)} %refs_2_.5, ...), custom_call_target="tpu_custom_call" | custom-call | tf_op jit(solution)/shard_map/shear_tile/pallas_call | solution.py:206
  269.0 3.1 %collective-permute-done.22.refs_1_ = bf16[8,2,32,128]{3,2,1,0:T(8,128)(2,1)S(1)} collective-permute-done((bf16[8,2,32,128]{3,2,1,0:T(8,128)(2,1)S(1)}, bf16[8,2,32,128]{3,2,1,0:T(8,128)(2,1)S(1)}, u32[]{:S(2)}, u32[]{:S(2)}) %collective-permute-start.22) | collective-permute-done | bytes 131104 | tf_op jit(solution)/shard_map/ppermute | solution.py:604
  272.7 4.1 %travel_first.3 = (bf16[8,2,512,128]{3,2,1,0:T(8,128)(2,1)}, bf16[2,32,512]{2,1,0:T(8,128)(2,1)}, bf16[2,32,512]{2,1,0:T(8,128)(2,1)}) custom-call(bf16[8,2,512,128]{3,2,1,0:T(8,128)(2,1)} %shear_tile.7.refs_0_, bf16[8,2,32,128]{3,2,1,0:T(8,128)(2,1)} %copy-done.23, bf16[8,2,32,128]{3,2,1,0:T(8,128)(2,1)} %copy-done.21, bf16[256,384]{1,0:T(8,128)(2,1)} %copy.23.refs_3_), custom_call_target="tpu_custom_call" | custom-call | tf_op jit(solution)/shard_map/travel_first/pallas_call | solution.py:542
  281.1 4.2 %collective-permute-done.25.right = bf16[2,32,512]{2,1,0:T(8,128)(2,1)S(1)} collective-permute-done((bf16[2,32,512]{2,1,0:T(8,128)(2,1)}, bf16[2,32,512]{2,1,0:T(8,128)(2,1)S(1)}, u32[]{:S(2)}, u32[]{:S(2)}) %collective-permute-start.25) | collective-permute-done | bytes 65568 | tf_op jit(solution)/shard_map/ppermute | solution.py:604
  285.9 4.4 %travel_second.3 = bf16[2,512,1024]{2,1,0:T(8,128)(2,1)} custom-call(bf16[2,32,512]{2,1,0:T(8,128)(2,1)} %copy-done.26, bf16[8,2,512,128]{3,2,1,0:T(8,128)(2,1)} %get-tuple-element.62.body, bf16[2,32,512]{2,1,0:T(8,128)(2,1)} %copy-done.27, bf16[768,256]{1,0:T(8,128)(2,1)} %get-tuple-element.90.matrix), custom_call_target="tpu_custom_call" | custom-call | tf_op jit(solution)/shard_map/travel_second/pallas_call | solution.py:584
  (148 shorter events, 71.5 us)
Async XLA Ops:
  0.6 42.8 %copy-start = (f32[2,1024]{1,0:T(2,128)S(1)}, f32[2,1024]{1,0:T(2,128)}, u32[]{:S(2)}) copy-start(f32[2,1024]{1,0:T(2,128)} %param.22) | copy-start | bytes 24580
  3.7 25.3 %collective-permute-start.2 = (bf16[2,256,896]{2,1,0:T(8,128)(2,1)}, bf16[2,256,896]{2,1,0:T(8,128)(2,1)S(1)}, u32[]{:S(2)}, u32[]{:S(2)}) collective-permute-start(bf16[2,256,896]{2,1,0:T(8,128)(2,1)} %get-tuple-element.88), channel_id=1, source_target_pairs={{1,0},{2,1},{3,2},{5,4},{6,5},{7,6},{9,8},{10,9},{11,10},{13,12},{... | collective-permute-start | bytes 2752520 | tf_op jit(solution)/shard_map/ppermute | solution.py:604
  5.0 25.6 %collective-permute-start = (bf16[2,256,896]{2,1,0:T(8,128)(2,1)}, bf16[2,256,896]{2,1,0:T(8,128)(2,1)}, u32[]{:S(2)}, u32[]{:S(2)}) collective-permute-start(bf16[2,256,896]{2,1,0:T(8,128)(2,1)} %get-tuple-element.89), channel_id=1, source_target_pairs={{0,1},{1,2},{2,3},{4,5},{5,6},{6,7},{8,9},{9,10},{10,11},{12,13},{... | collective-permute-start | bytes 2752520 | tf_op jit(solution)/shard_map/ppermute | solution.py:604
  12.7 38.6 %collective-permute-start.1 = (bf16[2,288,896]{2,1,0:T(8,128)(2,1)}, bf16[2,288,896]{2,1,0:T(8,128)(2,1)S(1)}, u32[]{:S(2)}, u32[]{:S(2)}) collective-permute-start(bf16[2,288,896]{2,1,0:T(8,128)(2,1)} %fusion.2), channel_id=1, source_target_pairs={{0,1},{1,2},{2,3},{4,5},{5,6},{6,7},{8,9},{9,10},{10,11},{12,13},{... | collective-permute-start | bytes 3096584 | tf_op jit(solution)/shard_map/ppermute | solution.py:604
  16.4 34.9 %collective-permute-start.3 = (bf16[2,288,896]{2,1,0:T(8,128)(2,1)}, bf16[2,288,896]{2,1,0:T(8,128)(2,1)S(1)}, u32[]{:S(2)}, u32[]{:S(2)}) collective-permute-start(bf16[2,288,896]{2,1,0:T(8,128)(2,1)} %fusion.3), channel_id=1, source_target_pairs={{1,0},{2,1},{3,2},{5,4},{6,5},{7,6},{9,8},{10,9},{11,10},{13,12},{... | collective-permute-start | bytes 3096584 | tf_op jit(solution)/shard_map/ppermute | solution.py:604
  37.1 22.0 %all-to-all-start = ((bf16[8,2,256,128]{3,2,1,0:T(8,128)(2,1)}), bf16[8,2,256,128]{3,2,1,0:T(8,128)(2,1)S(1)}, u32[]{:S(2)}, u32[]{:S(2)}) async-start(bf16[8,2,256,128]{3,2,1,0:T(8,128)(2,1)} %shear_tile.4), calls=%async_computation | async-start | bytes 2097152 | tf_op jit(solution)/shard_map/all_to_all | solution.py:766
  59.1 19.0 %all-to-all-start.1 = ((bf16[8,2,256,128]{3,2,1,0:T(8,128)(2,1)}), bf16[8,2,256,128]{3,2,1,0:T(8,128)(2,1)S(1)}, u32[]{:S(2)}, u32[]{:S(2)}) async-start(bf16[8,2,256,128]{3,2,1,0:T(8,128)(2,1)} %shear_tile.5), calls=%async_computation.1 | async-start | bytes 2097152 | tf_op jit(solution)/shard_map/all_to_all | solution.py:766
  87.5 56.0 %all-to-all-start.2 = ((bf16[32,2,128,128]{3,2,1,0:T(8,128)(2,1)}), bf16[32,2,128,128]{3,2,1,0:T(8,128)(2,1)S(1)}, u32[]{:S(2)}, u32[]{:S(2)}) async-start(bf16[32,2,128,128]{3,2,1,0:T(8,128)(2,1)} %shear_columns.2), calls=%async_computation.2 | async-start | bytes 4194304 | tf_op jit(solution)/shard_map/all_to_all | solution.py:775
  94.4 25.8 %collective-permute-start.10 = (bf16[1,2,512,128]{3,2,1,0:T(8,128)(2,1)}, bf16[1,2,512,128]{3,2,1,0:T(8,128)(2,1)}, u32[]{:S(2)}, u32[]{:S(2)}) collective-permute-start(bf16[1,2,512,128]{3,2,1,0:T(8,128)(2,1)} %get-tuple-element.76), channel_id=1, source_target_pairs={{0,28},{4,24},{8,20},{12,16},{16,12},{20,8},{24,4},{28,0},{1,29},{... | collective-permute-start | bytes 786440 | tf_op jit(solution)/shard_map/ppermute | solution.py:649
  95.7 34.4 %collective-permute-start.9 = (bf16[1,2,512,128]{3,2,1,0:T(8,128)(2,1)}, bf16[1,2,512,128]{3,2,1,0:T(8,128)(2,1)}, u32[]{:S(2)}, u32[]{:S(2)}) collective-permute-start(bf16[1,2,512,128]{3,2,1,0:T(8,128)(2,1)} %get-tuple-element.77), channel_id=1, source_target_pairs={{0,24},{4,28},{8,16},{12,20},{16,8},{20,12},{24,0},{28,4},{1,25},{... | collective-permute-start | bytes 786440 | tf_op jit(solution)/shard_map/ppermute | solution.py:649
  97.2 36.4 %collective-permute-start.8 = (bf16[1,2,512,128]{3,2,1,0:T(8,128)(2,1)}, bf16[1,2,512,128]{3,2,1,0:T(8,128)(2,1)}, u32[]{:S(2)}, u32[]{:S(2)}) collective-permute-start(bf16[1,2,512,128]{3,2,1,0:T(8,128)(2,1)} %get-tuple-element.78), channel_id=1, source_target_pairs={{0,20},{4,16},{8,28},{12,24},{16,4},{20,0},{24,12},{28,8},{1,21},{... | collective-permute-start | bytes 786440 | tf_op jit(solution)/shard_map/ppermute | solution.py:649
  98.3 43.0 %collective-permute-start.7 = (bf16[1,2,512,128]{3,2,1,0:T(8,128)(2,1)S(1)}, bf16[1,2,512,128]{3,2,1,0:T(8,128)(2,1)}, u32[]{:S(2)}, u32[]{:S(2)}) collective-permute-start(bf16[1,2,512,128]{3,2,1,0:T(8,128)(2,1)S(1)} %copy-done.12), channel_id=1, source_target_pairs={{0,16},{4,20},{8,24},{12,28},{16,0},{20,4},{24,8},{28,12},{1,17},{... | collective-permute-start | bytes 786440 | tf_op jit(solution)/shard_map/ppermute | solution.py:649
  98.9 42.4 %collective-permute-start.6 = (bf16[1,2,512,128]{3,2,1,0:T(8,128)(2,1)S(1)}, bf16[1,2,512,128]{3,2,1,0:T(8,128)(2,1)}, u32[]{:S(2)}, u32[]{:S(2)}) collective-permute-start(bf16[1,2,512,128]{3,2,1,0:T(8,128)(2,1)S(1)} %copy-done.11), channel_id=1, source_target_pairs={{0,12},{4,8},{8,4},{12,0},{16,28},{20,24},{24,20},{28,16},{1,13},{... | collective-permute-start | bytes 786440 | tf_op jit(solution)/shard_map/ppermute | solution.py:649
  120.3 23.2 %collective-permute-start.5 = (bf16[1,2,512,128]{3,2,1,0:T(8,128)(2,1)S(1)}, bf16[1,2,512,128]{3,2,1,0:T(8,128)(2,1)}, u32[]{:S(2)}, u32[]{:S(2)}) collective-permute-start(bf16[1,2,512,128]{3,2,1,0:T(8,128)(2,1)S(1)} %copy-done.10), channel_id=1, source_target_pairs={{0,8},{4,12},{8,0},{12,4},{16,24},{20,28},{24,16},{28,20},{1,9},{5... | collective-permute-start | bytes 786440 | tf_op jit(solution)/shard_map/ppermute | solution.py:649
  130.1 13.3 %collective-permute-start.4 = (bf16[1,2,512,128]{3,2,1,0:T(8,128)(2,1)S(1)}, bf16[1,2,512,128]{3,2,1,0:T(8,128)(2,1)}, u32[]{:S(2)}, u32[]{:S(2)}) collective-permute-start(bf16[1,2,512,128]{3,2,1,0:T(8,128)(2,1)S(1)} %get-tuple-element.82), channel_id=1, source_target_pairs={{0,4},{4,0},{8,12},{12,8},{16,20},{20,16},{24,28},{28,24},{1,5},{5... | collective-permute-start | bytes 786440 | tf_op jit(solution)/shard_map/ppermute | solution.py:649
  154.4 58.9 %all-to-all-start.3 = ((bf16[4,2,1088,128]{3,2,1,0:T(8,128)(2,1)}), bf16[4,2,1088,128]{3,2,1,0:T(8,128)(2,1)S(1)}, u32[]{:S(2)}, u32[]{:S(2)}) async-start(bf16[4,2,1088,128]{3,2,1,0:T(8,128)(2,1)} %shear_whole.1), calls=%async_computation.3 | async-start | bytes 4456448 | tf_op jit(solution)/shard_map/all_to_all | solution.py:789
  170.3 38.3 %copy-start.25 = (f32[256,128]{1,0:T(8,128)S(1)}, f32[256,128]{1,0:T(8,128)}, u32[]{:S(2)}) copy-start(f32[256,128]{1,0:T(8,128)} %constant.91.clone) | copy-start | bytes 393220
  170.3 9.6 %collective-permute-start.17 = (bf16[1,2,512,128]{3,2,1,0:T(8,128)(2,1)S(1)}, bf16[1,2,512,128]{3,2,1,0:T(8,128)(2,1)S(1)}, u32[]{:S(2)}, u32[]{:S(2)}) collective-permute-start(bf16[1,2,512,128]{3,2,1,0:T(8,128)(2,1)S(1)} %get-tuple-element.68), channel_id=1, source_target_pairs={{0,28},{4,24},{8,20},{12,16},{16,12},{20,8},{24,4},{28,0},{1,29},{... | collective-permute-start | bytes 786440 | tf_op jit(solution)/shard_map/ppermute | solution.py:649
  171.5 13.6 %collective-permute-start.16 = (bf16[1,2,512,128]{3,2,1,0:T(8,128)(2,1)S(1)}, bf16[1,2,512,128]{3,2,1,0:T(8,128)(2,1)S(1)}, u32[]{:S(2)}, u32[]{:S(2)}) collective-permute-start(bf16[1,2,512,128]{3,2,1,0:T(8,128)(2,1)S(1)} %get-tuple-element.69), channel_id=1, source_target_pairs={{0,24},{4,28},{8,16},{12,20},{16,8},{20,12},{24,0},{28,4},{1,25},{... | collective-permute-start | bytes 786440 | tf_op jit(solution)/shard_map/ppermute | solution.py:649
  172.5 18.2 %collective-permute-start.15 = (bf16[1,2,512,128]{3,2,1,0:T(8,128)(2,1)S(1)}, bf16[1,2,512,128]{3,2,1,0:T(8,128)(2,1)S(1)}, u32[]{:S(2)}, u32[]{:S(2)}) collective-permute-start(bf16[1,2,512,128]{3,2,1,0:T(8,128)(2,1)S(1)} %get-tuple-element.70), channel_id=1, source_target_pairs={{0,20},{4,16},{8,28},{12,24},{16,4},{20,0},{24,12},{28,8},{1,21},{... | collective-permute-start | bytes 786440 | tf_op jit(solution)/shard_map/ppermute | solution.py:649
  174.2 22.2 %collective-permute-start.14 = (bf16[1,2,512,128]{3,2,1,0:T(8,128)(2,1)S(1)}, bf16[1,2,512,128]{3,2,1,0:T(8,128)(2,1)S(1)}, u32[]{:S(2)}, u32[]{:S(2)}) collective-permute-start(bf16[1,2,512,128]{3,2,1,0:T(8,128)(2,1)S(1)} %get-tuple-element.71), channel_id=1, source_target_pairs={{0,16},{4,20},{8,24},{12,28},{16,0},{20,4},{24,8},{28,12},{1,17},{... | collective-permute-start | bytes 786440 | tf_op jit(solution)/shard_map/ppermute | solution.py:649
  174.7 21.8 %collective-permute-start.13 = (bf16[1,2,512,128]{3,2,1,0:T(8,128)(2,1)S(1)}, bf16[1,2,512,128]{3,2,1,0:T(8,128)(2,1)S(1)}, u32[]{:S(2)}, u32[]{:S(2)}) collective-permute-start(bf16[1,2,512,128]{3,2,1,0:T(8,128)(2,1)S(1)} %get-tuple-element.72), channel_id=1, source_target_pairs={{0,12},{4,8},{8,4},{12,0},{16,28},{20,24},{24,20},{28,16},{1,13},{... | collective-permute-start | bytes 786440 | tf_op jit(solution)/shard_map/ppermute | solution.py:649
  179.9 16.6 %collective-permute-start.12 = (bf16[1,2,512,128]{3,2,1,0:T(8,128)(2,1)S(1)}, bf16[1,2,512,128]{3,2,1,0:T(8,128)(2,1)S(1)}, u32[]{:S(2)}, u32[]{:S(2)}) collective-permute-start(bf16[1,2,512,128]{3,2,1,0:T(8,128)(2,1)S(1)} %get-tuple-element.73), channel_id=1, source_target_pairs={{0,8},{4,12},{8,0},{12,4},{16,24},{20,28},{24,16},{28,20},{1,9},{5... | collective-permute-start | bytes 786440 | tf_op jit(solution)/shard_map/ppermute | solution.py:649
  185.1 11.4 %collective-permute-start.11 = (bf16[1,2,512,128]{3,2,1,0:T(8,128)(2,1)S(1)}, bf16[1,2,512,128]{3,2,1,0:T(8,128)(2,1)S(1)}, u32[]{:S(2)}, u32[]{:S(2)}) collective-permute-start(bf16[1,2,512,128]{3,2,1,0:T(8,128)(2,1)S(1)} %get-tuple-element.74), channel_id=1, source_target_pairs={{0,4},{4,0},{8,12},{12,8},{16,20},{20,16},{24,28},{28,24},{1,5},{5... | collective-permute-start | bytes 786440 | tf_op jit(solution)/shard_map/ppermute | solution.py:649
  201.9 43.7 %collective-permute-start.18 = (bf16[7,2,512,128]{3,2,1,0:T(8,128)(2,1)}, bf16[7,2,512,128]{3,2,1,0:T(8,128)(2,1)}, u32[]{:S(2)}, u32[]{:S(2)}) collective-permute-start(bf16[7,2,512,128]{3,2,1,0:T(8,128)(2,1)} %get-tuple-element.53), channel_id=1, source_target_pairs={{0,1},{1,2},{2,3},{4,5},{5,6},{6,7},{8,9},{9,10},{10,11},{12,13},{... | collective-permute-start | bytes 5505032 | tf_op jit(solution)/shard_map/ppermute | solution.py:604
  207.1 43.9 %collective-permute-start.19 = (bf16[7,2,512,128]{3,2,1,0:T(8,128)(2,1)}, bf16[7,2,512,128]{3,2,1,0:T(8,128)(2,1)}, u32[]{:S(2)}, u32[]{:S(2)}) collective-permute-start(bf16[7,2,512,128]{3,2,1,0:T(8,128)(2,1)} %get-tuple-element.54), channel_id=1, source_target_pairs={{1,0},{2,1},{3,2},{5,4},{6,5},{7,6},{9,8},{10,9},{11,10},{13,12},{... | collective-permute-start | bytes 5505032 | tf_op jit(solution)/shard_map/ppermute | solution.py:604
  223.2 6.7 %collective-permute-start.20 = (bf16[2,32,1024]{2,1,0:T(8,128)(2,1)}, bf16[2,32,1024]{2,1,0:T(8,128)(2,1)S(1)}, u32[]{:S(2)}, u32[]{:S(2)}) collective-permute-start(bf16[2,32,1024]{2,1,0:T(8,128)(2,1)} %get-tuple-element.55), channel_id=1, source_target_pairs={{0,4},{4,8},{8,12},{12,16},{16,20},{20,24},{24,28},{1,5},{5,9},{9,... | collective-permute-start | bytes 393224 | tf_op jit(solution)/shard_map/ppermute | solution.py:604
  225.1 6.5 %collective-permute-start.21 = (bf16[2,32,1024]{2,1,0:T(8,128)(2,1)}, bf16[2,32,1024]{2,1,0:T(8,128)(2,1)S(1)}, u32[]{:S(2)}, u32[]{:S(2)}) collective-permute-start(bf16[2,32,1024]{2,1,0:T(8,128)(2,1)} %get-tuple-element.57), channel_id=1, source_target_pairs={{4,0},{8,4},{12,8},{16,12},{20,16},{24,20},{28,24},{5,1},{9,5},{13... | collective-permute-start | bytes 393224 | tf_op jit(solution)/shard_map/ppermute | solution.py:604
  263.8 5.2 %collective-permute-start.23 = (bf16[8,2,32,128]{3,2,1,0:T(8,128)(2,1)S(1)}, bf16[8,2,32,128]{3,2,1,0:T(8,128)(2,1)S(1)}, u32[]{:S(2)}, u32[]{:S(2)}) collective-permute-start(bf16[8,2,32,128]{3,2,1,0:T(8,128)(2,1)S(1)} %get-tuple-element.66), channel_id=1, source_target_pairs={{4,0},{8,4},{12,8},{16,12},{20,16},{24,20},{28,24},{5,1},{9,5},{13... | collective-permute-start | bytes 393224 | tf_op jit(solution)/shard_map/ppermute | solution.py:604
  265.7 6.3 %collective-permute-start.22 = (bf16[8,2,32,128]{3,2,1,0:T(8,128)(2,1)S(1)}, bf16[8,2,32,128]{3,2,1,0:T(8,128)(2,1)S(1)}, u32[]{:S(2)}, u32[]{:S(2)}) collective-permute-start(bf16[8,2,32,128]{3,2,1,0:T(8,128)(2,1)S(1)} %get-tuple-element.67), channel_id=1, source_target_pairs={{0,4},{4,8},{8,12},{12,16},{16,20},{20,24},{24,28},{1,5},{5,9},{9,... | collective-permute-start | bytes 393224 | tf_op jit(solution)/shard_map/ppermute | solution.py:604
  276.8 4.3 %collective-permute-start.24 = (bf16[2,32,512]{2,1,0:T(8,128)(2,1)}, bf16[2,32,512]{2,1,0:T(8,128)(2,1)S(1)}, u32[]{:S(2)}, u32[]{:S(2)}) collective-permute-start(bf16[2,32,512]{2,1,0:T(8,128)(2,1)} %get-tuple-element.61), channel_id=1, source_target_pairs={{0,1},{1,2},{2,3},{4,5},{5,6},{6,7},{8,9},{9,10},{10,11},{12,13},{... | collective-permute-start | bytes 196616 | tf_op jit(solution)/shard_map/ppermute | solution.py:604
  278.9 6.4 %collective-permute-start.25 = (bf16[2,32,512]{2,1,0:T(8,128)(2,1)}, bf16[2,32,512]{2,1,0:T(8,128)(2,1)S(1)}, u32[]{:S(2)}, u32[]{:S(2)}) collective-permute-start(bf16[2,32,512]{2,1,0:T(8,128)(2,1)} %get-tuple-element.63), channel_id=1, source_target_pairs={{1,0},{2,1},{3,2},{5,4},{6,5},{7,6},{9,8},{10,9},{11,10},{13,12},{... | collective-permute-start | bytes 196616 | tf_op jit(solution)/shard_map/ppermute | solution.py:604
  (29 other events, 210.7 us)

commit v13 on v12

--- a/solution.py
+++ b/solution.py
@@ -334,12 +334,13 @@
     )(base, *operands)
 
 
-def shear_columns_kernel(front, blocks, length, rows_out, place, base, rank, *refs):
+def shear_columns_kernel(front, blocks, steps, length, rows_out, place, base, rank, *refs):
     owns, refs = refs[: len(place)], refs[len(place) :]
-    offsets, fractions, forward, inverse, out, strip, shifted, cosine, sine = refs
+    offsets, fractions, forward, inverse = refs[:4]
+    outs, (strip, shifted, cosine, sine) = refs[4:-4], refs[-4:]
     step = pl.program_id(0)
     per_step = length // BLOCK
-    per_grid = blocks // pl.num_programs(0)
+    per_grid = blocks // steps
     total = strip.shape[1]
 
     @pl.when(step == 0)
@@ -379,7 +380,7 @@
                 jnp.concatenate(moved, 0).astype(jnp.bfloat16)
             )
 
-    def one_block(local, carry):
+    def one_block(local):
         block_rows = ((step * per_grid + local) ^ rank[0]) * length
         for chunk in range(per_step + 1):
             one_chunk(block_rows, chunk)
@@ -403,15 +404,20 @@
             piece, within = window * BLOCK // rows_out, window * BLOCK % rows_out
             for part in range(2):
                 lanes = (2 * window + part) * BLOCK
-                out[local * (length // rows_out) + piece, part, within : within + BLOCK, :] = (
-                    result[:, lanes : lanes + BLOCK]
-                )
-        return carry
-
-    lax.fori_loop(0, per_grid, one_block, 0)
-
-
-def shear_columns(owns, place, blocks, front, back, base, rank, spare, fractions, tables, rows_out):
+                value = result[:, lanes : lanes + BLOCK]
+                if len(outs) > 1:
+                    outs[local][piece, part, within : within + BLOCK, :] = value
+                else:
+                    index = local * (length // rows_out) + piece
+                    outs[0][index, part, within : within + BLOCK, :] = value
+
+    for local in range(blocks // steps):
+        one_block(local)
+
+
+def shear_columns(
+    owns, place, blocks, front, back, base, rank, spare, fractions, tables, rows_out, split
+):
     length = sum(own.shape[0] * own.shape[2] for own in owns) // blocks
     forward, inverse = tables
     operands = (
@@ -423,16 +429,19 @@
     )
     full = lambda shape: pl.BlockSpec(shape, lambda i, *_: (0,) * len(shape))
     pieces = blocks * length // rows_out
-    steps = STEPS if blocks % STEPS == 0 else 1
+    steps = STEPS if blocks % STEPS == 0 and not split else 1
+    parts = blocks if split else 1
+    shape = (pieces // parts, 2, rows_out, BLOCK)
     return pl.pallas_call(
-        functools.partial(shear_columns_kernel, front, blocks, length, rows_out, place),
+        functools.partial(shear_columns_kernel, front, blocks, steps, length, rows_out, place),
         grid_spec=pltpu.PrefetchScalarGridSpec(
             num_scalar_prefetch=2,
             grid=(steps,),
             in_specs=[full(x.shape) for x in operands],
-            out_specs=pl.BlockSpec(
-                (pieces // steps, 2, rows_out, BLOCK), lambda i, *_: (i, 0, 0, 0)
-            ),
+            out_specs=[
+                pl.BlockSpec((shape[0] // steps, *shape[1:]), lambda i, *_: (i, 0, 0, 0))
+            ]
+            * parts,
             scratch_shapes=[
                 pltpu.VMEM((2, front + blocks * length + back, BLOCK), jnp.bfloat16),
                 pltpu.VMEM((length + BLOCK, 2 * BLOCK), jnp.bfloat16),
@@ -440,7 +449,7 @@
                 pltpu.VMEM((BLOCK, BLOCK), jnp.float32),
             ],
         ),
-        out_shape=jax.ShapeDtypeStruct((pieces, 2, rows_out, BLOCK), jnp.bfloat16),
+        out_shape=[jax.ShapeDtypeStruct(shape, jnp.bfloat16)] * parts,
         compiler_params=pltpu.CompilerParams(vmem_limit_bytes=VMEM_LIMIT),
         name="shear_columns",
     )(base, rank, *operands)
@@ -724,7 +733,7 @@
             row_tables,
         )
 
-    def second(view, pieces, place, rank, rows_out):
+    def second(view, pieces, place, rank, rows_out, split):
         return shear_columns(
             pieces,
             place,
@@ -737,6 +746,7 @@
             column_fractions[view],
             column_tables,
             rows_out,
+            split,
         )
 
     matrices = travel_matrices(travel_distance, forward, inverse)
@@ -771,7 +781,7 @@
     pieces = swapped_shares(shares)
 
     place = [[(b, part * part_lines) for b in range(row_devices)] for part in range(PARTS)]
-    moved_b = second(1, spread, place, in_order, BLOCK)
+    (moved_b,) = second(1, spread, place, in_order, BLOCK, False)
     whole = lax.all_to_all(moved_b, ("row", "col"), split_axis=0, concat_axis=0, tiled=True)
     whole = after(whole, pieces)
     whole = whole.reshape(row_devices, column_devices, 2, BLOCK, BLOCK)
@@ -789,8 +799,8 @@
     sent = lax.all_to_all(turned, "col", split_axis=0, concat_axis=0, tiled=True)
 
     pieces = after(pieces, turned)
-    moved_a = second(0, pieces, [[(s, 0)] for s in range(row_devices)], by_rank, line_count)
-    pieces = swapped_shares([moved_a[s : s + 1] for s in range(row_devices)])
+    place = [[(s, 0)] for s in range(row_devices)]
+    pieces = swapped_shares(second(0, pieces, place, by_rank, line_count, True))
     tile, low, high = ordered(pieces, halo, by_rank)
     left, right = from_both_sides(low, high, "col")
 

time: 293 us -> 291 us (level)
    unnamed x62 -> x60, local copies, waits for them, and re-layouts: 7.91 us -> 7.87 us
  transfers between devices with their start and end apart: 30 -> 30, of which waited for: 18 -> 18; matrix products, arithmetic and copies ran while one was open for 8% -> 7% of each run, Pallas kernels for 17% -> 16%
where the time goes in v13:
time: 291 us; the launch traced here: 289 us
  waiting for transfers between devices  105 us (36%)
  Pallas kernels  85.6 us (29%)
  starting transfers between devices  63.7 us (22%)
  local copies, waits for them, and re-layouts  26.4 us (9%)
  other arithmetic  5.32 us (2%)
    ppermute x14, waiting for transfers between devices, swapped_shares(): lax.ppermute(slots[s], 'row', [(i, i ^ s) for i in range(devices)])  60.7 us
    ppermute x12, waiting for transfers between devices, from_both_sides(): return (lax.ppermute(last, axis, up), lax.ppermute(first, axis, down))  43.6 us
    pallas_call x4, Pallas kernels, shear_tile(): pl.pallas_call(kernel, grid_spec=pltpu.PrefetchScalarGridSpec(num_scalar_...  34.9 us
    ppermute x12, starting transfers between devices, from_both_sides(): return (lax.ppermute(last, axis, up), lax.ppermute(first, axis, down))  30.7 us
    pallas_call x2, Pallas kernels, shear_columns(): pl.pallas_call(functools.partial(shear_columns_kernel, front, blocks, ste...  15.1 us
    ppermute x14, starting transfers between devices, swapped_shares(): lax.ppermute(slots[s], 'row', [(i, i ^ s) for i in range(devices)])  13.5 us
    pallas_call x2, Pallas kernels, travel_first(): pl.pallas_call(functools.partial(travel_first_kernel, length, count, len(...  12.7 us
    pallas_call x1, Pallas kernels, shear_whole(): pl.pallas_call(functools.partial(shear_whole_kernel, halo, devices, tiles...  9.6 us
  transfers between devices with their start and end apart: 30, of which 18 were waited for; matrix products, arithmetic and copies ran while one was open for 7% of the time, Pallas kernels for 16%

profile of v13, /device:TPU:2, one launch (start us, length us, event | category | flops | bytes accessed | tf_op | source)
XLA Modules:
  0.0 288.8 jit_solution(7167129357202914729)
XLA Ops:
  0.7 3.0 %fusion.27 = (bf16[2,256,896]{2,1,0:T(8,128)(2,1)}, bf16[2,256,896]{2,1,0:T(8,128)(2,1)}) fusion(bf16[2,512,1024]{2,1,0:T(8,128)(2,1)} %refs_4_.2), kind=kLoop, calls=%fused_computation.73 | loop fusion | bytes 3670016 | tf_op jit(solution)/shard_map/slice | solution.py:700
  5.0 5.5 %collective-permute-start = (bf16[2,256,896]{2,1,0:T(8,128)(2,1)}, bf16[2,256,896]{2,1,0:T(8,128)(2,1)}, u32[]{:S(2)}, u32[]{:S(2)}) collective-permute-start(bf16[2,256,896]{2,1,0:T(8,128)(2,1)} %get-tuple-element.97), channel_id=1, source_target_pairs={{0,1},{1,2},{2,3},{4,5},{5,6},{6,7},{8,9},{9,10},{10,11},{12,13},{... | collective-permute-start | bytes 2752520 | tf_op jit(solution)/shard_map/ppermute | solution.py:613
  19.9 9.1 %collective-permute-done.2.refs_1_.refs_2_ = bf16[2,256,896]{2,1,0:T(8,128)(2,1)S(1)} collective-permute-done((bf16[2,256,896]{2,1,0:T(8,128)(2,1)}, bf16[2,256,896]{2,1,0:T(8,128)(2,1)S(1)}, u32[]{:S(2)}, u32[]{:S(2)}) %collective-permute-start.2) | collective-permute-done | bytes 917536 | tf_op jit(solution)/shard_map/ppermute | solution.py:613
  30.6 6.5 %shear_tile.4 = bf16[8,2,256,128]{3,2,1,0:T(8,128)(2,1)} custom-call(s32[16]{0:T(128)} %get-tuple-element.117.base, s32[1]{0:T(128)} %constant.69.clone.1.rank, bf16[2,256,896]{2,1,0:T(8,128)(2,1)} %collective-permute-done.refs_0_, bf16[2,256,896]{2,1,0:T(8,128)(2,1)} %copy-done.8, bf16[2,512,1024]{2,1,0:T(8,128)(2,1)} %refs_4_.2, f32[2,1,256]{2,1,0:T(1,128)} %bitcast.63, ...), custom_call_target="tpu_custom_call" | custom-call | tf_op jit(solution)/shard_map/shear_tile/pallas_call | solution.py:206
  37.1 4.3 %all-to-all-start = ((bf16[8,2,256,128]{3,2,1,0:T(8,128)(2,1)}), bf16[8,2,256,128]{3,2,1,0:T(8,128)(2,1)S(1)}, u32[]{:S(2)}, u32[]{:S(2)}) async-start(bf16[8,2,256,128]{3,2,1,0:T(8,128)(2,1)} %shear_tile.4), calls=%async_computation | async-start | bytes 2097152 | tf_op jit(solution)/shard_map/all_to_all | solution.py:776
  43.9 7.4 %collective-permute-done.1.refs_0_.refs_1_ = bf16[2,288,896]{2,1,0:T(8,128)(2,1)S(1)} collective-permute-done((bf16[2,288,896]{2,1,0:T(8,128)(2,1)}, bf16[2,288,896]{2,1,0:T(8,128)(2,1)S(1)}, u32[]{:S(2)}, u32[]{:S(2)}) %collective-permute-start.1) | collective-permute-done | bytes 1032224 | tf_op jit(solution)/shard_map/ppermute | solution.py:613
  52.6 6.5 %shear_tile.5 = bf16[8,2,256,128]{3,2,1,0:T(8,128)(2,1)} custom-call(s32[16]{0:T(128)} %get-tuple-element.118.base, s32[1]{0:T(128)} %constant.69.clone.1.rank, bf16[2,288,896]{2,1,0:T(8,128)(2,1)} %copy-done.4, bf16[2,288,896]{2,1,0:T(8,128)(2,1)} %copy-done.5, bf16[2,512,1024]{2,1,0:T(8,128)(2,1)} %refs_4_.2, f32[2,1,256]{2,1,0:T(1,128)} %bitcast.64, ...), custom_call_target="tpu_custom_call" | custom-call | tf_op jit(solution)/shard_map/shear_tile/pallas_call | solution.py:206
  59.1 4.3 %all-to-all-start.1 = ((bf16[8,2,256,128]{3,2,1,0:T(8,128)(2,1)}), bf16[8,2,256,128]{3,2,1,0:T(8,128)(2,1)S(1)}, u32[]{:S(2)}, u32[]{:S(2)}) async-start(bf16[8,2,256,128]{3,2,1,0:T(8,128)(2,1)} %shear_tile.5), calls=%async_computation.1 | async-start | bytes 2097152 | tf_op jit(solution)/shard_map/all_to_all | solution.py:776
  65.3 10.1 %shear_tile.6 = bf16[8,2,512,128]{3,2,1,0:T(8,128)(2,1)} custom-call(s32[32]{0:T(128)} %get-tuple-element.115.base, s32[1]{0:T(128)} %bitcast.1.rank, bf16[2,256,896]{2,1,0:T(8,128)(2,1)} %collective-permute-done.refs_0_, bf16[2,288,896]{2,1,0:T(8,128)(2,1)} %copy-done.4, bf16[2,256,896]{2,1,0:T(8,128)(2,1)} %copy-done.8, bf16[2,288,896]{2,1,0:T(8,128)(2,1)} %copy-done.5, ...), custom_call_target="tpu_custom_call" | custom-call | tf_op jit(solution)/shard_map/shear_tile/pallas_call | solution.py:206
  79.2 8.0 %shear_columns.2 = bf16[32,2,128,128]{3,2,1,0:T(8,128)(2,1)} custom-call(s32[1]{0:T(128)} %bitcast.12.base, s32[1]{0:T(128)} %constant.69.clone.1.rank, bf16[8,2,256,128]{3,2,1,0:T(8,128)(2,1)} %copy-done.6, bf16[8,2,256,128]{3,2,1,0:T(8,128)(2,1)} %copy-done.7, s32[1,128]{1,0:T(1,128)} %get-tuple-element.122.refs_2_, f32[1,128]{1,0:T(1,128)} %get-tuple-element.120.refs_3_, ...), custom_call_target="tpu_custom_call" | custom-call | tf_op jit(solution)/shard_map/shear_columns/pallas_call | solution.py:435
  87.2 6.9 %all-to-all-start.2 = ((bf16[32,2,128,128]{3,2,1,0:T(8,128)(2,1)}), bf16[32,2,128,128]{3,2,1,0:T(8,128)(2,1)S(1)}, u32[]{:S(2)}, u32[]{:S(2)}) async-start(bf16[32,2,128,128]{3,2,1,0:T(8,128)(2,1)} %shear_columns.2), calls=%async_computation.2 | async-start | bytes 4194304 | tf_op jit(solution)/shard_map/all_to_all | solution.py:785
  98.7 21.3 %collective-permute-done.10.refs_7_ = bf16[1,2,512,128]{3,2,1,0:T(8,128)(2,1)} collective-permute-done((bf16[1,2,512,128]{3,2,1,0:T(8,128)(2,1)}, bf16[1,2,512,128]{3,2,1,0:T(8,128)(2,1)}, u32[]{:S(2)}, u32[]{:S(2)}) %collective-permute-start.10) | collective-permute-done | bytes 262176 | tf_op jit(solution)/shard_map/ppermute | solution.py:658
  121.9 7.9 %collective-permute-done.9.refs_6_ = bf16[1,2,512,128]{3,2,1,0:T(8,128)(2,1)} collective-permute-done((bf16[1,2,512,128]{3,2,1,0:T(8,128)(2,1)}, bf16[1,2,512,128]{3,2,1,0:T(8,128)(2,1)}, u32[]{:S(2)}, u32[]{:S(2)}) %collective-permute-start.9) | collective-permute-done | bytes 262176 | tf_op jit(solution)/shard_map/ppermute | solution.py:658
  133.2 7.8 %collective-permute-done.7.refs_4_ = bf16[1,2,512,128]{3,2,1,0:T(8,128)(2,1)} collective-permute-done((bf16[1,2,512,128]{3,2,1,0:T(8,128)(2,1)S(1)}, bf16[1,2,512,128]{3,2,1,0:T(8,128)(2,1)}, u32[]{:S(2)}, u32[]{:S(2)}) %collective-permute-start.7) | collective-permute-done | bytes 262176 | tf_op jit(solution)/shard_map/ppermute | solution.py:658
  144.5 9.6 %shear_whole.1 = bf16[4,2,1088,128]{3,2,1,0:T(8,128)(2,1)} custom-call(s32[8]{0:T(128)} %fusion.16.base, bf16[8,4,2,128,128]{4,3,2,1,0:T(8,128)(2,1)} %bitcast.60, f32[1,128]{1,0:T(1,128)} %fusion.18.offsets, f32[1,128]{1,0:T(1,128)} %fusion.19.fractions, bf16[256,256]{1,0:T(8,128)(2,1)} %constant.86.clone.refs_5_.refs_7_.forward.refs_6_, ...), custom_call_target="tpu_custom_call" | custom-call | tf_op jit(solution)/shard_map/shear_whole/pallas_call | solution.py:316
  154.1 4.1 %all-to-all-start.3 = ((bf16[4,2,1088,128]{3,2,1,0:T(8,128)(2,1)}), bf16[4,2,1088,128]{3,2,1,0:T(8,128)(2,1)S(1)}, u32[]{:S(2)}, u32[]{:S(2)}) async-start(bf16[4,2,1088,128]{3,2,1,0:T(8,128)(2,1)} %shear_whole.1), calls=%async_computation.3 | async-start | bytes 4456448 | tf_op jit(solution)/shard_map/all_to_all | solution.py:799
  158.8 7.1 %shear_columns.3 = (bf16[1,2,512,128]{3,2,1,0:T(8,128)(2,1)}, bf16[1,2,512,128]{3,2,1,0:T(8,128)(2,1)}, bf16[1,2,512,128]{3,2,1,0:T(8,128)(2,1)}, bf16[1,2,512,1...) custom-call(s32[1]{0:T(128)} %bitcast.3.base, ...), custom_call_target="tpu_custom_call" | custom-call | tf_op jit(solution)/shard_map/shear_columns/pallas_call | solution.py:435
  171.8 3.5 %collective-permute-done.12.refs_2_ = bf16[1,2,512,128]{3,2,1,0:T(8,128)(2,1)S(1)} collective-permute-done((bf16[1,2,512,128]{3,2,1,0:T(8,128)(2,1)}, bf16[1,2,512,128]{3,2,1,0:T(8,128)(2,1)S(1)}, u32[]{:S(2)}, u32[]{:S(2)}) %collective-permute-start.12) | collective-permute-done | bytes 262176 | tf_op jit(solution)/shard_map/ppermute | solution.py:658
  176.4 3.7 %collective-permute-done.13.refs_3_ = bf16[1,2,512,128]{3,2,1,0:T(8,128)(2,1)S(1)} collective-permute-done((bf16[1,2,512,128]{3,2,1,0:T(8,128)(2,1)}, bf16[1,2,512,128]{3,2,1,0:T(8,128)(2,1)S(1)}, u32[]{:S(2)}, u32[]{:S(2)}) %collective-permute-start.13) | collective-permute-done | bytes 262176 | tf_op jit(solution)/shard_map/ppermute | solution.py:658
  180.1 12.7 %collective-permute-done.15.refs_5_ = bf16[1,2,512,128]{3,2,1,0:T(8,128)(2,1)S(1)} collective-permute-done((bf16[1,2,512,128]{3,2,1,0:T(8,128)(2,1)}, bf16[1,2,512,128]{3,2,1,0:T(8,128)(2,1)S(1)}, u32[]{:S(2)}, u32[]{:S(2)}) %collective-permute-start.15) | collective-permute-done | bytes 262176 | tf_op jit(solution)/shard_map/ppermute | solution.py:658
  193.7 4.5 %ordered.1 = (bf16[8,2,512,128]{3,2,1,0:T(8,128)(2,1)}, bf16[7,2,512,128]{3,2,1,0:T(8,128)(2,1)}, bf16[7,2,512,128]{3,2,1,0:T(8,128)(2,1)}) custom-call(s32[1]{0:T(128)} %bitcast.1.rank, bf16[1,2,512,128]{3,2,1,0:T(8,128)(2,1)} %get-tuple-element.61.refs_0_, bf16[1,2,512,128]{3,2,1,0:T(8,128)(2,1)} %copy-done.12, bf16[1,2,512,128]{3,2,1,0:T(8,128)(2,1)} %copy-done.13, ...), custom_call_target="tpu_custom_call" | custom-call | tf_op jit(solution)/shard_map/ordered/pallas_call | solution.py:641
  198.2 5.1 %collective-permute-start.18 = (bf16[7,2,512,128]{3,2,1,0:T(8,128)(2,1)}, bf16[7,2,512,128]{3,2,1,0:T(8,128)(2,1)}, u32[]{:S(2)}, u32[]{:S(2)}) collective-permute-start(bf16[7,2,512,128]{3,2,1,0:T(8,128)(2,1)} %get-tuple-element.69), channel_id=1, source_target_pairs={{0,1},{1,2},{2,3},{4,5},{5,6},{6,7},{8,9},{9,10},{10,11},{12,13},{... | collective-permute-start | bytes 5505032 | tf_op jit(solution)/shard_map/ppermute | solution.py:613
  211.3 8.5 %travel_first.2 = (bf16[4,2,1024,128]{3,2,1,0:T(8,128)(2,1)}, bf16[2,32,1024]{2,1,0:T(8,128)(2,1)}, bf16[2,32,1024]{2,1,0:T(8,128)(2,1)}) custom-call(bf16[4,2,1088,128]{3,2,1,0:T(8,128)(2,1)} %copy-done.2, bf16[2,1024,512]{2,1,0:T(8,128)(2,1)} %refs_1_.1, bf16[2,32,512]{2,1,0:T(8,128)(2,1)} %slice.222.refs_2_, bf16[2,32,512]{2,1,0:T(8,128)(2,1)} %slice.223.refs_3_, ...), custom_call_target="tpu_custom_call" | custom-call | tf_op jit(solution)/shard_map/travel_first/pallas_call | solution.py:551
  221.8 3.9 %collective-permute-start.21 = (bf16[2,32,1024]{2,1,0:T(8,128)(2,1)}, bf16[2,32,1024]{2,1,0:T(8,128)(2,1)S(1)}, u32[]{:S(2)}, u32[]{:S(2)}) collective-permute-start(bf16[2,32,1024]{2,1,0:T(8,128)(2,1)} %get-tuple-element.73), channel_id=1, source_target_pairs={{4,0},{8,4},{12,8},{16,12},{20,16},{24,20},{28,24},{5,1},{9,5},{13... | collective-permute-start | bytes 393224 | tf_op jit(solution)/shard_map/ppermute | solution.py:613
  228.9 4.4 %travel_second.2 = bf16[2,1024,512]{2,1,0:T(8,128)(2,1)} custom-call(bf16[2,32,1024]{2,1,0:T(8,128)(2,1)} %copy-done.21, bf16[4,2,1024,128]{3,2,1,0:T(8,128)(2,1)} %get-tuple-element.72.body, bf16[2,32,1024]{2,1,0:T(8,128)(2,1)} %copy-done.23, bf16[768,256]{1,0:T(8,128)(2,1)} %get-tuple-element.99.matrix), custom_call_target="tpu_custom_call" | custom-call | tf_op jit(solution)/shard_map/travel_second/pallas_call | solution.py:593
  233.3 9.3 %collective-permute-done.18.refs_0_ = bf16[7,2,512,128]{3,2,1,0:T(8,128)(2,1)} collective-permute-done((bf16[7,2,512,128]{3,2,1,0:T(8,128)(2,1)}, bf16[7,2,512,128]{3,2,1,0:T(8,128)(2,1)}, u32[]{:S(2)}, u32[]{:S(2)}) %collective-permute-start.18) | collective-permute-done | bytes 1835040 | tf_op jit(solution)/shard_map/ppermute | solution.py:613
  242.6 6.1 %collective-permute-done.19.refs_1_ = bf16[7,2,512,128]{3,2,1,0:T(8,128)(2,1)} collective-permute-done((bf16[7,2,512,128]{3,2,1,0:T(8,128)(2,1)}, bf16[7,2,512,128]{3,2,1,0:T(8,128)(2,1)}, u32[]{:S(2)}, u32[]{:S(2)}) %collective-permute-start.19) | collective-permute-done | bytes 1835040 | tf_op jit(solution)/shard_map/ppermute | solution.py:613
  248.7 11.8 %shear_tile.7.refs_0_ = bf16[8,2,512,128]{3,2,1,0:T(8,128)(2,1)} custom-call(s32[32]{0:T(128)} %get-tuple-element.116.base, s32[1]{0:T(128)} %constant.69.clone.1.rank, bf16[7,2,512,128]{3,2,1,0:T(8,128)(2,1)} %collective-permute-done.18.refs_0_, bf16[7,2,512,128]{3,2,1,0:T(8,128)(2,1)} %collective-permute-done.19.refs_1_, bf16[2,512,1024]{2,1,0:T(8,128)(2,1)} %refs_2_.5, ...), custom_call_target="tpu_custom_call" | custom-call | tf_op jit(solution)/shard_map/shear_tile/pallas_call | solution.py:206
  267.1 3.5 %collective-permute-done.22.refs_1_ = bf16[8,2,32,128]{3,2,1,0:T(8,128)(2,1)S(1)} collective-permute-done((bf16[8,2,32,128]{3,2,1,0:T(8,128)(2,1)S(1)}, bf16[8,2,32,128]{3,2,1,0:T(8,128)(2,1)S(1)}, u32[]{:S(2)}, u32[]{:S(2)}) %collective-permute-start.22) | collective-permute-done | bytes 131104 | tf_op jit(solution)/shard_map/ppermute | solution.py:613
  271.4 4.2 %travel_first.3 = (bf16[8,2,512,128]{3,2,1,0:T(8,128)(2,1)}, bf16[2,32,512]{2,1,0:T(8,128)(2,1)}, bf16[2,32,512]{2,1,0:T(8,128)(2,1)}) custom-call(bf16[8,2,512,128]{3,2,1,0:T(8,128)(2,1)} %shear_tile.7.refs_0_, bf16[8,2,32,128]{3,2,1,0:T(8,128)(2,1)} %copy-done.22, bf16[8,2,32,128]{3,2,1,0:T(8,128)(2,1)} %copy-done.20, bf16[256,384]{1,0:T(8,128)(2,1)} %copy.23.refs_3_), custom_call_target="tpu_custom_call" | custom-call | tf_op jit(solution)/shard_map/travel_first/pallas_call | solution.py:551
  279.6 4.2 %collective-permute-done.25.right = bf16[2,32,512]{2,1,0:T(8,128)(2,1)S(1)} collective-permute-done((bf16[2,32,512]{2,1,0:T(8,128)(2,1)}, bf16[2,32,512]{2,1,0:T(8,128)(2,1)S(1)}, u32[]{:S(2)}, u32[]{:S(2)}) %collective-permute-start.25) | collective-permute-done | bytes 65568 | tf_op jit(solution)/shard_map/ppermute | solution.py:613
  284.4 4.4 %travel_second.3 = bf16[2,512,1024]{2,1,0:T(8,128)(2,1)} custom-call(bf16[2,32,512]{2,1,0:T(8,128)(2,1)} %copy-done.25, bf16[8,2,512,128]{3,2,1,0:T(8,128)(2,1)} %get-tuple-element.78.body, bf16[2,32,512]{2,1,0:T(8,128)(2,1)} %copy-done.26, bf16[768,256]{1,0:T(8,128)(2,1)} %get-tuple-element.98.matrix), custom_call_target="tpu_custom_call" | custom-call | tf_op jit(solution)/shard_map/travel_second/pallas_call | solution.py:593
  (145 shorter events, 67.5 us)
Async XLA Ops:
  3.7 25.3 %collective-permute-start.2 = (bf16[2,256,896]{2,1,0:T(8,128)(2,1)}, bf16[2,256,896]{2,1,0:T(8,128)(2,1)S(1)}, u32[]{:S(2)}, u32[]{:S(2)}) collective-permute-start(bf16[2,256,896]{2,1,0:T(8,128)(2,1)} %get-tuple-element.96), channel_id=1, source_target_pairs={{1,0},{2,1},{3,2},{5,4},{6,5},{7,6},{9,8},{10,9},{11,10},{13,12},{... | collective-permute-start | bytes 2752520 | tf_op jit(solution)/shard_map/ppermute | solution.py:613
  5.0 25.6 %collective-permute-start = (bf16[2,256,896]{2,1,0:T(8,128)(2,1)}, bf16[2,256,896]{2,1,0:T(8,128)(2,1)}, u32[]{:S(2)}, u32[]{:S(2)}) collective-permute-start(bf16[2,256,896]{2,1,0:T(8,128)(2,1)} %get-tuple-element.97), channel_id=1, source_target_pairs={{0,1},{1,2},{2,3},{4,5},{5,6},{6,7},{8,9},{9,10},{10,11},{12,13},{... | collective-permute-start | bytes 2752520 | tf_op jit(solution)/shard_map/ppermute | solution.py:613
  12.7 38.6 %collective-permute-start.1 = (bf16[2,288,896]{2,1,0:T(8,128)(2,1)}, bf16[2,288,896]{2,1,0:T(8,128)(2,1)S(1)}, u32[]{:S(2)}, u32[]{:S(2)}) collective-permute-start(bf16[2,288,896]{2,1,0:T(8,128)(2,1)} %fusion.2), channel_id=1, source_target_pairs={{0,1},{1,2},{2,3},{4,5},{5,6},{6,7},{8,9},{9,10},{10,11},{12,13},{... | collective-permute-start | bytes 3096584 | tf_op jit(solution)/shard_map/ppermute | solution.py:613
  16.4 34.9 %collective-permute-start.3 = (bf16[2,288,896]{2,1,0:T(8,128)(2,1)}, bf16[2,288,896]{2,1,0:T(8,128)(2,1)S(1)}, u32[]{:S(2)}, u32[]{:S(2)}) collective-permute-start(bf16[2,288,896]{2,1,0:T(8,128)(2,1)} %fusion.3), channel_id=1, source_target_pairs={{1,0},{2,1},{3,2},{5,4},{6,5},{7,6},{9,8},{10,9},{11,10},{13,12},{... | collective-permute-start | bytes 3096584 | tf_op jit(solution)/shard_map/ppermute | solution.py:613
  37.1 22.0 %all-to-all-start = ((bf16[8,2,256,128]{3,2,1,0:T(8,128)(2,1)}), bf16[8,2,256,128]{3,2,1,0:T(8,128)(2,1)S(1)}, u32[]{:S(2)}, u32[]{:S(2)}) async-start(bf16[8,2,256,128]{3,2,1,0:T(8,128)(2,1)} %shear_tile.4), calls=%async_computation | async-start | bytes 2097152 | tf_op jit(solution)/shard_map/all_to_all | solution.py:776
  59.1 19.0 %all-to-all-start.1 = ((bf16[8,2,256,128]{3,2,1,0:T(8,128)(2,1)}), bf16[8,2,256,128]{3,2,1,0:T(8,128)(2,1)S(1)}, u32[]{:S(2)}, u32[]{:S(2)}) async-start(bf16[8,2,256,128]{3,2,1,0:T(8,128)(2,1)} %shear_tile.5), calls=%async_computation.1 | async-start | bytes 2097152 | tf_op jit(solution)/shard_map/all_to_all | solution.py:776
  87.2 56.0 %all-to-all-start.2 = ((bf16[32,2,128,128]{3,2,1,0:T(8,128)(2,1)}), bf16[32,2,128,128]{3,2,1,0:T(8,128)(2,1)S(1)}, u32[]{:S(2)}, u32[]{:S(2)}) async-start(bf16[32,2,128,128]{3,2,1,0:T(8,128)(2,1)} %shear_columns.2), calls=%async_computation.2 | async-start | bytes 4194304 | tf_op jit(solution)/shard_map/all_to_all | solution.py:785
  94.1 25.8 %collective-permute-start.10 = (bf16[1,2,512,128]{3,2,1,0:T(8,128)(2,1)}, bf16[1,2,512,128]{3,2,1,0:T(8,128)(2,1)}, u32[]{:S(2)}, u32[]{:S(2)}) collective-permute-start(bf16[1,2,512,128]{3,2,1,0:T(8,128)(2,1)} %get-tuple-element.84), channel_id=1, source_target_pairs={{0,28},{4,24},{8,20},{12,16},{16,12},{20,8},{24,4},{28,0},{1,29},{... | collective-permute-start | bytes 786440 | tf_op jit(solution)/shard_map/ppermute | solution.py:658
  95.4 34.4 %collective-permute-start.9 = (bf16[1,2,512,128]{3,2,1,0:T(8,128)(2,1)}, bf16[1,2,512,128]{3,2,1,0:T(8,128)(2,1)}, u32[]{:S(2)}, u32[]{:S(2)}) collective-permute-start(bf16[1,2,512,128]{3,2,1,0:T(8,128)(2,1)} %get-tuple-element.85), channel_id=1, source_target_pairs={{0,24},{4,28},{8,16},{12,20},{16,8},{20,12},{24,0},{28,4},{1,25},{... | collective-permute-start | bytes 786440 | tf_op jit(solution)/shard_map/ppermute | solution.py:658
  96.9 36.4 %collective-permute-start.8 = (bf16[1,2,512,128]{3,2,1,0:T(8,128)(2,1)}, bf16[1,2,512,128]{3,2,1,0:T(8,128)(2,1)}, u32[]{:S(2)}, u32[]{:S(2)}) collective-permute-start(bf16[1,2,512,128]{3,2,1,0:T(8,128)(2,1)} %get-tuple-element.86), channel_id=1, source_target_pairs={{0,20},{4,16},{8,28},{12,24},{16,4},{20,0},{24,12},{28,8},{1,21},{... | collective-permute-start | bytes 786440 | tf_op jit(solution)/shard_map/ppermute | solution.py:658
  98.0 43.0 %collective-permute-start.7 = (bf16[1,2,512,128]{3,2,1,0:T(8,128)(2,1)S(1)}, bf16[1,2,512,128]{3,2,1,0:T(8,128)(2,1)}, u32[]{:S(2)}, u32[]{:S(2)}) collective-permute-start(bf16[1,2,512,128]{3,2,1,0:T(8,128)(2,1)S(1)} %copy-done.11), channel_id=1, source_target_pairs={{0,16},{4,20},{8,24},{12,28},{16,0},{20,4},{24,8},{28,12},{1,17},{... | collective-permute-start | bytes 786440 | tf_op jit(solution)/shard_map/ppermute | solution.py:658
  98.6 42.4 %collective-permute-start.6 = (bf16[1,2,512,128]{3,2,1,0:T(8,128)(2,1)S(1)}, bf16[1,2,512,128]{3,2,1,0:T(8,128)(2,1)}, u32[]{:S(2)}, u32[]{:S(2)}) collective-permute-start(bf16[1,2,512,128]{3,2,1,0:T(8,128)(2,1)S(1)} %copy-done.10), channel_id=1, source_target_pairs={{0,12},{4,8},{8,4},{12,0},{16,28},{20,24},{24,20},{28,16},{1,13},{... | collective-permute-start | bytes 786440 | tf_op jit(solution)/shard_map/ppermute | solution.py:658
  120.0 23.2 %collective-permute-start.5 = (bf16[1,2,512,128]{3,2,1,0:T(8,128)(2,1)S(1)}, bf16[1,2,512,128]{3,2,1,0:T(8,128)(2,1)}, u32[]{:S(2)}, u32[]{:S(2)}) collective-permute-start(bf16[1,2,512,128]{3,2,1,0:T(8,128)(2,1)S(1)} %copy-done.9), channel_id=1, source_target_pairs={{0,8},{4,12},{8,0},{12,4},{16,24},{20,28},{24,16},{28,20},{1,9},{5... | collective-permute-start | bytes 786440 | tf_op jit(solution)/shard_map/ppermute | solution.py:658
  129.8 13.3 %collective-permute-start.4 = (bf16[1,2,512,128]{3,2,1,0:T(8,128)(2,1)S(1)}, bf16[1,2,512,128]{3,2,1,0:T(8,128)(2,1)}, u32[]{:S(2)}, u32[]{:S(2)}) collective-permute-start(bf16[1,2,512,128]{3,2,1,0:T(8,128)(2,1)S(1)} %get-tuple-element.90), channel_id=1, source_target_pairs={{0,4},{4,0},{8,12},{12,8},{16,20},{20,16},{24,28},{28,24},{1,5},{5... | collective-permute-start | bytes 786440 | tf_op jit(solution)/shard_map/ppermute | solution.py:658
  154.1 55.9 %all-to-all-start.3 = ((bf16[4,2,1088,128]{3,2,1,0:T(8,128)(2,1)}), bf16[4,2,1088,128]{3,2,1,0:T(8,128)(2,1)S(1)}, u32[]{:S(2)}, u32[]{:S(2)}) async-start(bf16[4,2,1088,128]{3,2,1,0:T(8,128)(2,1)} %shear_whole.1), calls=%async_computation.3 | async-start | bytes 4456448 | tf_op jit(solution)/shard_map/all_to_all | solution.py:799
  158.8 45.9 %copy-start.19 = (f32[192,256,1,1]{1,0,2,3:T(8,128)S(1)}, f32[192,256,1,1]{1,0,2,3:T(8,128)}, u32[]{:S(2)}) copy-start(f32[192,256,1,1]{1,0,2,3:T(8,128)} %constant.99) | copy-start | bytes 589828
  158.8 45.9 %copy-start.24 = (f32[256,128]{1,0:T(8,128)S(1)}, f32[256,128]{1,0:T(8,128)}, u32[]{:S(2)}) copy-start(f32[256,128]{1,0:T(8,128)} %constant.91.clone) | copy-start | bytes 393220
  165.9 3.7 %collective-permute-start.11 = (bf16[1,2,512,128]{3,2,1,0:T(8,128)(2,1)}, bf16[1,2,512,128]{3,2,1,0:T(8,128)(2,1)S(1)}, u32[]{:S(2)}, u32[]{:S(2)}) collective-permute-start(bf16[1,2,512,128]{3,2,1,0:T(8,128)(2,1)} %get-tuple-element.62), channel_id=1, source_target_pairs={{0,4},{4,0},{8,12},{12,8},{16,20},{20,16},{24,28},{28,24},{1,5},{5... | collective-permute-start | bytes 786440 | tf_op jit(solution)/shard_map/ppermute | solution.py:658
  165.9 9.4 %collective-permute-start.12 = (bf16[1,2,512,128]{3,2,1,0:T(8,128)(2,1)}, bf16[1,2,512,128]{3,2,1,0:T(8,128)(2,1)S(1)}, u32[]{:S(2)}, u32[]{:S(2)}) collective-permute-start(bf16[1,2,512,128]{3,2,1,0:T(8,128)(2,1)} %get-tuple-element.63), channel_id=1, source_target_pairs={{0,8},{4,12},{8,0},{12,4},{16,24},{20,28},{24,16},{28,20},{1,9},{5... | collective-permute-start | bytes 786440 | tf_op jit(solution)/shard_map/ppermute | solution.py:658
  167.6 12.6 %collective-permute-start.13 = (bf16[1,2,512,128]{3,2,1,0:T(8,128)(2,1)}, bf16[1,2,512,128]{3,2,1,0:T(8,128)(2,1)S(1)}, u32[]{:S(2)}, u32[]{:S(2)}) collective-permute-start(bf16[1,2,512,128]{3,2,1,0:T(8,128)(2,1)} %get-tuple-element.64), channel_id=1, source_target_pairs={{0,12},{4,8},{8,4},{12,0},{16,28},{20,24},{24,20},{28,16},{1,13},{... | collective-permute-start | bytes 786440 | tf_op jit(solution)/shard_map/ppermute | solution.py:658
  167.8 12.4 %collective-permute-start.14 = (bf16[1,2,512,128]{3,2,1,0:T(8,128)(2,1)}, bf16[1,2,512,128]{3,2,1,0:T(8,128)(2,1)S(1)}, u32[]{:S(2)}, u32[]{:S(2)}) collective-permute-start(bf16[1,2,512,128]{3,2,1,0:T(8,128)(2,1)} %get-tuple-element.65), channel_id=1, source_target_pairs={{0,16},{4,20},{8,24},{12,28},{16,0},{20,4},{24,8},{28,12},{1,17},{... | collective-permute-start | bytes 786440 | tf_op jit(solution)/shard_map/ppermute | solution.py:658
  169.6 23.2 %collective-permute-start.15 = (bf16[1,2,512,128]{3,2,1,0:T(8,128)(2,1)}, bf16[1,2,512,128]{3,2,1,0:T(8,128)(2,1)S(1)}, u32[]{:S(2)}, u32[]{:S(2)}) collective-permute-start(bf16[1,2,512,128]{3,2,1,0:T(8,128)(2,1)} %get-tuple-element.66), channel_id=1, source_target_pairs={{0,20},{4,16},{8,28},{12,24},{16,4},{20,0},{24,12},{28,8},{1,21},{... | collective-permute-start | bytes 786440 | tf_op jit(solution)/shard_map/ppermute | solution.py:658
  169.6 23.2 %collective-permute-start.16 = (bf16[1,2,512,128]{3,2,1,0:T(8,128)(2,1)}, bf16[1,2,512,128]{3,2,1,0:T(8,128)(2,1)S(1)}, u32[]{:S(2)}, u32[]{:S(2)}) collective-permute-start(bf16[1,2,512,128]{3,2,1,0:T(8,128)(2,1)} %get-tuple-element.67), channel_id=1, source_target_pairs={{0,24},{4,28},{8,16},{12,20},{16,8},{20,12},{24,0},{28,4},{1,25},{... | collective-permute-start | bytes 786440 | tf_op jit(solution)/shard_map/ppermute | solution.py:658
  175.3 17.5 %collective-permute-start.17 = (bf16[1,2,512,128]{3,2,1,0:T(8,128)(2,1)}, bf16[1,2,512,128]{3,2,1,0:T(8,128)(2,1)S(1)}, u32[]{:S(2)}, u32[]{:S(2)}) collective-permute-start(bf16[1,2,512,128]{3,2,1,0:T(8,128)(2,1)} %get-tuple-element.68), channel_id=1, source_target_pairs={{0,28},{4,24},{8,20},{12,16},{16,12},{20,8},{24,4},{28,0},{1,29},{... | collective-permute-start | bytes 786440 | tf_op jit(solution)/shard_map/ppermute | solution.py:658
  198.2 44.4 %collective-permute-start.18 = (bf16[7,2,512,128]{3,2,1,0:T(8,128)(2,1)}, bf16[7,2,512,128]{3,2,1,0:T(8,128)(2,1)}, u32[]{:S(2)}, u32[]{:S(2)}) collective-permute-start(bf16[7,2,512,128]{3,2,1,0:T(8,128)(2,1)} %get-tuple-element.69), channel_id=1, source_target_pairs={{0,1},{1,2},{2,3},{4,5},{5,6},{6,7},{8,9},{9,10},{10,11},{12,13},{... | collective-permute-start | bytes 5505032 | tf_op jit(solution)/shard_map/ppermute | solution.py:613
  203.3 45.4 %collective-permute-start.19 = (bf16[7,2,512,128]{3,2,1,0:T(8,128)(2,1)}, bf16[7,2,512,128]{3,2,1,0:T(8,128)(2,1)}, u32[]{:S(2)}, u32[]{:S(2)}) collective-permute-start(bf16[7,2,512,128]{3,2,1,0:T(8,128)(2,1)} %get-tuple-element.70), channel_id=1, source_target_pairs={{1,0},{2,1},{3,2},{5,4},{6,5},{7,6},{9,8},{10,9},{11,10},{13,12},{... | collective-permute-start | bytes 5505032 | tf_op jit(solution)/shard_map/ppermute | solution.py:613
  219.9 6.8 %collective-permute-start.20 = (bf16[2,32,1024]{2,1,0:T(8,128)(2,1)}, bf16[2,32,1024]{2,1,0:T(8,128)(2,1)S(1)}, u32[]{:S(2)}, u32[]{:S(2)}) collective-permute-start(bf16[2,32,1024]{2,1,0:T(8,128)(2,1)} %get-tuple-element.71), channel_id=1, source_target_pairs={{0,4},{4,8},{8,12},{12,16},{16,20},{20,24},{24,28},{1,5},{5,9},{9,... | collective-permute-start | bytes 393224 | tf_op jit(solution)/shard_map/ppermute | solution.py:613
  221.8 6.4 %collective-permute-start.21 = (bf16[2,32,1024]{2,1,0:T(8,128)(2,1)}, bf16[2,32,1024]{2,1,0:T(8,128)(2,1)S(1)}, u32[]{:S(2)}, u32[]{:S(2)}) collective-permute-start(bf16[2,32,1024]{2,1,0:T(8,128)(2,1)} %get-tuple-element.73), channel_id=1, source_target_pairs={{4,0},{8,4},{12,8},{16,12},{20,16},{24,20},{28,24},{5,1},{9,5},{13... | collective-permute-start | bytes 393224 | tf_op jit(solution)/shard_map/ppermute | solution.py:613
  261.5 5.6 %collective-permute-start.23 = (bf16[8,2,32,128]{3,2,1,0:T(8,128)(2,1)S(1)}, bf16[8,2,32,128]{3,2,1,0:T(8,128)(2,1)S(1)}, u32[]{:S(2)}, u32[]{:S(2)}) collective-permute-start(bf16[8,2,32,128]{3,2,1,0:T(8,128)(2,1)S(1)} %get-tuple-element.82), channel_id=1, source_target_pairs={{4,0},{8,4},{12,8},{16,12},{20,16},{24,20},{28,24},{5,1},{9,5},{13... | collective-permute-start | bytes 393224 | tf_op jit(solution)/shard_map/ppermute | solution.py:613
  264.4 6.3 %collective-permute-start.22 = (bf16[8,2,32,128]{3,2,1,0:T(8,128)(2,1)S(1)}, bf16[8,2,32,128]{3,2,1,0:T(8,128)(2,1)S(1)}, u32[]{:S(2)}, u32[]{:S(2)}) collective-permute-start(bf16[8,2,32,128]{3,2,1,0:T(8,128)(2,1)S(1)} %get-tuple-element.83), channel_id=1, source_target_pairs={{0,4},{4,8},{8,12},{12,16},{16,20},{20,24},{24,28},{1,5},{5,9},{9,... | collective-permute-start | bytes 393224 | tf_op jit(solution)/shard_map/ppermute | solution.py:613
  275.5 4.1 %collective-permute-start.24 = (bf16[2,32,512]{2,1,0:T(8,128)(2,1)}, bf16[2,32,512]{2,1,0:T(8,128)(2,1)S(1)}, u32[]{:S(2)}, u32[]{:S(2)}) collective-permute-start(bf16[2,32,512]{2,1,0:T(8,128)(2,1)} %get-tuple-element.77), channel_id=1, source_target_pairs={{0,1},{1,2},{2,3},{4,5},{5,6},{6,7},{8,9},{9,10},{10,11},{12,13},{... | collective-permute-start | bytes 196616 | tf_op jit(solution)/shard_map/ppermute | solution.py:613
  277.4 6.4 %collective-permute-start.25 = (bf16[2,32,512]{2,1,0:T(8,128)(2,1)}, bf16[2,32,512]{2,1,0:T(8,128)(2,1)S(1)}, u32[]{:S(2)}, u32[]{:S(2)}) collective-permute-start(bf16[2,32,512]{2,1,0:T(8,128)(2,1)} %get-tuple-element.79), channel_id=1, source_target_pairs={{1,0},{2,1},{3,2},{5,4},{6,5},{7,6},{9,8},{10,9},{11,10},{13,12},{... | collective-permute-start | bytes 196616 | tf_op jit(solution)/shard_map/ppermute | solution.py:613
  (28 other events, 242.9 us)
